TPU v7x, 256 devices: a whole 4x4x8 slice. The times are simulated.
256 devices in a mesh: cache: 16 (over y_lo, x, core), head: 16 (over z, y_hi).
Axes of the slice: x: 4, y: 4 (y_hi: 2, y_lo: 2; y = y_hi * 2 + y_lo), z: 8, core: 2. Of those that a mesh axis runs over, the one named last changes fastest.
Arguments:
- q_nope: bfloat16 [2048, 8192], P('cache', 'head'), may hold values from -6 to 6
- q_rope: bfloat16 [2048, 4096], P('cache', 'head'), may hold values from -8 to 8
- new_latent: bfloat16 [2048, 512], P('cache'), may hold values from -6 to 6
- new_rope: bfloat16 [16, 64, 128], P('cache'), may hold values from -6 to 6
- pool_latent: bfloat16 [64, 128, 512], P('cache'), may hold values from -6 to 6
- pool_rope: bfloat16 [64, 64, 128], P('cache'), may hold values from -8 to 8
- block_table: int32 [16, 32], replicated, may hold values from 0 to 63, as said below
- prefix_len: int32 [16], replicated, may hold values from 1025 to 4096
- w_uk: bfloat16 [64, 128, 512], P('head'), may hold values from -0.5 to 0.5
- w_uv: bfloat16 [64, 512, 128], P('head'), may hold values from -4 to 4
- w_out: bfloat16 [8192, 7168], P('head', 'cache'), may hold values from -0.0625 to 0.0625
Outputs:
- attended: bfloat16 [2048, 7168], P(('cache', 'head'))
Inputs may be any that keep to these rules, and one draw needn't show every extreme that they name: `block_table`: row r lists the pool blocks that hold request r's prefix, in order; a row names a block at most once; the first 8 entries are the same in every row.
All inputs are finite; a program needn't handle non-finite values.
Results may differ from a plain program's by a relative error of at most 0.02.
Values may be sent and summed in bfloat16 or wider, within the bound.
No kernel may reach another device: no remote copies, remote signals or barrier semaphores. Data moves between devices by JAX's collectives and lax.ppermute only.
A program may use at most 128 MiB of HBM per device.

v0:
```python
import jax
import jax.numpy as jnp
from jax import lax
from jax.sharding import PartitionSpec as P

LAT = 512
NOPE = 128
ROPE = 64
VD = 128
BLOCK = 128


masked_score = -1e30


def local(
    q_nope,
    q_rope,
    new_latent,
    new_rope,
    pool_latent,
    pool_rope,
    block_table,
    prefix_len,
    w_uk,
    w_uv,
    w_out,
):
    softmax_scale = (NOPE + ROPE) ** (-0.5)
    head_count = w_uk.shape[0]
    tok_rows = q_nope.shape[0]
    q_lat = jnp.einsum(
        "thn,hnc->thc",
        q_nope.reshape(tok_rows, head_count, NOPE),
        w_uk,
        preferred_element_type=jnp.float32,
    ).astype(jnp.bfloat16)
    q_rot = q_rope.reshape(tok_rows, head_count, ROPE)

    def score_of(key_rows, rotary):
        latent_part = jnp.einsum("thc,kc->thk", q_lat, key_rows, preferred_element_type=jnp.float32)
        rotary_part = jnp.einsum("thr,rk->thk", q_rot, rotary, preferred_element_type=jnp.float32)
        return (latent_part + rotary_part) * softmax_scale

    own_rotary = jnp.transpose(new_rope, (1, 0, 2)).reshape(ROPE, tok_rows)
    own_scores = score_of(new_latent, own_rotary)
    causal = (jnp.arange(tok_rows)[None, :] <= jnp.arange(tok_rows)[:, None])[:, None, :]
    highest = jnp.max(jnp.where(causal, own_scores, masked_score), axis=-1)
    weights = jnp.where(causal, jnp.exp(own_scores - highest[..., None]), 0.0)
    totals = jnp.sum(weights, axis=-1)
    summed = jnp.einsum(
        "thk,kc->thc", weights.astype(jnp.bfloat16), new_latent, preferred_element_type=jnp.float32
    )
    request = lax.axis_index("cache")
    table_row = block_table[request]
    limit_len = prefix_len[request]
    table_slots = jnp.arange(table_row.shape[0], dtype=jnp.int32)
    sums = totals
    latent_sum = summed
    latent = lax.all_gather(pool_latent, "cache", axis=0, tiled=True)
    rotary = lax.all_gather(pool_rope, "cache", axis=0, tiled=True)
    blocks = latent.shape[0]
    block_ids = jnp.arange(blocks, dtype=jnp.int32)
    matches = table_row[None, :] == block_ids[:, None]
    present = jnp.any(matches, axis=1)
    offset = jnp.sum(jnp.where(matches, table_slots[None, :], 0), axis=1)
    positions = offset[:, None] * BLOCK + jnp.arange(BLOCK, dtype=jnp.int32)[None, :]
    allowed = (present[:, None] & (positions < limit_len)).reshape(blocks * BLOCK)
    key_rows = latent.reshape(blocks * BLOCK, LAT)
    key_rotary = jnp.transpose(rotary, (1, 0, 2)).reshape(ROPE, blocks * BLOCK)
    scores = score_of(key_rows, key_rotary)
    new_best = jnp.maximum(highest, jnp.max(jnp.where(allowed, scores, masked_score), axis=-1))
    factor = jnp.exp(highest - new_best)
    piece_weights = jnp.where(allowed, jnp.exp(scores - new_best[..., None]), 0.0)
    sums = sums * factor + jnp.sum(piece_weights, axis=-1)
    latent_sum = latent_sum * factor[..., None] + jnp.einsum(
        "thk,kc->thc",
        piece_weights.astype(jnp.bfloat16),
        key_rows,
        preferred_element_type=jnp.float32,
    )
    latent_out = (latent_sum / sums[..., None]).astype(jnp.bfloat16)
    head_out = jnp.einsum("thc,hcv->thv", latent_out, w_uv, preferred_element_type=jnp.float32)
    head_out = head_out.astype(jnp.bfloat16).reshape(tok_rows, head_count * VD)
    partials = jnp.dot(
        head_out,
        lax.all_gather(w_out, "cache", axis=1, tiled=True),
        preferred_element_type=jnp.float32,
    )
    return lax.psum_scatter(partials.astype(jnp.bfloat16), "head", scatter_dimension=0, tiled=True)


def solution(mesh):
    return jax.shard_map(
        local,
        mesh=mesh,
        in_specs=(
            P("cache", "head"),
            P("cache", "head"),
            P("cache", None),
            P("cache", None, None),
            P("cache", None, None),
            P("cache", None, None),
            P(),
            P(),
            P("head", None, None),
            P("head", None, None),
            P("head", "cache"),
        ),
        out_specs=P(("cache", "head"), None),
        check_vma=False,
    )
```

profile of v0, /device:TPU:6, one launch (start us, length us, event | category | flops | bytes accessed | tf_op | source)
XLA Modules:
  0.0 377.4 jit_solution(16166856860694811971)
XLA Ops:
  6.5 0.0 copy-start
  6.5 0.0 all-gather.6.cloned.1.call-start
  6.5 0.7 all-gather.6.cloned.1.call-update
  7.3 0.0 all-gather.4.cloned.1.call-start
  7.3 0.7 all-gather.4.cloned.1.call-update
  8.0 0.0 all-gather.8.cloned.1.call-start
  8.1 0.7 all-gather.8.cloned.1.call-update
  8.7 0.0 reduce-scatter.2.cloned.1.call-start
  8.8 0.9 copy.38
  9.7 1.2 dynamic_slice.7
  11.0 0.7 dynamic-slice_bitcast_fusion
  11.7 0.1 select_reduce_fusion.2
  11.8 0.1 fusion.35
  11.9 0.9 fusion.33
  12.8 0.0 copy-done
  12.8 1.3 fusion.11
  14.1 1.2 select_reduce_fusion.1
  15.3 0.1 fusion.16
  15.3 0.7 fusion.32
  16.1 30.1 %all-gather.6.cloned.1.call-done = bf16[64,64,128]{2,1,0:T(8,128)(2,1)} async-done(((bf16[4,64,128]{2,1,0:T(8,128)(2,1)}), bf16[64,64,128]{2,1,0:T(8,128)(2,1)}) %all-gather.6.cloned.1.call-update) | async-done | bytes 1048592 | tf_op jit(solution)/shard_map/all_gather | solution.py:61
  46.2 1.9 copy.41
  48.1 0.5 reshape.69
  48.6 55.1 %all-gather.4.cloned.1.call-done = bf16[64,128,512]{2,1,0:T(8,128)(2,1)} async-done(((bf16[4,128,512]{2,1,0:T(8,128)(2,1)}), bf16[64,128,512]{2,1,0:T(8,128)(2,1)}) %all-gather.4.cloned.1.call-update) | async-done | bytes 8388624 | tf_op jit(solution)/shard_map/all_gather | solution.py:60
  103.7 11.5 %fusion.39 = f32[128,4,8192]{2,0,1:T(8,128)} fusion(bf16[128,4,512]{0,2,1:T(8,128)(2,1)S(1)} %fusion.11, bf16[8192,512,1]{1,0,2:T(8,128)(2,1)} %bitcast.45), kind=kOutput, calls=%fused_computation.48 | convolution fusion | flops 4294967296 | bytes 25690112 | tf_op jit(solution)/shard_map/thc,kc->thk/dot_general | solution.py:41
  115.2 11.0 %select_reduce_fusion = (f32[128,4]{0,1:T(4,128)S(1)}, f32[128,4,8192]{2,0,1:T(8,128)}) fusion(pred[8192]{0:T(1024)(128)(4,1)S(1)} %fusion.32, f32[128,4,8192]{2,0,1:T(8,128)} %fusion.39, bf16[128,4,64]{0,2,1:T(8,128)(2,1)S(1)} %bitcast.48, bf16[64,8192,1]{1,0,2:T(8,128)(2,1)S(1)} %reshape.69), kind=kOutput, calls=%fused_computation.1 | convolution fusion | flops 553647616 | bytes 34678784 | tf_op jit(solution)/shard_map/thr,rk->thk/dot_general | solution.py:42
  126.2 9.4 %fusion = f32[128,4]{0,1:T(4,128)S(1)} fusion(f32[128,4,8192]{2,0,1:T(8,128)} %get-tuple-element.10, f32[128,4]{0,1:T(4,128)S(1)} %max.13, pred[8192]{0:T(1024)(128)(4,1)S(1)} %fusion.32), kind=kLoop, calls=%fused_computation.3 | loop fusion | flops 12582400 | bytes 16789504 | tf_op jit(solution)/shard_map/reduce_sum | solution.py:75
  135.6 0.0 copy-start.1
  135.6 0.0 copy-start.2
  135.6 11.1 %fusion.2 = f32[128,4,512]{2,0,1:T(8,128)S(1)} fusion(bf16[8192,512,1]{1,0,2:T(8,128)(2,1)} %bitcast.46, f32[128,4,8192]{2,0,1:T(8,128)} %get-tuple-element.10, f32[128,4]{0,1:T(4,128)S(1)} %max.13, pred[8192]{0:T(1024)(128)(4,1)S(1)} %fusion.32), kind=kOutput, calls=%fused_computation.6 | convolution fusion | flops 4307550208 | bytes 26224640 | tf_op jit(solution)/shard_map/thk,kc->thc/dot_general | solution.py:76
  146.7 0.0 copy-done.1
  146.8 0.0 copy-done.2
  146.8 0.6 fusion.13
  147.4 8.8 %all-gather.8.cloned.1.call-done = bf16[512,7168]{0,1:T(8,128)(2,1)} async-done(((bf16[512,448]{0,1:T(8,128)(2,1)}), bf16[512,7168]{0,1:T(8,128)(2,1)}) %all-gather.8.cloned.1.call-update) | async-done | bytes 7340048 | tf_op jit(solution)/shard_map/all_gather | solution.py:87
  156.2 6.8 %convolution_convert_fusion = bf16[128,7168]{1,0:T(8,128)(2,1)} fusion(bf16[128,512]{0,1:T(8,128)(2,1)S(1)} %bitcast.50, bf16[512,7168]{0,1:T(8,128)(2,1)} %all-gather.8.cloned.1.call-done), kind=kOutput, calls=%fused_computation.5 | convolution fusion | flops 940441600 | bytes 9306112 | tf_op jit(solution)/shard_map/dot_general | solution.py:85
  163.0 0.0 reduce-scatter.2.cloned.1.call-update
  163.1 207.8 %reduce-scatter.2.cloned.1.call-done = bf16[8,7168]{1,0:T(8,128)(2,1)} async-done(((bf16[128,7168]{1,0:T(8,128)(2,1)}), bf16[8,7168]{1,0:T(8,128)(2,1)}) %reduce-scatter.2.cloned.1.call-update) | async-done | bytes 114704 | tf_op jit(solution)/shard_map/reduce_scatter | solution.py:90
  (4 shorter events, 0.0 us)
Async XLA Ops:
  6.5 6.3 %copy-start = (bf16[4,128,512]{2,1,0:T(8,128)(2,1)S(1)}, bf16[4,128,512]{2,1,0:T(8,128)(2,1)}, u32[]{:S(2)}) copy-start(bf16[4,128,512]{2,1,0:T(8,128)(2,1)} %param.19) | copy-start | bytes 1572868
  6.5 39.7 %all-gather.6.cloned.1.call-start = ((), (), s32[]{:S(2)}) async-start(), calls=%async_computation.2 | async-start | bytes 1114112 | tf_op jit(solution)/shard_map/all_gather | solution.py:61
  7.3 96.4 %all-gather.4.cloned.1.call-start = ((), (), s32[]{:S(2)}) async-start(), calls=%async_computation.1 | async-start | bytes 8912896 | tf_op jit(solution)/shard_map/all_gather | solution.py:60
  8.0 148.2 %all-gather.8.cloned.1.call-start = ((), (), s32[]{:S(2)}) async-start(), calls=%async_computation.3 | async-start | bytes 7798784 | tf_op jit(solution)/shard_map/all_gather | solution.py:87
  8.7 362.1 %reduce-scatter.2.cloned.1.call-start = ((), (), s32[]{:S(2)}) async-start(), calls=%async_computation.4 | async-start | bytes 1949696 | tf_op jit(solution)/shard_map/reduce_scatter | solution.py:90
  135.6 11.2 %copy-start.1 = (bf16[128,512]{1,0:T(8,128)(2,1)S(1)}, bf16[128,512]{1,0:T(8,128)(2,1)}, u32[]{:S(2)}) copy-start(bf16[128,512]{1,0:T(8,128)(2,1)} %param.13) | copy-start | bytes 393220
  135.6 11.2 %copy-start.2 = (bf16[4,512,128]{2,1,0:T(8,128)(2,1)S(1)}, bf16[4,512,128]{2,1,0:T(8,128)(2,1)}, u32[]{:S(2)}) copy-start(bf16[4,512,128]{2,1,0:T(8,128)(2,1)} %param.20) | copy-start | bytes 1572868
Sparse Core Ops, SparseCore 0:
  9.2 36.9 all-gather.5
  48.1 55.5 all-gather.3
  105.5 50.6 all-gather.7
  163.2 207.6 reduce-scatter.1
where the time goes:
time: 378 us; the launch traced here: 377 us
  waiting for transfers between devices  304 us (80%)
  matrix products  44.5 us (12%)
  between operations  13.2 us (3%)
  other arithmetic  10.4 us (3%)
  local copies, waits for them, and re-layouts  5.3 us (1%)
    reduce_scatter x1, waiting for transfers between devices, local(): lax.psum_scatter(partials.astype(jnp.bfloat16), 'head', scatter_dimension...  208 us
    all_gather x1, waiting for transfers between devices, local(): latent = lax.all_gather(pool_latent, 'cache', axis=0, tiled=True)  55.1 us
    all_gather x1, waiting for transfers between devices, local(): rotary = lax.all_gather(pool_rope, 'cache', axis=0, tiled=True)  30.1 us
    dot_general x2, matrix products, score_of(): jnp.einsum('thc,kc->thk', q_lat, key_rows, preferred_element_type=jnp.flo...  12.7 us
    dot_general x2, matrix products, score_of(): jnp.einsum('thr,rk->thk', q_rot, rotary, preferred_element_type=jnp.float32)  11.9 us
    dot_general x1, matrix products, local(): jnp.einsum('thk,kc->thc', piece_weights.astype(jnp.bfloat16), key_rows, p...  11.1 us
    reduce_sum x1, other arithmetic, local(): sums = sums * factor + jnp.sum(piece_weights, axis=-1)  9.38 us
    all_gather x1, waiting for transfers between devices, local(): lax.all_gather(w_out, 'cache', axis=1, tiled=True)  8.79 us
  transfers between devices with their start and end apart: 4, of which 4 were waited for; matrix products, arithmetic and copies ran while one was open for 14% of the time, Pallas kernels for 0%

commit v1 on v0

v1 whole, which is shorter than its diff:
```python
import functools

import jax
import jax.numpy as jnp
from jax import lax
from jax.experimental import pallas as pl
from jax.experimental.pallas import tpu as pltpu
from jax.sharding import Mesh, PartitionSpec as P

LAT = 512
NOPE = 128
ROPE = 64
VD = 128
BLOCK = 128
HEADS = 4
TOK = 128
ROWS = HEADS * TOK
SLOTS = 4
LOG2E = 1.4426950408889634
SCALE2 = (NOPE + ROPE) ** -0.5 * LOG2E
LOW = -1e30
STAT = HEADS * VD
MSG = STAT + 128

VMEM = pltpu.VMEM
SMEM = pltpu.SMEM


def dot_nn(a, b):
    return lax.dot_general(a, b, (((1,), (0,)), ((), ())), preferred_element_type=jnp.float32)


def dot_nt(a, b):
    return lax.dot_general(a, b, (((1,), (1,)), ((), ())), preferred_element_type=jnp.float32)


def attention_kernel(slots, own, ids, table, lens, *refs):
    count = len(slots)
    refs = list(refs)

    def take(n):
        got = refs[:n]
        del refs[:n]
        return got

    queries = take(count)
    pools = take(4)
    w_uk, w_uv = take(2)
    new_latent, new_rope = take(2) if own else (None, None)
    outs = take(count)
    keys, rots, sems, q_lat, q_rot, acc, top, tot = refs
    yl, x, k = ids[0], ids[1], ids[2]

    def fetch(s, src, i, at):
        chunk, half = at // 2, pl.multiple_of((at % 2) * BLOCK, BLOCK)
        return (
            pltpu.make_async_copy(
                src.at[pl.ds(pl.multiple_of(i * BLOCK, BLOCK), BLOCK), :],
                keys.at[s, chunk, pl.ds(half, BLOCK), :],
                sems.at[s, at, 0],
            ),
            pltpu.make_async_copy(
                src.at[pl.ds(4 * BLOCK, ROPE), pl.ds(pl.multiple_of(i * BLOCK, BLOCK), BLOCK)],
                rots.at[s, chunk, :, pl.ds(half, BLOCK)],
                sems.at[s, at, 1],
            ),
        )

    counts, totals = [], []
    for s, slot in enumerate(slots):
        request = yl * 8 + ((x + slot) % 4) * 2 + k
        limit = lens[request]

        def scan(m, carry):
            found, valid = carry
            block = table[request, m]
            owner, i = block >> 2, block & 3
            here = jnp.logical_and(m * BLOCK < limit, ((owner >> 1) & 3) == x)
            source = ((owner >> 3) ^ yl) + 2 * ((owner & 1) ^ k)
            for j in range(4):

                @pl.when(jnp.logical_and(here, source == j))
                def _():
                    for copy in fetch(s, pools[j], i, found):
                        copy.start()

            step = here.astype(jnp.int32)
            return found + step, valid + step * jnp.minimum(limit - m * BLOCK, BLOCK)

        found, valid = lax.fori_loop(0, 32, scan, (jnp.int32(0), jnp.int32(0)))
        counts.append(found)
        totals.append(valid)

        @pl.when(found % 2 == 1)
        def _():
            keys[s, found // 2, BLOCK:, :] = jnp.zeros((BLOCK, LAT), jnp.bfloat16)
            rots[s, found // 2, :, BLOCK:] = jnp.zeros((ROPE, BLOCK), jnp.bfloat16)

    for s in range(count):
        for h in range(HEADS):
            rows = slice(h * TOK, (h + 1) * TOK)
            q_lat[rows, :] = dot_nn(queries[s][:, h * NOPE : (h + 1) * NOPE], w_uk[h]).astype(jnp.bfloat16)
            first = HEADS * NOPE + h * ROPE
            q_rot[rows, :] = queries[s][:, first : first + ROPE]
        if own:
            for g in range(2):
                rows = slice(g * 256, (g + 1) * 256)
                fresh = new_latent[...]
                score = dot_nt(q_lat[rows, :], fresh) + dot_nn(q_rot[rows, :], new_rope[...])
                at = lax.broadcasted_iota(jnp.int32, score.shape, 0) % TOK
                seen = lax.broadcasted_iota(jnp.int32, score.shape, 1) <= at
                score = jnp.where(seen, score, LOW)
                best = jnp.broadcast_to(jnp.max(score, axis=1, keepdims=True), (256, 128))
                weight = jnp.exp2((score - best) * SCALE2)
                top[rows, :] = best
                tot[rows, :] = weight
                acc[rows, :] = dot_nn(weight.astype(jnp.bfloat16), fresh)
        else:
            top[...] = jnp.full((ROWS, 128), LOW, jnp.float32)
            tot[...] = jnp.zeros((ROWS, 128), jnp.float32)
            acc[...] = jnp.zeros((ROWS, LAT), jnp.float32)

        def step(chunk, carry):
            for copy in fetch(s, pools[0], 0, chunk * 2):
                copy.wait()

            @pl.when(chunk * 2 + 1 < counts[s])
            def _():
                for copy in fetch(s, pools[0], 0, chunk * 2 + 1):
                    copy.wait()

            left = totals[s] - chunk * 2 * BLOCK
            for g in range(2):
                rows = slice(g * 256, (g + 1) * 256)
                latent = keys[s, chunk]
                score = dot_nt(q_lat[rows, :], latent) + dot_nn(q_rot[rows, :], rots[s, chunk])
                seen = lax.broadcasted_iota(jnp.int32, score.shape, 1) < left
                score = jnp.where(seen, score, LOW)
                before = top[rows, :]
                best = jnp.maximum(before, jnp.max(score, axis=1, keepdims=True))
                keep = jnp.exp2((before - best) * SCALE2)
                weight = jnp.exp2((score - jnp.concatenate([best, best], axis=1)) * SCALE2)
                top[rows, :] = best
                tot[rows, :] = tot[rows, :] * keep + weight[:, :128] + weight[:, 128:]
                acc[rows, :] = acc[rows, :] * jnp.concatenate([keep] * 4, axis=1) + dot_nn(
                    weight.astype(jnp.bfloat16), latent
                )
            return carry

        lax.fori_loop(0, (counts[s] + 1) // 2, step, 0)

        lane = lax.broadcasted_iota(jnp.int32, (TOK, 128), 1)
        stat = jnp.zeros((TOK, 128), jnp.float32)
        for h in range(HEADS):
            rows = slice(h * TOK, (h + 1) * TOK)
            total = jnp.broadcast_to(jnp.sum(tot[rows, :], axis=1, keepdims=True), (TOK, 128))
            some = total > 0.0
            safe = jnp.where(some, total, 1.0)
            inverse = 1.0 / safe
            latent_out = (acc[rows, :] * jnp.concatenate([inverse] * 4, axis=1)).astype(jnp.bfloat16)
            outs[s][:, h * VD : (h + 1) * VD] = dot_nn(latent_out, w_uv[h]).astype(jnp.bfloat16)
            level = jnp.where(some, top[rows, :] * SCALE2 + jnp.log2(safe), LOW)
            high = level.astype(jnp.bfloat16).astype(jnp.float32)
            middle = (level - high).astype(jnp.bfloat16).astype(jnp.float32)
            low = level - high - middle
            stat = jnp.where(lane == h, high, stat)
            stat = jnp.where(lane == HEADS + h, middle, stat)
            stat = jnp.where(lane == 2 * HEADS + h, low, stat)
        outs[s][:, STAT:] = stat.astype(jnp.bfloat16)


def attention(slots, own, ids, table, lens, queries, pools, w_uk, w_uv, fresh):
    count = len(slots)
    full = pl.BlockSpec(memory_space=VMEM)
    scalar = pl.BlockSpec(memory_space=SMEM)
    return pl.pallas_call(
        functools.partial(attention_kernel, slots, own),
        out_shape=[jax.ShapeDtypeStruct((TOK, MSG), jnp.bfloat16)] * count,
        in_specs=[scalar] * 3
        + [full] * count
        + [pl.BlockSpec(memory_space=pl.ANY)] * 4
        + [full] * (4 if own else 2),
        out_specs=[full] * count,
        scratch_shapes=[
            pltpu.VMEM((count, 8, 2 * BLOCK, LAT), jnp.bfloat16),
            pltpu.VMEM((count, 8, ROPE, 2 * BLOCK), jnp.bfloat16),
            pltpu.SemaphoreType.DMA((count, 16, 2)),
            pltpu.VMEM((ROWS, LAT), jnp.bfloat16),
            pltpu.VMEM((ROWS, ROPE), jnp.bfloat16),
            pltpu.VMEM((ROWS, LAT), jnp.float32),
            pltpu.VMEM((ROWS, 128), jnp.float32),
            pltpu.VMEM((ROWS, 128), jnp.float32),
        ],
        compiler_params=pltpu.CompilerParams(vmem_limit_bytes=40 * 2**20),
        cost_estimate=pl.CostEstimate(
            flops=count * 2 * ROWS * 1024 * 1088, bytes_accessed=count * 2**21, transcendentals=count * ROWS * 1024
        ),
        name="attend",
    )(ids, table, lens, *queries, *pools, w_uk, w_uv, *fresh)


def combine_kernel(*refs):
    parts, out = refs[:SLOTS], refs[SLOTS]
    stats = [p[:, STAT:].astype(jnp.float32) for p in parts]
    for h in range(HEADS):
        columns = slice(h * VD, (h + 1) * VD)
        levels = [
            s[:, h : h + 1] + s[:, HEADS + h : HEADS + h + 1] + s[:, 2 * HEADS + h : 2 * HEADS + h + 1]
            for s in stats
        ]
        best = functools.reduce(jnp.maximum, levels)
        shares = [jnp.exp2(v - best) for v in levels]
        inverse = 1.0 / sum(shares)
        out[:, columns] = sum(
            p[:, columns].astype(jnp.float32) * (share * inverse) for p, share in zip(parts, shares)
        ).astype(jnp.bfloat16)


def project_kernel(ids, *refs):
    heads, mine, other = refs[:8], refs[8:12], refs[12:16]
    outs = refs[16:20]
    weights, sems, stacked, total = refs[20:]
    yl, x, k, zb, a = ids[0], ids[1], ids[2], ids[3], ids[4]
    copies = []
    for j in range(4):
        for side, pieces in enumerate((mine, other)):
            first = pl.multiple_of((k ^ side) * 448, 64)
            copy = pltpu.make_async_copy(pieces[j], weights.at[j, pl.ds(first, 448), :], sems.at[j, side])
            copy.start()
            copies.append(copy)
    for m in range(8):
        stacked[a ^ (m & 3), pl.ds(pl.multiple_of((yl ^ (m >> 2)) * TOK, TOK), TOK), :] = heads[m][...]
    for copy in copies:
        copy.wait()
    value = None
    for j in range(4):
        part = dot_nt(stacked[(x + j) % 4], weights[j])
        value = part if value is None else value + part
    total[...] = value
    for d in range(4):
        first = pl.multiple_of(((zb + d) % 4) * 32, 32)
        for half in range(2):
            outs[d][half * 32 : (half + 1) * 32, :] = total[pl.ds(first + half * TOK, 32), :].astype(jnp.bfloat16)


def share_kernel(ids, *refs):
    parts, outs, total = refs[:4], refs[4:12], refs[12]
    yl, a = ids[0], ids[4]
    total[...] = sum(p[...].astype(jnp.float32) for p in parts)
    for m in range(8):
        first = (yl ^ (m >> 2)) * 32 + (a ^ (m & 3)) * 8
        outs[m][...] = total[pl.ds(pl.multiple_of(first, 8), 8), :]


def place_kernel(ids, *refs):
    parts, out = refs[:8], refs[8]
    yl, a = ids[0], ids[4]
    for m in range(8):
        first = ((yl ^ (m >> 2)) * 4 + (a ^ (m & 3))) * 896
        out[:, pl.ds(pl.multiple_of(first, 128), 896)] = parts[m][...].astype(jnp.bfloat16)


def simple(kernel, name, out_shape, args, scratch=(), any_from=None):
    full = pl.BlockSpec(memory_space=VMEM)
    specs = [
        pl.BlockSpec(memory_space=SMEM)
        if arg.dtype == jnp.int32
        else pl.BlockSpec(memory_space=pl.ANY)
        if any_from is not None and i >= any_from
        else full
        for i, arg in enumerate(args)
    ]
    return pl.pallas_call(
        kernel,
        out_shape=out_shape,
        in_specs=specs,
        out_specs=jax.tree.map(lambda _: full, out_shape),
        scratch_shapes=scratch,
        compiler_params=pltpu.CompilerParams(vmem_limit_bytes=40 * 2**20),
        name=name,
    )(*args)


GROUP = ("yl", "z0", "yh")


def turn(value, axis, size, shift):
    return lax.ppermute(value, axis, [((i + shift) % size, i) for i in range(size)])


def flip(value, axis, size, bits):
    return lax.ppermute(value, axis, [(i, i ^ bits) for i in range(size)])


def local(
    q_nope,
    q_rope,
    new_latent,
    new_rope,
    pool_latent,
    pool_rope,
    block_table,
    prefix_len,
    w_uk,
    w_uv,
    w_out,
):
    ids = jnp.stack(
        [
            lax.axis_index("yl"),
            lax.axis_index("x"),
            lax.axis_index("k"),
            lax.axis_index("zb"),
            lax.axis_index("z0") * 2 + lax.axis_index("yh"),
        ]
    ).astype(jnp.int32)
    query = jnp.concatenate([q_nope, q_rope], axis=1)
    pool = jnp.concatenate(
        [pool_latent.reshape(4 * BLOCK, LAT), jnp.transpose(pool_rope, (1, 0, 2)).reshape(ROPE, 4 * BLOCK)], axis=0
    )
    weight = w_out.T

    pool_y = flip(pool, "yl", 2, 1)
    queries = [turn(query, "x", 4, s) for s in (1, 2, 3)]
    pool_k = flip(pool, "k", 2, 1)
    pool_yk = flip(pool_y, "k", 2, 1)
    pools = [pool, pool_y, pool_k, pool_yk]

    turned = lax.ppermute(
        weight, ("x", "z0", "yh"), [(i * 4 + j, j * 4 + i) for i in range(4) for j in range(4)]
    )
    mine = [turned] + [turn(turned, "x", 4, s) for s in (1, 2, 3)]
    other = [flip(w, "k", 2, 1) for w in mine]

    away = attention((1, 2, 3), False, ids, block_table, prefix_len, queries, pools, w_uk, w_uv, ())
    came = [
        lax.ppermute(part, "x", [(i, (i + s) % 4) for i in range(4)]) for s, part in zip((1, 2, 3), away)
    ]
    (home,) = attention(
        (0,), True, ids, block_table, prefix_len, [query], pools, w_uk, w_uv, (new_latent, new_rope[0])
    )
    head_out = simple(
        combine_kernel, "combine", jax.ShapeDtypeStruct((TOK, HEADS * VD), jnp.bfloat16), [home, *came]
    )
    heads = [head_out] + [flip(head_out, GROUP, 8, m) for m in range(1, 8)]
    partial = simple(
        project_kernel,
        "project",
        [jax.ShapeDtypeStruct((64, 896), jnp.bfloat16)] * 4,
        [ids, *heads, *mine, *other],
        scratch=[
            pltpu.VMEM((4, 896, 512), jnp.bfloat16),
            pltpu.SemaphoreType.DMA((4, 2)),
            pltpu.VMEM((4, 256, 512), jnp.bfloat16),
            pltpu.VMEM((256, 896), jnp.float32),
        ],
        any_from=9,
    )
    sums = [partial[0]] + [
        lax.ppermute(partial[d], "zb", [(i, (i + d) % 4) for i in range(4)]) for d in (1, 2, 3)
    ]
    pieces = simple(
        share_kernel,
        "share",
        [jax.ShapeDtypeStruct((8, 896), jnp.float32)] * 8,
        [ids, *sums],
        scratch=[pltpu.VMEM((64, 896), jnp.float32)],
    )
    pieces = [pieces[0]] + [flip(pieces[m], GROUP, 8, m) for m in range(1, 8)]
    return simple(place_kernel, "place", jax.ShapeDtypeStruct((8, 7168), jnp.bfloat16), [ids, *pieces])


def solution(mesh):
    fine = Mesh(mesh.devices.reshape(2, 4, 2, 4, 2, 2), ("yl", "x", "k", "zb", "z0", "yh"))
    cache, head = ("yl", "x", "k"), ("zb", "z0", "yh")
    return jax.shard_map(
        local,
        mesh=fine,
        in_specs=(
            P(cache, head),
            P(cache, head),
            P(cache, None),
            P(cache, None, None),
            P(cache, None, None),
            P(cache, None, None),
            P(),
            P(),
            P(head, None, None),
            P(head, None, None),
            P(head, cache),
        ),
        out_specs=P(cache + head, None),
        check_vma=False,
    )
```

time: 378 us -> 155 us (0.41)
  waiting for transfers between devices: 304 us -> 42.9 us
  starting transfers between devices: 0.12 us -> 67.3 us
  matrix products: 44.5 us -> 0 us
  Pallas kernels: 0 us -> 38 us
  between operations: 13.2 us -> 0.22 us
  other arithmetic: 10.4 us -> 1.16 us
    reduce_scatter x1 -> x0, waiting for transfers between devices: 208 us -> none  [local(): lax.psum_scatter(partials.astype(jnp.bfloat16), 'head', scatter_dimension...]
    all_gather x3 -> x0, waiting for transfers between devices: 94 us -> none  [the longest x1 55.1 us: local(): latent = lax.all_gather(pool_latent, 'cache', axis=0, tiled=True)]
    ppermute x0 -> x34, starting transfers between devices: none -> 67.3 us  [the longest x21 32.4 us: flip(): return lax.ppermute(value, axis, [(i, i ^ bits) for i in range(size)])]
    dot_general x8 -> x0, matrix products: 44.5 us -> none  [the longest x2 12.7 us: score_of(): jnp.einsum('thc,kc->thk', q_lat, key_rows, preferred_element_type=jnp.flo...]
    ppermute x0 -> x34, waiting for transfers between devices: none -> 42.9 us  [the longest x21 19.5 us: flip(): return lax.ppermute(value, axis, [(i, i ^ bits) for i in range(size)])]
    pallas_call x0 -> x6, Pallas kernels: none -> 38 us  [the longest x2 31.5 us: attention(): pl.pallas_call(functools.partial(attention_kernel, slots, own), out_shape...]
    reduce_sum x3 -> x0, other arithmetic: 9.54 us -> none  [the longest x1 9.38 us: local(): sums = sums * factor + jnp.sum(piece_weights, axis=-1)]
  transfers between devices with their start and end apart: 4 -> 34, of which waited for: 4 -> 14; matrix products, arithmetic and copies ran while one was open for 14% -> 0% of each run, Pallas kernels for 0% -> 21%
where the time goes in v1:
time: 155 us; the launch traced here: 153 us
  starting transfers between devices  67.3 us (43%)
  waiting for transfers between devices  42.9 us (28%)
  Pallas kernels  38 us (25%)
  local copies, waits for them, and re-layouts  3.06 us (2%)
    ppermute x21, starting transfers between devices, flip(): return lax.ppermute(value, axis, [(i, i ^ bits) for i in range(size)])  32.4 us
    pallas_call x2, Pallas kernels, attention(): pl.pallas_call(functools.partial(attention_kernel, slots, own), out_shape...  31.5 us
    ppermute x21, waiting for transfers between devices, flip(): return lax.ppermute(value, axis, [(i, i ^ bits) for i in range(size)])  19.5 us
    ppermute x6, starting transfers between devices, turn(): lax.ppermute(value, axis, [((i + shift) % size, i) for i in range(size)])  16.6 us
    ppermute x3, starting transfers between devices, local(): lax.ppermute(partial[d], 'zb', [(i, (i + d) % 4) for i in range(4)])  10.5 us
    ppermute x6, waiting for transfers between devices, turn(): lax.ppermute(value, axis, [((i + shift) % size, i) for i in range(size)])  9.76 us
    ppermute x3, waiting for transfers between devices, local(): lax.ppermute(part, 'x', [(i, (i + s) % 4) for i in range(4)])  8.03 us
    pallas_call x4, Pallas kernels, simple(): pl.pallas_call(kernel, out_shape=out_shape, in_specs=specs, out_specs=jax...  6.55 us
  transfers between devices with their start and end apart: 34, of which 14 were waited for; matrix products, arithmetic and copies ran while one was open for 0% of the time, Pallas kernels for 21%

profile of v1, /device:TPU:6, one launch (start us, length us, event | category | flops | bytes accessed | tf_op | source)
XLA Modules:
  0.0 152.7 jit_solution(8139781792544156076)
XLA Ops:
  0.0 0.8 copy-done
  0.9 0.0 copy-start.8
  0.9 0.0 copy-start.9
  0.9 0.0 copy-start.6
  0.9 0.0 copy-start.7
  0.9 1.2 pad_maximum_fusion.refs_1_.refs_3_
  2.1 1.7 %collective-permute-start = (bf16[576,512]{1,0:T(8,128)(2,1)S(1)}, bf16[576,512]{1,0:T(8,128)(2,1)S(1)}, u32[]{:S(2)}, u32[]{:S(2)}) collective-permute-start(bf16[576,512]{1,0:T(8,128)(2,1)S(1)} %pad_maximum_fusion.refs_1_.refs_3_), channel_id=1, source_target_pairs={{0,128},{128,0},{1,129},{129,1},{2,130},{130,2},{3,131},{131,3},{4... | collective-permute-start | bytes 1769480 | tf_op jit(solution)/shard_map/ppermute | solution.py:292
  3.7 6.1 %collective-permute-start.16 = (bf16[448,512]{1,0:T(8,128)(2,1)}, bf16[448,512]{1,0:T(8,128)(2,1)S(1)}, u32[]{:S(2)}, u32[]{:S(2)}) collective-permute-start(bf16[448,512]{1,0:T(8,128)(2,1)} %bitcast.8), channel_id=1, source_target_pairs={{0,0},{1,32},{2,64},{3,96},{32,1},{33,33},{34,65},{35,97},{64,2},{... | collective-permute-start | bytes 1376264 | tf_op jit(solution)/shard_map/ppermute | solution.py:329
  9.8 7.4 %collective-permute-done.refs_2_.refs_4_ = bf16[576,512]{1,0:T(8,128)(2,1)S(1)} collective-permute-done((bf16[576,512]{1,0:T(8,128)(2,1)S(1)}, bf16[576,512]{1,0:T(8,128)(2,1)S(1)}, u32[]{:S(2)}, u32[]{:S(2)}) %collective-permute-start) | collective-permute-done | bytes 589856 | tf_op jit(solution)/shard_map/ppermute | solution.py:292
  17.3 5.5 %collective-permute-start.3 = (bf16[128,768]{1,0:T(8,128)(2,1)S(1)}, bf16[128,768]{1,0:T(8,128)(2,1)S(1)}, u32[]{:S(2)}, u32[]{:S(2)}) collective-permute-start(bf16[128,768]{1,0:T(8,128)(2,1)S(1)} %constant_dynamic-update-slice_fusion.refs_0_), channel_id=1, source_target_pairs={{32,0},{64,32},{96,64},{0,96},{33,1},{65,33},{97,65},{1,97},{34,2}... | collective-permute-start | bytes 589832 | tf_op jit(solution)/shard_map/ppermute | solution.py:288
  22.8 6.2 %collective-permute-start.4 = (bf16[128,768]{1,0:T(8,128)(2,1)S(1)}, bf16[128,768]{1,0:T(8,128)(2,1)S(1)}, u32[]{:S(2)}, u32[]{:S(2)}) collective-permute-start(bf16[128,768]{1,0:T(8,128)(2,1)S(1)} %constant_dynamic-update-slice_fusion.refs_0_), channel_id=1, source_target_pairs={{64,0},{96,32},{0,64},{32,96},{65,1},{97,33},{1,65},{33,97},{66,2}... | collective-permute-start | bytes 589832 | tf_op jit(solution)/shard_map/ppermute | solution.py:288
  28.9 4.1 %collective-permute-done.3.refs_0_ = bf16[128,768]{1,0:T(8,128)(2,1)S(1)} collective-permute-done((bf16[128,768]{1,0:T(8,128)(2,1)S(1)}, bf16[128,768]{1,0:T(8,128)(2,1)S(1)}, u32[]{:S(2)}, u32[]{:S(2)}) %collective-permute-start.3) | collective-permute-done | bytes 196640 | tf_op jit(solution)/shard_map/ppermute | solution.py:288
  33.1 2.1 %collective-permute-start.5 = (bf16[128,768]{1,0:T(8,128)(2,1)S(1)}, bf16[128,768]{1,0:T(8,128)(2,1)}, u32[]{:S(2)}, u32[]{:S(2)}) collective-permute-start(bf16[128,768]{1,0:T(8,128)(2,1)S(1)} %constant_dynamic-update-slice_fusion.refs_0_), channel_id=1, source_target_pairs={{96,0},{0,32},{32,64},{64,96},{97,1},{1,33},{33,65},{65,97},{98,2}... | collective-permute-start | bytes 589832 | tf_op jit(solution)/shard_map/ppermute | solution.py:288
  35.2 0.1 stack.23.ids
  35.3 0.0 collective-permute-done.16.refs_8_
  35.3 0.0 collective-permute-start.17
  35.3 3.5 %collective-permute-done.4.refs_1_ = bf16[128,768]{1,0:T(8,128)(2,1)S(1)} collective-permute-done((bf16[128,768]{1,0:T(8,128)(2,1)S(1)}, bf16[128,768]{1,0:T(8,128)(2,1)S(1)}, u32[]{:S(2)}, u32[]{:S(2)}) %collective-permute-start.4) | collective-permute-done | bytes 196640 | tf_op jit(solution)/shard_map/ppermute | solution.py:288
  38.8 2.1 %collective-permute-done.5.refs_2_ = bf16[128,768]{1,0:T(8,128)(2,1)} collective-permute-done((bf16[128,768]{1,0:T(8,128)(2,1)S(1)}, bf16[128,768]{1,0:T(8,128)(2,1)}, u32[]{:S(2)}, u32[]{:S(2)}) %collective-permute-start.5) | collective-permute-done | bytes 196640 | tf_op jit(solution)/shard_map/ppermute | solution.py:288
  40.9 2.8 %collective-permute-start.19 = (bf16[448,512]{1,0:T(8,128)(2,1)S(1)}, bf16[448,512]{1,0:T(8,128)(2,1)S(1)}, u32[]{:S(2)}, u32[]{:S(2)}) collective-permute-start(bf16[448,512]{1,0:T(8,128)(2,1)S(1)} %collective-permute-done.16.refs_8_), channel_id=1, source_target_pairs={{96,0},{0,32},{32,64},{64,96},{97,1},{1,33},{33,65},{65,97},{98,2}... | collective-permute-start | bytes 1376264 | tf_op jit(solution)/shard_map/ppermute | solution.py:288
  43.7 0.0 collective-permute-done.1.refs_3_.refs_5_
  43.7 0.0 copy-start.1
  43.7 1.0 copy-done.1
  44.8 1.0 copy-done.2
  45.8 20.7 %attend.3 = (bf16[128,640]{1,0:T(8,128)(2,1)S(1)}, bf16[128,640]{1,0:T(8,128)(2,1)S(1)}, bf16[128,640]{1,0:T(8,128)(2,1)S(1)}) custom-call(s32[5]{0:T(128)S(1)} %stack.23.ids, s32[16,32]{1,0:T(8,128)S(1)} %copy-done.6, s32[16]{0:T(128)S(1)} %copy-done.7, bf16[128,768]{1,0:T(8,128)(2,1)S(1)} %collective-permute-done.3.refs_0_, ...), custom_call_target="tpu_custom_call" | custom-call | flops 3422552064 | bytes 6291456 | tf_op jit(solution)/shard_map/attend/pallas_call | solution.py:176
  66.5 0.1 collective-permute-start.6
  66.6 0.3 collective-permute-start.20
  66.9 0.0 collective-permute-done.17.refs_9_
  66.9 0.5 collective-permute-start.21
  67.4 0.1 collective-permute-start.22
  67.5 0.0 collective-permute-done.19.refs_11_
  67.5 0.0 collective-permute-start.7
  67.5 5.9 %collective-permute-done.6.refs_1_ = bf16[128,640]{1,0:T(8,128)(2,1)S(1)} collective-permute-done((bf16[128,640]{1,0:T(8,128)(2,1)S(1)}, bf16[128,640]{1,0:T(8,128)(2,1)S(1)}, u32[]{:S(2)}, u32[]{:S(2)}) %collective-permute-start.6) | collective-permute-done | bytes 163872 | tf_op jit(solution)/shard_map/ppermute | solution.py:337
  73.4 2.1 %collective-permute-done.7.refs_2_ = bf16[128,640]{1,0:T(8,128)(2,1)S(1)} collective-permute-done((bf16[128,640]{1,0:T(8,128)(2,1)S(1)}, bf16[128,640]{1,0:T(8,128)(2,1)S(1)}, u32[]{:S(2)}, u32[]{:S(2)}) %collective-permute-start.7) | collective-permute-done | bytes 163872 | tf_op jit(solution)/shard_map/ppermute | solution.py:337
  75.5 1.7 %collective-permute-start.8 = (bf16[128,640]{1,0:T(8,128)(2,1)S(1)}, bf16[128,640]{1,0:T(8,128)(2,1)S(1)}, u32[]{:S(2)}, u32[]{:S(2)}) collective-permute-start(bf16[128,640]{1,0:T(8,128)(2,1)S(1)} %get-tuple-element.22), channel_id=1, source_target_pairs={{0,96},{32,0},{64,32},{96,64},{1,97},{33,1},{65,33},{97,65},{2,98}... | collective-permute-start | bytes 491528 | tf_op jit(solution)/shard_map/ppermute | solution.py:337
  77.2 10.8 %attend.2.refs_0_ = bf16[128,640]{1,0:T(8,128)(2,1)S(1)} custom-call(s32[5]{0:T(128)S(1)} %stack.23.ids, s32[16,32]{1,0:T(8,128)S(1)} %copy-done.6, s32[16]{0:T(128)S(1)} %copy-done.7, bf16[128,768]{1,0:T(8,128)(2,1)S(1)} %constant_dynamic-update-slice_fusion.refs_0_, bf16[576,512]{1,0:T(8,128)(2,1)S(1)} %pad_maximum_fusion.refs_1_.refs_3_, ...), custom_call_target="tpu_custom_call" | custom-call | flops 1140850688 | bytes 2097152 | tf_op jit(solution)/shard_map/attend/pallas_call | solution.py:176
  88.1 0.5 combine.1.refs_0_
  88.6 0.1 collective-permute-start.10
  88.7 0.0 collective-permute-done.20.refs_12_
  88.7 9.1 %collective-permute-start.11 = (bf16[128,512]{1,0:T(8,128)(2,1)S(1)}, bf16[128,512]{1,0:T(8,128)(2,1)S(1)}, u32[]{:S(2)}, u32[]{:S(2)}) collective-permute-start(bf16[128,512]{1,0:T(8,128)(2,1)S(1)} %combine.1.refs_0_), channel_id=1, source_target_pairs={{0,3},{1,2},{2,1},{3,0},{128,131},{129,130},{130,129},{131,128},{4... | collective-permute-start | bytes 393224 | tf_op jit(solution)/shard_map/ppermute | solution.py:292
  97.8 3.8 %collective-permute-start.12 = (bf16[128,512]{1,0:T(8,128)(2,1)S(1)}, bf16[128,512]{1,0:T(8,128)(2,1)S(1)}, u32[]{:S(2)}, u32[]{:S(2)}) collective-permute-start(bf16[128,512]{1,0:T(8,128)(2,1)S(1)} %combine.1.refs_0_), channel_id=1, source_target_pairs={{0,128},{1,129},{2,130},{3,131},{128,0},{129,1},{130,2},{131,3},{4... | collective-permute-start | bytes 393224 | tf_op jit(solution)/shard_map/ppermute | solution.py:292
  101.6 1.5 %collective-permute-start.14 = (bf16[128,512]{1,0:T(8,128)(2,1)S(1)}, bf16[128,512]{1,0:T(8,128)(2,1)S(1)}, u32[]{:S(2)}, u32[]{:S(2)}) collective-permute-start(bf16[128,512]{1,0:T(8,128)(2,1)S(1)} %combine.1.refs_0_), channel_id=1, source_target_pairs={{0,130},{1,131},{2,128},{3,129},{128,2},{129,3},{130,0},{131,1},{4... | collective-permute-start | bytes 393224 | tf_op jit(solution)/shard_map/ppermute | solution.py:292
  103.2 3.9 %collective-permute-start.15 = (bf16[128,512]{1,0:T(8,128)(2,1)S(1)}, bf16[128,512]{1,0:T(8,128)(2,1)S(1)}, u32[]{:S(2)}, u32[]{:S(2)}) collective-permute-start(bf16[128,512]{1,0:T(8,128)(2,1)S(1)} %combine.1.refs_0_), channel_id=1, source_target_pairs={{0,131},{1,130},{2,129},{3,128},{128,3},{129,2},{130,1},{131,0},{4... | collective-permute-start | bytes 393224 | tf_op jit(solution)/shard_map/ppermute | solution.py:292
  107.1 0.7 collective-permute-start.9
  107.8 3.6 %collective-permute-done.12.refs_4_ = bf16[128,512]{1,0:T(8,128)(2,1)S(1)} collective-permute-done((bf16[128,512]{1,0:T(8,128)(2,1)S(1)}, bf16[128,512]{1,0:T(8,128)(2,1)S(1)}, u32[]{:S(2)}, u32[]{:S(2)}) %collective-permute-start.12) | collective-permute-done | bytes 131104 | tf_op jit(solution)/shard_map/ppermute | solution.py:292
  111.4 2.2 %collective-permute-done.15.refs_7_ = bf16[128,512]{1,0:T(8,128)(2,1)S(1)} collective-permute-done((bf16[128,512]{1,0:T(8,128)(2,1)S(1)}, bf16[128,512]{1,0:T(8,128)(2,1)S(1)}, u32[]{:S(2)}, u32[]{:S(2)}) %collective-permute-start.15) | collective-permute-done | bytes 131104 | tf_op jit(solution)/shard_map/ppermute | solution.py:292
  113.5 0.8 collective-permute-done.9.refs_1_
  114.3 4.2 %project.1 = (bf16[64,896]{1,0:T(8,128)(2,1)S(1)}, bf16[64,896]{1,0:T(8,128)(2,1)S(1)}, bf16[64,896]{1,0:T(8,128)(2,1)S(1)}, bf16[64,896]{1,0:T(8,128)(2,1)S(1)}) custom-call(s32[5]{0:T(128)S(1)} %stack.23.ids, bf16[128,512]{1,0:T(8,128)(2,1)S(1)} %combine.1.refs_0_, bf16[128,512]{1,0:T(8,128)(2,1)S(1)} %collective-permute-done.9.refs_1_, ...), custom_call_target="tpu_custom_call" | custom-call | tf_op jit(solution)/shard_map/project/pallas_call | solution.py:273
  118.5 3.4 %collective-permute-start.24 = (bf16[64,896]{1,0:T(8,128)(2,1)S(1)}, bf16[64,896]{1,0:T(8,128)(2,1)S(1)}, u32[]{:S(2)}, u32[]{:S(2)}) collective-permute-start(bf16[64,896]{1,0:T(8,128)(2,1)S(1)} %get-tuple-element.24), channel_id=1, source_target_pairs={{0,4},{4,8},{8,12},{12,0},{1,5},{5,9},{9,13},{13,1},{2,6},{6,10},{... | collective-permute-start | bytes 344072 | tf_op jit(solution)/shard_map/ppermute | solution.py:360
  121.8 4.5 %collective-permute-start.25 = (bf16[64,896]{1,0:T(8,128)(2,1)S(1)}, bf16[64,896]{1,0:T(8,128)(2,1)S(1)}, u32[]{:S(2)}, u32[]{:S(2)}) collective-permute-start(bf16[64,896]{1,0:T(8,128)(2,1)S(1)} %get-tuple-element.25), channel_id=1, source_target_pairs={{0,8},{4,12},{8,0},{12,4},{1,9},{5,13},{9,1},{13,5},{2,10},{6,14},... | collective-permute-start | bytes 344072 | tf_op jit(solution)/shard_map/ppermute | solution.py:360
  126.3 2.7 %collective-permute-start.26 = (bf16[64,896]{1,0:T(8,128)(2,1)S(1)}, bf16[64,896]{1,0:T(8,128)(2,1)S(1)}, u32[]{:S(2)}, u32[]{:S(2)}) collective-permute-start(bf16[64,896]{1,0:T(8,128)(2,1)S(1)} %get-tuple-element.26), channel_id=1, source_target_pairs={{0,12},{4,0},{8,4},{12,8},{1,13},{5,1},{9,5},{13,9},{2,14},{6,2},{... | collective-permute-start | bytes 344072 | tf_op jit(solution)/shard_map/ppermute | solution.py:360
  129.0 0.6 collective-permute-done.24.refs_1_
  129.6 2.7 %collective-permute-done.25.refs_2_ = bf16[64,896]{1,0:T(8,128)(2,1)S(1)} collective-permute-done((bf16[64,896]{1,0:T(8,128)(2,1)S(1)}, bf16[64,896]{1,0:T(8,128)(2,1)S(1)}, u32[]{:S(2)}, u32[]{:S(2)}) %collective-permute-start.25) | collective-permute-done | bytes 114720 | tf_op jit(solution)/shard_map/ppermute | solution.py:360
  132.3 2.3 %collective-permute-done.26.refs_3_ = bf16[64,896]{1,0:T(8,128)(2,1)S(1)} collective-permute-done((bf16[64,896]{1,0:T(8,128)(2,1)S(1)}, bf16[64,896]{1,0:T(8,128)(2,1)S(1)}, u32[]{:S(2)}, u32[]{:S(2)}) %collective-permute-start.26) | collective-permute-done | bytes 114720 | tf_op jit(solution)/shard_map/ppermute | solution.py:360
  134.6 0.6 share.1
  135.2 1.8 %collective-permute-start.27 = (f32[8,896]{1,0:T(8,128)S(1)}, f32[8,896]{1,0:T(8,128)S(1)}, u32[]{:S(2)}, u32[]{:S(2)}) collective-permute-start(f32[8,896]{1,0:T(8,128)S(1)} %get-tuple-element.28), channel_id=1, source_target_pairs={{0,1},{1,0},{2,3},{3,2},{128,129},{129,128},{130,131},{131,130},{4... | collective-permute-start | bytes 86024 | tf_op jit(solution)/shard_map/ppermute | solution.py:292
  137.1 0.5 collective-permute-start.28
  137.5 2.8 %collective-permute-start.29 = (f32[8,896]{1,0:T(8,128)S(1)}, f32[8,896]{1,0:T(8,128)S(1)}, u32[]{:S(2)}, u32[]{:S(2)}) collective-permute-start(f32[8,896]{1,0:T(8,128)S(1)} %get-tuple-element.30), channel_id=1, source_target_pairs={{0,3},{1,2},{2,1},{3,0},{128,131},{129,130},{130,129},{131,128},{4... | collective-permute-start | bytes 86024 | tf_op jit(solution)/shard_map/ppermute | solution.py:292
  140.3 2.1 %collective-permute-start.30 = (f32[8,896]{1,0:T(8,128)S(1)}, f32[8,896]{1,0:T(8,128)S(1)}, u32[]{:S(2)}, u32[]{:S(2)}) collective-permute-start(f32[8,896]{1,0:T(8,128)S(1)} %get-tuple-element.31), channel_id=1, source_target_pairs={{0,128},{1,129},{2,130},{3,131},{128,0},{129,1},{130,2},{131,3},{4... | collective-permute-start | bytes 86024 | tf_op jit(solution)/shard_map/ppermute | solution.py:292
  142.4 0.5 collective-permute-start.31
  142.9 2.6 %collective-permute-start.32 = (f32[8,896]{1,0:T(8,128)S(1)}, f32[8,896]{1,0:T(8,128)S(1)}, u32[]{:S(2)}, u32[]{:S(2)}) collective-permute-start(f32[8,896]{1,0:T(8,128)S(1)} %get-tuple-element.33), channel_id=1, source_target_pairs={{0,130},{1,131},{2,128},{3,129},{128,2},{129,3},{130,0},{131,1},{4... | collective-permute-start | bytes 86024 | tf_op jit(solution)/shard_map/ppermute | solution.py:292
  145.5 0.4 collective-permute-start.33
  145.9 1.7 %collective-permute-done.31.refs_5_ = f32[8,896]{1,0:T(8,128)S(1)} collective-permute-done((f32[8,896]{1,0:T(8,128)S(1)}, f32[8,896]{1,0:T(8,128)S(1)}, u32[]{:S(2)}, u32[]{:S(2)}) %collective-permute-start.31) | collective-permute-done | bytes 28704 | tf_op jit(solution)/shard_map/ppermute | solution.py:292
  147.7 3.8 %collective-permute-done.33.refs_7_ = f32[8,896]{1,0:T(8,128)S(1)} collective-permute-done((f32[8,896]{1,0:T(8,128)S(1)}, f32[8,896]{1,0:T(8,128)S(1)}, u32[]{:S(2)}, u32[]{:S(2)}) %collective-permute-start.33) | collective-permute-done | bytes 28704 | tf_op jit(solution)/shard_map/ppermute | solution.py:292
  151.5 1.2 place.1
  (35 shorter events, 0.1 us)
Async XLA Ops:
  0.0 0.8 copy-start
  0.9 16.4 %copy-start.8 = (bf16[128,512]{1,0:T(8,128)(2,1)S(1)}, bf16[128,512]{1,0:T(8,128)(2,1)}, u32[]{:S(2)}) copy-start(bf16[128,512]{1,0:T(8,128)(2,1)} %param.11) | copy-start | bytes 393220
  0.9 16.4 %copy-start.9 = (bf16[128,256]{1,0:T(8,128)(2,1)S(1)}, bf16[128,256]{1,0:T(8,128)(2,1)}, u32[]{:S(2)}) copy-start(bf16[128,256]{1,0:T(8,128)(2,1)} %param.12) | copy-start | bytes 196612
  0.9 42.8 %copy-start.6 = (s32[16,32]{1,0:T(8,128)S(1)}, s32[16,32]{1,0:T(8,128)}, u32[]{:S(2)}) copy-start(s32[16,32]{1,0:T(8,128)} %table.3) | copy-start | bytes 6148
  0.9 42.8 %copy-start.7 = (s32[16]{0:T(128)S(1)}, s32[16]{0:T(128)}, u32[]{:S(2)}) copy-start(s32[16]{0:T(128)} %lens.3) | copy-start | bytes 196
  2.1 15.2 %collective-permute-start = (bf16[576,512]{1,0:T(8,128)(2,1)S(1)}, bf16[576,512]{1,0:T(8,128)(2,1)S(1)}, u32[]{:S(2)}, u32[]{:S(2)}) collective-permute-start(bf16[576,512]{1,0:T(8,128)(2,1)S(1)} %pad_maximum_fusion.refs_1_.refs_3_), channel_id=1, source_target_pairs={{0,128},{128,0},{1,129},{129,1},{2,130},{130,2},{3,131},{131,3},{4... | collective-permute-start | bytes 1769480 | tf_op jit(solution)/shard_map/ppermute | solution.py:292
  3.7 40.0 %collective-permute-start.1 = (bf16[576,512]{1,0:T(8,128)(2,1)S(1)}, bf16[576,512]{1,0:T(8,128)(2,1)S(1)}, u32[]{:S(2)}, u32[]{:S(2)}) collective-permute-start(bf16[576,512]{1,0:T(8,128)(2,1)S(1)} %pad_maximum_fusion.refs_1_.refs_3_), channel_id=1, source_target_pairs={{0,16},{16,0},{1,17},{17,1},{2,18},{18,2},{3,19},{19,3},{4,20},{20... | collective-permute-start | bytes 1769480 | tf_op jit(solution)/shard_map/ppermute | solution.py:292
  3.7 31.5 %collective-permute-start.16 = (bf16[448,512]{1,0:T(8,128)(2,1)}, bf16[448,512]{1,0:T(8,128)(2,1)S(1)}, u32[]{:S(2)}, u32[]{:S(2)}) collective-permute-start(bf16[448,512]{1,0:T(8,128)(2,1)} %bitcast.8), channel_id=1, source_target_pairs={{0,0},{1,32},{2,64},{3,96},{32,1},{33,33},{34,65},{35,97},{64,2},{... | collective-permute-start | bytes 1376264 | tf_op jit(solution)/shard_map/ppermute | solution.py:329
  17.2 26.5 %collective-permute-start.2 = (bf16[576,512]{1,0:T(8,128)(2,1)S(1)}, bf16[576,512]{1,0:T(8,128)(2,1)S(1)}, u32[]{:S(2)}, u32[]{:S(2)}) collective-permute-start(bf16[576,512]{1,0:T(8,128)(2,1)S(1)} %collective-permute-done.refs_2_.refs_4_), channel_id=1, source_target_pairs={{0,16},{16,0},{1,17},{17,1},{2,18},{18,2},{3,19},{19,3},{4,20},{20... | collective-permute-start | bytes 1769480 | tf_op jit(solution)/shard_map/ppermute | solution.py:292
  17.3 15.8 %collective-permute-start.3 = (bf16[128,768]{1,0:T(8,128)(2,1)S(1)}, bf16[128,768]{1,0:T(8,128)(2,1)S(1)}, u32[]{:S(2)}, u32[]{:S(2)}) collective-permute-start(bf16[128,768]{1,0:T(8,128)(2,1)S(1)} %constant_dynamic-update-slice_fusion.refs_0_), channel_id=1, source_target_pairs={{32,0},{64,32},{96,64},{0,96},{33,1},{65,33},{97,65},{1,97},{34,2}... | collective-permute-start | bytes 589832 | tf_op jit(solution)/shard_map/ppermute | solution.py:288
  22.8 16.1 %collective-permute-start.4 = (bf16[128,768]{1,0:T(8,128)(2,1)S(1)}, bf16[128,768]{1,0:T(8,128)(2,1)S(1)}, u32[]{:S(2)}, u32[]{:S(2)}) collective-permute-start(bf16[128,768]{1,0:T(8,128)(2,1)S(1)} %constant_dynamic-update-slice_fusion.refs_0_), channel_id=1, source_target_pairs={{64,0},{96,32},{0,64},{32,96},{65,1},{97,33},{1,65},{33,97},{66,2}... | collective-permute-start | bytes 589832 | tf_op jit(solution)/shard_map/ppermute | solution.py:288
  33.1 7.9 %collective-permute-start.5 = (bf16[128,768]{1,0:T(8,128)(2,1)S(1)}, bf16[128,768]{1,0:T(8,128)(2,1)}, u32[]{:S(2)}, u32[]{:S(2)}) collective-permute-start(bf16[128,768]{1,0:T(8,128)(2,1)S(1)} %constant_dynamic-update-slice_fusion.refs_0_), channel_id=1, source_target_pairs={{96,0},{0,32},{32,64},{64,96},{97,1},{1,33},{33,65},{65,97},{98,2}... | collective-permute-start | bytes 589832 | tf_op jit(solution)/shard_map/ppermute | solution.py:288
  35.3 31.6 %collective-permute-start.17 = (bf16[448,512]{1,0:T(8,128)(2,1)S(1)}, bf16[448,512]{1,0:T(8,128)(2,1)S(1)}, u32[]{:S(2)}, u32[]{:S(2)}) collective-permute-start(bf16[448,512]{1,0:T(8,128)(2,1)S(1)} %collective-permute-done.16.refs_8_), channel_id=1, source_target_pairs={{32,0},{64,32},{96,64},{0,96},{33,1},{65,33},{97,65},{1,97},{34,2}... | collective-permute-start | bytes 1376264 | tf_op jit(solution)/shard_map/ppermute | solution.py:288
  38.8 28.5 %collective-permute-start.18 = (bf16[448,512]{1,0:T(8,128)(2,1)S(1)}, bf16[448,512]{1,0:T(8,128)(2,1)S(1)}, u32[]{:S(2)}, u32[]{:S(2)}) collective-permute-start(bf16[448,512]{1,0:T(8,128)(2,1)S(1)} %collective-permute-done.16.refs_8_), channel_id=1, source_target_pairs={{64,0},{96,32},{0,64},{32,96},{65,1},{97,33},{1,65},{33,97},{66,2}... | collective-permute-start | bytes 1376264 | tf_op jit(solution)/shard_map/ppermute | solution.py:288
  40.9 26.5 %collective-permute-start.19 = (bf16[448,512]{1,0:T(8,128)(2,1)S(1)}, bf16[448,512]{1,0:T(8,128)(2,1)S(1)}, u32[]{:S(2)}, u32[]{:S(2)}) collective-permute-start(bf16[448,512]{1,0:T(8,128)(2,1)S(1)} %collective-permute-done.16.refs_8_), channel_id=1, source_target_pairs={{96,0},{0,32},{32,64},{64,96},{97,1},{1,33},{33,65},{65,97},{98,2}... | collective-permute-start | bytes 1376264 | tf_op jit(solution)/shard_map/ppermute | solution.py:288
  43.7 1.0 copy-start.1
  44.8 1.0 copy-start.2
  45.8 31.4 %copy-start.3 = (bf16[4,512,128]{2,1,0:T(8,128)(2,1)S(1)}, bf16[4,512,128]{2,1,0:T(8,128)(2,1)}, u32[]{:S(2)}) copy-start(bf16[4,512,128]{2,1,0:T(8,128)(2,1)} %refs_8_.1) | copy-start | bytes 1572868
  45.8 31.4 %copy-start.4 = (bf16[128,512]{1,0:T(8,128)(2,1)S(1)}, bf16[128,512]{1,0:T(8,128)(2,1)}, u32[]{:S(2)}) copy-start(bf16[128,512]{1,0:T(8,128)(2,1)} %refs_7_.2) | copy-start | bytes 393220
  45.8 31.4 %copy-start.5 = (bf16[1,64,128]{2,1,0:T(8,128)(2,1)S(1)}, bf16[1,64,128]{2,1,0:T(8,128)(2,1)}, u32[]{:S(2)}) copy-start(bf16[1,64,128]{2,1,0:T(8,128)(2,1)} %param.14) | copy-start | bytes 49156
  66.5 6.9 %collective-permute-start.6 = (bf16[128,640]{1,0:T(8,128)(2,1)S(1)}, bf16[128,640]{1,0:T(8,128)(2,1)S(1)}, u32[]{:S(2)}, u32[]{:S(2)}) collective-permute-start(bf16[128,640]{1,0:T(8,128)(2,1)S(1)} %get-tuple-element.20), channel_id=1, source_target_pairs={{0,32},{32,64},{64,96},{96,0},{1,33},{33,65},{65,97},{97,1},{2,34}... | collective-permute-start | bytes 491528 | tf_op jit(solution)/shard_map/ppermute | solution.py:337
  66.6 22.2 %collective-permute-start.20 = (bf16[448,512]{1,0:T(8,128)(2,1)S(1)}, bf16[448,512]{1,0:T(8,128)(2,1)S(1)}, u32[]{:S(2)}, u32[]{:S(2)}) collective-permute-start(bf16[448,512]{1,0:T(8,128)(2,1)S(1)} %collective-permute-done.16.refs_8_), channel_id=1, source_target_pairs={{0,16},{16,0},{1,17},{17,1},{2,18},{18,2},{3,19},{19,3},{4,20},{20... | collective-permute-start | bytes 1376264 | tf_op jit(solution)/shard_map/ppermute | solution.py:292
  66.9 31.0 %collective-permute-start.21 = (bf16[448,512]{1,0:T(8,128)(2,1)S(1)}, bf16[448,512]{1,0:T(8,128)(2,1)S(1)}, u32[]{:S(2)}, u32[]{:S(2)}) collective-permute-start(bf16[448,512]{1,0:T(8,128)(2,1)S(1)} %collective-permute-done.17.refs_9_), channel_id=1, source_target_pairs={{0,16},{16,0},{1,17},{17,1},{2,18},{18,2},{3,19},{19,3},{4,20},{20... | collective-permute-start | bytes 1376264 | tf_op jit(solution)/shard_map/ppermute | solution.py:292
  67.4 34.3 %collective-permute-start.22 = (bf16[448,512]{1,0:T(8,128)(2,1)S(1)}, bf16[448,512]{1,0:T(8,128)(2,1)S(1)}, u32[]{:S(2)}, u32[]{:S(2)}) collective-permute-start(bf16[448,512]{1,0:T(8,128)(2,1)S(1)} %collective-permute-done.18.refs_10_), channel_id=1, source_target_pairs={{0,16},{16,0},{1,17},{17,1},{2,18},{18,2},{3,19},{19,3},{4,20},{20... | collective-permute-start | bytes 1376264 | tf_op jit(solution)/shard_map/ppermute | solution.py:292
  67.5 8.0 %collective-permute-start.7 = (bf16[128,640]{1,0:T(8,128)(2,1)S(1)}, bf16[128,640]{1,0:T(8,128)(2,1)S(1)}, u32[]{:S(2)}, u32[]{:S(2)}) collective-permute-start(bf16[128,640]{1,0:T(8,128)(2,1)S(1)} %get-tuple-element.21), channel_id=1, source_target_pairs={{0,64},{32,96},{64,0},{96,32},{1,65},{33,97},{65,1},{97,33},{2,66}... | collective-permute-start | bytes 491528 | tf_op jit(solution)/shard_map/ppermute | solution.py:337
  73.4 28.3 %collective-permute-start.23 = (bf16[448,512]{1,0:T(8,128)(2,1)S(1)}, bf16[448,512]{1,0:T(8,128)(2,1)S(1)}, u32[]{:S(2)}, u32[]{:S(2)}) collective-permute-start(bf16[448,512]{1,0:T(8,128)(2,1)S(1)} %collective-permute-done.19.refs_11_), channel_id=1, source_target_pairs={{0,16},{16,0},{1,17},{17,1},{2,18},{18,2},{3,19},{19,3},{4,20},{20... | collective-permute-start | bytes 1376264 | tf_op jit(solution)/shard_map/ppermute | solution.py:292
  75.5 12.6 %collective-permute-start.8 = (bf16[128,640]{1,0:T(8,128)(2,1)S(1)}, bf16[128,640]{1,0:T(8,128)(2,1)S(1)}, u32[]{:S(2)}, u32[]{:S(2)}) collective-permute-start(bf16[128,640]{1,0:T(8,128)(2,1)S(1)} %get-tuple-element.22), channel_id=1, source_target_pairs={{0,96},{32,0},{64,32},{96,64},{1,97},{33,1},{65,33},{97,65},{2,98}... | collective-permute-start | bytes 491528 | tf_op jit(solution)/shard_map/ppermute | solution.py:337
  88.6 14.6 %collective-permute-start.10 = (bf16[128,512]{1,0:T(8,128)(2,1)S(1)}, bf16[128,512]{1,0:T(8,128)(2,1)S(1)}, u32[]{:S(2)}, u32[]{:S(2)}) collective-permute-start(bf16[128,512]{1,0:T(8,128)(2,1)S(1)} %combine.1.refs_0_), channel_id=1, source_target_pairs={{0,2},{1,3},{2,0},{3,1},{128,130},{129,131},{130,128},{131,129},{4... | collective-permute-start | bytes 393224 | tf_op jit(solution)/shard_map/ppermute | solution.py:292
  88.7 18.4 %collective-permute-start.11 = (bf16[128,512]{1,0:T(8,128)(2,1)S(1)}, bf16[128,512]{1,0:T(8,128)(2,1)S(1)}, u32[]{:S(2)}, u32[]{:S(2)}) collective-permute-start(bf16[128,512]{1,0:T(8,128)(2,1)S(1)} %combine.1.refs_0_), channel_id=1, source_target_pairs={{0,3},{1,2},{2,1},{3,0},{128,131},{129,130},{130,129},{131,128},{4... | collective-permute-start | bytes 393224 | tf_op jit(solution)/shard_map/ppermute | solution.py:292
  97.8 13.5 %collective-permute-start.12 = (bf16[128,512]{1,0:T(8,128)(2,1)S(1)}, bf16[128,512]{1,0:T(8,128)(2,1)S(1)}, u32[]{:S(2)}, u32[]{:S(2)}) collective-permute-start(bf16[128,512]{1,0:T(8,128)(2,1)S(1)} %combine.1.refs_0_), channel_id=1, source_target_pairs={{0,128},{1,129},{2,130},{3,131},{128,0},{129,1},{130,2},{131,3},{4... | collective-permute-start | bytes 393224 | tf_op jit(solution)/shard_map/ppermute | solution.py:292
  101.6 9.7 %collective-permute-start.13 = (bf16[128,512]{1,0:T(8,128)(2,1)S(1)}, bf16[128,512]{1,0:T(8,128)(2,1)S(1)}, u32[]{:S(2)}, u32[]{:S(2)}) collective-permute-start(bf16[128,512]{1,0:T(8,128)(2,1)S(1)} %combine.1.refs_0_), channel_id=1, source_target_pairs={{0,129},{1,128},{2,131},{3,130},{128,1},{129,0},{130,3},{131,2},{4... | collective-permute-start | bytes 393224 | tf_op jit(solution)/shard_map/ppermute | solution.py:292
  101.6 9.7 %collective-permute-start.14 = (bf16[128,512]{1,0:T(8,128)(2,1)S(1)}, bf16[128,512]{1,0:T(8,128)(2,1)S(1)}, u32[]{:S(2)}, u32[]{:S(2)}) collective-permute-start(bf16[128,512]{1,0:T(8,128)(2,1)S(1)} %combine.1.refs_0_), channel_id=1, source_target_pairs={{0,130},{1,131},{2,128},{3,129},{128,2},{129,3},{130,0},{131,1},{4... | collective-permute-start | bytes 393224 | tf_op jit(solution)/shard_map/ppermute | solution.py:292
  103.2 10.3 %collective-permute-start.15 = (bf16[128,512]{1,0:T(8,128)(2,1)S(1)}, bf16[128,512]{1,0:T(8,128)(2,1)S(1)}, u32[]{:S(2)}, u32[]{:S(2)}) collective-permute-start(bf16[128,512]{1,0:T(8,128)(2,1)S(1)} %combine.1.refs_0_), channel_id=1, source_target_pairs={{0,131},{1,130},{2,129},{3,128},{128,3},{129,2},{130,1},{131,0},{4... | collective-permute-start | bytes 393224 | tf_op jit(solution)/shard_map/ppermute | solution.py:292
  107.1 7.2 %collective-permute-start.9 = (bf16[128,512]{1,0:T(8,128)(2,1)S(1)}, bf16[128,512]{1,0:T(8,128)(2,1)S(1)}, u32[]{:S(2)}, u32[]{:S(2)}) collective-permute-start(bf16[128,512]{1,0:T(8,128)(2,1)S(1)} %combine.1.refs_0_), channel_id=1, source_target_pairs={{0,1},{1,0},{2,3},{3,2},{128,129},{129,128},{130,131},{131,130},{4... | collective-permute-start | bytes 393224 | tf_op jit(solution)/shard_map/ppermute | solution.py:292
  118.5 11.1 %collective-permute-start.24 = (bf16[64,896]{1,0:T(8,128)(2,1)S(1)}, bf16[64,896]{1,0:T(8,128)(2,1)S(1)}, u32[]{:S(2)}, u32[]{:S(2)}) collective-permute-start(bf16[64,896]{1,0:T(8,128)(2,1)S(1)} %get-tuple-element.24), channel_id=1, source_target_pairs={{0,4},{4,8},{8,12},{12,0},{1,5},{5,9},{9,13},{13,1},{2,6},{6,10},{... | collective-permute-start | bytes 344072 | tf_op jit(solution)/shard_map/ppermute | solution.py:360
  121.8 10.5 %collective-permute-start.25 = (bf16[64,896]{1,0:T(8,128)(2,1)S(1)}, bf16[64,896]{1,0:T(8,128)(2,1)S(1)}, u32[]{:S(2)}, u32[]{:S(2)}) collective-permute-start(bf16[64,896]{1,0:T(8,128)(2,1)S(1)} %get-tuple-element.25), channel_id=1, source_target_pairs={{0,8},{4,12},{8,0},{12,4},{1,9},{5,13},{9,1},{13,5},{2,10},{6,14},... | collective-permute-start | bytes 344072 | tf_op jit(solution)/shard_map/ppermute | solution.py:360
  126.3 8.3 %collective-permute-start.26 = (bf16[64,896]{1,0:T(8,128)(2,1)S(1)}, bf16[64,896]{1,0:T(8,128)(2,1)S(1)}, u32[]{:S(2)}, u32[]{:S(2)}) collective-permute-start(bf16[64,896]{1,0:T(8,128)(2,1)S(1)} %get-tuple-element.26), channel_id=1, source_target_pairs={{0,12},{4,0},{8,4},{12,8},{1,13},{5,1},{9,5},{13,9},{2,14},{6,2},{... | collective-permute-start | bytes 344072 | tf_op jit(solution)/shard_map/ppermute | solution.py:360
  135.2 7.6 %collective-permute-start.27 = (f32[8,896]{1,0:T(8,128)S(1)}, f32[8,896]{1,0:T(8,128)S(1)}, u32[]{:S(2)}, u32[]{:S(2)}) collective-permute-start(f32[8,896]{1,0:T(8,128)S(1)} %get-tuple-element.28), channel_id=1, source_target_pairs={{0,1},{1,0},{2,3},{3,2},{128,129},{129,128},{130,131},{131,130},{4... | collective-permute-start | bytes 86024 | tf_op jit(solution)/shard_map/ppermute | solution.py:292
  137.1 8.5 %collective-permute-start.28 = (f32[8,896]{1,0:T(8,128)S(1)}, f32[8,896]{1,0:T(8,128)S(1)}, u32[]{:S(2)}, u32[]{:S(2)}) collective-permute-start(f32[8,896]{1,0:T(8,128)S(1)} %get-tuple-element.29), channel_id=1, source_target_pairs={{0,2},{1,3},{2,0},{3,1},{128,130},{129,131},{130,128},{131,129},{4... | collective-permute-start | bytes 86024 | tf_op jit(solution)/shard_map/ppermute | solution.py:292
  137.5 8.4 %collective-permute-start.29 = (f32[8,896]{1,0:T(8,128)S(1)}, f32[8,896]{1,0:T(8,128)S(1)}, u32[]{:S(2)}, u32[]{:S(2)}) collective-permute-start(f32[8,896]{1,0:T(8,128)S(1)} %get-tuple-element.30), channel_id=1, source_target_pairs={{0,3},{1,2},{2,1},{3,0},{128,131},{129,130},{130,129},{131,128},{4... | collective-permute-start | bytes 86024 | tf_op jit(solution)/shard_map/ppermute | solution.py:292
  140.3 5.6 %collective-permute-start.30 = (f32[8,896]{1,0:T(8,128)S(1)}, f32[8,896]{1,0:T(8,128)S(1)}, u32[]{:S(2)}, u32[]{:S(2)}) collective-permute-start(f32[8,896]{1,0:T(8,128)S(1)} %get-tuple-element.31), channel_id=1, source_target_pairs={{0,128},{1,129},{2,130},{3,131},{128,0},{129,1},{130,2},{131,3},{4... | collective-permute-start | bytes 86024 | tf_op jit(solution)/shard_map/ppermute | solution.py:292
  142.4 5.3 %collective-permute-start.31 = (f32[8,896]{1,0:T(8,128)S(1)}, f32[8,896]{1,0:T(8,128)S(1)}, u32[]{:S(2)}, u32[]{:S(2)}) collective-permute-start(f32[8,896]{1,0:T(8,128)S(1)} %get-tuple-element.32), channel_id=1, source_target_pairs={{0,129},{1,128},{2,131},{3,130},{128,1},{129,0},{130,3},{131,2},{4... | collective-permute-start | bytes 86024 | tf_op jit(solution)/shard_map/ppermute | solution.py:292
  142.9 4.8 %collective-permute-start.32 = (f32[8,896]{1,0:T(8,128)S(1)}, f32[8,896]{1,0:T(8,128)S(1)}, u32[]{:S(2)}, u32[]{:S(2)}) collective-permute-start(f32[8,896]{1,0:T(8,128)S(1)} %get-tuple-element.33), channel_id=1, source_target_pairs={{0,130},{1,131},{2,128},{3,129},{128,2},{129,3},{130,0},{131,1},{4... | collective-permute-start | bytes 86024 | tf_op jit(solution)/shard_map/ppermute | solution.py:292
  145.5 6.0 %collective-permute-start.33 = (f32[8,896]{1,0:T(8,128)S(1)}, f32[8,896]{1,0:T(8,128)S(1)}, u32[]{:S(2)}, u32[]{:S(2)}) collective-permute-start(f32[8,896]{1,0:T(8,128)S(1)} %get-tuple-element.34), channel_id=1, source_target_pairs={{0,131},{1,130},{2,129},{3,128},{128,3},{129,2},{130,1},{131,0},{4... | collective-permute-start | bytes 86024 | tf_op jit(solution)/shard_map/ppermute | solution.py:292

commit v2 on v1

v2 whole, which is shorter than its diff:
```python
import functools

import jax
import jax.numpy as jnp
from jax import lax
from jax.experimental import pallas as pl
from jax.experimental.pallas import tpu as pltpu
from jax.sharding import Mesh, PartitionSpec as P

LAT = 512
NOPE = 128
ROPE = 64
VD = 128
BLOCK = 128
HEADS = 4
TOK = 128
ROWS = HEADS * TOK
SLOTS = 4
STEP = 4
LOG2E = 1.4426950408889634
SCALE2 = (NOPE + ROPE) ** -0.5 * LOG2E
LOW = -1e30
STAT = HEADS * VD
MSG = STAT + 128

VMEM = pltpu.VMEM
SMEM = pltpu.SMEM


def dot_nn(a, b):
    return lax.dot_general(a, b, (((1,), (0,)), ((), ())), preferred_element_type=jnp.float32)


def dot_nt(a, b):
    return lax.dot_general(a, b, (((1,), (1,)), ((), ())), preferred_element_type=jnp.float32)


def attention_kernel(slots, own, ids, table, lens, *refs):
    count = len(slots)
    refs = list(refs)

    def take(n):
        got = refs[:n]
        del refs[:n]
        return got

    queries = take(count)
    pools = take(4)
    weights = take(2)
    new_latent, new_rope = take(2) if own else (None, None)
    outs = take(count)
    w_uk, w_uv, keys, rots, sems, weight_sems, found_of, valid_of, q_lat, q_rot, acc, top, tot, latents, levels = refs
    yl, x, k = ids[0], ids[1], ids[2]
    loads = [pltpu.make_async_copy(weights[i], (w_uk, w_uv)[i], weight_sems.at[i]) for i in range(2)]
    for load in loads:
        load.start()

    def fetch(s, src, i, at):
        chunk, part = at // STEP, pl.multiple_of((at % STEP) * BLOCK, BLOCK)
        return (
            pltpu.make_async_copy(
                src.at[pl.ds(pl.multiple_of(i * BLOCK, BLOCK), BLOCK), :],
                keys.at[s, chunk, pl.ds(part, BLOCK), :],
                sems.at[s, at, 0],
            ),
            pltpu.make_async_copy(
                src.at[pl.ds(4 * BLOCK, ROPE), pl.ds(pl.multiple_of(i * BLOCK, BLOCK), BLOCK)],
                rots.at[s, chunk, :, pl.ds(part, BLOCK)],
                sems.at[s, at, 1],
            ),
        )

    for s, slot in enumerate(slots):
        request = yl * 8 + ((x + slot) % 4) * 2 + k
        limit = lens[request]

        def scan(m, carry):
            found, valid = carry
            block = table[request, m]
            owner, i = block >> 2, block & 3
            here = ((owner >> 1) & 3) == x

            @pl.when(here)
            def _():
                source = ((owner >> 3) ^ yl) + 2 * ((owner & 1) ^ k)
                for j in range(4):

                    @pl.when(source == j)
                    def _():
                        for copy in fetch(s, pools[j], i, found):
                            copy.start()

            step = here.astype(jnp.int32)
            return found + step, valid + step * jnp.minimum(limit - m * BLOCK, BLOCK)

        blocks = jnp.minimum((limit + BLOCK - 1) // BLOCK, 32)
        found, valid = lax.fori_loop(0, blocks, scan, (jnp.int32(0), jnp.int32(0)))
        found_of[s] = found
        valid_of[s] = valid

    def clear(s):
        found = found_of[s]
        for extra in range(STEP):
            at = found + extra

            @pl.when(jnp.logical_and(at < jnp.maximum((found + STEP - 1) // STEP, 1) * STEP, at < 16))
            def _():
                part = pl.multiple_of((at % STEP) * BLOCK, BLOCK)
                keys[s, at // STEP, pl.ds(part, BLOCK), :] = jnp.zeros((BLOCK, LAT), jnp.bfloat16)
                rots[s, at // STEP, :, pl.ds(part, BLOCK)] = jnp.zeros((ROPE, BLOCK), jnp.bfloat16)

    for s in range(count):
        clear(s)
    loads[0].wait()
    for h in range(HEADS):
        rows = slice(h * TOK, (h + 1) * TOK)
        part = jnp.concatenate([q[:, h * NOPE : (h + 1) * NOPE] for q in queries], axis=0)
        part = dot_nn(part, w_uk[h]).astype(jnp.bfloat16)
        first = HEADS * NOPE + h * ROPE
        for s in range(count):
            q_lat[s, rows, :] = part[s * TOK : (s + 1) * TOK]
            q_rot[s, rows, :] = queries[s][:, first : first + ROPE]

    def wide(value, times):
        return jnp.concatenate([value] * times, axis=1)

    def begin(score, latent):
        best = jnp.broadcast_to(jnp.max(score, axis=1, keepdims=True), (ROWS, 128))
        times = score.shape[1] // 128
        weight = jnp.exp2((score - wide(best, times)) * SCALE2)
        top[...] = best
        tot[...] = sum(weight[:, i * 128 : (i + 1) * 128] for i in range(times))
        acc[...] = dot_nn(weight.astype(jnp.bfloat16), latent)

    def scores(s, chunk):
        for b in range(STEP):

            @pl.when(chunk * STEP + b < found_of[s])
            def _():
                for copy in fetch(s, pools[0], 0, chunk * STEP + b):
                    copy.wait()

        score = dot_nt(q_lat[s], keys[s, chunk]) + dot_nn(q_rot[s], rots[s, chunk])
        seen = lax.broadcasted_iota(jnp.int32, score.shape, 1) < valid_of[s] - chunk * STEP * BLOCK
        return jnp.where(seen, score, LOW)

    def one_slot(s, carry):
        if own:
            score = dot_nt(q_lat[s], new_latent[...]) + dot_nn(q_rot[s], new_rope[...])
            at = lax.broadcasted_iota(jnp.int32, score.shape, 0) % TOK
            seen = lax.broadcasted_iota(jnp.int32, score.shape, 1) <= at
            begin(jnp.where(seen, score, LOW), new_latent[...])
        else:
            begin(scores(s, 0), keys[s, 0])

        def step(chunk, inner):
            score = scores(s, chunk)
            before = top[...]
            best = jnp.maximum(before, jnp.max(score, axis=1, keepdims=True))
            keep = jnp.exp2((before - best) * SCALE2)
            weight = jnp.exp2((score - wide(best, STEP)) * SCALE2)
            top[...] = best
            tot[...] = tot[...] * keep + sum(weight[:, i * 128 : (i + 1) * 128] for i in range(STEP))
            acc[...] = acc[...] * wide(keep, 4) + dot_nn(weight.astype(jnp.bfloat16), keys[s, chunk])
            return inner

        lax.fori_loop(0 if own else 1, (found_of[s] + STEP - 1) // STEP, step, 0)
        total = jnp.broadcast_to(jnp.sum(tot[...], axis=1, keepdims=True), (ROWS, 128))
        latents[s] = (acc[...] * wide(1.0 / total, 4)).astype(jnp.bfloat16)
        level = top[...] * SCALE2 + jnp.log2(total)
        levels[s] = level if own else jnp.where(found_of[s] > 0, level, LOW)
        return carry

    lax.fori_loop(0, count, one_slot, 0)
    loads[1].wait()
    lane = lax.broadcasted_iota(jnp.int32, (TOK, 128), 1)
    for h in range(HEADS):
        rows = slice(h * TOK, (h + 1) * TOK)
        part = jnp.concatenate([latents[s, rows, :] for s in range(count)], axis=0)
        part = dot_nn(part, w_uv[h]).astype(jnp.bfloat16)
        for s in range(count):
            outs[s][:, h * VD : (h + 1) * VD] = part[s * TOK : (s + 1) * TOK]
    for s in range(count):
        level = levels[s, 0:TOK, :]
        for h in range(1, HEADS):
            level = jnp.where(lane % HEADS == h, levels[s, h * TOK : (h + 1) * TOK, :], level)
        high = level.astype(jnp.bfloat16).astype(jnp.float32)
        middle = (level - high).astype(jnp.bfloat16).astype(jnp.float32)
        low = level - high - middle
        stat = jnp.where(lane < HEADS, high, jnp.where(lane < 2 * HEADS, middle, low))
        outs[s][:, STAT:] = stat.astype(jnp.bfloat16)


def attention(slots, own, ids, table, lens, queries, pools, w_uk, w_uv, fresh):
    count = len(slots)
    full = pl.BlockSpec(memory_space=VMEM)
    scalar = pl.BlockSpec(memory_space=SMEM)
    free = pl.BlockSpec(memory_space=pl.ANY)
    chunks = 16 // STEP
    return pl.pallas_call(
        functools.partial(attention_kernel, slots, own),
        out_shape=[jax.ShapeDtypeStruct((TOK, MSG), jnp.bfloat16)] * count,
        in_specs=[scalar] * 3 + [full] * count + [free] * 6 + [full] * (2 if own else 0),
        out_specs=[full] * count,
        scratch_shapes=[
            pltpu.VMEM((HEADS, NOPE, LAT), jnp.bfloat16),
            pltpu.VMEM((HEADS, LAT, VD), jnp.bfloat16),
            pltpu.VMEM((count, chunks, STEP * BLOCK, LAT), jnp.bfloat16),
            pltpu.VMEM((count, chunks, ROPE, STEP * BLOCK), jnp.bfloat16),
            pltpu.SemaphoreType.DMA((count, 16, 2)),
            pltpu.SemaphoreType.DMA((2,)),
            pltpu.SMEM((count,), jnp.int32),
            pltpu.SMEM((count,), jnp.int32),
            pltpu.VMEM((count, ROWS, LAT), jnp.bfloat16),
            pltpu.VMEM((count, ROWS, ROPE), jnp.bfloat16),
            pltpu.VMEM((ROWS, LAT), jnp.float32),
            pltpu.VMEM((ROWS, 128), jnp.float32),
            pltpu.VMEM((ROWS, 128), jnp.float32),
            pltpu.VMEM((count, ROWS, LAT), jnp.bfloat16),
            pltpu.VMEM((count, ROWS, 128), jnp.float32),
        ],
        compiler_params=pltpu.CompilerParams(vmem_limit_bytes=40 * 2**20),
        cost_estimate=pl.CostEstimate(
            flops=count * 2 * ROWS * 1024 * 1088, bytes_accessed=count * 2**21, transcendentals=count * ROWS * 1024
        ),
        name="attend",
    )(ids, table, lens, *queries, *pools, w_uk, w_uv, *fresh)


def combine_kernel(*refs):
    parts, out = refs[:SLOTS], refs[SLOTS]
    stats = [p[:, STAT:].astype(jnp.float32) for p in parts]
    for h in range(HEADS):
        columns = slice(h * VD, (h + 1) * VD)
        levels = [
            s[:, h : h + 1] + s[:, HEADS + h : HEADS + h + 1] + s[:, 2 * HEADS + h : 2 * HEADS + h + 1]
            for s in stats
        ]
        best = functools.reduce(jnp.maximum, levels)
        shares = [jnp.exp2(v - best) for v in levels]
        inverse = 1.0 / sum(shares)
        out[:, columns] = sum(
            p[:, columns].astype(jnp.float32) * (share * inverse) for p, share in zip(parts, shares)
        ).astype(jnp.bfloat16)


def project_kernel(ids, *refs):
    heads, mine, other = refs[:8], refs[8:12], refs[12:16]
    outs = refs[16:20]
    weights, sems, stacked, total = refs[20:]
    yl, x, k, zb, a = ids[0], ids[1], ids[2], ids[3], ids[4]
    copies = []
    for j in range(4):
        for side, pieces in enumerate((mine, other)):
            first = pl.multiple_of((k ^ side) * 448, 64)
            copy = pltpu.make_async_copy(pieces[j], weights.at[j, pl.ds(first, 448), :], sems.at[j, side])
            copy.start()
            copies.append(copy)
    for m in range(8):
        stacked[a ^ (m & 3), pl.ds(pl.multiple_of((yl ^ (m >> 2)) * TOK, TOK), TOK), :] = heads[m][...]
    for copy in copies:
        copy.wait()
    value = None
    for j in range(4):
        part = dot_nt(stacked[(x + j) % 4], weights[j])
        value = part if value is None else value + part
    total[...] = value
    for d in range(4):
        first = pl.multiple_of(((zb + d) % 4) * 32, 32)
        for half in range(2):
            outs[d][half * 32 : (half + 1) * 32, :] = total[pl.ds(first + half * TOK, 32), :].astype(jnp.bfloat16)


def share_kernel(*refs):
    parts, out = refs[:4], refs[4]
    out[...] = sum(p[...].astype(jnp.float32) for p in parts).reshape(8, 8, 896)


def place_kernel(parts, out):
    for m in range(8):
        out[:, m * 896 : (m + 1) * 896] = parts[m].astype(jnp.bfloat16)


def tie_kernel(*refs):
    pass


def tie(value, *others):
    free = pl.BlockSpec(memory_space=pl.ANY)
    return pl.pallas_call(
        tie_kernel,
        out_shape=jax.ShapeDtypeStruct(value.shape, value.dtype),
        in_specs=[free] * (1 + len(others)),
        out_specs=free,
        input_output_aliases={0: 0},
        name="tie",
    )(value, *others)


def simple(kernel, name, out_shape, args, scratch=(), any_from=None):
    full = pl.BlockSpec(memory_space=VMEM)
    specs = [
        pl.BlockSpec(memory_space=SMEM)
        if arg.dtype == jnp.int32
        else pl.BlockSpec(memory_space=pl.ANY)
        if any_from is not None and i >= any_from
        else full
        for i, arg in enumerate(args)
    ]
    return pl.pallas_call(
        kernel,
        out_shape=out_shape,
        in_specs=specs,
        out_specs=jax.tree.map(lambda _: full, out_shape),
        scratch_shapes=scratch,
        compiler_params=pltpu.CompilerParams(vmem_limit_bytes=40 * 2**20),
        name=name,
    )(*args)


GROUP = ("yl", "z0", "yh")


def turn(value, axis, size, shift):
    return lax.ppermute(value, axis, [((i + shift) % size, i) for i in range(size)])


def flip(value, axis, size, bits):
    return lax.ppermute(value, axis, [(i, i ^ bits) for i in range(size)])


def local(
    q_nope,
    q_rope,
    new_latent,
    new_rope,
    pool_latent,
    pool_rope,
    block_table,
    prefix_len,
    w_uk,
    w_uv,
    w_out,
):
    ids = jnp.stack(
        [
            lax.axis_index("yl"),
            lax.axis_index("x"),
            lax.axis_index("k"),
            lax.axis_index("zb"),
            lax.axis_index("z0") * 2 + lax.axis_index("yh"),
        ]
    ).astype(jnp.int32)
    query = jnp.concatenate([q_nope, q_rope], axis=1)
    pool = jnp.concatenate(
        [pool_latent.reshape(4 * BLOCK, LAT), jnp.transpose(pool_rope, (1, 0, 2)).reshape(ROPE, 4 * BLOCK)], axis=0
    )
    weight = w_out.T

    pool_y = flip(pool, "yl", 2, 1)
    queries = [turn(query, "x", 4, s) for s in (1, 2, 3)]
    pool_k = flip(pool, "k", 2, 1)
    pool_y = tie(pool_y, pool_k, *queries)
    pool_yk = flip(pool_y, "k", 2, 1)
    pools = [pool, pool_y, pool_k, pool_yk]

    turned = lax.ppermute(
        weight, ("x", "z0", "yh"), [(i * 4 + j, j * 4 + i) for i in range(4) for j in range(4)]
    )
    mine = [turned] + [turn(turned, "x", 4, s) for s in (1, 2, 3)]
    other = [flip(w, "k", 2, 1) for w in mine]

    away = attention((1, 2, 3), False, ids, block_table, prefix_len, queries, pools, w_uk, w_uv, ())
    came = [
        lax.ppermute(part, "x", [(i, (i + s) % 4) for i in range(4)]) for s, part in zip((1, 2, 3), away)
    ]
    (home,) = attention(
        (0,), True, ids, block_table, prefix_len, [query], pools, w_uk, w_uv, (new_latent, new_rope[0])
    )
    head_out = simple(
        combine_kernel, "combine", jax.ShapeDtypeStruct((TOK, HEADS * VD), jnp.bfloat16), [home, *came]
    )
    heads = [head_out] + [flip(head_out, GROUP, 8, m) for m in range(1, 8)]
    partial = simple(
        project_kernel,
        "project",
        [jax.ShapeDtypeStruct((64, 896), jnp.bfloat16)] * 4,
        [ids, *heads, *mine, *other],
        scratch=[
            pltpu.VMEM((4, 896, 512), jnp.bfloat16),
            pltpu.SemaphoreType.DMA((4, 2)),
            pltpu.VMEM((4, 256, 512), jnp.bfloat16),
            pltpu.VMEM((256, 896), jnp.float32),
        ],
        any_from=9,
    )
    sums = [partial[0]] + [
        lax.ppermute(partial[d], "zb", [(i, (i + d) % 4) for i in range(4)]) for d in (1, 2, 3)
    ]
    pieces = simple(share_kernel, "share", jax.ShapeDtypeStruct((8, 8, 896), jnp.float32), sums)
    pieces = lax.all_to_all(pieces, GROUP, 0, 0, tiled=True)
    return simple(place_kernel, "place", jax.ShapeDtypeStruct((8, 7168), jnp.bfloat16), [pieces])


def solution(mesh):
    fine = Mesh(mesh.devices.reshape(2, 4, 2, 4, 2, 2), ("yl", "x", "k", "zb", "z0", "yh"))
    cache, head = ("yl", "x", "k"), ("zb", "z0", "yh")
    return jax.shard_map(
        local,
        mesh=fine,
        in_specs=(
            P(cache, head),
            P(cache, head),
            P(cache, None),
            P(cache, None, None),
            P(cache, None, None),
            P(cache, None, None),
            P(),
            P(),
            P(head, None, None),
            P(head, None, None),
            P(head, cache),
        ),
        out_specs=P(cache + head, None),
        check_vma=False,
    )
```

time: 155 us -> 144 us (0.929)
  starting transfers between devices: 67.3 us -> 43.4 us
  blocking collectives: 0 us -> 10.5 us
  Pallas kernels: 38 us -> 31.5 us
  waiting for transfers between devices: 42.9 us -> 48.2 us
  local copies, waits for them, and re-layouts: 3.06 us -> 7.78 us
    ppermute x1, waiting for transfers between devices: 0.01 us -> 21.1 us  [local(): lax.ppermute(weight, ('x', 'z0', 'yh'), [(i * 4 + j, j * 4 + i) for i in...]
    ppermute x21 -> x14, starting transfers between devices: 32.4 us -> 14.7 us  [flip(): return lax.ppermute(value, axis, [(i, i ^ bits) for i in range(size)])]
    ppermute x21 -> x14, waiting for transfers between devices: 19.5 us -> 7.58 us  [flip(): return lax.ppermute(value, axis, [(i, i ^ bits) for i in range(size)])]
    all_to_all x0 -> x1, blocking collectives: none -> 10.5 us  [local(): pieces = lax.all_to_all(pieces, GROUP, 0, 0, tiled=True)]
    ppermute x6, starting transfers between devices: 16.6 us -> 7.35 us  [turn(): lax.ppermute(value, axis, [((i + shift) % size, i) for i in range(size)])]
    pallas_call x2, Pallas kernels: 31.5 us -> 26.1 us  [attention(): pl.pallas_call(functools.partial(attention_kernel, slots, own), out_shape...]
    unnamed x21 -> x39, local copies, waits for them, and re-layouts: 2.96 us -> 7.68 us
    ppermute x1, starting transfers between devices: 6.07 us -> 8.16 us  [local(): lax.ppermute(weight, ('x', 'z0', 'yh'), [(i * 4 + j, j * 4 + i) for i in...]
  transfers between devices with their start and end apart: 34 -> 27, of which waited for: 14 -> 11; matrix products, arithmetic and copies ran while one was open for 0% -> 0% of each run, Pallas kernels for 21% -> 19%
where the time goes in v2:
time: 144 us; the launch traced here: 143 us
  waiting for transfers between devices  48.2 us (33%)
  starting transfers between devices  43.4 us (30%)
  Pallas kernels  31.5 us (22%)
  blocking collectives  10.5 us (7%)
  local copies, waits for them, and re-layouts  7.78 us (5%)
    pallas_call x2, Pallas kernels, attention(): pl.pallas_call(functools.partial(attention_kernel, slots, own), out_shape...  26.1 us
    ppermute x1, waiting for transfers between devices, local(): lax.ppermute(weight, ('x', 'z0', 'yh'), [(i * 4 + j, j * 4 + i) for i in...  21.1 us
    ppermute x14, starting transfers between devices, flip(): return lax.ppermute(value, axis, [(i, i ^ bits) for i in range(size)])  14.7 us
    ppermute x3, starting transfers between devices, local(): lax.ppermute(partial[d], 'zb', [(i, (i + d) % 4) for i in range(4)])  10.8 us
    all_to_all x1, blocking collectives, local(): pieces = lax.all_to_all(pieces, GROUP, 0, 0, tiled=True)  10.5 us
    ppermute x6, waiting for transfers between devices, turn(): lax.ppermute(value, axis, [((i + shift) % size, i) for i in range(size)])  8.96 us
    ppermute x1, starting transfers between devices, local(): lax.ppermute(weight, ('x', 'z0', 'yh'), [(i * 4 + j, j * 4 + i) for i in...  8.16 us
    unnamed x39, local copies, waits for them, and re-layouts  7.68 us
  transfers between devices with their start and end apart: 27, of which 11 were waited for; matrix products, arithmetic and copies ran while one was open for 0% of the time, Pallas kernels for 19%

profile of v2, /device:TPU:6, one launch (start us, length us, event | category | flops | bytes accessed | tf_op | source)
XLA Modules:
  0.0 142.8 jit_solution(8785190192307256290)
XLA Ops:
  0.0 0.8 copy-done
  0.9 0.0 copy-start.17
  0.9 0.0 copy-start.18
  0.9 1.1 pad_maximum_fusion.refs_1_.refs_3_
  2.0 0.1 collective-permute-start.1
  2.1 1.7 %collective-permute-start = (bf16[576,512]{1,0:T(8,128)(2,1)S(1)}, bf16[576,512]{1,0:T(8,128)(2,1)S(1)}, u32[]{:S(2)}, u32[]{:S(2)}) collective-permute-start(bf16[576,512]{1,0:T(8,128)(2,1)S(1)} %pad_maximum_fusion.refs_1_.refs_3_), channel_id=1, source_target_pairs={{0,128},{128,0},{1,129},{129,1},{2,130},{130,2},{3,131},{131,3},{4... | collective-permute-start | bytes 1769480 | tf_op jit(solution)/shard_map/ppermute | solution.py:329
  3.8 0.0 copy-start.11
  3.8 0.0 copy-start.15
  3.8 0.0 copy-start.16
  3.8 0.9 collective-permute-start.2
  4.7 1.3 collective-permute-start.3
  6.1 1.9 %collective-permute-start.4 = (bf16[128,768]{1,0:T(8,128)(2,1)S(1)}, bf16[128,768]{1,0:T(8,128)(2,1)S(1)}, u32[]{:S(2)}, u32[]{:S(2)}) collective-permute-start(bf16[128,768]{1,0:T(8,128)(2,1)S(1)} %constant_dynamic-update-slice_fusion.refs_0_), channel_id=1, source_target_pairs={{96,0},{0,32},{32,64},{64,96},{97,1},{1,33},{33,65},{65,97},{98,2}... | collective-permute-start | bytes 589832 | tf_op jit(solution)/shard_map/ppermute | solution.py:325
  8.0 8.3 %collective-permute-done.2.refs_2_.refs_0_ = bf16[128,768]{1,0:T(8,128)(2,1)S(1)} collective-permute-done((bf16[128,768]{1,0:T(8,128)(2,1)S(1)}, bf16[128,768]{1,0:T(8,128)(2,1)S(1)}, u32[]{:S(2)}, u32[]{:S(2)}) %collective-permute-start.2) | collective-permute-done | bytes 196640 | tf_op jit(solution)/shard_map/ppermute | solution.py:325
  16.3 0.0 collective-permute-done.3.refs_3_.refs_1_
  16.3 0.6 collective-permute-done.4.refs_4_.refs_2_
  16.9 0.0 collective-permute-done.1.refs_1_.refs_3_.refs_5_
  16.9 0.9 collective-permute-done.refs_0_
  17.9 0.8 copy-done.3
  18.7 8.2 %collective-permute-start.16 = (bf16[448,512]{1,0:T(8,128)(2,1)}, bf16[448,512]{1,0:T(8,128)(2,1)S(1)}, u32[]{:S(2)}, u32[]{:S(2)}) collective-permute-start(bf16[448,512]{1,0:T(8,128)(2,1)} %bitcast.16), channel_id=1, source_target_pairs={{0,0},{1,32},{2,64},{3,96},{32,1},{33,33},{34,65},{35,97},{64,2},{... | collective-permute-start | bytes 1376264 | tf_op jit(solution)/shard_map/ppermute | solution.py:367
  26.9 0.1 stack.23.ids
  27.0 21.1 %collective-permute-done.16.refs_8_ = bf16[448,512]{1,0:T(8,128)(2,1)S(1)} collective-permute-done((bf16[448,512]{1,0:T(8,128)(2,1)}, bf16[448,512]{1,0:T(8,128)(2,1)S(1)}, u32[]{:S(2)}, u32[]{:S(2)}) %collective-permute-start.16) | collective-permute-done | bytes 458784 | tf_op jit(solution)/shard_map/ppermute | solution.py:367
  48.1 0.0 collective-permute-start.17
  48.1 3.2 %collective-permute-start.19 = (bf16[448,512]{1,0:T(8,128)(2,1)S(1)}, bf16[448,512]{1,0:T(8,128)(2,1)S(1)}, u32[]{:S(2)}, u32[]{:S(2)}) collective-permute-start(bf16[448,512]{1,0:T(8,128)(2,1)S(1)} %collective-permute-done.16.refs_8_), channel_id=1, source_target_pairs={{96,0},{0,32},{32,64},{64,96},{97,1},{1,33},{33,65},{65,97},{98,2}... | collective-permute-start | bytes 1376264 | tf_op jit(solution)/shard_map/ppermute | solution.py:325
  51.3 0.0 collective-permute-done.5.refs_4_.refs_6_
  51.4 1.1 copy-done.2
  52.4 1.1 copy-done.4
  53.5 0.9 copy-done.6
  54.4 0.9 copy-done.8
  55.3 0.9 copy-done.10
  56.3 1.0 copy-done.12
  57.3 16.4 %attend.3 = (bf16[128,640]{1,0:T(8,128)(2,1)S(1)}, bf16[128,640]{1,0:T(8,128)(2,1)S(1)}, bf16[128,640]{1,0:T(8,128)(2,1)S(1)}) custom-call(s32[5]{0:T(128)S(1)} %stack.23.ids, s32[16,32]{1,0:T(8,128)S(1)} %copy-done.15, s32[16]{0:T(128)S(1)} %copy-done.16, bf16[128,768]{1,0:T(8,128)(2,1)S(1)} %copy-done.6, bf16[128,768]{1,0:T(8,128)(2,1)S(1)} %copy-done.8, ...), custom_call_target="tpu_custom_call" | custom-call | flops 3422552064 | bytes 6291456 | tf_op jit(solution)/shard_map/attend/pallas_call | solution.py:200
  73.7 0.1 collective-permute-start.6
  73.8 1.5 %collective-permute-start.20 = (bf16[448,512]{1,0:T(8,128)(2,1)S(1)}, bf16[448,512]{1,0:T(8,128)(2,1)S(1)}, u32[]{:S(2)}, u32[]{:S(2)}) collective-permute-start(bf16[448,512]{1,0:T(8,128)(2,1)S(1)} %collective-permute-done.16.refs_8_), channel_id=1, source_target_pairs={{0,16},{16,0},{1,17},{17,1},{2,18},{18,2},{3,19},{19,3},{4,20},{20... | collective-permute-start | bytes 1376264 | tf_op jit(solution)/shard_map/ppermute | solution.py:329
  75.3 0.0 collective-permute-done.17.refs_9_
  75.3 0.1 collective-permute-start.21
  75.4 0.4 collective-permute-start.22
  75.8 0.0 collective-permute-done.19.refs_11_
  75.8 0.7 collective-permute-start.7
  76.5 4.0 %collective-permute-done.6.refs_1_ = bf16[128,640]{1,0:T(8,128)(2,1)S(1)} collective-permute-done((bf16[128,640]{1,0:T(8,128)(2,1)S(1)}, bf16[128,640]{1,0:T(8,128)(2,1)S(1)}, u32[]{:S(2)}, u32[]{:S(2)}) %collective-permute-start.6) | collective-permute-done | bytes 163872 | tf_op jit(solution)/shard_map/ppermute | solution.py:375
  80.5 0.8 collective-permute-start.23
  81.3 2.4 %collective-permute-done.7.refs_2_ = bf16[128,640]{1,0:T(8,128)(2,1)S(1)} collective-permute-done((bf16[128,640]{1,0:T(8,128)(2,1)S(1)}, bf16[128,640]{1,0:T(8,128)(2,1)S(1)}, u32[]{:S(2)}, u32[]{:S(2)}) %collective-permute-start.7) | collective-permute-done | bytes 163872 | tf_op jit(solution)/shard_map/ppermute | solution.py:375
  83.7 1.6 %collective-permute-start.8 = (bf16[128,640]{1,0:T(8,128)(2,1)S(1)}, bf16[128,640]{1,0:T(8,128)(2,1)S(1)}, u32[]{:S(2)}, u32[]{:S(2)}) collective-permute-start(bf16[128,640]{1,0:T(8,128)(2,1)S(1)} %get-tuple-element.14), channel_id=1, source_target_pairs={{0,96},{32,0},{64,32},{96,64},{1,97},{33,1},{65,33},{97,65},{2,98}... | collective-permute-start | bytes 491528 | tf_op jit(solution)/shard_map/ppermute | solution.py:375
  85.3 9.7 %attend.2.refs_0_ = bf16[128,640]{1,0:T(8,128)(2,1)S(1)} custom-call(s32[5]{0:T(128)S(1)} %stack.23.ids, s32[16,32]{1,0:T(8,128)S(1)} %copy-done.15, s32[16]{0:T(128)S(1)} %copy-done.16, bf16[128,768]{1,0:T(8,128)(2,1)S(1)} %constant_dynamic-update-slice_fusion.refs_0_, bf16[576,512]{1,0:T(8,128)(2,1)S(1)} %pad_maximum_fusion.refs_1_.refs_3_, ...), custom_call_target="tpu_custom_call" | custom-call | flops 1140850688 | bytes 2097152 | tf_op jit(solution)/shard_map/attend/pallas_call | solution.py:200
  95.0 0.5 combine.1.refs_0_
  95.6 0.7 collective-permute-start.10
  96.3 0.0 collective-permute-done.20.refs_12_
  96.3 2.6 %collective-permute-start.11 = (bf16[128,512]{1,0:T(8,128)(2,1)S(1)}, bf16[128,512]{1,0:T(8,128)(2,1)S(1)}, u32[]{:S(2)}, u32[]{:S(2)}) collective-permute-start(bf16[128,512]{1,0:T(8,128)(2,1)S(1)} %combine.1.refs_0_), channel_id=1, source_target_pairs={{0,3},{1,2},{2,1},{3,0},{128,131},{129,130},{130,129},{131,128},{4... | collective-permute-start | bytes 393224 | tf_op jit(solution)/shard_map/ppermute | solution.py:329
  98.9 2.3 %collective-permute-start.13 = (bf16[128,512]{1,0:T(8,128)(2,1)S(1)}, bf16[128,512]{1,0:T(8,128)(2,1)S(1)}, u32[]{:S(2)}, u32[]{:S(2)}) collective-permute-start(bf16[128,512]{1,0:T(8,128)(2,1)S(1)} %combine.1.refs_0_), channel_id=1, source_target_pairs={{0,129},{1,128},{2,131},{3,130},{128,1},{129,0},{130,3},{131,2},{4... | collective-permute-start | bytes 393224 | tf_op jit(solution)/shard_map/ppermute | solution.py:329
  101.2 0.0 collective-permute-done.23.refs_15_
  101.2 1.1 collective-permute-start.14
  102.4 2.1 %collective-permute-start.15 = (bf16[128,512]{1,0:T(8,128)(2,1)S(1)}, bf16[128,512]{1,0:T(8,128)(2,1)S(1)}, u32[]{:S(2)}, u32[]{:S(2)}) collective-permute-start(bf16[128,512]{1,0:T(8,128)(2,1)S(1)} %combine.1.refs_0_), channel_id=1, source_target_pairs={{0,131},{1,130},{2,129},{3,128},{128,3},{129,2},{130,1},{131,0},{4... | collective-permute-start | bytes 393224 | tf_op jit(solution)/shard_map/ppermute | solution.py:329
  104.4 1.5 %collective-permute-done.11.refs_3_ = bf16[128,512]{1,0:T(8,128)(2,1)S(1)} collective-permute-done((bf16[128,512]{1,0:T(8,128)(2,1)S(1)}, bf16[128,512]{1,0:T(8,128)(2,1)S(1)}, u32[]{:S(2)}, u32[]{:S(2)}) %collective-permute-start.11) | collective-permute-done | bytes 131104 | tf_op jit(solution)/shard_map/ppermute | solution.py:329
  105.9 1.3 collective-permute-start.9
  107.2 2.5 %collective-permute-done.15.refs_7_ = bf16[128,512]{1,0:T(8,128)(2,1)S(1)} collective-permute-done((bf16[128,512]{1,0:T(8,128)(2,1)S(1)}, bf16[128,512]{1,0:T(8,128)(2,1)S(1)}, u32[]{:S(2)}, u32[]{:S(2)}) %collective-permute-start.15) | collective-permute-done | bytes 131104 | tf_op jit(solution)/shard_map/ppermute | solution.py:329
  109.7 2.7 %collective-permute-done.9.refs_1_ = bf16[128,512]{1,0:T(8,128)(2,1)S(1)} collective-permute-done((bf16[128,512]{1,0:T(8,128)(2,1)S(1)}, bf16[128,512]{1,0:T(8,128)(2,1)S(1)}, u32[]{:S(2)}, u32[]{:S(2)}) %collective-permute-start.9) | collective-permute-done | bytes 131104 | tf_op jit(solution)/shard_map/ppermute | solution.py:329
  112.4 4.2 %project.1 = (bf16[64,896]{1,0:T(8,128)(2,1)S(1)}, bf16[64,896]{1,0:T(8,128)(2,1)S(1)}, bf16[64,896]{1,0:T(8,128)(2,1)S(1)}, bf16[64,896]{1,0:T(8,128)(2,1)S(1)}) custom-call(s32[5]{0:T(128)S(1)} %stack.23.ids, bf16[128,512]{1,0:T(8,128)(2,1)S(1)} %combine.1.refs_0_, bf16[128,512]{1,0:T(8,128)(2,1)S(1)} %collective-permute-done.9.refs_1_, ...), custom_call_target="tpu_custom_call" | custom-call | tf_op jit(solution)/shard_map/project/pallas_call | solution.py:310
  116.6 3.4 %collective-permute-start.24 = (bf16[64,896]{1,0:T(8,128)(2,1)S(1)}, bf16[64,896]{1,0:T(8,128)(2,1)S(1)}, u32[]{:S(2)}, u32[]{:S(2)}) collective-permute-start(bf16[64,896]{1,0:T(8,128)(2,1)S(1)} %get-tuple-element.16), channel_id=1, source_target_pairs={{0,4},{4,8},{8,12},{12,0},{1,5},{5,9},{9,13},{13,1},{2,6},{6,10},{... | collective-permute-start | bytes 344072 | tf_op jit(solution)/shard_map/ppermute | solution.py:398
  119.9 4.6 %collective-permute-start.25 = (bf16[64,896]{1,0:T(8,128)(2,1)S(1)}, bf16[64,896]{1,0:T(8,128)(2,1)S(1)}, u32[]{:S(2)}, u32[]{:S(2)}) collective-permute-start(bf16[64,896]{1,0:T(8,128)(2,1)S(1)} %get-tuple-element.17), channel_id=1, source_target_pairs={{0,8},{4,12},{8,0},{12,4},{1,9},{5,13},{9,1},{13,5},{2,10},{6,14},... | collective-permute-start | bytes 344072 | tf_op jit(solution)/shard_map/ppermute | solution.py:398
  124.6 2.8 %collective-permute-start.26 = (bf16[64,896]{1,0:T(8,128)(2,1)S(1)}, bf16[64,896]{1,0:T(8,128)(2,1)S(1)}, u32[]{:S(2)}, u32[]{:S(2)}) collective-permute-start(bf16[64,896]{1,0:T(8,128)(2,1)S(1)} %get-tuple-element.18), channel_id=1, source_target_pairs={{0,12},{4,0},{8,4},{12,8},{1,13},{5,1},{9,5},{13,9},{2,14},{6,2},{... | collective-permute-start | bytes 344072 | tf_op jit(solution)/shard_map/ppermute | solution.py:398
  127.4 2.5 %collective-permute-done.24.refs_1_ = bf16[64,896]{1,0:T(8,128)(2,1)S(1)} collective-permute-done((bf16[64,896]{1,0:T(8,128)(2,1)S(1)}, bf16[64,896]{1,0:T(8,128)(2,1)S(1)}, u32[]{:S(2)}, u32[]{:S(2)}) %collective-permute-start.24) | collective-permute-done | bytes 114720 | tf_op jit(solution)/shard_map/ppermute | solution.py:398
  129.8 1.7 %collective-permute-done.26.refs_3_ = bf16[64,896]{1,0:T(8,128)(2,1)S(1)} collective-permute-done((bf16[64,896]{1,0:T(8,128)(2,1)S(1)}, bf16[64,896]{1,0:T(8,128)(2,1)S(1)}, u32[]{:S(2)}, u32[]{:S(2)}) %collective-permute-start.26) | collective-permute-done | bytes 114720 | tf_op jit(solution)/shard_map/ppermute | solution.py:398
  131.5 0.1 share.1
  131.6 10.5 %all_to_all.5.parts = f32[8,8,896]{2,1,0:T(8,128)S(1)} all-to-all(f32[8,8,896]{2,1,0:T(8,128)S(1)} %share.1), channel_id=1, replica_groups=mesh['yl'=2,'x'=4,'k'=2,'zb'=4,'z0'=2,'yh'=2] {'yl','z0','yh'}, dimensions={0} | all-to-all | bytes 458752 | tf_op jit(solution)/shard_map/all_to_all | solution.py:401
  142.1 0.7 place.1
  (41 shorter events, 0.1 us)
Async XLA Ops:
  0.0 0.8 copy-start
  0.9 2.9 %copy-start.17 = (bf16[128,512]{1,0:T(8,128)(2,1)S(1)}, bf16[128,512]{1,0:T(8,128)(2,1)}, u32[]{:S(2)}) copy-start(bf16[128,512]{1,0:T(8,128)(2,1)} %param.11) | copy-start | bytes 393220
  0.9 2.9 %copy-start.18 = (bf16[128,256]{1,0:T(8,128)(2,1)S(1)}, bf16[128,256]{1,0:T(8,128)(2,1)}, u32[]{:S(2)}) copy-start(bf16[128,256]{1,0:T(8,128)(2,1)} %param.12) | copy-start | bytes 196612
  2.0 14.9 %collective-permute-start.1 = (bf16[576,512]{1,0:T(8,128)(2,1)S(1)}, bf16[576,512]{1,0:T(8,128)(2,1)S(1)}, u32[]{:S(2)}, u32[]{:S(2)}) collective-permute-start(bf16[576,512]{1,0:T(8,128)(2,1)S(1)} %pad_maximum_fusion.refs_1_.refs_3_), channel_id=1, source_target_pairs={{0,16},{16,0},{1,17},{17,1},{2,18},{18,2},{3,19},{19,3},{4,20},{20... | collective-permute-start | bytes 1769480 | tf_op jit(solution)/shard_map/ppermute | solution.py:329
  2.1 15.7 %collective-permute-start = (bf16[576,512]{1,0:T(8,128)(2,1)S(1)}, bf16[576,512]{1,0:T(8,128)(2,1)S(1)}, u32[]{:S(2)}, u32[]{:S(2)}) collective-permute-start(bf16[576,512]{1,0:T(8,128)(2,1)S(1)} %pad_maximum_fusion.refs_1_.refs_3_), channel_id=1, source_target_pairs={{0,128},{128,0},{1,129},{129,1},{2,130},{130,2},{3,131},{131,3},{4... | collective-permute-start | bytes 1769480 | tf_op jit(solution)/shard_map/ppermute | solution.py:329
  3.8 47.5 %copy-start.11 = (bf16[4,128,512]{2,1,0:T(8,128)(2,1)S(1)}, bf16[4,128,512]{2,1,0:T(8,128)(2,1)}, u32[]{:S(2)}) copy-start(bf16[4,128,512]{2,1,0:T(8,128)(2,1)} %refs_7_.3) | copy-start | bytes 1572868
  3.8 47.5 %copy-start.15 = (s32[16,32]{1,0:T(8,128)S(1)}, s32[16,32]{1,0:T(8,128)}, u32[]{:S(2)}) copy-start(s32[16,32]{1,0:T(8,128)} %table.3) | copy-start | bytes 6148
  3.8 47.5 %copy-start.16 = (s32[16]{0:T(128)S(1)}, s32[16]{0:T(128)}, u32[]{:S(2)}) copy-start(s32[16]{0:T(128)} %lens.3) | copy-start | bytes 196
  3.8 12.5 %collective-permute-start.2 = (bf16[128,768]{1,0:T(8,128)(2,1)S(1)}, bf16[128,768]{1,0:T(8,128)(2,1)S(1)}, u32[]{:S(2)}, u32[]{:S(2)}) collective-permute-start(bf16[128,768]{1,0:T(8,128)(2,1)S(1)} %constant_dynamic-update-slice_fusion.refs_0_), channel_id=1, source_target_pairs={{32,0},{64,32},{96,64},{0,96},{33,1},{65,33},{97,65},{1,97},{34,2}... | collective-permute-start | bytes 589832 | tf_op jit(solution)/shard_map/ppermute | solution.py:325
  4.7 11.6 %collective-permute-start.3 = (bf16[128,768]{1,0:T(8,128)(2,1)S(1)}, bf16[128,768]{1,0:T(8,128)(2,1)S(1)}, u32[]{:S(2)}, u32[]{:S(2)}) collective-permute-start(bf16[128,768]{1,0:T(8,128)(2,1)S(1)} %constant_dynamic-update-slice_fusion.refs_0_), channel_id=1, source_target_pairs={{64,0},{96,32},{0,64},{32,96},{65,1},{97,33},{1,65},{33,97},{66,2}... | collective-permute-start | bytes 589832 | tf_op jit(solution)/shard_map/ppermute | solution.py:325
  6.1 10.8 %collective-permute-start.4 = (bf16[128,768]{1,0:T(8,128)(2,1)S(1)}, bf16[128,768]{1,0:T(8,128)(2,1)S(1)}, u32[]{:S(2)}, u32[]{:S(2)}) collective-permute-start(bf16[128,768]{1,0:T(8,128)(2,1)S(1)} %constant_dynamic-update-slice_fusion.refs_0_), channel_id=1, source_target_pairs={{96,0},{0,32},{32,64},{64,96},{97,1},{1,33},{33,65},{65,97},{98,2}... | collective-permute-start | bytes 589832 | tf_op jit(solution)/shard_map/ppermute | solution.py:325
  16.3 1.6 %copy-start.5 = (bf16[128,768]{1,0:T(8,128)(2,1)}, bf16[128,768]{1,0:T(8,128)(2,1)S(1)}, u32[]{:S(2)}) copy-start(bf16[128,768]{1,0:T(8,128)(2,1)S(1)} %collective-permute-done.2.refs_2_.refs_0_) | copy-start | bytes 589828
  16.3 1.6 %copy-start.7 = (bf16[128,768]{1,0:T(8,128)(2,1)}, bf16[128,768]{1,0:T(8,128)(2,1)S(1)}, u32[]{:S(2)}) copy-start(bf16[128,768]{1,0:T(8,128)(2,1)S(1)} %collective-permute-done.3.refs_3_.refs_1_) | copy-start | bytes 589828
  16.9 0.9 copy-start.9
  16.9 0.9 copy-start.1
  17.9 0.8 copy-start.3
  18.7 32.6 %collective-permute-start.5 = (bf16[576,512]{1,0:T(8,128)(2,1)}, bf16[576,512]{1,0:T(8,128)(2,1)S(1)}, u32[]{:S(2)}, u32[]{:S(2)}) collective-permute-start(bf16[576,512]{1,0:T(8,128)(2,1)} %tie.1.refs_2_.refs_4_), channel_id=1, source_target_pairs={{0,16},{16,0},{1,17},{17,1},{2,18},{18,2},{3,19},{19,3},{4,20},{20... | collective-permute-start | bytes 1769480 | tf_op jit(solution)/shard_map/ppermute | solution.py:329
  18.7 29.4 %collective-permute-start.16 = (bf16[448,512]{1,0:T(8,128)(2,1)}, bf16[448,512]{1,0:T(8,128)(2,1)S(1)}, u32[]{:S(2)}, u32[]{:S(2)}) collective-permute-start(bf16[448,512]{1,0:T(8,128)(2,1)} %bitcast.16), channel_id=1, source_target_pairs={{0,0},{1,32},{2,64},{3,96},{32,1},{33,33},{34,65},{35,97},{64,2},{... | collective-permute-start | bytes 1376264 | tf_op jit(solution)/shard_map/ppermute | solution.py:367
  48.1 27.2 %collective-permute-start.17 = (bf16[448,512]{1,0:T(8,128)(2,1)S(1)}, bf16[448,512]{1,0:T(8,128)(2,1)S(1)}, u32[]{:S(2)}, u32[]{:S(2)}) collective-permute-start(bf16[448,512]{1,0:T(8,128)(2,1)S(1)} %collective-permute-done.16.refs_8_), channel_id=1, source_target_pairs={{32,0},{64,32},{96,64},{0,96},{33,1},{65,33},{97,65},{1,97},{34,2}... | collective-permute-start | bytes 1376264 | tf_op jit(solution)/shard_map/ppermute | solution.py:325
  48.1 27.3 %collective-permute-start.18 = (bf16[448,512]{1,0:T(8,128)(2,1)S(1)}, bf16[448,512]{1,0:T(8,128)(2,1)S(1)}, u32[]{:S(2)}, u32[]{:S(2)}) collective-permute-start(bf16[448,512]{1,0:T(8,128)(2,1)S(1)} %collective-permute-done.16.refs_8_), channel_id=1, source_target_pairs={{64,0},{96,32},{0,64},{32,96},{65,1},{97,33},{1,65},{33,97},{66,2}... | collective-permute-start | bytes 1376264 | tf_op jit(solution)/shard_map/ppermute | solution.py:325
  48.1 27.7 %collective-permute-start.19 = (bf16[448,512]{1,0:T(8,128)(2,1)S(1)}, bf16[448,512]{1,0:T(8,128)(2,1)S(1)}, u32[]{:S(2)}, u32[]{:S(2)}) collective-permute-start(bf16[448,512]{1,0:T(8,128)(2,1)S(1)} %collective-permute-done.16.refs_8_), channel_id=1, source_target_pairs={{96,0},{0,32},{32,64},{64,96},{97,1},{1,33},{33,65},{65,97},{98,2}... | collective-permute-start | bytes 1376264 | tf_op jit(solution)/shard_map/ppermute | solution.py:325
  51.4 1.1 copy-start.2
  52.4 1.1 copy-start.4
  53.5 0.9 copy-start.6
  54.4 0.9 copy-start.8
  55.3 0.9 copy-start.10
  56.3 1.0 copy-start.12
  57.3 28.0 %copy-start.13 = (bf16[128,512]{1,0:T(8,128)(2,1)S(1)}, bf16[128,512]{1,0:T(8,128)(2,1)}, u32[]{:S(2)}) copy-start(bf16[128,512]{1,0:T(8,128)(2,1)} %refs_7_.2) | copy-start | bytes 393220
  57.3 28.0 %copy-start.14 = (bf16[1,64,128]{2,1,0:T(8,128)(2,1)S(1)}, bf16[1,64,128]{2,1,0:T(8,128)(2,1)}, u32[]{:S(2)}) copy-start(bf16[1,64,128]{2,1,0:T(8,128)(2,1)} %param.14) | copy-start | bytes 49156
  73.7 6.8 %collective-permute-start.6 = (bf16[128,640]{1,0:T(8,128)(2,1)S(1)}, bf16[128,640]{1,0:T(8,128)(2,1)S(1)}, u32[]{:S(2)}, u32[]{:S(2)}) collective-permute-start(bf16[128,640]{1,0:T(8,128)(2,1)S(1)} %get-tuple-element.12), channel_id=1, source_target_pairs={{0,32},{32,64},{64,96},{96,0},{1,33},{33,65},{65,97},{97,1},{2,34}... | collective-permute-start | bytes 491528 | tf_op jit(solution)/shard_map/ppermute | solution.py:375
  73.8 22.5 %collective-permute-start.20 = (bf16[448,512]{1,0:T(8,128)(2,1)S(1)}, bf16[448,512]{1,0:T(8,128)(2,1)S(1)}, u32[]{:S(2)}, u32[]{:S(2)}) collective-permute-start(bf16[448,512]{1,0:T(8,128)(2,1)S(1)} %collective-permute-done.16.refs_8_), channel_id=1, source_target_pairs={{0,16},{16,0},{1,17},{17,1},{2,18},{18,2},{3,19},{19,3},{4,20},{20... | collective-permute-start | bytes 1376264 | tf_op jit(solution)/shard_map/ppermute | solution.py:329
  75.3 23.6 %collective-permute-start.21 = (bf16[448,512]{1,0:T(8,128)(2,1)S(1)}, bf16[448,512]{1,0:T(8,128)(2,1)S(1)}, u32[]{:S(2)}, u32[]{:S(2)}) collective-permute-start(bf16[448,512]{1,0:T(8,128)(2,1)S(1)} %collective-permute-done.17.refs_9_), channel_id=1, source_target_pairs={{0,16},{16,0},{1,17},{17,1},{2,18},{18,2},{3,19},{19,3},{4,20},{20... | collective-permute-start | bytes 1376264 | tf_op jit(solution)/shard_map/ppermute | solution.py:329
  75.4 23.5 %collective-permute-start.22 = (bf16[448,512]{1,0:T(8,128)(2,1)S(1)}, bf16[448,512]{1,0:T(8,128)(2,1)S(1)}, u32[]{:S(2)}, u32[]{:S(2)}) collective-permute-start(bf16[448,512]{1,0:T(8,128)(2,1)S(1)} %collective-permute-done.18.refs_10_), channel_id=1, source_target_pairs={{0,16},{16,0},{1,17},{17,1},{2,18},{18,2},{3,19},{19,3},{4,20},{20... | collective-permute-start | bytes 1376264 | tf_op jit(solution)/shard_map/ppermute | solution.py:329
  75.8 7.9 %collective-permute-start.7 = (bf16[128,640]{1,0:T(8,128)(2,1)S(1)}, bf16[128,640]{1,0:T(8,128)(2,1)S(1)}, u32[]{:S(2)}, u32[]{:S(2)}) collective-permute-start(bf16[128,640]{1,0:T(8,128)(2,1)S(1)} %get-tuple-element.13), channel_id=1, source_target_pairs={{0,64},{32,96},{64,0},{96,32},{1,65},{33,97},{65,1},{97,33},{2,66}... | collective-permute-start | bytes 491528 | tf_op jit(solution)/shard_map/ppermute | solution.py:375
  80.5 20.7 %collective-permute-start.23 = (bf16[448,512]{1,0:T(8,128)(2,1)S(1)}, bf16[448,512]{1,0:T(8,128)(2,1)S(1)}, u32[]{:S(2)}, u32[]{:S(2)}) collective-permute-start(bf16[448,512]{1,0:T(8,128)(2,1)S(1)} %collective-permute-done.19.refs_11_), channel_id=1, source_target_pairs={{0,16},{16,0},{1,17},{17,1},{2,18},{18,2},{3,19},{19,3},{4,20},{20... | collective-permute-start | bytes 1376264 | tf_op jit(solution)/shard_map/ppermute | solution.py:329
  83.7 11.3 %collective-permute-start.8 = (bf16[128,640]{1,0:T(8,128)(2,1)S(1)}, bf16[128,640]{1,0:T(8,128)(2,1)S(1)}, u32[]{:S(2)}, u32[]{:S(2)}) collective-permute-start(bf16[128,640]{1,0:T(8,128)(2,1)S(1)} %get-tuple-element.14), channel_id=1, source_target_pairs={{0,96},{32,0},{64,32},{96,64},{1,97},{33,1},{65,33},{97,65},{2,98}... | collective-permute-start | bytes 491528 | tf_op jit(solution)/shard_map/ppermute | solution.py:375
  95.6 6.8 %collective-permute-start.10 = (bf16[128,512]{1,0:T(8,128)(2,1)S(1)}, bf16[128,512]{1,0:T(8,128)(2,1)S(1)}, u32[]{:S(2)}, u32[]{:S(2)}) collective-permute-start(bf16[128,512]{1,0:T(8,128)(2,1)S(1)} %combine.1.refs_0_), channel_id=1, source_target_pairs={{0,2},{1,3},{2,0},{3,1},{128,130},{129,131},{130,128},{131,129},{4... | collective-permute-start | bytes 393224 | tf_op jit(solution)/shard_map/ppermute | solution.py:329
  96.3 9.6 %collective-permute-start.11 = (bf16[128,512]{1,0:T(8,128)(2,1)S(1)}, bf16[128,512]{1,0:T(8,128)(2,1)S(1)}, u32[]{:S(2)}, u32[]{:S(2)}) collective-permute-start(bf16[128,512]{1,0:T(8,128)(2,1)S(1)} %combine.1.refs_0_), channel_id=1, source_target_pairs={{0,3},{1,2},{2,1},{3,0},{128,131},{129,130},{130,129},{131,128},{4... | collective-permute-start | bytes 393224 | tf_op jit(solution)/shard_map/ppermute | solution.py:329
  98.9 8.3 %collective-permute-start.12 = (bf16[128,512]{1,0:T(8,128)(2,1)S(1)}, bf16[128,512]{1,0:T(8,128)(2,1)S(1)}, u32[]{:S(2)}, u32[]{:S(2)}) collective-permute-start(bf16[128,512]{1,0:T(8,128)(2,1)S(1)} %combine.1.refs_0_), channel_id=1, source_target_pairs={{0,128},{1,129},{2,130},{3,131},{128,0},{129,1},{130,2},{131,3},{4... | collective-permute-start | bytes 393224 | tf_op jit(solution)/shard_map/ppermute | solution.py:329
  98.9 8.3 %collective-permute-start.13 = (bf16[128,512]{1,0:T(8,128)(2,1)S(1)}, bf16[128,512]{1,0:T(8,128)(2,1)S(1)}, u32[]{:S(2)}, u32[]{:S(2)}) collective-permute-start(bf16[128,512]{1,0:T(8,128)(2,1)S(1)} %combine.1.refs_0_), channel_id=1, source_target_pairs={{0,129},{1,128},{2,131},{3,130},{128,1},{129,0},{130,3},{131,2},{4... | collective-permute-start | bytes 393224 | tf_op jit(solution)/shard_map/ppermute | solution.py:329
  101.2 6.0 %collective-permute-start.14 = (bf16[128,512]{1,0:T(8,128)(2,1)S(1)}, bf16[128,512]{1,0:T(8,128)(2,1)S(1)}, u32[]{:S(2)}, u32[]{:S(2)}) collective-permute-start(bf16[128,512]{1,0:T(8,128)(2,1)S(1)} %combine.1.refs_0_), channel_id=1, source_target_pairs={{0,130},{1,131},{2,128},{3,129},{128,2},{129,3},{130,0},{131,1},{4... | collective-permute-start | bytes 393224 | tf_op jit(solution)/shard_map/ppermute | solution.py:329
  102.4 7.3 %collective-permute-start.15 = (bf16[128,512]{1,0:T(8,128)(2,1)S(1)}, bf16[128,512]{1,0:T(8,128)(2,1)S(1)}, u32[]{:S(2)}, u32[]{:S(2)}) collective-permute-start(bf16[128,512]{1,0:T(8,128)(2,1)S(1)} %combine.1.refs_0_), channel_id=1, source_target_pairs={{0,131},{1,130},{2,129},{3,128},{128,3},{129,2},{130,1},{131,0},{4... | collective-permute-start | bytes 393224 | tf_op jit(solution)/shard_map/ppermute | solution.py:329
  105.9 6.5 %collective-permute-start.9 = (bf16[128,512]{1,0:T(8,128)(2,1)S(1)}, bf16[128,512]{1,0:T(8,128)(2,1)S(1)}, u32[]{:S(2)}, u32[]{:S(2)}) collective-permute-start(bf16[128,512]{1,0:T(8,128)(2,1)S(1)} %combine.1.refs_0_), channel_id=1, source_target_pairs={{0,1},{1,0},{2,3},{3,2},{128,129},{129,128},{130,131},{131,130},{4... | collective-permute-start | bytes 393224 | tf_op jit(solution)/shard_map/ppermute | solution.py:329
  116.6 13.2 %collective-permute-start.24 = (bf16[64,896]{1,0:T(8,128)(2,1)S(1)}, bf16[64,896]{1,0:T(8,128)(2,1)S(1)}, u32[]{:S(2)}, u32[]{:S(2)}) collective-permute-start(bf16[64,896]{1,0:T(8,128)(2,1)S(1)} %get-tuple-element.16), channel_id=1, source_target_pairs={{0,4},{4,8},{8,12},{12,0},{1,5},{5,9},{9,13},{13,1},{2,6},{6,10},{... | collective-permute-start | bytes 344072 | tf_op jit(solution)/shard_map/ppermute | solution.py:398
  119.9 9.9 %collective-permute-start.25 = (bf16[64,896]{1,0:T(8,128)(2,1)S(1)}, bf16[64,896]{1,0:T(8,128)(2,1)S(1)}, u32[]{:S(2)}, u32[]{:S(2)}) collective-permute-start(bf16[64,896]{1,0:T(8,128)(2,1)S(1)} %get-tuple-element.17), channel_id=1, source_target_pairs={{0,8},{4,12},{8,0},{12,4},{1,9},{5,13},{9,1},{13,5},{2,10},{6,14},... | collective-permute-start | bytes 344072 | tf_op jit(solution)/shard_map/ppermute | solution.py:398
  124.6 6.9 %collective-permute-start.26 = (bf16[64,896]{1,0:T(8,128)(2,1)S(1)}, bf16[64,896]{1,0:T(8,128)(2,1)S(1)}, u32[]{:S(2)}, u32[]{:S(2)}) collective-permute-start(bf16[64,896]{1,0:T(8,128)(2,1)S(1)} %get-tuple-element.18), channel_id=1, source_target_pairs={{0,12},{4,0},{8,4},{12,8},{1,13},{5,1},{9,5},{13,9},{2,14},{6,2},{... | collective-permute-start | bytes 344072 | tf_op jit(solution)/shard_map/ppermute | solution.py:398

commit v3 on v2

v3 whole, which is shorter than its diff:
```python
import functools

import jax
import jax.numpy as jnp
from jax import lax
from jax.experimental import pallas as pl
from jax.experimental.pallas import tpu as pltpu
from jax.sharding import Mesh, PartitionSpec as P

LAT = 512
NOPE = 128
ROPE = 64
VD = 128
BLOCK = 128
HEADS = 4
TOK = 128
ROWS = HEADS * TOK
SLOTS = 4
STEP = 4
LOG2E = 1.4426950408889634
SCALE2 = (NOPE + ROPE) ** -0.5 * LOG2E
LOW = -1e30
STAT = HEADS * VD
MSG = STAT + 128

VMEM = pltpu.VMEM
SMEM = pltpu.SMEM


def dot_nn(a, b):
    return lax.dot_general(a, b, (((1,), (0,)), ((), ())), preferred_element_type=jnp.float32)


def dot_nt(a, b):
    return lax.dot_general(a, b, (((1,), (1,)), ((), ())), preferred_element_type=jnp.float32)


def prepare_kernel(ids, table, lens, *refs):
    queries = refs[:SLOTS]
    weight, q_lat, q_rot, lists, counts, w_uk, sem = refs[SLOTS:]
    yl, x, k = ids[0], ids[1], ids[2]
    load = pltpu.make_async_copy(weight, w_uk, sem)
    load.start()
    for s in range(SLOTS):
        limit = lens[yl * 8 + ((x + s) % 4) * 2 + k]

        def scan(m, carry):
            found, valid = carry
            block = table[yl * 8 + ((x + s) % 4) * 2 + k, m]
            owner = block >> 2
            here = ((owner >> 1) & 3) == x

            @pl.when(here)
            def _():
                source = ((owner >> 3) ^ yl) + 2 * ((owner & 1) ^ k)
                lists[s * 16 + found] = source * 4 + (block & 3)

            step = here.astype(jnp.int32)
            return found + step, valid + step * jnp.minimum(limit - m * BLOCK, BLOCK)

        blocks = jnp.minimum((limit + BLOCK - 1) // BLOCK, 32)
        found, valid = lax.fori_loop(0, blocks, scan, (jnp.int32(0), jnp.int32(0)))
        counts[s] = found
        counts[SLOTS + s] = valid
    load.wait()
    for h in range(HEADS):
        rows = slice(h * TOK, (h + 1) * TOK)
        part = jnp.concatenate([q[:, h * NOPE : (h + 1) * NOPE] for q in queries], axis=0)
        part = dot_nn(part, w_uk[h]).astype(jnp.bfloat16)
        first = HEADS * NOPE + h * ROPE
        for s in range(SLOTS):
            q_lat[s, rows, :] = part[s * TOK : (s + 1) * TOK]
            q_rot[s, rows, :] = queries[s][:, first : first + ROPE]


def prepare(ids, table, lens, queries, w_uk):
    full = pl.BlockSpec(memory_space=VMEM)
    scalar = pl.BlockSpec(memory_space=SMEM)
    return pl.pallas_call(
        prepare_kernel,
        out_shape=[
            jax.ShapeDtypeStruct((SLOTS, ROWS, LAT), jnp.bfloat16),
            jax.ShapeDtypeStruct((SLOTS, ROWS, ROPE), jnp.bfloat16),
            jax.ShapeDtypeStruct((SLOTS * 16,), jnp.int32),
            jax.ShapeDtypeStruct((2 * SLOTS,), jnp.int32),
        ],
        in_specs=[scalar] * 3 + [full] * SLOTS + [pl.BlockSpec(memory_space=pltpu.HBM)],
        out_specs=[full, full, scalar, scalar],
        scratch_shapes=[pltpu.VMEM((HEADS, NOPE, LAT), jnp.bfloat16), pltpu.SemaphoreType.DMA],
        compiler_params=pltpu.CompilerParams(vmem_limit_bytes=40 * 2**20),
        name="prepare",
    )(ids, table, lens, *queries, w_uk)


def attention_kernel(slots, own, lists, counts, q_lat, q_rot, *refs):
    count = len(slots)
    refs = list(refs)

    def take(n):
        got = refs[:n]
        del refs[:n]
        return got

    pools = take(4)
    (weight,) = take(1)
    new_latent, new_rope = take(2) if own else (None, None)
    outs = take(count)
    w_uv, keys, rots, sems, weight_sem, acc, top, tot, latents, levels = refs
    load = pltpu.make_async_copy(weight, w_uv, weight_sem)

    def fetch(s, src, i, at):
        chunk, part = at // STEP, pl.multiple_of((at % STEP) * BLOCK, BLOCK)
        return (
            pltpu.make_async_copy(
                src.at[pl.ds(pl.multiple_of(i * BLOCK, BLOCK), BLOCK), :],
                keys.at[s, chunk, pl.ds(part, BLOCK), :],
                sems.at[s, at, 0],
            ),
            pltpu.make_async_copy(
                src.at[pl.ds(4 * BLOCK, ROPE), pl.ds(pl.multiple_of(i * BLOCK, BLOCK), BLOCK)],
                rots.at[s, chunk, :, pl.ds(part, BLOCK)],
                sems.at[s, at, 1],
            ),
        )

    for s, slot in enumerate(slots):

        def bring(at, carry):
            code = lists[slot * 16 + at]
            for j in range(4):

                @pl.when((code >> 2) == j)
                def _():
                    for copy in fetch(s, pools[j], code & 3, at):
                        copy.start()

            return carry

        lax.fori_loop(0, counts[slot], bring, 0)
        if s == 0:
            load.start()

    for s, slot in enumerate(slots):
        found = counts[slot]
        for extra in range(STEP):
            at = found + extra

            @pl.when(at < jnp.maximum((found + STEP - 1) // STEP, 1) * STEP)
            def _():
                part = pl.multiple_of((at % STEP) * BLOCK, BLOCK)
                keys[s, at // STEP, pl.ds(part, BLOCK), :] = jnp.zeros((BLOCK, LAT), jnp.bfloat16)
                rots[s, at // STEP, :, pl.ds(part, BLOCK)] = jnp.zeros((ROPE, BLOCK), jnp.bfloat16)

    def wide(value, times):
        return jnp.concatenate([value] * times, axis=1)

    def begin(score, latent):
        best = jnp.broadcast_to(jnp.max(score, axis=1, keepdims=True), (ROWS, 128))
        times = score.shape[1] // 128
        weight = jnp.exp2((score - wide(best, times)) * SCALE2)
        top[...] = best
        tot[...] = sum(weight[:, i * 128 : (i + 1) * 128] for i in range(times))
        acc[...] = dot_nn(weight.astype(jnp.bfloat16), latent)

    def scores(s, found, valid, q, r, chunk):
        for b in range(STEP):

            @pl.when(chunk * STEP + b < found)
            def _():
                for copy in fetch(s, pools[0], 0, chunk * STEP + b):
                    copy.wait()

        score = dot_nt(q, keys[s, chunk]) + dot_nn(r, rots[s, chunk])
        seen = lax.broadcasted_iota(jnp.int32, score.shape, 1) < valid - chunk * STEP * BLOCK
        return jnp.where(seen, score, LOW)

    def one_slot(s, carry):
        slot = s + slots[0]
        found, valid = counts[slot], counts[SLOTS + slot]
        q, r = q_lat[slot], q_rot[slot]
        if own:
            score = dot_nt(q, new_latent[...]) + dot_nn(r, new_rope[...])
            at = lax.broadcasted_iota(jnp.int32, score.shape, 0) % TOK
            seen = lax.broadcasted_iota(jnp.int32, score.shape, 1) <= at
            begin(jnp.where(seen, score, LOW), new_latent[...])
        else:
            begin(scores(s, found, valid, q, r, 0), keys[s, 0])

        def step(chunk, inner):
            score = scores(s, found, valid, q_lat[slot], q_rot[slot], chunk)
            before = top[...]
            best = jnp.maximum(before, jnp.max(score, axis=1, keepdims=True))
            keep = jnp.exp2((before - best) * SCALE2)
            weight = jnp.exp2((score - wide(best, STEP)) * SCALE2)
            top[...] = best
            tot[...] = tot[...] * keep + sum(weight[:, i * 128 : (i + 1) * 128] for i in range(STEP))
            acc[...] = acc[...] * wide(keep, 4) + dot_nn(weight.astype(jnp.bfloat16), keys[s, chunk])
            return inner

        lax.fori_loop(0 if own else 1, (found + STEP - 1) // STEP, step, 0)
        total = jnp.broadcast_to(jnp.sum(tot[...], axis=1, keepdims=True), (ROWS, 128))
        latents[s] = (acc[...] * wide(1.0 / total, 4)).astype(jnp.bfloat16)
        level = top[...] * SCALE2 + jnp.log2(total)
        levels[s] = level if own else jnp.where(found > 0, level, LOW)
        return carry

    lax.fori_loop(0, count, one_slot, 0)
    load.wait()
    lane = lax.broadcasted_iota(jnp.int32, (TOK, 128), 1)
    for h in range(HEADS):
        rows = slice(h * TOK, (h + 1) * TOK)
        part = jnp.concatenate([latents[s, rows, :] for s in range(count)], axis=0)
        part = dot_nn(part, w_uv[h]).astype(jnp.bfloat16)
        for s in range(count):
            outs[s][:, h * VD : (h + 1) * VD] = part[s * TOK : (s + 1) * TOK]
    for s in range(count):
        level = levels[s, 0:TOK, :]
        for h in range(1, HEADS):
            level = jnp.where(lane % HEADS == h, levels[s, h * TOK : (h + 1) * TOK, :], level)
        high = level.astype(jnp.bfloat16).astype(jnp.float32)
        middle = (level - high).astype(jnp.bfloat16).astype(jnp.float32)
        low = level - high - middle
        stat = jnp.where(lane < HEADS, high, jnp.where(lane < 2 * HEADS, middle, low))
        outs[s][:, STAT:] = stat.astype(jnp.bfloat16)


def attention(slots, own, lists, counts, q_lat, q_rot, pools, w_uv, fresh):
    count = len(slots)
    full = pl.BlockSpec(memory_space=VMEM)
    scalar = pl.BlockSpec(memory_space=SMEM)
    chunks = 16 // STEP
    return pl.pallas_call(
        functools.partial(attention_kernel, slots, own),
        out_shape=[jax.ShapeDtypeStruct((TOK, MSG), jnp.bfloat16)] * count,
        in_specs=[scalar] * 2
        + [full] * 2
        + [pl.BlockSpec(memory_space=pl.ANY)] * 4
        + [pl.BlockSpec(memory_space=pltpu.HBM)]
        + [full] * (2 if own else 0),
        out_specs=[full] * count,
        scratch_shapes=[
            pltpu.VMEM((HEADS, LAT, VD), jnp.bfloat16),
            pltpu.VMEM((count, chunks, STEP * BLOCK, LAT), jnp.bfloat16),
            pltpu.VMEM((count, chunks, ROPE, STEP * BLOCK), jnp.bfloat16),
            pltpu.SemaphoreType.DMA((count, 16, 2)),
            pltpu.SemaphoreType.DMA,
            pltpu.VMEM((ROWS, LAT), jnp.float32),
            pltpu.VMEM((ROWS, 128), jnp.float32),
            pltpu.VMEM((ROWS, 128), jnp.float32),
            pltpu.VMEM((count, ROWS, LAT), jnp.bfloat16),
            pltpu.VMEM((count, ROWS, 128), jnp.float32),
        ],
        compiler_params=pltpu.CompilerParams(vmem_limit_bytes=40 * 2**20),
        name="attend",
    )(lists, counts, q_lat, q_rot, *pools, w_uv, *fresh)


def combine_kernel(*refs):
    parts, out = refs[:SLOTS], refs[SLOTS]
    stats = [p[:, STAT:].astype(jnp.float32) for p in parts]
    for h in range(HEADS):
        columns = slice(h * VD, (h + 1) * VD)
        levels = [
            s[:, h : h + 1] + s[:, HEADS + h : HEADS + h + 1] + s[:, 2 * HEADS + h : 2 * HEADS + h + 1]
            for s in stats
        ]
        best = functools.reduce(jnp.maximum, levels)
        shares = [jnp.exp2(v - best) for v in levels]
        inverse = 1.0 / sum(shares)
        out[:, columns] = sum(
            p[:, columns].astype(jnp.float32) * (share * inverse) for p, share in zip(parts, shares)
        ).astype(jnp.bfloat16)


def stack_kernel(*refs):
    for d in range(4):
        refs[4][d] = refs[d][...]


def assemble_kernel(ids, mine, other, out):
    k = ids[2]
    for side, pieces in enumerate((mine, other)):
        first = pl.multiple_of((k ^ side) * 448, 64)
        for d in range(4):
            out[d, pl.ds(first, 448), :] = pieces[d]


def project_kernel(ids, *refs):
    heads, weights = refs[:8], refs[8]
    outs, total = refs[9:13], refs[13]
    yl, zb = ids[0], ids[3]
    value = None
    for d in range(4):
        part = dot_nt(jnp.concatenate([heads[d][...], heads[4 + d][...]], axis=0), weights[d])
        value = part if value is None else value + part
    total[pl.ds(pl.multiple_of(yl * TOK, TOK), TOK), :] = value[:TOK]
    total[pl.ds(pl.multiple_of((1 - yl) * TOK, TOK), TOK), :] = value[TOK:]
    for d in range(4):
        first = pl.multiple_of(((zb + d) % 4) * 32, 32)
        for half in range(2):
            outs[d][half * 32 : (half + 1) * 32, :] = total[pl.ds(first + half * TOK, 32), :].astype(jnp.bfloat16)


def share_kernel(*refs):
    parts, out = refs[:4], refs[4]
    out[...] = sum(p[...].astype(jnp.float32) for p in parts).reshape(8, 8, 896)


def place_kernel(ids, parts, out):
    x = ids[1]
    for m in range(8):
        first = ((m // 4) * 4 + (x ^ (m % 4))) * 896
        out[:, pl.ds(pl.multiple_of(first, 128), 896)] = parts[m].astype(jnp.bfloat16)


def hold_kernel(value, *refs):
    refs[-1][...] = value[...]


def tie_kernel(*refs):
    pass


def tie(values, others):
    free = pl.BlockSpec(memory_space=pl.ANY)
    return pl.pallas_call(
        tie_kernel,
        out_shape=[jax.ShapeDtypeStruct(v.shape, v.dtype) for v in values],
        in_specs=[free] * (len(values) + len(others)),
        out_specs=[free] * len(values),
        input_output_aliases={i: i for i in range(len(values))},
        compiler_params=pltpu.CompilerParams(vmem_limit_bytes=2**20),
        name="tie",
    )(*values, *others)


def simple(kernel, name, out_shape, args, scratch=()):
    full = pl.BlockSpec(memory_space=VMEM)
    return pl.pallas_call(
        kernel,
        out_shape=out_shape,
        in_specs=[pl.BlockSpec(memory_space=SMEM) if arg.dtype == jnp.int32 else full for arg in args],
        out_specs=jax.tree.map(lambda _: full, out_shape),
        scratch_shapes=scratch,
        compiler_params=pltpu.CompilerParams(vmem_limit_bytes=40 * 2**20),
        name=name,
    )(*args)


GROUP = ("yl", "z0", "yh")


def turn(value, axis, size, shift):
    return lax.ppermute(value, axis, [((i + shift) % size, i) for i in range(size)])


def flip(value, axis, size, bits):
    return lax.ppermute(value, axis, [(i, i ^ bits) for i in range(size)])


def local(
    q_nope,
    q_rope,
    new_latent,
    new_rope,
    pool_latent,
    pool_rope,
    block_table,
    prefix_len,
    w_uk,
    w_uv,
    w_out,
):
    ids = jnp.stack(
        [
            lax.axis_index("yl"),
            lax.axis_index("x"),
            lax.axis_index("k"),
            lax.axis_index("zb"),
            lax.axis_index("z0") * 2 + lax.axis_index("yh"),
        ]
    ).astype(jnp.int32)
    query = jnp.concatenate([q_nope, q_rope], axis=1)
    pool = jnp.concatenate(
        [pool_latent.reshape(4 * BLOCK, LAT), jnp.transpose(pool_rope, (1, 0, 2)).reshape(ROPE, 4 * BLOCK)], axis=0
    )
    weight = w_out.T

    pool_y = flip(pool, "yl", 2, 1)
    queries = [query] + [turn(query, "x", 4, s) for s in (1, 2, 3)]
    pool_k = flip(pool, "k", 2, 1)
    weight = simple(
        hold_kernel, "hold", jax.ShapeDtypeStruct(weight.shape, weight.dtype), [weight, *queries[1:]]
    )
    (pool_y,) = tie([pool_y], [pool_k, weight])
    pool_yk = flip(pool_y, "k", 2, 1)
    pools = [pool, pool_y, pool_k, pool_yk]
    q_lat, q_rot, lists, counts = prepare(ids, block_table, prefix_len, queries, w_uk)
    mine = [
        lax.ppermute(
            weight,
            ("x", "z0", "yh"),
            [((i ^ a) * 4 + (a ^ d), i * 4 + a) for i in range(4) for a in range(4)],
        )
        for d in range(4)
    ]

    away = attention((1, 2, 3), False, lists, counts, q_lat, q_rot, pools, w_uv, ())
    came = [
        lax.ppermute(part, "x", [(i, (i + s) % 4) for i in range(4)]) for s, part in zip((1, 2, 3), away)
    ]
    (home,) = attention((0,), True, lists, counts, q_lat, q_rot, pools, w_uv, (new_latent, new_rope[0]))
    mine = simple(
        stack_kernel, "stack", jax.ShapeDtypeStruct((4, 448, 512), jnp.bfloat16), tie(mine, [home, *came])
    )
    weights = simple(
        assemble_kernel,
        "assemble",
        jax.ShapeDtypeStruct((4, 896, 512), jnp.bfloat16),
        [ids, mine, flip(mine, "k", 2, 1)],
    )
    head_out = simple(
        combine_kernel, "combine", jax.ShapeDtypeStruct((TOK, HEADS * VD), jnp.bfloat16), [home, *came]
    )
    heads = [head_out] + [flip(head_out, GROUP, 8, m) for m in range(1, 8)]
    partial = simple(
        project_kernel,
        "project",
        [jax.ShapeDtypeStruct((64, 896), jnp.bfloat16)] * 4,
        [ids, *heads, weights],
        scratch=[pltpu.VMEM((256, 896), jnp.float32)],
    )
    sums = [partial[0]] + [
        lax.ppermute(partial[d], "zb", [(i, (i + d) % 4) for i in range(4)]) for d in (1, 2, 3)
    ]
    pieces = simple(share_kernel, "share", jax.ShapeDtypeStruct((8, 8, 896), jnp.float32), sums)
    pieces = lax.all_to_all(pieces, GROUP, 0, 0, tiled=True)
    return simple(place_kernel, "place", jax.ShapeDtypeStruct((8, 7168), jnp.bfloat16), [ids, pieces])


def solution(mesh):
    fine = Mesh(mesh.devices.reshape(2, 4, 2, 4, 2, 2), ("yl", "x", "k", "zb", "z0", "yh"))
    cache, head = ("yl", "x", "k"), ("zb", "z0", "yh")
    return jax.shard_map(
        local,
        mesh=fine,
        in_specs=(
            P(cache, head),
            P(cache, head),
            P(cache, None),
            P(cache, None, None),
            P(cache, None, None),
            P(cache, None, None),
            P(),
            P(),
            P(head, None, None),
            P(head, None, None),
            P(head, cache),
        ),
        out_specs=P(cache + head, None),
        check_vma=False,
    )
```

time: 144 us -> 131 us (0.910)
  waiting for transfers between devices: 48.2 us -> 26 us
  starting transfers between devices: 43.4 us -> 58.7 us
  Pallas kernels: 31.5 us -> 26 us
    ppermute x1 -> x4, waiting for transfers between devices: 21.1 us -> 0.01 us  [local(): lax.ppermute(weight, ('x', 'z0', 'yh'), [((i ^ a) * 4 + (a ^ d), i * 4 +...]
    ppermute x14 -> x11, starting transfers between devices: 14.7 us -> 25.3 us  [flip(): return lax.ppermute(value, axis, [(i, i ^ bits) for i in range(size)])]
    pallas_call x2, Pallas kernels: 26.1 us -> 16.1 us  [attention(): pl.pallas_call(functools.partial(attention_kernel, slots, own), out_shape...]
    ppermute x3, starting transfers between devices: 2.43 us -> 6.89 us  [local(): lax.ppermute(part, 'x', [(i, (i + s) % 4) for i in range(4)])]
    pallas_call x5 -> x10, Pallas kernels: 5.43 us -> 9.88 us  [the longest x7 6.64 us: simple(): pl.pallas_call(kernel, out_shape=out_shape, in_specs=[pl.BlockSpec(memory...]
    ppermute x3, waiting for transfers between devices: 6.4 us -> 2.03 us  [local(): lax.ppermute(part, 'x', [(i, (i + s) % 4) for i in range(4)])]
    ppermute x1 -> x4, starting transfers between devices: 8.16 us -> 11.9 us  [local(): lax.ppermute(weight, ('x', 'z0', 'yh'), [((i ^ a) * 4 + (a ^ d), i * 4 +...]
    ppermute x6 -> x3, starting transfers between devices: 7.35 us -> 4.04 us  [turn(): lax.ppermute(value, axis, [((i + shift) % size, i) for i in range(size)])]
  transfers between devices with their start and end apart: 27 -> 24, of which waited for: 11 -> 8; matrix products, arithmetic and copies ran while one was open for 0% -> 1% of each run, Pallas kernels for 19% -> 17%
where the time goes in v3:
time: 131 us; the launch traced here: 130 us
  starting transfers between devices  58.7 us (45%)
  waiting for transfers between devices  26 us (20%)
  Pallas kernels  26 us (20%)
  blocking collectives  10.3 us (8%)
  local copies, waits for them, and re-layouts  7.48 us (6%)
    ppermute x11, starting transfers between devices, flip(): return lax.ppermute(value, axis, [(i, i ^ bits) for i in range(size)])  25.3 us
    pallas_call x2, Pallas kernels, attention(): pl.pallas_call(functools.partial(attention_kernel, slots, own), out_shape...  16.1 us
    ppermute x4, starting transfers between devices, local(): lax.ppermute(weight, ('x', 'z0', 'yh'), [((i ^ a) * 4 + (a ^ d), i * 4 +...  11.9 us
    ppermute x3, starting transfers between devices, local(): lax.ppermute(partial[d], 'zb', [(i, (i + d) % 4) for i in range(4)])  10.5 us
    all_to_all x1, blocking collectives, local(): pieces = lax.all_to_all(pieces, GROUP, 0, 0, tiled=True)  10.3 us
    ppermute x11, waiting for transfers between devices, flip(): return lax.ppermute(value, axis, [(i, i ^ bits) for i in range(size)])  9.21 us
    ppermute x3, waiting for transfers between devices, turn(): lax.ppermute(value, axis, [((i + shift) % size, i) for i in range(size)])  8.96 us
    ppermute x3, starting transfers between devices, local(): lax.ppermute(part, 'x', [(i, (i + s) % 4) for i in range(4)])  6.89 us
  transfers between devices with their start and end apart: 24, of which 8 were waited for; matrix products, arithmetic and copies ran while one was open for 1% of the time, Pallas kernels for 17%

profile of v3, /device:TPU:6, one launch (start us, length us, event | category | flops | bytes accessed | tf_op | source)
XLA Modules:
  0.0 129.8 jit_solution(13647752997766233739)
XLA Ops:
  0.0 0.8 copy-done
  0.9 1.1 pad_maximum_fusion.refs_0_
  1.9 0.1 collective-permute-start.4
  2.0 1.7 %collective-permute-start.3 = (bf16[576,512]{1,0:T(8,128)(2,1)S(1)}, bf16[576,512]{1,0:T(8,128)(2,1)S(1)}, u32[]{:S(2)}, u32[]{:S(2)}) collective-permute-start(bf16[576,512]{1,0:T(8,128)(2,1)S(1)} %pad_maximum_fusion.refs_0_), channel_id=1, source_target_pairs={{0,128},{128,0},{1,129},{129,1},{2,130},{130,2},{3,131},{131,3},{4... | collective-permute-start | bytes 1769480 | tf_op jit(solution)/shard_map/ppermute | solution.py:358
  3.7 0.9 constant_dynamic-update-slice_fusion.1
  4.6 0.8 constant_dynamic-update-slice_fusion.refs_0_
  5.5 0.8 collective-permute-start
  6.3 1.3 collective-permute-start.1
  7.6 1.9 %collective-permute-start.2 = (bf16[128,768]{1,0:T(8,128)(2,1)S(1)}, bf16[128,768]{1,0:T(8,128)(2,1)S(1)}, u32[]{:S(2)}, u32[]{:S(2)}) collective-permute-start(bf16[128,768]{1,0:T(8,128)(2,1)S(1)} %constant_dynamic-update-slice_fusion.refs_0_), channel_id=1, source_target_pairs={{96,0},{0,32},{32,64},{64,96},{97,1},{1,33},{33,65},{65,97},{98,2}... | collective-permute-start | bytes 589832 | tf_op jit(solution)/shard_map/ppermute | solution.py:354
  9.5 8.3 %collective-permute-done.refs_1_.refs_0_ = bf16[128,768]{1,0:T(8,128)(2,1)S(1)} collective-permute-done((bf16[128,768]{1,0:T(8,128)(2,1)S(1)}, bf16[128,768]{1,0:T(8,128)(2,1)S(1)}, u32[]{:S(2)}, u32[]{:S(2)}) %collective-permute-start) | collective-permute-done | bytes 196640 | tf_op jit(solution)/shard_map/ppermute | solution.py:354
  17.9 0.0 collective-permute-done.1.refs_2_.refs_1_
  17.9 0.6 collective-permute-done.2.refs_3_.refs_2_
  18.5 0.8 hold.1.refs_2_
  19.3 0.0 collective-permute-done.4.refs_1_.refs_2_
  19.3 0.0 collective-permute-done.3.refs_0_
  19.3 0.1 collective-permute-start.5
  19.4 1.7 %collective-permute-start.16 = (bf16[448,512]{1,0:T(8,128)(2,1)}, bf16[448,512]{1,0:T(8,128)(2,1)S(1)}, u32[]{:S(2)}, u32[]{:S(2)}) collective-permute-start(bf16[448,512]{1,0:T(8,128)(2,1)} %hold.1.refs_2_), channel_id=1, source_target_pairs={{0,0},{33,1},{66,2},{99,3},{32,32},{1,33},{98,34},{67,35},{64,64},... | collective-permute-start | bytes 1376264 | tf_op jit(solution)/shard_map/ppermute | solution.py:400
  21.1 4.7 %collective-permute-start.17 = (bf16[448,512]{1,0:T(8,128)(2,1)}, bf16[448,512]{1,0:T(8,128)(2,1)}, u32[]{:S(2)}, u32[]{:S(2)}) collective-permute-start(bf16[448,512]{1,0:T(8,128)(2,1)} %hold.1.refs_2_), channel_id=1, source_target_pairs={{1,0},{32,1},{67,2},{98,3},{33,32},{0,33},{99,34},{66,35},{65,64},... | collective-permute-start | bytes 1376264 | tf_op jit(solution)/shard_map/ppermute | solution.py:400
  25.8 2.8 %collective-permute-start.18 = (bf16[448,512]{1,0:T(8,128)(2,1)}, bf16[448,512]{1,0:T(8,128)(2,1)}, u32[]{:S(2)}, u32[]{:S(2)}) collective-permute-start(bf16[448,512]{1,0:T(8,128)(2,1)} %hold.1.refs_2_), channel_id=1, source_target_pairs={{2,0},{35,1},{64,2},{97,3},{34,32},{3,33},{96,34},{65,35},{66,64},... | collective-permute-start | bytes 1376264 | tf_op jit(solution)/shard_map/ppermute | solution.py:400
  28.6 2.8 %collective-permute-start.19 = (bf16[448,512]{1,0:T(8,128)(2,1)}, bf16[448,512]{1,0:T(8,128)(2,1)}, u32[]{:S(2)}, u32[]{:S(2)}) collective-permute-start(bf16[448,512]{1,0:T(8,128)(2,1)} %hold.1.refs_2_), channel_id=1, source_target_pairs={{3,0},{34,1},{65,2},{96,3},{35,32},{2,33},{97,34},{64,35},{67,64},... | collective-permute-start | bytes 1376264 | tf_op jit(solution)/shard_map/ppermute | solution.py:400
  31.4 0.1 stack.24.ids
  31.4 0.9 copy-done.3
  32.4 0.9 copy-done.5
  33.3 0.9 copy-done.7
  34.2 0.9 copy-done.9
  35.2 1.0 copy-done.10
  36.2 3.2 %prepare.1 = (bf16[4,512,512]{2,1,0:T(8,128)(2,1)S(1)}, bf16[4,512,64]{2,1,0:T(8,128)(2,1)S(1)}, s32[64]{0:T(128)S(1)}, s32[8]{0:T(128)S(1)}) custom-call(s32[5]{0:T(128)S(1)} %stack.24.ids, s32[16,32]{1,0:T(8,128)S(1)} %copy-done.14, s32[16]{0:T(128)S(1)} %copy-done.15, bf16[128,768]{1,0:T(8,128)(2,1)S(1)} %copy-done.9, bf16[128,768]{1,0:T(8,128)(2,1)S(1)} %copy-done.3, ...), custom_call_target="tpu_custom_call" | custom-call | tf_op jit(solution)/shard_map/prepare/pallas_call | solution.py:79
  39.5 0.0 copy-start.12
  39.5 0.0 copy-start.13
  39.5 10.9 %attend.3 = (bf16[128,640]{1,0:T(8,128)(2,1)S(1)}, bf16[128,640]{1,0:T(8,128)(2,1)S(1)}, bf16[128,640]{1,0:T(8,128)(2,1)S(1)}) custom-call(s32[64]{0:T(128)S(1)} %get-tuple-element.20.lists, s32[8]{0:T(128)S(1)} %get-tuple-element.21.counts, bf16[4,512,512]{2,1,0:T(8,128)(2,1)S(1)} %get-tuple-element.22.q_lat, ...), custom_call_target="tpu_custom_call" | custom-call | tf_op jit(solution)/shard_map/attend/pallas_call | solution.py:232
  50.4 0.1 collective-permute-start.6
  50.5 5.5 %collective-permute-start.7 = (bf16[128,640]{1,0:T(8,128)(2,1)S(1)}, bf16[128,640]{1,0:T(8,128)(2,1)S(1)}, u32[]{:S(2)}, u32[]{:S(2)}) collective-permute-start(bf16[128,640]{1,0:T(8,128)(2,1)S(1)} %get-tuple-element.25), channel_id=1, source_target_pairs={{0,64},{32,96},{64,0},{96,32},{1,65},{33,97},{65,1},{97,33},{2,66}... | collective-permute-start | bytes 491528 | tf_op jit(solution)/shard_map/ppermute | solution.py:410
  56.0 1.3 %collective-permute-start.8 = (bf16[128,640]{1,0:T(8,128)(2,1)S(1)}, bf16[128,640]{1,0:T(8,128)(2,1)S(1)}, u32[]{:S(2)}, u32[]{:S(2)}) collective-permute-start(bf16[128,640]{1,0:T(8,128)(2,1)S(1)} %get-tuple-element.26), channel_id=1, source_target_pairs={{0,96},{32,0},{64,32},{96,64},{1,97},{33,1},{65,33},{97,65},{2,98}... | collective-permute-start | bytes 491528 | tf_op jit(solution)/shard_map/ppermute | solution.py:410
  57.3 5.2 %attend.2.refs_0_.refs_4_ = bf16[128,640]{1,0:T(8,128)(2,1)S(1)} custom-call(s32[64]{0:T(128)S(1)} %get-tuple-element.20.lists, s32[8]{0:T(128)S(1)} %get-tuple-element.21.counts, bf16[4,512,512]{2,1,0:T(8,128)(2,1)S(1)} %get-tuple-element.22.q_lat, bf16[4,512,64]{2,1,0:T(8,128)(2,1)S(1)} %get-tuple-element.23.q_rot, ...), custom_call_target="tpu_custom_call" | custom-call | tf_op jit(solution)/shard_map/attend/pallas_call | solution.py:232
  62.5 0.0 collective-permute-done.18.refs_2_
  62.5 0.0 collective-permute-done.19.refs_3_
  62.5 0.0 collective-permute-done.7.refs_2_.refs_6_
  62.6 2.0 %collective-permute-done.8.refs_3_.refs_7_ = bf16[128,640]{1,0:T(8,128)(2,1)S(1)} collective-permute-done((bf16[128,640]{1,0:T(8,128)(2,1)S(1)}, bf16[128,640]{1,0:T(8,128)(2,1)S(1)}, u32[]{:S(2)}, u32[]{:S(2)}) %collective-permute-start.8) | collective-permute-done | bytes 163872 | tf_op jit(solution)/shard_map/ppermute | solution.py:410
  64.6 1.4 %stack.25.mine = bf16[4,448,512]{2,1,0:T(8,128)(2,1)S(1)} custom-call(bf16[448,512]{1,0:T(8,128)(2,1)S(1)} %get-tuple-element.27.refs_0_, bf16[448,512]{1,0:T(8,128)(2,1)} %get-tuple-element.28.refs_1_, bf16[448,512]{1,0:T(8,128)(2,1)} %get-tuple-element.29.refs_2_, bf16[448,512]{1,0:T(8,128)(2,1)} %get-tuple-element.30.refs_3_), custom_call_target="tpu_custom_call" | custom-call | tf_op jit(solution)/shard_map/stack/pallas_call | solution.py:339
  66.0 0.1 collective-permute-start.20
  66.1 0.5 combine.1.refs_0_
  66.6 12.8 %collective-permute-start.10 = (bf16[128,512]{1,0:T(8,128)(2,1)S(1)}, bf16[128,512]{1,0:T(8,128)(2,1)S(1)}, u32[]{:S(2)}, u32[]{:S(2)}) collective-permute-start(bf16[128,512]{1,0:T(8,128)(2,1)S(1)} %combine.1.refs_0_), channel_id=1, source_target_pairs={{0,2},{1,3},{2,0},{3,1},{128,130},{129,131},{130,128},{131,129},{4... | collective-permute-start | bytes 393224 | tf_op jit(solution)/shard_map/ppermute | solution.py:358
  79.4 3.6 %collective-permute-start.11 = (bf16[128,512]{1,0:T(8,128)(2,1)S(1)}, bf16[128,512]{1,0:T(8,128)(2,1)S(1)}, u32[]{:S(2)}, u32[]{:S(2)}) collective-permute-start(bf16[128,512]{1,0:T(8,128)(2,1)S(1)} %combine.1.refs_0_), channel_id=1, source_target_pairs={{0,3},{1,2},{2,1},{3,0},{128,131},{129,130},{130,129},{131,128},{4... | collective-permute-start | bytes 393224 | tf_op jit(solution)/shard_map/ppermute | solution.py:358
  83.0 0.4 collective-permute-start.12
  83.4 0.6 collective-permute-start.13
  84.0 0.0 collective-permute-done.10.refs_2_
  84.0 2.4 %collective-permute-start.14 = (bf16[128,512]{1,0:T(8,128)(2,1)S(1)}, bf16[128,512]{1,0:T(8,128)(2,1)S(1)}, u32[]{:S(2)}, u32[]{:S(2)}) collective-permute-start(bf16[128,512]{1,0:T(8,128)(2,1)S(1)} %combine.1.refs_0_), channel_id=1, source_target_pairs={{0,130},{1,131},{2,128},{3,129},{128,2},{129,3},{130,0},{131,1},{4... | collective-permute-start | bytes 393224 | tf_op jit(solution)/shard_map/ppermute | solution.py:358
  86.4 3.6 %collective-permute-done.11.refs_3_ = bf16[128,512]{1,0:T(8,128)(2,1)S(1)} collective-permute-done((bf16[128,512]{1,0:T(8,128)(2,1)S(1)}, bf16[128,512]{1,0:T(8,128)(2,1)S(1)}, u32[]{:S(2)}, u32[]{:S(2)}) %collective-permute-start.11) | collective-permute-done | bytes 131104 | tf_op jit(solution)/shard_map/ppermute | solution.py:358
  90.0 1.1 collective-permute-start.15
  91.2 2.5 %collective-permute-start.9 = (bf16[128,512]{1,0:T(8,128)(2,1)S(1)}, bf16[128,512]{1,0:T(8,128)(2,1)S(1)}, u32[]{:S(2)}, u32[]{:S(2)}) collective-permute-start(bf16[128,512]{1,0:T(8,128)(2,1)S(1)} %combine.1.refs_0_), channel_id=1, source_target_pairs={{0,1},{1,0},{2,3},{3,2},{128,129},{129,128},{130,131},{131,130},{4... | collective-permute-start | bytes 393224 | tf_op jit(solution)/shard_map/ppermute | solution.py:358
  93.7 0.8 assemble.1.refs_8_
  94.5 0.0 collective-permute-done.13.refs_5_
  94.5 0.0 collective-permute-done.14.refs_6_
  94.5 5.6 %collective-permute-done.15.refs_7_ = bf16[128,512]{1,0:T(8,128)(2,1)S(1)} collective-permute-done((bf16[128,512]{1,0:T(8,128)(2,1)S(1)}, bf16[128,512]{1,0:T(8,128)(2,1)S(1)}, u32[]{:S(2)}, u32[]{:S(2)}) %collective-permute-start.15) | collective-permute-done | bytes 131104 | tf_op jit(solution)/shard_map/ppermute | solution.py:358
  100.0 1.9 %project.1 = (bf16[64,896]{1,0:T(8,128)(2,1)S(1)}, bf16[64,896]{1,0:T(8,128)(2,1)S(1)}, bf16[64,896]{1,0:T(8,128)(2,1)S(1)}, bf16[64,896]{1,0:T(8,128)(2,1)S(1)}) custom-call(s32[5]{0:T(128)S(1)} %stack.24.ids, bf16[128,512]{1,0:T(8,128)(2,1)S(1)} %combine.1.refs_0_, bf16[128,512]{1,0:T(8,128)(2,1)S(1)} %collective-permute-done.9.refs_1_, ...), custom_call_target="tpu_custom_call" | custom-call | tf_op jit(solution)/shard_map/project/pallas_call | solution.py:339
  101.9 3.3 %collective-permute-start.21 = (bf16[64,896]{1,0:T(8,128)(2,1)S(1)}, bf16[64,896]{1,0:T(8,128)(2,1)S(1)}, u32[]{:S(2)}, u32[]{:S(2)}) collective-permute-start(bf16[64,896]{1,0:T(8,128)(2,1)S(1)} %get-tuple-element.32), channel_id=1, source_target_pairs={{0,4},{4,8},{8,12},{12,0},{1,5},{5,9},{9,13},{13,1},{2,6},{6,10},{... | collective-permute-start | bytes 344072 | tf_op jit(solution)/shard_map/ppermute | solution.py:434
  105.3 4.5 %collective-permute-start.22 = (bf16[64,896]{1,0:T(8,128)(2,1)S(1)}, bf16[64,896]{1,0:T(8,128)(2,1)S(1)}, u32[]{:S(2)}, u32[]{:S(2)}) collective-permute-start(bf16[64,896]{1,0:T(8,128)(2,1)S(1)} %get-tuple-element.33), channel_id=1, source_target_pairs={{0,8},{4,12},{8,0},{12,4},{1,9},{5,13},{9,1},{13,5},{2,10},{6,14},... | collective-permute-start | bytes 344072 | tf_op jit(solution)/shard_map/ppermute | solution.py:434
  109.8 2.7 %collective-permute-start.23 = (bf16[64,896]{1,0:T(8,128)(2,1)S(1)}, bf16[64,896]{1,0:T(8,128)(2,1)S(1)}, u32[]{:S(2)}, u32[]{:S(2)}) collective-permute-start(bf16[64,896]{1,0:T(8,128)(2,1)S(1)} %get-tuple-element.34), channel_id=1, source_target_pairs={{0,12},{4,0},{8,4},{12,8},{1,13},{5,1},{9,5},{13,9},{2,14},{6,2},{... | collective-permute-start | bytes 344072 | tf_op jit(solution)/shard_map/ppermute | solution.py:434
  112.4 0.2 collective-permute-done.21.refs_1_
  112.6 3.4 %collective-permute-done.22.refs_2_ = bf16[64,896]{1,0:T(8,128)(2,1)S(1)} collective-permute-done((bf16[64,896]{1,0:T(8,128)(2,1)S(1)}, bf16[64,896]{1,0:T(8,128)(2,1)S(1)}, u32[]{:S(2)}, u32[]{:S(2)}) %collective-permute-start.22) | collective-permute-done | bytes 114720 | tf_op jit(solution)/shard_map/ppermute | solution.py:434
  116.0 2.2 %collective-permute-done.23.refs_3_ = bf16[64,896]{1,0:T(8,128)(2,1)S(1)} collective-permute-done((bf16[64,896]{1,0:T(8,128)(2,1)S(1)}, bf16[64,896]{1,0:T(8,128)(2,1)S(1)}, u32[]{:S(2)}, u32[]{:S(2)}) %collective-permute-start.23) | collective-permute-done | bytes 114720 | tf_op jit(solution)/shard_map/ppermute | solution.py:434
  118.2 0.1 share.1
  118.3 10.3 %all_to_all.5.parts = f32[8,8,896]{2,1,0:T(8,128)S(1)} all-to-all(f32[8,8,896]{2,1,0:T(8,128)S(1)} %share.1), channel_id=1, replica_groups=mesh['yl'=2,'x'=4,'k'=2,'zb'=4,'z0'=2,'yh'=2] {'yl','z0','yh'}, dimensions={0} | all-to-all | bytes 458752 | tf_op jit(solution)/shard_map/all_to_all | solution.py:437
  128.6 1.2 place.1
  (34 shorter events, 0.1 us)
Async XLA Ops:
  0.0 0.8 copy-start
  0.0 18.5 %copy-start.11 = (bf16[512,448]{0,1:T(8,128)(2,1)S(1)}, bf16[512,448]{0,1:T(8,128)(2,1)}, u32[]{:S(2)}) copy-start(bf16[512,448]{0,1:T(8,128)(2,1)} %param.21) | copy-start | bytes 1376260
  1.9 17.3 %collective-permute-start.4 = (bf16[576,512]{1,0:T(8,128)(2,1)S(1)}, bf16[576,512]{1,0:T(8,128)(2,1)S(1)}, u32[]{:S(2)}, u32[]{:S(2)}) collective-permute-start(bf16[576,512]{1,0:T(8,128)(2,1)S(1)} %pad_maximum_fusion.refs_0_), channel_id=1, source_target_pairs={{0,16},{16,0},{1,17},{17,1},{2,18},{18,2},{3,19},{19,3},{4,20},{20... | collective-permute-start | bytes 1769480 | tf_op jit(solution)/shard_map/ppermute | solution.py:358
  2.0 17.2 %collective-permute-start.3 = (bf16[576,512]{1,0:T(8,128)(2,1)S(1)}, bf16[576,512]{1,0:T(8,128)(2,1)S(1)}, u32[]{:S(2)}, u32[]{:S(2)}) collective-permute-start(bf16[576,512]{1,0:T(8,128)(2,1)S(1)} %pad_maximum_fusion.refs_0_), channel_id=1, source_target_pairs={{0,128},{128,0},{1,129},{129,1},{2,130},{130,2},{3,131},{131,3},{4... | collective-permute-start | bytes 1769480 | tf_op jit(solution)/shard_map/ppermute | solution.py:358
  5.5 13.8 %copy-start.8 = (bf16[128,768]{1,0:T(8,128)(2,1)}, bf16[128,768]{1,0:T(8,128)(2,1)S(1)}, u32[]{:S(2)}) copy-start(bf16[128,768]{1,0:T(8,128)(2,1)S(1)} %constant_dynamic-update-slice_fusion.refs_0_) | copy-start | bytes 589828
  5.5 12.4 %collective-permute-start = (bf16[128,768]{1,0:T(8,128)(2,1)S(1)}, bf16[128,768]{1,0:T(8,128)(2,1)S(1)}, u32[]{:S(2)}, u32[]{:S(2)}) collective-permute-start(bf16[128,768]{1,0:T(8,128)(2,1)S(1)} %constant_dynamic-update-slice_fusion.refs_0_), channel_id=1, source_target_pairs={{32,0},{64,32},{96,64},{0,96},{33,1},{65,33},{97,65},{1,97},{34,2}... | collective-permute-start | bytes 589832 | tf_op jit(solution)/shard_map/ppermute | solution.py:354
  6.3 11.6 %collective-permute-start.1 = (bf16[128,768]{1,0:T(8,128)(2,1)S(1)}, bf16[128,768]{1,0:T(8,128)(2,1)S(1)}, u32[]{:S(2)}, u32[]{:S(2)}) collective-permute-start(bf16[128,768]{1,0:T(8,128)(2,1)S(1)} %constant_dynamic-update-slice_fusion.refs_0_), channel_id=1, source_target_pairs={{64,0},{96,32},{0,64},{32,96},{65,1},{97,33},{1,65},{33,97},{66,2}... | collective-permute-start | bytes 589832 | tf_op jit(solution)/shard_map/ppermute | solution.py:354
  7.6 10.9 %collective-permute-start.2 = (bf16[128,768]{1,0:T(8,128)(2,1)S(1)}, bf16[128,768]{1,0:T(8,128)(2,1)S(1)}, u32[]{:S(2)}, u32[]{:S(2)}) collective-permute-start(bf16[128,768]{1,0:T(8,128)(2,1)S(1)} %constant_dynamic-update-slice_fusion.refs_0_), channel_id=1, source_target_pairs={{96,0},{0,32},{32,64},{64,96},{97,1},{1,33},{33,65},{65,97},{98,2}... | collective-permute-start | bytes 589832 | tf_op jit(solution)/shard_map/ppermute | solution.py:354
  17.8 1.5 %copy-start.2 = (bf16[128,768]{1,0:T(8,128)(2,1)}, bf16[128,768]{1,0:T(8,128)(2,1)S(1)}, u32[]{:S(2)}) copy-start(bf16[128,768]{1,0:T(8,128)(2,1)S(1)} %collective-permute-done.refs_1_.refs_0_) | copy-start | bytes 589828
  17.9 1.5 %copy-start.4 = (bf16[128,768]{1,0:T(8,128)(2,1)}, bf16[128,768]{1,0:T(8,128)(2,1)S(1)}, u32[]{:S(2)}) copy-start(bf16[128,768]{1,0:T(8,128)(2,1)S(1)} %collective-permute-done.1.refs_2_.refs_1_) | copy-start | bytes 589828
  18.5 0.9 copy-start.6
  18.5 13.0 %copy-start.14 = (s32[16,32]{1,0:T(8,128)S(1)}, s32[16,32]{1,0:T(8,128)}, u32[]{:S(2)}) copy-start(s32[16,32]{1,0:T(8,128)} %table.1) | copy-start | bytes 6148
  18.5 13.0 %copy-start.15 = (s32[16]{0:T(128)S(1)}, s32[16]{0:T(128)}, u32[]{:S(2)}) copy-start(s32[16]{0:T(128)} %lens.1) | copy-start | bytes 196
  19.3 20.2 %copy-start.1 = (bf16[4,512,128]{2,1,0:T(8,128)(2,1)S(1)}, bf16[4,512,128]{2,1,0:T(8,128)(2,1)}, u32[]{:S(2)}) copy-start(bf16[4,512,128]{2,1,0:T(8,128)(2,1)} %refs_4_.5) | copy-start | bytes 1572868
  19.3 20.1 %collective-permute-start.5 = (bf16[576,512]{1,0:T(8,128)(2,1)S(1)}, bf16[576,512]{1,0:T(8,128)(2,1)S(1)}, u32[]{:S(2)}, u32[]{:S(2)}) collective-permute-start(bf16[576,512]{1,0:T(8,128)(2,1)S(1)} %tie.2.refs_1_), channel_id=1, source_target_pairs={{0,16},{16,0},{1,17},{17,1},{2,18},{18,2},{3,19},{19,3},{4,20},{20... | collective-permute-start | bytes 1769480 | tf_op jit(solution)/shard_map/ppermute | solution.py:358
  19.4 31.1 %collective-permute-start.16 = (bf16[448,512]{1,0:T(8,128)(2,1)}, bf16[448,512]{1,0:T(8,128)(2,1)S(1)}, u32[]{:S(2)}, u32[]{:S(2)}) collective-permute-start(bf16[448,512]{1,0:T(8,128)(2,1)} %hold.1.refs_2_), channel_id=1, source_target_pairs={{0,0},{33,1},{66,2},{99,3},{32,32},{1,33},{98,34},{67,35},{64,64},... | collective-permute-start | bytes 1376264 | tf_op jit(solution)/shard_map/ppermute | solution.py:400
  21.1 34.9 %collective-permute-start.17 = (bf16[448,512]{1,0:T(8,128)(2,1)}, bf16[448,512]{1,0:T(8,128)(2,1)}, u32[]{:S(2)}, u32[]{:S(2)}) collective-permute-start(bf16[448,512]{1,0:T(8,128)(2,1)} %hold.1.refs_2_), channel_id=1, source_target_pairs={{1,0},{32,1},{67,2},{98,3},{33,32},{0,33},{99,34},{66,35},{65,64},... | collective-permute-start | bytes 1376264 | tf_op jit(solution)/shard_map/ppermute | solution.py:400
  25.8 36.7 %collective-permute-start.18 = (bf16[448,512]{1,0:T(8,128)(2,1)}, bf16[448,512]{1,0:T(8,128)(2,1)}, u32[]{:S(2)}, u32[]{:S(2)}) collective-permute-start(bf16[448,512]{1,0:T(8,128)(2,1)} %hold.1.refs_2_), channel_id=1, source_target_pairs={{2,0},{35,1},{64,2},{97,3},{34,32},{3,33},{96,34},{65,35},{66,64},... | collective-permute-start | bytes 1376264 | tf_op jit(solution)/shard_map/ppermute | solution.py:400
  28.6 34.0 %collective-permute-start.19 = (bf16[448,512]{1,0:T(8,128)(2,1)}, bf16[448,512]{1,0:T(8,128)(2,1)}, u32[]{:S(2)}, u32[]{:S(2)}) collective-permute-start(bf16[448,512]{1,0:T(8,128)(2,1)} %hold.1.refs_2_), channel_id=1, source_target_pairs={{3,0},{34,1},{65,2},{96,3},{35,32},{2,33},{97,34},{64,35},{67,64},... | collective-permute-start | bytes 1376264 | tf_op jit(solution)/shard_map/ppermute | solution.py:400
  31.4 0.9 copy-start.3
  32.4 0.9 copy-start.5
  33.3 0.9 copy-start.7
  34.2 0.9 copy-start.9
  35.2 1.0 copy-start.10
  39.5 17.9 %copy-start.12 = (bf16[128,512]{1,0:T(8,128)(2,1)S(1)}, bf16[128,512]{1,0:T(8,128)(2,1)}, u32[]{:S(2)}) copy-start(bf16[128,512]{1,0:T(8,128)(2,1)} %refs_5_.1) | copy-start | bytes 393220
  39.5 17.9 %copy-start.13 = (bf16[1,64,128]{2,1,0:T(8,128)(2,1)S(1)}, bf16[1,64,128]{2,1,0:T(8,128)(2,1)}, u32[]{:S(2)}) copy-start(bf16[1,64,128]{2,1,0:T(8,128)(2,1)} %param.14) | copy-start | bytes 49156
  50.4 12.1 %collective-permute-start.6 = (bf16[128,640]{1,0:T(8,128)(2,1)S(1)}, bf16[128,640]{1,0:T(8,128)(2,1)S(1)}, u32[]{:S(2)}, u32[]{:S(2)}) collective-permute-start(bf16[128,640]{1,0:T(8,128)(2,1)S(1)} %get-tuple-element.24), channel_id=1, source_target_pairs={{0,32},{32,64},{64,96},{96,0},{1,33},{33,65},{65,97},{97,1},{2,34}... | collective-permute-start | bytes 491528 | tf_op jit(solution)/shard_map/ppermute | solution.py:410
  50.5 12.0 %collective-permute-start.7 = (bf16[128,640]{1,0:T(8,128)(2,1)S(1)}, bf16[128,640]{1,0:T(8,128)(2,1)S(1)}, u32[]{:S(2)}, u32[]{:S(2)}) collective-permute-start(bf16[128,640]{1,0:T(8,128)(2,1)S(1)} %get-tuple-element.25), channel_id=1, source_target_pairs={{0,64},{32,96},{64,0},{96,32},{1,65},{33,97},{65,1},{97,33},{2,66}... | collective-permute-start | bytes 491528 | tf_op jit(solution)/shard_map/ppermute | solution.py:410
  56.0 8.6 %collective-permute-start.8 = (bf16[128,640]{1,0:T(8,128)(2,1)S(1)}, bf16[128,640]{1,0:T(8,128)(2,1)S(1)}, u32[]{:S(2)}, u32[]{:S(2)}) collective-permute-start(bf16[128,640]{1,0:T(8,128)(2,1)S(1)} %get-tuple-element.26), channel_id=1, source_target_pairs={{0,96},{32,0},{64,32},{96,64},{1,97},{33,1},{65,33},{97,65},{2,98}... | collective-permute-start | bytes 491528 | tf_op jit(solution)/shard_map/ppermute | solution.py:410
  66.0 25.2 %collective-permute-start.20 = (bf16[4,448,512]{2,1,0:T(8,128)(2,1)S(1)}, bf16[4,448,512]{2,1,0:T(8,128)(2,1)S(1)}, u32[]{:S(2)}, u32[]{:S(2)}) collective-permute-start(bf16[4,448,512]{2,1,0:T(8,128)(2,1)S(1)} %stack.25.mine), channel_id=1, source_target_pairs={{0,16},{16,0},{1,17},{17,1},{2,18},{18,2},{3,19},{19,3},{4,20},{20... | collective-permute-start | bytes 5505032 | tf_op jit(solution)/shard_map/ppermute | solution.py:358
  66.6 17.4 %collective-permute-start.10 = (bf16[128,512]{1,0:T(8,128)(2,1)S(1)}, bf16[128,512]{1,0:T(8,128)(2,1)S(1)}, u32[]{:S(2)}, u32[]{:S(2)}) collective-permute-start(bf16[128,512]{1,0:T(8,128)(2,1)S(1)} %combine.1.refs_0_), channel_id=1, source_target_pairs={{0,2},{1,3},{2,0},{3,1},{128,130},{129,131},{130,128},{131,129},{4... | collective-permute-start | bytes 393224 | tf_op jit(solution)/shard_map/ppermute | solution.py:358
  79.4 10.6 %collective-permute-start.11 = (bf16[128,512]{1,0:T(8,128)(2,1)S(1)}, bf16[128,512]{1,0:T(8,128)(2,1)S(1)}, u32[]{:S(2)}, u32[]{:S(2)}) collective-permute-start(bf16[128,512]{1,0:T(8,128)(2,1)S(1)} %combine.1.refs_0_), channel_id=1, source_target_pairs={{0,3},{1,2},{2,1},{3,0},{128,131},{129,130},{130,129},{131,128},{4... | collective-permute-start | bytes 393224 | tf_op jit(solution)/shard_map/ppermute | solution.py:358
  83.0 11.5 %collective-permute-start.12 = (bf16[128,512]{1,0:T(8,128)(2,1)S(1)}, bf16[128,512]{1,0:T(8,128)(2,1)S(1)}, u32[]{:S(2)}, u32[]{:S(2)}) collective-permute-start(bf16[128,512]{1,0:T(8,128)(2,1)S(1)} %combine.1.refs_0_), channel_id=1, source_target_pairs={{0,128},{1,129},{2,130},{3,131},{128,0},{129,1},{130,2},{131,3},{4... | collective-permute-start | bytes 393224 | tf_op jit(solution)/shard_map/ppermute | solution.py:358
  83.4 11.0 %collective-permute-start.13 = (bf16[128,512]{1,0:T(8,128)(2,1)S(1)}, bf16[128,512]{1,0:T(8,128)(2,1)S(1)}, u32[]{:S(2)}, u32[]{:S(2)}) collective-permute-start(bf16[128,512]{1,0:T(8,128)(2,1)S(1)} %combine.1.refs_0_), channel_id=1, source_target_pairs={{0,129},{1,128},{2,131},{3,130},{128,1},{129,0},{130,3},{131,2},{4... | collective-permute-start | bytes 393224 | tf_op jit(solution)/shard_map/ppermute | solution.py:358
  84.0 10.4 %collective-permute-start.14 = (bf16[128,512]{1,0:T(8,128)(2,1)S(1)}, bf16[128,512]{1,0:T(8,128)(2,1)S(1)}, u32[]{:S(2)}, u32[]{:S(2)}) collective-permute-start(bf16[128,512]{1,0:T(8,128)(2,1)S(1)} %combine.1.refs_0_), channel_id=1, source_target_pairs={{0,130},{1,131},{2,128},{3,129},{128,2},{129,3},{130,0},{131,1},{4... | collective-permute-start | bytes 393224 | tf_op jit(solution)/shard_map/ppermute | solution.py:358
  90.0 10.0 %collective-permute-start.15 = (bf16[128,512]{1,0:T(8,128)(2,1)S(1)}, bf16[128,512]{1,0:T(8,128)(2,1)S(1)}, u32[]{:S(2)}, u32[]{:S(2)}) collective-permute-start(bf16[128,512]{1,0:T(8,128)(2,1)S(1)} %combine.1.refs_0_), channel_id=1, source_target_pairs={{0,131},{1,130},{2,129},{3,128},{128,3},{129,2},{130,1},{131,0},{4... | collective-permute-start | bytes 393224 | tf_op jit(solution)/shard_map/ppermute | solution.py:358
  91.2 8.9 %collective-permute-start.9 = (bf16[128,512]{1,0:T(8,128)(2,1)S(1)}, bf16[128,512]{1,0:T(8,128)(2,1)S(1)}, u32[]{:S(2)}, u32[]{:S(2)}) collective-permute-start(bf16[128,512]{1,0:T(8,128)(2,1)S(1)} %combine.1.refs_0_), channel_id=1, source_target_pairs={{0,1},{1,0},{2,3},{3,2},{128,129},{129,128},{130,131},{131,130},{4... | collective-permute-start | bytes 393224 | tf_op jit(solution)/shard_map/ppermute | solution.py:358
  101.9 10.7 %collective-permute-start.21 = (bf16[64,896]{1,0:T(8,128)(2,1)S(1)}, bf16[64,896]{1,0:T(8,128)(2,1)S(1)}, u32[]{:S(2)}, u32[]{:S(2)}) collective-permute-start(bf16[64,896]{1,0:T(8,128)(2,1)S(1)} %get-tuple-element.32), channel_id=1, source_target_pairs={{0,4},{4,8},{8,12},{12,0},{1,5},{5,9},{9,13},{13,1},{2,6},{6,10},{... | collective-permute-start | bytes 344072 | tf_op jit(solution)/shard_map/ppermute | solution.py:434
  105.3 10.8 %collective-permute-start.22 = (bf16[64,896]{1,0:T(8,128)(2,1)S(1)}, bf16[64,896]{1,0:T(8,128)(2,1)S(1)}, u32[]{:S(2)}, u32[]{:S(2)}) collective-permute-start(bf16[64,896]{1,0:T(8,128)(2,1)S(1)} %get-tuple-element.33), channel_id=1, source_target_pairs={{0,8},{4,12},{8,0},{12,4},{1,9},{5,13},{9,1},{13,5},{2,10},{6,14},... | collective-permute-start | bytes 344072 | tf_op jit(solution)/shard_map/ppermute | solution.py:434
  109.8 8.5 %collective-permute-start.23 = (bf16[64,896]{1,0:T(8,128)(2,1)S(1)}, bf16[64,896]{1,0:T(8,128)(2,1)S(1)}, u32[]{:S(2)}, u32[]{:S(2)}) collective-permute-start(bf16[64,896]{1,0:T(8,128)(2,1)S(1)} %get-tuple-element.34), channel_id=1, source_target_pairs={{0,12},{4,0},{8,4},{12,8},{1,13},{5,1},{9,5},{13,9},{2,14},{6,2},{... | collective-permute-start | bytes 344072 | tf_op jit(solution)/shard_map/ppermute | solution.py:434

commit v4 on v3

--- a/solution.py
+++ b/solution.py
@@ -272,49 +272,49 @@
         ).astype(jnp.bfloat16)
 
 
-def stack_kernel(*refs):
+def project_kernel(ids, heads, weights, *refs):
+    outs, total = refs[:4], refs[4]
+    a = ids[4]
+    total[...] = dot_nt(heads[...], weights[...])
     for d in range(4):
-        refs[4][d] = refs[d][...]
-
-
-def assemble_kernel(ids, mine, other, out):
-    k = ids[2]
-    for side, pieces in enumerate((mine, other)):
-        first = pl.multiple_of((k ^ side) * 448, 64)
-        for d in range(4):
-            out[d, pl.ds(first, 448), :] = pieces[d]
-
-
-def project_kernel(ids, *refs):
-    heads, weights = refs[:8], refs[8]
-    outs, total = refs[9:13], refs[13]
-    yl, zb = ids[0], ids[3]
-    value = None
+        first = pl.multiple_of((a ^ d) * 8, 8)
+        rows = [total[pl.ds(zb * 32 + first, 8), :] for zb in range(4)]
+        outs[d][...] = jnp.concatenate(rows, axis=0).astype(jnp.bfloat16)
+
+
+def project(ids, heads, weights):
+    wide = 1024
+    return pl.pallas_call(
+        project_kernel,
+        out_shape=[jax.ShapeDtypeStruct((32, 7168), jnp.bfloat16)] * 4,
+        grid=(7168 // wide,),
+        in_specs=[
+            pl.BlockSpec(memory_space=SMEM),
+            pl.BlockSpec((TOK, 512), lambda j: (0, 0)),
+            pl.BlockSpec((wide, 512), lambda j: (j, 0)),
+        ],
+        out_specs=[pl.BlockSpec((32, wide), lambda j: (0, j))] * 4,
+        scratch_shapes=[pltpu.VMEM((TOK, wide), jnp.float32)],
+        compiler_params=pltpu.CompilerParams(vmem_limit_bytes=16 * 2**20),
+        name="project",
+    )(ids, heads, weights)
+
+
+def share_kernel(ids, *refs):
+    parts, outs, total = refs[:4], refs[4:8], refs[8]
+    zb = ids[3]
+    total[...] = sum(p[...].astype(jnp.float32) for p in parts)
     for d in range(4):
-        part = dot_nt(jnp.concatenate([heads[d][...], heads[4 + d][...]], axis=0), weights[d])
-        value = part if value is None else value + part
-    total[pl.ds(pl.multiple_of(yl * TOK, TOK), TOK), :] = value[:TOK]
-    total[pl.ds(pl.multiple_of((1 - yl) * TOK, TOK), TOK), :] = value[TOK:]
-    for d in range(4):
-        first = pl.multiple_of(((zb + d) % 4) * 32, 32)
-        for half in range(2):
-            outs[d][half * 32 : (half + 1) * 32, :] = total[pl.ds(first + half * TOK, 32), :].astype(jnp.bfloat16)
-
-
-def share_kernel(*refs):
+        first = pl.multiple_of(((zb + d) % 4) * 8, 8)
+        rows = [total[pl.ds(first, 8), q * 1792 : (q + 1) * 1792] for q in range(4)]
+        outs[d][...] = jnp.concatenate(rows, axis=0).astype(jnp.bfloat16)
+
+
+def place_kernel(*refs):
     parts, out = refs[:4], refs[4]
-    out[...] = sum(p[...].astype(jnp.float32) for p in parts).reshape(8, 8, 896)
-
-
-def place_kernel(ids, parts, out):
-    x = ids[1]
-    for m in range(8):
-        first = ((m // 4) * 4 + (x ^ (m % 4))) * 896
-        out[:, pl.ds(pl.multiple_of(first, 128), 896)] = parts[m].astype(jnp.bfloat16)
-
-
-def hold_kernel(value, *refs):
-    refs[-1][...] = value[...]
+    total = sum(p[...].astype(jnp.float32) for p in parts)
+    for q in range(4):
+        out[:, q * 1792 : (q + 1) * 1792] = total[q * 8 : (q + 1) * 8].astype(jnp.bfloat16)
 
 
 def tie_kernel(*refs):
@@ -342,12 +342,9 @@
         in_specs=[pl.BlockSpec(memory_space=SMEM) if arg.dtype == jnp.int32 else full for arg in args],
         out_specs=jax.tree.map(lambda _: full, out_shape),
         scratch_shapes=scratch,
-        compiler_params=pltpu.CompilerParams(vmem_limit_bytes=40 * 2**20),
+        compiler_params=pltpu.CompilerParams(vmem_limit_bytes=16 * 2**20),
         name=name,
     )(*args)
-
-
-GROUP = ("yl", "z0", "yh")
 
 
 def turn(value, axis, size, shift):
@@ -384,58 +381,37 @@
     pool = jnp.concatenate(
         [pool_latent.reshape(4 * BLOCK, LAT), jnp.transpose(pool_rope, (1, 0, 2)).reshape(ROPE, 4 * BLOCK)], axis=0
     )
-    weight = w_out.T
+    weights = lax.all_gather(w_out.T, ("yl", "x", "k"), axis=0, tiled=True)
 
     pool_y = flip(pool, "yl", 2, 1)
     queries = [query] + [turn(query, "x", 4, s) for s in (1, 2, 3)]
     pool_k = flip(pool, "k", 2, 1)
-    weight = simple(
-        hold_kernel, "hold", jax.ShapeDtypeStruct(weight.shape, weight.dtype), [weight, *queries[1:]]
-    )
-    (pool_y,) = tie([pool_y], [pool_k, weight])
+    (pool_y,) = tie([pool_y], [pool_k, *queries[1:]])
     pool_yk = flip(pool_y, "k", 2, 1)
     pools = [pool, pool_y, pool_k, pool_yk]
     q_lat, q_rot, lists, counts = prepare(ids, block_table, prefix_len, queries, w_uk)
-    mine = [
-        lax.ppermute(
-            weight,
-            ("x", "z0", "yh"),
-            [((i ^ a) * 4 + (a ^ d), i * 4 + a) for i in range(4) for a in range(4)],
-        )
-        for d in range(4)
-    ]
 
     away = attention((1, 2, 3), False, lists, counts, q_lat, q_rot, pools, w_uv, ())
     came = [
         lax.ppermute(part, "x", [(i, (i + s) % 4) for i in range(4)]) for s, part in zip((1, 2, 3), away)
     ]
     (home,) = attention((0,), True, lists, counts, q_lat, q_rot, pools, w_uv, (new_latent, new_rope[0]))
-    mine = simple(
-        stack_kernel, "stack", jax.ShapeDtypeStruct((4, 448, 512), jnp.bfloat16), tie(mine, [home, *came])
-    )
-    weights = simple(
-        assemble_kernel,
-        "assemble",
-        jax.ShapeDtypeStruct((4, 896, 512), jnp.bfloat16),
-        [ids, mine, flip(mine, "k", 2, 1)],
-    )
     head_out = simple(
         combine_kernel, "combine", jax.ShapeDtypeStruct((TOK, HEADS * VD), jnp.bfloat16), [home, *came]
     )
-    heads = [head_out] + [flip(head_out, GROUP, 8, m) for m in range(1, 8)]
-    partial = simple(
-        project_kernel,
-        "project",
-        [jax.ShapeDtypeStruct((64, 896), jnp.bfloat16)] * 4,
-        [ids, *heads, weights],
-        scratch=[pltpu.VMEM((256, 896), jnp.float32)],
+    partial = project(ids, head_out, weights)
+    sums = [partial[0]] + [flip(partial[d], ("z0", "yh"), 4, d) for d in (1, 2, 3)]
+    pieces = simple(
+        share_kernel,
+        "share",
+        [jax.ShapeDtypeStruct((32, 1792), jnp.bfloat16)] * 4,
+        [ids, *sums],
+        scratch=[pltpu.VMEM((32, 7168), jnp.float32)],
     )
-    sums = [partial[0]] + [
-        lax.ppermute(partial[d], "zb", [(i, (i + d) % 4) for i in range(4)]) for d in (1, 2, 3)
+    pieces = [pieces[0]] + [
+        lax.ppermute(pieces[d], "zb", [(i, (i + d) % 4) for i in range(4)]) for d in (1, 2, 3)
     ]
-    pieces = simple(share_kernel, "share", jax.ShapeDtypeStruct((8, 8, 896), jnp.float32), sums)
-    pieces = lax.all_to_all(pieces, GROUP, 0, 0, tiled=True)
-    return simple(place_kernel, "place", jax.ShapeDtypeStruct((8, 7168), jnp.bfloat16), [ids, pieces])
+    return simple(place_kernel, "place", jax.ShapeDtypeStruct((8, 7168), jnp.bfloat16), pieces)
 
 
 def solution(mesh):

time: 131 us -> 130 us (level)
  waiting for transfers between devices: 26 us -> 58.4 us
  starting transfers between devices: 58.7 us -> 27.6 us
  between operations: 0.27 us -> 13.5 us
  blocking collectives: 10.3 us -> 0 us
  Pallas kernels: 26 us -> 22.7 us
  local copies, waits for them, and re-layouts: 7.48 us -> 6.04 us
    ppermute x11 -> x6, starting transfers between devices: 25.3 us -> 6.84 us  [flip(): return lax.ppermute(value, axis, [(i, i ^ bits) for i in range(size)])]
    ppermute x11 -> x6, waiting for transfers between devices: 9.21 us -> 23.9 us  [flip(): return lax.ppermute(value, axis, [(i, i ^ bits) for i in range(size)])]
    ppermute x7 -> x3, starting transfers between devices: 22.4 us -> 9.95 us  [local(): lax.ppermute(pieces[d], 'zb', [(i, (i + d) % 4) for i in range(4)])]
    all_to_all x1 -> x0, blocking collectives: 10.3 us -> none  [local(): pieces = lax.all_to_all(pieces, GROUP, 0, 0, tiled=True)]
    all_gather x0 -> x1, waiting for transfers between devices: none -> 8.29 us  [local(): weights = lax.all_gather(w_out.T, ('yl', 'x', 'k'), axis=0, tiled=True)]
    ppermute x3, waiting for transfers between devices: 2.03 us -> 9.99 us  [local(): lax.ppermute(part, 'x', [(i, (i + s) % 4) for i in range(4)])]
    pallas_call x7 -> x3, Pallas kernels: 6.64 us -> 2.21 us  [simple(): pl.pallas_call(kernel, out_shape=out_shape, in_specs=[pl.BlockSpec(memory...]
    pallas_call x0 -> x1, Pallas kernels: none -> 4.31 us  [project(): pl.pallas_call(project_kernel, out_shape=[jax.ShapeDtypeStruct((32, 7168)...]
  transfers between devices with their start and end apart: 24 -> 16, of which waited for: 8 -> 12; matrix products, arithmetic and copies ran while one was open for 1% -> 1% of each run, Pallas kernels for 17% -> 13%
where the time goes in v4:
time: 130 us; the launch traced here: 129 us
  waiting for transfers between devices  58.4 us (45%)
  starting transfers between devices  27.6 us (21%)
  Pallas kernels  22.7 us (17%)
  between operations  13.5 us (10%)
  local copies, waits for them, and re-layouts  6.04 us (5%)
    ppermute x6, waiting for transfers between devices, flip(): return lax.ppermute(value, axis, [(i, i ^ bits) for i in range(size)])  23.9 us
    pallas_call x2, Pallas kernels, attention(): pl.pallas_call(functools.partial(attention_kernel, slots, own), out_shape...  13 us
    ppermute x3, waiting for transfers between devices, local(): lax.ppermute(part, 'x', [(i, (i + s) % 4) for i in range(4)])  9.99 us
    ppermute x3, starting transfers between devices, local(): lax.ppermute(pieces[d], 'zb', [(i, (i + d) % 4) for i in range(4)])  9.95 us
    all_gather x1, waiting for transfers between devices, local(): weights = lax.all_gather(w_out.T, ('yl', 'x', 'k'), axis=0, tiled=True)  8.29 us
    ppermute x3, waiting for transfers between devices, turn(): lax.ppermute(value, axis, [((i + shift) % size, i) for i in range(size)])  8.29 us
    ppermute x3, waiting for transfers between devices, local(): lax.ppermute(pieces[d], 'zb', [(i, (i + d) % 4) for i in range(4)])  7.26 us
    ppermute x6, starting transfers between devices, flip(): return lax.ppermute(value, axis, [(i, i ^ bits) for i in range(size)])  6.84 us
  transfers between devices with their start and end apart: 16, of which 12 were waited for; matrix products, arithmetic and copies ran while one was open for 1% of the time, Pallas kernels for 13%

profile of v4, /device:TPU:6, one launch (start us, length us, event | category | flops | bytes accessed | tf_op | source)
XLA Modules:
  0.0 129.4 jit_solution(13819143343638138609)
XLA Ops:
  6.5 0.0 copy-start
  6.5 0.0 copy-start.10
  6.5 0.0 copy-start.11
  6.5 0.0 all-gather.2.cloned.1.call-start
  6.5 0.7 all-gather.2.cloned.1.call-update
  7.3 0.1 copy-done
  7.4 1.1 pad_maximum_fusion.refs_0_
  8.5 0.1 collective-permute-start.4
  8.6 1.7 %collective-permute-start.3 = (bf16[576,512]{1,0:T(8,128)(2,1)S(1)}, bf16[576,512]{1,0:T(8,128)(2,1)S(1)}, u32[]{:S(2)}, u32[]{:S(2)}) collective-permute-start(bf16[576,512]{1,0:T(8,128)(2,1)S(1)} %pad_maximum_fusion.refs_0_), channel_id=1, source_target_pairs={{0,128},{128,0},{1,129},{129,1},{2,130},{130,2},{3,131},{131,3},{4... | collective-permute-start | bytes 1769480 | tf_op jit(solution)/shard_map/ppermute | solution.py:355
  10.2 0.0 copy-done.10
  10.3 0.0 copy-done.11
  10.3 0.0 copy-start.8
  10.3 0.0 copy-start.9
  10.3 0.9 collective-permute-start
  11.2 1.3 %collective-permute-start.1 = (bf16[128,768]{1,0:T(8,128)(2,1)S(1)}, bf16[128,768]{1,0:T(8,128)(2,1)S(1)}, u32[]{:S(2)}, u32[]{:S(2)}) collective-permute-start(bf16[128,768]{1,0:T(8,128)(2,1)S(1)} %constant_dynamic-update-slice_fusion.refs_0_), channel_id=1, source_target_pairs={{64,0},{96,32},{0,64},{32,96},{65,1},{97,33},{1,65},{33,97},{66,2}... | collective-permute-start | bytes 589832 | tf_op jit(solution)/shard_map/ppermute | solution.py:351
  12.5 1.9 %collective-permute-start.2 = (bf16[128,768]{1,0:T(8,128)(2,1)S(1)}, bf16[128,768]{1,0:T(8,128)(2,1)S(1)}, u32[]{:S(2)}, u32[]{:S(2)}) collective-permute-start(bf16[128,768]{1,0:T(8,128)(2,1)S(1)} %constant_dynamic-update-slice_fusion.refs_0_), channel_id=1, source_target_pairs={{96,0},{0,32},{32,64},{64,96},{97,1},{1,33},{33,65},{65,97},{98,2}... | collective-permute-start | bytes 589832 | tf_op jit(solution)/shard_map/ppermute | solution.py:351
  14.4 0.0 copy-start.3
  14.4 0.7 copy-done.3
  15.1 7.7 %collective-permute-done.refs_1_.refs_2_ = bf16[128,768]{1,0:T(8,128)(2,1)S(1)} collective-permute-done((bf16[128,768]{1,0:T(8,128)(2,1)S(1)}, bf16[128,768]{1,0:T(8,128)(2,1)S(1)}, u32[]{:S(2)}, u32[]{:S(2)}) %collective-permute-start) | collective-permute-done | bytes 196640 | tf_op jit(solution)/shard_map/ppermute | solution.py:351
  22.8 0.0 collective-permute-done.1.refs_2_.refs_3_
  22.8 0.6 collective-permute-done.2.refs_3_.refs_4_
  23.4 0.0 collective-permute-done.4.refs_1_.refs_2_
  23.4 0.9 collective-permute-done.3.refs_0_
  24.3 0.0 copy-start.2
  24.3 0.0 collective-permute-start.5
  24.3 0.1 stack.23.ids
  24.4 0.0 copy-done.8
  24.4 0.0 copy-done.9
  24.4 0.0 copy-start.4
  24.4 1.0 copy-done.4
  25.4 1.0 copy-done.5
  26.4 3.2 %prepare.1 = (bf16[4,512,512]{2,1,0:T(8,128)(2,1)S(1)}, bf16[4,512,64]{2,1,0:T(8,128)(2,1)S(1)}, s32[64]{0:T(128)S(1)}, s32[8]{0:T(128)S(1)}) custom-call(s32[5]{0:T(128)S(1)} %stack.23.ids, s32[16,32]{1,0:T(8,128)S(1)} %copy-done.8, s32[16]{0:T(128)S(1)} %copy-done.9, bf16[128,768]{1,0:T(8,128)(2,1)S(1)} %copy-done.4, ...), custom_call_target="tpu_custom_call" | custom-call | tf_op jit(solution)/shard_map/prepare/pallas_call | solution.py:79
  29.7 0.0 collective-permute-done.5.refs_3_
  29.7 0.0 copy-done.2
  29.7 0.0 copy-start.6
  29.7 0.0 copy-start.7
  29.7 9.5 %attend.3 = (bf16[128,640]{1,0:T(8,128)(2,1)S(1)}, bf16[128,640]{1,0:T(8,128)(2,1)S(1)}, bf16[128,640]{1,0:T(8,128)(2,1)S(1)}) custom-call(s32[64]{0:T(128)S(1)} %get-tuple-element.20.lists, s32[8]{0:T(128)S(1)} %get-tuple-element.21.counts, bf16[4,512,512]{2,1,0:T(8,128)(2,1)S(1)} %get-tuple-element.22.q_lat, ...), custom_call_target="tpu_custom_call" | custom-call | tf_op jit(solution)/shard_map/attend/pallas_call | solution.py:232
  39.2 5.7 %collective-permute-start.6 = (bf16[128,640]{1,0:T(8,128)(2,1)S(1)}, bf16[128,640]{1,0:T(8,128)(2,1)S(1)}, u32[]{:S(2)}, u32[]{:S(2)}) collective-permute-start(bf16[128,640]{1,0:T(8,128)(2,1)S(1)} %get-tuple-element.24), channel_id=1, source_target_pairs={{0,32},{32,64},{64,96},{96,0},{1,33},{33,65},{65,97},{97,1},{2,34}... | collective-permute-start | bytes 491528 | tf_op jit(solution)/shard_map/ppermute | solution.py:396
  44.9 0.0 collective-permute-start.7
  44.9 1.0 collective-permute-start.8
  45.9 0.0 copy-done.6
  45.9 0.0 copy-done.7
  45.9 3.5 %attend.2.refs_0_ = bf16[128,640]{1,0:T(8,128)(2,1)S(1)} custom-call(s32[64]{0:T(128)S(1)} %get-tuple-element.20.lists, s32[8]{0:T(128)S(1)} %get-tuple-element.21.counts, bf16[4,512,512]{2,1,0:T(8,128)(2,1)S(1)} %get-tuple-element.22.q_lat, bf16[4,512,64]{2,1,0:T(8,128)(2,1)S(1)} %get-tuple-element.23.q_rot, bf16[576,512]{1,0:T(8,128)(2,1)S(1)} %pad_maximum_fusion.refs_0_, ...), custom_call_target="tpu_custom_call" | custom-call | tf_op jit(solution)/shard_map/attend/pallas_call | solution.py:232
  49.4 0.1 collective-permute-done.6.refs_1_
  49.6 7.4 %collective-permute-done.7.refs_2_ = bf16[128,640]{1,0:T(8,128)(2,1)S(1)} collective-permute-done((bf16[128,640]{1,0:T(8,128)(2,1)S(1)}, bf16[128,640]{1,0:T(8,128)(2,1)S(1)}, u32[]{:S(2)}, u32[]{:S(2)}) %collective-permute-start.7) | collective-permute-done | bytes 163872 | tf_op jit(solution)/shard_map/ppermute | solution.py:396
  57.0 2.5 %collective-permute-done.8.refs_3_ = bf16[128,640]{1,0:T(8,128)(2,1)S(1)} collective-permute-done((bf16[128,640]{1,0:T(8,128)(2,1)S(1)}, bf16[128,640]{1,0:T(8,128)(2,1)S(1)}, u32[]{:S(2)}, u32[]{:S(2)}) %collective-permute-start.8) | collective-permute-done | bytes 163872 | tf_op jit(solution)/shard_map/ppermute | solution.py:396
  59.4 0.5 combine.1.heads
  60.0 8.3 %all-gather.2.cloned.1.call-done.weights = bf16[7168,512]{1,0:T(8,128)(2,1)} async-done(((bf16[448,512]{1,0:T(8,128)(2,1)}), bf16[7168,512]{1,0:T(8,128)(2,1)}) %all-gather.2.cloned.1.call-update) | async-done | bytes 7340048 | tf_op jit(solution)/shard_map/all_gather | solution.py:384
  68.3 3.1 %copy-done.1 = bf16[7168,512]{1,0:T(8,128)(2,1)S(1)} copy-done((bf16[7168,512]{1,0:T(8,128)(2,1)S(1)}, bf16[7168,512]{1,0:T(8,128)(2,1)}, u32[]{:S(2)}) %copy-start.1) | copy-done | bytes 7340056
  71.3 4.3 %project.1 = (bf16[32,7168]{1,0:T(8,128)(2,1)S(1)}, bf16[32,7168]{1,0:T(8,128)(2,1)S(1)}, bf16[32,7168]{1,0:T(8,128)(2,1)S(1)}, bf16[32,7168]{1,0:T(8,128)(2,1)S(1)}) custom-call(s32[5]{0:T(128)S(1)} %stack.23.ids, bf16[128,512]{1,0:T(8,128)(2,1)S(1)} %combine.1.heads, bf16[7168,512]{1,0:T(8,128)(2,1)S(1)} %copy-done.1), custom_call_target="tpu_custom_call" | custom-call | tf_op jit(solution)/shard_map/project/pallas_call | solution.py:287
  75.7 1.6 %collective-permute-start.10 = (bf16[32,7168]{1,0:T(8,128)(2,1)S(1)}, bf16[32,7168]{1,0:T(8,128)(2,1)S(1)}, u32[]{:S(2)}, u32[]{:S(2)}) collective-permute-start(bf16[32,7168]{1,0:T(8,128)(2,1)S(1)} %get-tuple-element.29), channel_id=1, source_target_pairs={{0,2},{1,3},{2,0},{3,1},{4,6},{5,7},{6,4},{7,5},{8,10},{9,11},{10,... | collective-permute-start | bytes 1376264 | tf_op jit(solution)/shard_map/ppermute | solution.py:355
  77.3 2.9 %collective-permute-start.11 = (bf16[32,7168]{1,0:T(8,128)(2,1)S(1)}, bf16[32,7168]{1,0:T(8,128)(2,1)S(1)}, u32[]{:S(2)}, u32[]{:S(2)}) collective-permute-start(bf16[32,7168]{1,0:T(8,128)(2,1)S(1)} %get-tuple-element.30), channel_id=1, source_target_pairs={{0,3},{1,2},{2,1},{3,0},{4,7},{5,6},{6,5},{7,4},{8,11},{9,10},{10,... | collective-permute-start | bytes 1376264 | tf_op jit(solution)/shard_map/ppermute | solution.py:355
  80.2 0.5 collective-permute-start.9
  80.7 8.4 %collective-permute-done.10.refs_2_ = bf16[32,7168]{1,0:T(8,128)(2,1)S(1)} collective-permute-done((bf16[32,7168]{1,0:T(8,128)(2,1)S(1)}, bf16[32,7168]{1,0:T(8,128)(2,1)S(1)}, u32[]{:S(2)}, u32[]{:S(2)}) %collective-permute-start.10) | collective-permute-done | bytes 458784 | tf_op jit(solution)/shard_map/ppermute | solution.py:355
  89.1 11.7 %collective-permute-done.11.refs_3_ = bf16[32,7168]{1,0:T(8,128)(2,1)S(1)} collective-permute-done((bf16[32,7168]{1,0:T(8,128)(2,1)S(1)}, bf16[32,7168]{1,0:T(8,128)(2,1)S(1)}, u32[]{:S(2)}, u32[]{:S(2)}) %collective-permute-start.11) | collective-permute-done | bytes 458784 | tf_op jit(solution)/shard_map/ppermute | solution.py:355
  100.8 2.9 %collective-permute-done.9.refs_1_ = bf16[32,7168]{1,0:T(8,128)(2,1)S(1)} collective-permute-done((bf16[32,7168]{1,0:T(8,128)(2,1)S(1)}, bf16[32,7168]{1,0:T(8,128)(2,1)S(1)}, u32[]{:S(2)}, u32[]{:S(2)}) %collective-permute-start.9) | collective-permute-done | bytes 458784 | tf_op jit(solution)/shard_map/ppermute | solution.py:355
  103.7 1.0 share.1
  104.6 2.6 %collective-permute-start.12 = (bf16[32,1792]{1,0:T(8,128)(2,1)S(1)}, bf16[32,1792]{1,0:T(8,128)(2,1)S(1)}, u32[]{:S(2)}, u32[]{:S(2)}) collective-permute-start(bf16[32,1792]{1,0:T(8,128)(2,1)S(1)} %get-tuple-element.32), channel_id=1, source_target_pairs={{0,4},{4,8},{8,12},{12,0},{1,5},{5,9},{9,13},{13,1},{2,6},{6,10},{... | collective-permute-start | bytes 344072 | tf_op jit(solution)/shard_map/ppermute | solution.py:412
  107.3 4.3 %collective-permute-start.13 = (bf16[32,1792]{1,0:T(8,128)(2,1)S(1)}, bf16[32,1792]{1,0:T(8,128)(2,1)S(1)}, u32[]{:S(2)}, u32[]{:S(2)}) collective-permute-start(bf16[32,1792]{1,0:T(8,128)(2,1)S(1)} %get-tuple-element.33), channel_id=1, source_target_pairs={{0,8},{4,12},{8,0},{12,4},{1,9},{5,13},{9,1},{13,5},{2,10},{6,14},... | collective-permute-start | bytes 344072 | tf_op jit(solution)/shard_map/ppermute | solution.py:412
  111.5 3.1 %collective-permute-start.14 = (bf16[32,1792]{1,0:T(8,128)(2,1)S(1)}, bf16[32,1792]{1,0:T(8,128)(2,1)S(1)}, u32[]{:S(2)}, u32[]{:S(2)}) collective-permute-start(bf16[32,1792]{1,0:T(8,128)(2,1)S(1)} %get-tuple-element.34), channel_id=1, source_target_pairs={{0,12},{4,0},{8,4},{12,8},{1,13},{5,1},{9,5},{13,9},{2,14},{6,2},{... | collective-permute-start | bytes 344072 | tf_op jit(solution)/shard_map/ppermute | solution.py:412
  114.6 0.0 collective-permute-done.12.refs_1_
  114.6 4.0 %collective-permute-done.13.refs_2_ = bf16[32,1792]{1,0:T(8,128)(2,1)S(1)} collective-permute-done((bf16[32,1792]{1,0:T(8,128)(2,1)S(1)}, bf16[32,1792]{1,0:T(8,128)(2,1)S(1)}, u32[]{:S(2)}, u32[]{:S(2)}) %collective-permute-start.13) | collective-permute-done | bytes 114720 | tf_op jit(solution)/shard_map/ppermute | solution.py:412
  118.6 3.3 %collective-permute-done.14.refs_3_ = bf16[32,1792]{1,0:T(8,128)(2,1)S(1)} collective-permute-done((bf16[32,1792]{1,0:T(8,128)(2,1)S(1)}, bf16[32,1792]{1,0:T(8,128)(2,1)S(1)}, u32[]{:S(2)}, u32[]{:S(2)}) %collective-permute-start.14) | collective-permute-done | bytes 114720 | tf_op jit(solution)/shard_map/ppermute | solution.py:412
  121.9 0.7 place.1
  (6 shorter events, 0.0 us)
Async XLA Ops:
  6.5 0.8 copy-start
  6.5 3.7 %copy-start.10 = (bf16[128,512]{1,0:T(8,128)(2,1)S(1)}, bf16[128,512]{1,0:T(8,128)(2,1)}, u32[]{:S(2)}) copy-start(bf16[128,512]{1,0:T(8,128)(2,1)} %param.11) | copy-start | bytes 393220
  6.5 3.7 %copy-start.11 = (bf16[128,256]{1,0:T(8,128)(2,1)S(1)}, bf16[128,256]{1,0:T(8,128)(2,1)}, u32[]{:S(2)}) copy-start(bf16[128,256]{1,0:T(8,128)(2,1)} %param.12) | copy-start | bytes 196612
  6.5 61.7 %all-gather.2.cloned.1.call-start = ((), (), s32[]{:S(2)}) async-start(), calls=%async_computation | async-start | bytes 7798784 | tf_op jit(solution)/shard_map/all_gather | solution.py:384
  8.5 14.9 %collective-permute-start.4 = (bf16[576,512]{1,0:T(8,128)(2,1)S(1)}, bf16[576,512]{1,0:T(8,128)(2,1)S(1)}, u32[]{:S(2)}, u32[]{:S(2)}) collective-permute-start(bf16[576,512]{1,0:T(8,128)(2,1)S(1)} %pad_maximum_fusion.refs_0_), channel_id=1, source_target_pairs={{0,16},{16,0},{1,17},{17,1},{2,18},{18,2},{3,19},{19,3},{4,20},{20... | collective-permute-start | bytes 1769480 | tf_op jit(solution)/shard_map/ppermute | solution.py:355
  8.6 15.7 %collective-permute-start.3 = (bf16[576,512]{1,0:T(8,128)(2,1)S(1)}, bf16[576,512]{1,0:T(8,128)(2,1)S(1)}, u32[]{:S(2)}, u32[]{:S(2)}) collective-permute-start(bf16[576,512]{1,0:T(8,128)(2,1)S(1)} %pad_maximum_fusion.refs_0_), channel_id=1, source_target_pairs={{0,128},{128,0},{1,129},{129,1},{2,130},{130,2},{3,131},{131,3},{4... | collective-permute-start | bytes 1769480 | tf_op jit(solution)/shard_map/ppermute | solution.py:355
  10.3 14.1 %copy-start.8 = (s32[16,32]{1,0:T(8,128)S(1)}, s32[16,32]{1,0:T(8,128)}, u32[]{:S(2)}) copy-start(s32[16,32]{1,0:T(8,128)} %table.1) | copy-start | bytes 6148
  10.3 14.1 %copy-start.9 = (s32[16]{0:T(128)S(1)}, s32[16]{0:T(128)}, u32[]{:S(2)}) copy-start(s32[16]{0:T(128)} %lens.1) | copy-start | bytes 196
  10.3 12.5 %collective-permute-start = (bf16[128,768]{1,0:T(8,128)(2,1)S(1)}, bf16[128,768]{1,0:T(8,128)(2,1)S(1)}, u32[]{:S(2)}, u32[]{:S(2)}) collective-permute-start(bf16[128,768]{1,0:T(8,128)(2,1)S(1)} %constant_dynamic-update-slice_fusion.refs_0_), channel_id=1, source_target_pairs={{32,0},{64,32},{96,64},{0,96},{33,1},{65,33},{97,65},{1,97},{34,2}... | collective-permute-start | bytes 589832 | tf_op jit(solution)/shard_map/ppermute | solution.py:351
  11.2 11.6 %collective-permute-start.1 = (bf16[128,768]{1,0:T(8,128)(2,1)S(1)}, bf16[128,768]{1,0:T(8,128)(2,1)S(1)}, u32[]{:S(2)}, u32[]{:S(2)}) collective-permute-start(bf16[128,768]{1,0:T(8,128)(2,1)S(1)} %constant_dynamic-update-slice_fusion.refs_0_), channel_id=1, source_target_pairs={{64,0},{96,32},{0,64},{32,96},{65,1},{97,33},{1,65},{33,97},{66,2}... | collective-permute-start | bytes 589832 | tf_op jit(solution)/shard_map/ppermute | solution.py:351
  12.5 10.8 %collective-permute-start.2 = (bf16[128,768]{1,0:T(8,128)(2,1)S(1)}, bf16[128,768]{1,0:T(8,128)(2,1)S(1)}, u32[]{:S(2)}, u32[]{:S(2)}) collective-permute-start(bf16[128,768]{1,0:T(8,128)(2,1)S(1)} %constant_dynamic-update-slice_fusion.refs_0_), channel_id=1, source_target_pairs={{96,0},{0,32},{32,64},{64,96},{97,1},{1,33},{33,65},{65,97},{98,2}... | collective-permute-start | bytes 589832 | tf_op jit(solution)/shard_map/ppermute | solution.py:351
  14.4 0.7 copy-start.3
  24.3 5.4 %copy-start.2 = (bf16[4,512,128]{2,1,0:T(8,128)(2,1)S(1)}, bf16[4,512,128]{2,1,0:T(8,128)(2,1)}, u32[]{:S(2)}) copy-start(bf16[4,512,128]{2,1,0:T(8,128)(2,1)} %refs_4_.5) | copy-start | bytes 1572868
  24.3 5.3 %collective-permute-start.5 = (bf16[576,512]{1,0:T(8,128)(2,1)S(1)}, bf16[576,512]{1,0:T(8,128)(2,1)S(1)}, u32[]{:S(2)}, u32[]{:S(2)}) collective-permute-start(bf16[576,512]{1,0:T(8,128)(2,1)S(1)} %tie.1.refs_1_), channel_id=1, source_target_pairs={{0,16},{16,0},{1,17},{17,1},{2,18},{18,2},{3,19},{19,3},{4,20},{20... | collective-permute-start | bytes 1769480 | tf_op jit(solution)/shard_map/ppermute | solution.py:355
  24.4 1.0 copy-start.4
  25.4 1.0 copy-start.5
  29.7 16.2 %copy-start.6 = (bf16[128,512]{1,0:T(8,128)(2,1)S(1)}, bf16[128,512]{1,0:T(8,128)(2,1)}, u32[]{:S(2)}) copy-start(bf16[128,512]{1,0:T(8,128)(2,1)} %refs_5_.1) | copy-start | bytes 393220
  29.7 16.2 %copy-start.7 = (bf16[1,64,128]{2,1,0:T(8,128)(2,1)S(1)}, bf16[1,64,128]{2,1,0:T(8,128)(2,1)}, u32[]{:S(2)}) copy-start(bf16[1,64,128]{2,1,0:T(8,128)(2,1)} %param.14) | copy-start | bytes 49156
  39.2 10.4 %collective-permute-start.6 = (bf16[128,640]{1,0:T(8,128)(2,1)S(1)}, bf16[128,640]{1,0:T(8,128)(2,1)S(1)}, u32[]{:S(2)}, u32[]{:S(2)}) collective-permute-start(bf16[128,640]{1,0:T(8,128)(2,1)S(1)} %get-tuple-element.24), channel_id=1, source_target_pairs={{0,32},{32,64},{64,96},{96,0},{1,33},{33,65},{65,97},{97,1},{2,34}... | collective-permute-start | bytes 491528 | tf_op jit(solution)/shard_map/ppermute | solution.py:396
  44.9 12.0 %collective-permute-start.7 = (bf16[128,640]{1,0:T(8,128)(2,1)S(1)}, bf16[128,640]{1,0:T(8,128)(2,1)S(1)}, u32[]{:S(2)}, u32[]{:S(2)}) collective-permute-start(bf16[128,640]{1,0:T(8,128)(2,1)S(1)} %get-tuple-element.25), channel_id=1, source_target_pairs={{0,64},{32,96},{64,0},{96,32},{1,65},{33,97},{65,1},{97,33},{2,66}... | collective-permute-start | bytes 491528 | tf_op jit(solution)/shard_map/ppermute | solution.py:396
  44.9 14.5 %collective-permute-start.8 = (bf16[128,640]{1,0:T(8,128)(2,1)S(1)}, bf16[128,640]{1,0:T(8,128)(2,1)S(1)}, u32[]{:S(2)}, u32[]{:S(2)}) collective-permute-start(bf16[128,640]{1,0:T(8,128)(2,1)S(1)} %get-tuple-element.26), channel_id=1, source_target_pairs={{0,96},{32,0},{64,32},{96,64},{1,97},{33,1},{65,33},{97,65},{2,98}... | collective-permute-start | bytes 491528 | tf_op jit(solution)/shard_map/ppermute | solution.py:396
  68.3 3.1 %copy-start.1 = (bf16[7168,512]{1,0:T(8,128)(2,1)S(1)}, bf16[7168,512]{1,0:T(8,128)(2,1)}, u32[]{:S(2)}) copy-start(bf16[7168,512]{1,0:T(8,128)(2,1)} %all-gather.2.cloned.1.call-done.weights) | copy-start | bytes 22020100
  75.7 13.4 %collective-permute-start.10 = (bf16[32,7168]{1,0:T(8,128)(2,1)S(1)}, bf16[32,7168]{1,0:T(8,128)(2,1)S(1)}, u32[]{:S(2)}, u32[]{:S(2)}) collective-permute-start(bf16[32,7168]{1,0:T(8,128)(2,1)S(1)} %get-tuple-element.29), channel_id=1, source_target_pairs={{0,2},{1,3},{2,0},{3,1},{4,6},{5,7},{6,4},{7,5},{8,10},{9,11},{10,... | collective-permute-start | bytes 1376264 | tf_op jit(solution)/shard_map/ppermute | solution.py:355
  77.3 23.5 %collective-permute-start.11 = (bf16[32,7168]{1,0:T(8,128)(2,1)S(1)}, bf16[32,7168]{1,0:T(8,128)(2,1)S(1)}, u32[]{:S(2)}, u32[]{:S(2)}) collective-permute-start(bf16[32,7168]{1,0:T(8,128)(2,1)S(1)} %get-tuple-element.30), channel_id=1, source_target_pairs={{0,3},{1,2},{2,1},{3,0},{4,7},{5,6},{6,5},{7,4},{8,11},{9,10},{10,... | collective-permute-start | bytes 1376264 | tf_op jit(solution)/shard_map/ppermute | solution.py:355
  80.2 23.4 %collective-permute-start.9 = (bf16[32,7168]{1,0:T(8,128)(2,1)S(1)}, bf16[32,7168]{1,0:T(8,128)(2,1)S(1)}, u32[]{:S(2)}, u32[]{:S(2)}) collective-permute-start(bf16[32,7168]{1,0:T(8,128)(2,1)S(1)} %get-tuple-element.28), channel_id=1, source_target_pairs={{0,1},{1,0},{2,3},{3,2},{4,5},{5,4},{6,7},{7,6},{8,9},{9,8},{10,11... | collective-permute-start | bytes 1376264 | tf_op jit(solution)/shard_map/ppermute | solution.py:355
  104.6 10.0 %collective-permute-start.12 = (bf16[32,1792]{1,0:T(8,128)(2,1)S(1)}, bf16[32,1792]{1,0:T(8,128)(2,1)S(1)}, u32[]{:S(2)}, u32[]{:S(2)}) collective-permute-start(bf16[32,1792]{1,0:T(8,128)(2,1)S(1)} %get-tuple-element.32), channel_id=1, source_target_pairs={{0,4},{4,8},{8,12},{12,0},{1,5},{5,9},{9,13},{13,1},{2,6},{6,10},{... | collective-permute-start | bytes 344072 | tf_op jit(solution)/shard_map/ppermute | solution.py:412
  107.3 11.3 %collective-permute-start.13 = (bf16[32,1792]{1,0:T(8,128)(2,1)S(1)}, bf16[32,1792]{1,0:T(8,128)(2,1)S(1)}, u32[]{:S(2)}, u32[]{:S(2)}) collective-permute-start(bf16[32,1792]{1,0:T(8,128)(2,1)S(1)} %get-tuple-element.33), channel_id=1, source_target_pairs={{0,8},{4,12},{8,0},{12,4},{1,9},{5,13},{9,1},{13,5},{2,10},{6,14},... | collective-permute-start | bytes 344072 | tf_op jit(solution)/shard_map/ppermute | solution.py:412
  111.5 10.3 %collective-permute-start.14 = (bf16[32,1792]{1,0:T(8,128)(2,1)S(1)}, bf16[32,1792]{1,0:T(8,128)(2,1)S(1)}, u32[]{:S(2)}, u32[]{:S(2)}) collective-permute-start(bf16[32,1792]{1,0:T(8,128)(2,1)S(1)} %get-tuple-element.34), channel_id=1, source_target_pairs={{0,12},{4,0},{8,4},{12,8},{1,13},{5,1},{9,5},{13,9},{2,14},{6,2},{... | collective-permute-start | bytes 344072 | tf_op jit(solution)/shard_map/ppermute | solution.py:412
Sparse Core Ops, SparseCore 0:
  9.2 58.9 all-gather.1

commit v5 on v4

--- a/solution.py
+++ b/solution.py
@@ -87,7 +87,7 @@
         in_specs=[scalar] * 3 + [full] * SLOTS + [pl.BlockSpec(memory_space=pltpu.HBM)],
         out_specs=[full, full, scalar, scalar],
         scratch_shapes=[pltpu.VMEM((HEADS, NOPE, LAT), jnp.bfloat16), pltpu.SemaphoreType.DMA],
-        compiler_params=pltpu.CompilerParams(vmem_limit_bytes=40 * 2**20),
+        compiler_params=pltpu.CompilerParams(vmem_limit_bytes=16 * 2**20),
         name="prepare",
     )(ids, table, lens, *queries, w_uk)
 
@@ -250,13 +250,14 @@
             pltpu.VMEM((count, ROWS, LAT), jnp.bfloat16),
             pltpu.VMEM((count, ROWS, 128), jnp.float32),
         ],
-        compiler_params=pltpu.CompilerParams(vmem_limit_bytes=40 * 2**20),
+        compiler_params=pltpu.CompilerParams(vmem_limit_bytes=24 * 2**20),
         name="attend",
     )(lists, counts, q_lat, q_rot, *pools, w_uv, *fresh)
 
 
-def combine_kernel(*refs):
-    parts, out = refs[:SLOTS], refs[SLOTS]
+def combine_kernel(ids, *refs):
+    parts, outs, total = refs[:SLOTS], refs[SLOTS : SLOTS + 4], refs[SLOTS + 4]
+    a = ids[4]
     stats = [p[:, STAT:].astype(jnp.float32) for p in parts]
     for h in range(HEADS):
         columns = slice(h * VD, (h + 1) * VD)
@@ -267,54 +268,63 @@
         best = functools.reduce(jnp.maximum, levels)
         shares = [jnp.exp2(v - best) for v in levels]
         inverse = 1.0 / sum(shares)
-        out[:, columns] = sum(
+        total[:, columns] = sum(
             p[:, columns].astype(jnp.float32) * (share * inverse) for p, share in zip(parts, shares)
-        ).astype(jnp.bfloat16)
-
-
-def project_kernel(ids, heads, weights, *refs):
-    outs, total = refs[:4], refs[4]
-    a = ids[4]
-    total[...] = dot_nt(heads[...], weights[...])
+        )
     for d in range(4):
         first = pl.multiple_of((a ^ d) * 8, 8)
-        rows = [total[pl.ds(zb * 32 + first, 8), :] for zb in range(4)]
+        rows = [total[pl.ds(first + q * 32, 8), :] for q in range(4)]
         outs[d][...] = jnp.concatenate(rows, axis=0).astype(jnp.bfloat16)
 
 
-def project(ids, heads, weights):
-    wide = 1024
-    return pl.pallas_call(
-        project_kernel,
-        out_shape=[jax.ShapeDtypeStruct((32, 7168), jnp.bfloat16)] * 4,
-        grid=(7168 // wide,),
-        in_specs=[
-            pl.BlockSpec(memory_space=SMEM),
-            pl.BlockSpec((TOK, 512), lambda j: (0, 0)),
-            pl.BlockSpec((wide, 512), lambda j: (j, 0)),
-        ],
-        out_specs=[pl.BlockSpec((32, wide), lambda j: (0, j))] * 4,
-        scratch_shapes=[pltpu.VMEM((TOK, wide), jnp.float32)],
-        compiler_params=pltpu.CompilerParams(vmem_limit_bytes=16 * 2**20),
-        name="project",
-    )(ids, heads, weights)
-
-
-def share_kernel(ids, *refs):
-    parts, outs, total = refs[:4], refs[4:8], refs[8]
+def join_kernel(*refs):
+    for d in range(4):
+        refs[4][:, d * 512 : (d + 1) * 512] = refs[d][...]
+
+
+def pair_kernel(one, two, out):
+    out[0] = one[...]
+    out[1] = two[...]
+
+
+def project_kernel(ids, *refs):
+    heads, mine, other = refs[:4], refs[4:9], refs[9:14]
+    outs, total = refs[14:18], refs[18]
     zb = ids[3]
-    total[...] = sum(p[...].astype(jnp.float32) for p in parts)
+    rows = jnp.concatenate([h[...] for h in heads], axis=0)
+    for side_y in range(2):
+        sides = []
+        for pieces in (mine, other):
+            value = None
+            for d in range(4):
+                m, dz = side_y * 2 + (d & 1), d >> 1
+                weight = pieces[3 + dz][...] if m == 1 else pieces[max(m - 1, 0)][dz]
+                part = dot_nt(rows[:, d * 512 : (d + 1) * 512], weight)
+                value = part if value is None else value + part
+            sides.append(value)
+        total[:, side_y * 896 : (side_y + 1) * 896] = jnp.concatenate(sides, axis=1)
     for d in range(4):
         first = pl.multiple_of(((zb + d) % 4) * 8, 8)
-        rows = [total[pl.ds(first, 8), q * 1792 : (q + 1) * 1792] for q in range(4)]
-        outs[d][...] = jnp.concatenate(rows, axis=0).astype(jnp.bfloat16)
-
-
-def place_kernel(*refs):
+        parts = [total[pl.ds(first + s * 32, 8), :] for s in range(4)]
+        outs[d][...] = jnp.concatenate(parts, axis=0).astype(jnp.bfloat16)
+
+
+def share_kernel(*refs):
+    total = sum(p[...].astype(jnp.float32) for p in refs[:4])
+    for s in range(4):
+        refs[4 + s][...] = total[s * 8 : (s + 1) * 8]
+
+
+def place_kernel(ids, *refs):
     parts, out = refs[:4], refs[4]
-    total = sum(p[...].astype(jnp.float32) for p in parts)
-    for q in range(4):
-        out[:, q * 1792 : (q + 1) * 1792] = total[q * 8 : (q + 1) * 8].astype(jnp.bfloat16)
+    yl, x, k = ids[0], ids[1], ids[2]
+    for s in range(4):
+        for side_y in range(2):
+            first = ((yl ^ side_y) * 4 + (x - s + 4) % 4) * 896
+            columns = pl.ds(pl.multiple_of(first, 128), 896)
+            value = parts[s][:, side_y * 896 : (side_y + 1) * 896]
+            swapped = jnp.concatenate([value[:, 448:], value[:, :448]], axis=1)
+            out[:, columns] = jnp.where(k == 0, value, swapped).astype(jnp.bfloat16)
 
 
 def tie_kernel(*refs):
@@ -381,37 +391,61 @@
     pool = jnp.concatenate(
         [pool_latent.reshape(4 * BLOCK, LAT), jnp.transpose(pool_rope, (1, 0, 2)).reshape(ROPE, 4 * BLOCK)], axis=0
     )
-    weights = lax.all_gather(w_out.T, ("yl", "x", "k"), axis=0, tiled=True)
-
+    weight = w_out.T
+
+    queries = [query] + [turn(query, "x", 4, s) for s in (1, 2, 3)]
     pool_y = flip(pool, "yl", 2, 1)
-    queries = [query] + [turn(query, "x", 4, s) for s in (1, 2, 3)]
+    weight_z = flip(weight, "z0", 2, 1)
+    q_lat, q_rot, lists, counts = prepare(ids, block_table, prefix_len, queries, w_uk)
+    pool, pool_y, weight_z = tie([pool, pool_y, weight_z], [q_lat])
     pool_k = flip(pool, "k", 2, 1)
-    (pool_y,) = tie([pool_y], [pool_k, *queries[1:]])
     pool_yk = flip(pool_y, "k", 2, 1)
+    pair = simple(
+        pair_kernel, "pair", jax.ShapeDtypeStruct((2, 448, 512), jnp.bfloat16), [weight, weight_z]
+    )
+    ring = ("yl", "yh")
+    mine = [pair, flip(pair, ring, 4, 2), flip(pair, ring, 4, 3)]
+    other = [flip(pair, "k", 2, 1)]
+    pool_k, other[0] = tie([pool_k, other[0]], [])
     pools = [pool, pool_y, pool_k, pool_yk]
-    q_lat, q_rot, lists, counts = prepare(ids, block_table, prefix_len, queries, w_uk)
 
     away = attention((1, 2, 3), False, lists, counts, q_lat, q_rot, pools, w_uv, ())
+    *away, mine[1], mine[2] = tie([*away, mine[1], mine[2]], [])
+    far = [flip(mine[2][0], ring, 4, 2), flip(mine[1][1], ring, 4, 3)]
     came = [
         lax.ppermute(part, "x", [(i, (i + s) % 4) for i in range(4)]) for s, part in zip((1, 2, 3), away)
     ]
     (home,) = attention((0,), True, lists, counts, q_lat, q_rot, pools, w_uv, (new_latent, new_rope[0]))
-    head_out = simple(
-        combine_kernel, "combine", jax.ShapeDtypeStruct((TOK, HEADS * VD), jnp.bfloat16), [home, *came]
+    mine[1], mine[2] = tie([mine[1], mine[2]], [*came, *far, home])
+    other += [flip(m, "k", 2, 1) for m in mine[1:]]
+    heads = simple(
+        combine_kernel,
+        "combine",
+        [jax.ShapeDtypeStruct((32, HEADS * VD), jnp.bfloat16)] * 4,
+        [ids, home, *came],
+        scratch=[pltpu.VMEM((TOK, HEADS * VD), jnp.float32)],
     )
-    partial = project(ids, head_out, weights)
-    sums = [partial[0]] + [flip(partial[d], ("z0", "yh"), 4, d) for d in (1, 2, 3)]
-    pieces = simple(
-        share_kernel,
-        "share",
+    heads = [heads[0]] + [flip(heads[d], ("z0", "yh"), 4, d) for d in (1, 2, 3)]
+    heads = simple(join_kernel, "join", jax.ShapeDtypeStruct((32, 2048), jnp.bfloat16), heads)
+    heads, *far = tie([heads, *far], other[1:])
+    mine += far
+    other += [flip(f, "k", 2, 1) for f in far]
+    heads = [heads] + [turn(heads, "x", 4, s) for s in (1, 2, 3)]
+    partial = simple(
+        project_kernel,
+        "project",
         [jax.ShapeDtypeStruct((32, 1792), jnp.bfloat16)] * 4,
-        [ids, *sums],
-        scratch=[pltpu.VMEM((32, 7168), jnp.float32)],
+        [ids, *heads, *mine, *other],
+        scratch=[pltpu.VMEM((TOK, 1792), jnp.float32)],
     )
+    sums = [partial[0]] + [
+        lax.ppermute(partial[d], "zb", [(i, (i + d) % 4) for i in range(4)]) for d in (1, 2, 3)
+    ]
+    pieces = simple(share_kernel, "share", [jax.ShapeDtypeStruct((8, 1792), jnp.float32)] * 4, sums)
     pieces = [pieces[0]] + [
-        lax.ppermute(pieces[d], "zb", [(i, (i + d) % 4) for i in range(4)]) for d in (1, 2, 3)
+        lax.ppermute(pieces[s], "x", [(i, (i + s) % 4) for i in range(4)]) for s in (1, 2, 3)
     ]
-    return simple(place_kernel, "place", jax.ShapeDtypeStruct((8, 7168), jnp.bfloat16), pieces)
+    return simple(place_kernel, "place", jax.ShapeDtypeStruct((8, 7168), jnp.bfloat16), [ids, *pieces])
 
 
 def solution(mesh):

time: 130 us -> 114 us (0.88)
  starting transfers between devices: 27.6 us -> 44.5 us
  between operations: 13.5 us -> 0.24 us
  waiting for transfers between devices: 58.4 us -> 45.6 us
  local copies, waits for them, and re-layouts: 6.04 us -> 1 us
    ppermute x6 -> x16, starting transfers between devices: 6.84 us -> 17.1 us  [flip(): return lax.ppermute(value, axis, [(i, i ^ bits) for i in range(size)])]
    ppermute x6 -> x16, waiting for transfers between devices: 23.9 us -> 13.8 us  [flip(): return lax.ppermute(value, axis, [(i, i ^ bits) for i in range(size)])]
    all_gather x1 -> x0, waiting for transfers between devices: 8.29 us -> none  [local(): weights = lax.all_gather(w_out.T, ('yl', 'x', 'k'), axis=0, tiled=True)]
    ppermute x3 -> x6, starting transfers between devices: 9.95 us -> 15.9 us  [the longest x3 11.2 us: local(): lax.ppermute(partial[d], 'zb', [(i, (i + d) % 4) for i in range(4)])]
    ppermute x3 -> x6, waiting for transfers between devices: 8.29 us -> 14.3 us  [turn(): lax.ppermute(value, axis, [((i + shift) % size, i) for i in range(size)])]
    ppermute x3 -> x6, waiting for transfers between devices: 7.26 us -> 12.5 us  [the longest x3 7.28 us: local(): lax.ppermute(partial[d], 'zb', [(i, (i + d) % 4) for i in range(4)])]
    unnamed x25 -> x21, local copies, waits for them, and re-layouts: 5.94 us -> 0.84 us
    ppermute x3, waiting for transfers between devices: 9.99 us -> 4.97 us  [local(): lax.ppermute(part, 'x', [(i, (i + s) % 4) for i in range(4)])]
  transfers between devices with their start and end apart: 16 -> 31, of which waited for: 12 -> 20; matrix products, arithmetic and copies ran while one was open for 1% -> 0% of each run, Pallas kernels for 13% -> 15%
where the time goes in v5:
time: 114 us
  waiting for transfers between devices  45.6 us (40%)
  starting transfers between devices  44.5 us (39%)
  Pallas kernels  21.8 us (19%)
    ppermute x16, starting transfers between devices, flip(): return lax.ppermute(value, axis, [(i, i ^ bits) for i in range(size)])  17.1 us
    ppermute x6, waiting for transfers between devices, turn(): lax.ppermute(value, axis, [((i + shift) % size, i) for i in range(size)])  14.3 us
    ppermute x16, waiting for transfers between devices, flip(): return lax.ppermute(value, axis, [(i, i ^ bits) for i in range(size)])  13.8 us
    pallas_call x2, Pallas kernels, attention(): pl.pallas_call(functools.partial(attention_kernel, slots, own), out_shape...  13.2 us
    ppermute x3, starting transfers between devices, local(): lax.ppermute(partial[d], 'zb', [(i, (i + d) % 4) for i in range(4)])  11.2 us
    ppermute x6, starting transfers between devices, turn(): lax.ppermute(value, axis, [((i + shift) % size, i) for i in range(size)])  7.94 us
    ppermute x3, waiting for transfers between devices, local(): lax.ppermute(partial[d], 'zb', [(i, (i + d) % 4) for i in range(4)])  7.28 us
    pallas_call x6, Pallas kernels, simple(): pl.pallas_call(kernel, out_shape=out_shape, in_specs=[pl.BlockSpec(memory...  5.45 us
  transfers between devices with their start and end apart: 31, of which 20 were waited for; matrix products, arithmetic and copies ran while one was open for 0% of the time, Pallas kernels for 15%

profile of v5, /device:TPU:6, one launch (start us, length us, event | category | flops | bytes accessed | tf_op | source)
XLA Modules:
  0.0 114.2 jit_solution(9400101831389336281)
XLA Ops:
  0.1 0.8 copy-done
  0.9 1.1 pad_maximum_fusion.refs_0_
  1.9 1.7 %collective-permute-start.3 = (bf16[576,512]{1,0:T(8,128)(2,1)S(1)}, bf16[576,512]{1,0:T(8,128)(2,1)S(1)}, u32[]{:S(2)}, u32[]{:S(2)}) collective-permute-start(bf16[576,512]{1,0:T(8,128)(2,1)S(1)} %pad_maximum_fusion.refs_0_), channel_id=1, source_target_pairs={{0,128},{128,0},{1,129},{129,1},{2,130},{130,2},{3,131},{131,3},{4... | collective-permute-start | bytes 1769480 | tf_op jit(solution)/shard_map/ppermute | solution.py:365
  3.6 1.9 %collective-permute-start.4 = (bf16[448,512]{1,0:T(8,128)(2,1)S(1)}, bf16[448,512]{1,0:T(8,128)(2,1)S(1)}, u32[]{:S(2)}, u32[]{:S(2)}) collective-permute-start(bf16[448,512]{1,0:T(8,128)(2,1)S(1)} %bitcast.18), channel_id=1, source_target_pairs={{0,2},{2,0},{1,3},{3,1},{4,6},{6,4},{5,7},{7,5},{8,10},{10,8},{9,1... | collective-permute-start | bytes 1376264 | tf_op jit(solution)/shard_map/ppermute | solution.py:365
  5.6 0.9 collective-permute-start
  6.5 1.1 collective-permute-start.1
  7.6 2.1 %collective-permute-start.2 = (bf16[128,768]{1,0:T(8,128)(2,1)S(1)}, bf16[128,768]{1,0:T(8,128)(2,1)S(1)}, u32[]{:S(2)}, u32[]{:S(2)}) collective-permute-start(bf16[128,768]{1,0:T(8,128)(2,1)S(1)} %constant_dynamic-update-slice_fusion.refs_0_), channel_id=1, source_target_pairs={{96,0},{0,32},{32,64},{64,96},{97,1},{1,33},{33,65},{65,97},{98,2}... | collective-permute-start | bytes 589832 | tf_op jit(solution)/shard_map/ppermute | solution.py:361
  9.7 0.1 stack.23.ids
  9.8 7.4 %collective-permute-done.refs_1_ = bf16[128,768]{1,0:T(8,128)(2,1)S(1)} collective-permute-done((bf16[128,768]{1,0:T(8,128)(2,1)S(1)}, bf16[128,768]{1,0:T(8,128)(2,1)S(1)}, u32[]{:S(2)}, u32[]{:S(2)}) %collective-permute-start) | collective-permute-done | bytes 196640 | tf_op jit(solution)/shard_map/ppermute | solution.py:361
  17.2 0.6 collective-permute-done.2.refs_3_
  17.8 3.1 %prepare.1 = (bf16[4,512,512]{2,1,0:T(8,128)(2,1)S(1)}, bf16[4,512,64]{2,1,0:T(8,128)(2,1)S(1)}, s32[64]{0:T(128)S(1)}, s32[8]{0:T(128)S(1)}) custom-call(s32[5]{0:T(128)S(1)} %stack.23.ids, s32[16,32]{1,0:T(8,128)S(1)} %copy-done.6, s32[16]{0:T(128)S(1)} %copy-done.7, bf16[128,768]{1,0:T(8,128)(2,1)S(1)} %constant_dynamic-update-slice_fusion.refs_0_, ...), custom_call_target="tpu_custom_call" | custom-call | tf_op jit(solution)/shard_map/prepare/pallas_call | solution.py:79
  20.9 0.0 collective-permute-done.4.refs_2_
  20.9 0.0 collective-permute-done.3.refs_1_
  20.9 0.1 pair.1.refs_4_
  21.0 0.0 copy-start.1
  21.0 0.1 collective-permute-start.6
  21.1 0.3 collective-permute-start.8
  21.4 3.2 %collective-permute-start.9 = (bf16[2,448,512]{2,1,0:T(8,128)(2,1)S(1)}, bf16[2,448,512]{2,1,0:T(8,128)(2,1)S(1)}, u32[]{:S(2)}, u32[]{:S(2)}) collective-permute-start(bf16[2,448,512]{2,1,0:T(8,128)(2,1)S(1)} %pair.1.refs_4_), channel_id=1, source_target_pairs={{0,129},{1,128},{128,1},{129,0},{2,131},{3,130},{130,3},{131,2},{4... | collective-permute-start | bytes 2752520 | tf_op jit(solution)/shard_map/ppermute | solution.py:365
  24.7 0.5 collective-permute-start.7
  25.2 1.5 %collective-permute-done.5.refs_0_ = bf16[576,512]{1,0:T(8,128)(2,1)S(1)} collective-permute-done((bf16[576,512]{1,0:T(8,128)(2,1)S(1)}, bf16[576,512]{1,0:T(8,128)(2,1)S(1)}, u32[]{:S(2)}, u32[]{:S(2)}) %collective-permute-start.5) | collective-permute-done | bytes 589856 | tf_op jit(solution)/shard_map/ppermute | solution.py:365
  26.7 0.8 collective-permute-done.7.refs_3_
  27.5 9.5 %attend.3 = (bf16[128,640]{1,0:T(8,128)(2,1)S(1)}, bf16[128,640]{1,0:T(8,128)(2,1)S(1)}, bf16[128,640]{1,0:T(8,128)(2,1)S(1)}) custom-call(s32[64]{0:T(128)S(1)} %get-tuple-element.39.lists, s32[8]{0:T(128)S(1)} %get-tuple-element.40.counts, bf16[4,512,512]{2,1,0:T(8,128)(2,1)S(1)} %get-tuple-element.41.refs_3_.q_lat, ...), custom_call_target="tpu_custom_call" | custom-call | tf_op jit(solution)/shard_map/attend/pallas_call | solution.py:232
  37.0 6.9 %collective-permute-done.8.refs_3_ = bf16[2,448,512]{2,1,0:T(8,128)(2,1)S(1)} collective-permute-done((bf16[2,448,512]{2,1,0:T(8,128)(2,1)S(1)}, bf16[2,448,512]{2,1,0:T(8,128)(2,1)S(1)}, u32[]{:S(2)}, u32[]{:S(2)}) %collective-permute-start.8) | collective-permute-done | bytes 917536 | tf_op jit(solution)/shard_map/ppermute | solution.py:365
  43.9 1.4 %collective-permute-done.9.refs_4_ = bf16[2,448,512]{2,1,0:T(8,128)(2,1)S(1)} collective-permute-done((bf16[2,448,512]{2,1,0:T(8,128)(2,1)S(1)}, bf16[2,448,512]{2,1,0:T(8,128)(2,1)S(1)}, u32[]{:S(2)}, u32[]{:S(2)}) %collective-permute-start.9) | collective-permute-done | bytes 917536 | tf_op jit(solution)/shard_map/ppermute | solution.py:365
  45.4 0.4 collective-permute-start.16
  45.8 2.8 %collective-permute-start.17 = (bf16[448,512]{1,0:T(8,128)(2,1)S(1)}, bf16[448,512]{1,0:T(8,128)(2,1)S(1)}, u32[]{:S(2)}, u32[]{:S(2)}) collective-permute-start(bf16[448,512]{1,0:T(8,128)(2,1)S(1)} %slice_bitcast_fusion), channel_id=1, source_target_pairs={{0,129},{1,128},{128,1},{129,0},{2,131},{3,130},{130,3},{131,2},{4... | collective-permute-start | bytes 1376264 | tf_op jit(solution)/shard_map/ppermute | solution.py:365
  48.5 2.6 %collective-permute-start.10 = (bf16[128,640]{1,0:T(8,128)(2,1)S(1)}, bf16[128,640]{1,0:T(8,128)(2,1)S(1)}, u32[]{:S(2)}, u32[]{:S(2)}) collective-permute-start(bf16[128,640]{1,0:T(8,128)(2,1)S(1)} %get-tuple-element.50), channel_id=1, source_target_pairs={{0,32},{32,64},{64,96},{96,0},{1,33},{33,65},{65,97},{97,1},{2,34}... | collective-permute-start | bytes 491528 | tf_op jit(solution)/shard_map/ppermute | solution.py:416
  51.2 0.2 collective-permute-start.11
  51.4 0.7 collective-permute-start.12
  52.0 3.7 %attend.2.refs_0_.refs_7_ = bf16[128,640]{1,0:T(8,128)(2,1)S(1)} custom-call(s32[64]{0:T(128)S(1)} %get-tuple-element.39.lists, s32[8]{0:T(128)S(1)} %get-tuple-element.40.counts, bf16[4,512,512]{2,1,0:T(8,128)(2,1)S(1)} %get-tuple-element.41.refs_3_.q_lat, bf16[4,512,64]{2,1,0:T(8,128)(2,1)S(1)} %get-tuple-element.42.q_rot, ...), custom_call_target="tpu_custom_call" | custom-call | tf_op jit(solution)/shard_map/attend/pallas_call | solution.py:232
  55.8 1.6 %collective-permute-done.10.refs_1_.refs_2_ = bf16[128,640]{1,0:T(8,128)(2,1)S(1)} collective-permute-done((bf16[128,640]{1,0:T(8,128)(2,1)S(1)}, bf16[128,640]{1,0:T(8,128)(2,1)S(1)}, u32[]{:S(2)}, u32[]{:S(2)}) %collective-permute-start.10) | collective-permute-done | bytes 163872 | tf_op jit(solution)/shard_map/ppermute | solution.py:416
  57.4 2.0 %collective-permute-done.11.refs_2_.refs_3_ = bf16[128,640]{1,0:T(8,128)(2,1)S(1)} collective-permute-done((bf16[128,640]{1,0:T(8,128)(2,1)S(1)}, bf16[128,640]{1,0:T(8,128)(2,1)S(1)}, u32[]{:S(2)}, u32[]{:S(2)}) %collective-permute-start.11) | collective-permute-done | bytes 163872 | tf_op jit(solution)/shard_map/ppermute | solution.py:416
  59.4 1.4 %collective-permute-done.12.refs_3_.refs_4_ = bf16[128,640]{1,0:T(8,128)(2,1)S(1)} collective-permute-done((bf16[128,640]{1,0:T(8,128)(2,1)S(1)}, bf16[128,640]{1,0:T(8,128)(2,1)S(1)}, u32[]{:S(2)}, u32[]{:S(2)}) %collective-permute-start.12) | collective-permute-done | bytes 163872 | tf_op jit(solution)/shard_map/ppermute | solution.py:416
  60.8 0.1 collective-permute-start.18
  60.9 0.5 collective-permute-start.19
  61.4 1.1 combine.1
  62.4 1.6 %collective-permute-start.13 = (bf16[32,512]{1,0:T(8,128)(2,1)S(1)}, bf16[32,512]{1,0:T(8,128)(2,1)S(1)}, u32[]{:S(2)}, u32[]{:S(2)}) collective-permute-start(bf16[32,512]{1,0:T(8,128)(2,1)S(1)} %get-tuple-element.54), channel_id=1, source_target_pairs={{0,1},{1,0},{2,3},{3,2},{4,5},{5,4},{6,7},{7,6},{8,9},{9,8},{10,11... | collective-permute-start | bytes 98312 | tf_op jit(solution)/shard_map/ppermute | solution.py:365
  64.1 0.3 collective-permute-start.14
  64.3 3.2 %collective-permute-start.15 = (bf16[32,512]{1,0:T(8,128)(2,1)S(1)}, bf16[32,512]{1,0:T(8,128)(2,1)S(1)}, u32[]{:S(2)}, u32[]{:S(2)}) collective-permute-start(bf16[32,512]{1,0:T(8,128)(2,1)S(1)} %get-tuple-element.56), channel_id=1, source_target_pairs={{0,3},{1,2},{2,1},{3,0},{4,7},{5,6},{6,5},{7,4},{8,11},{9,10},{10,... | collective-permute-start | bytes 98312 | tf_op jit(solution)/shard_map/ppermute | solution.py:365
  67.5 0.4 collective-permute-done.13.refs_1_
  67.9 0.1 collective-permute-done.14.refs_2_
  68.0 2.6 %collective-permute-done.15.refs_3_ = bf16[32,512]{1,0:T(8,128)(2,1)S(1)} collective-permute-done((bf16[32,512]{1,0:T(8,128)(2,1)S(1)}, bf16[32,512]{1,0:T(8,128)(2,1)S(1)}, u32[]{:S(2)}, u32[]{:S(2)}) %collective-permute-start.15) | collective-permute-done | bytes 32800 | tf_op jit(solution)/shard_map/ppermute | solution.py:365
  70.7 0.1 collective-permute-start.23
  70.8 0.5 collective-permute-start.24
  71.3 1.2 %collective-permute-start.20 = (bf16[32,2048]{1,0:T(8,128)(2,1)S(1)}, bf16[32,2048]{1,0:T(8,128)(2,1)S(1)}, u32[]{:S(2)}, u32[]{:S(2)}) collective-permute-start(bf16[32,2048]{1,0:T(8,128)(2,1)S(1)} %get-tuple-element.61.refs_0_), channel_id=1, source_target_pairs={{32,0},{64,32},{96,64},{0,96},{33,1},{65,33},{97,65},{1,97},{34,2}... | collective-permute-start | bytes 393224 | tf_op jit(solution)/shard_map/ppermute | solution.py:361
  72.5 2.0 %collective-permute-start.21 = (bf16[32,2048]{1,0:T(8,128)(2,1)S(1)}, bf16[32,2048]{1,0:T(8,128)(2,1)S(1)}, u32[]{:S(2)}, u32[]{:S(2)}) collective-permute-start(bf16[32,2048]{1,0:T(8,128)(2,1)S(1)} %get-tuple-element.61.refs_0_), channel_id=1, source_target_pairs={{64,0},{96,32},{0,64},{32,96},{65,1},{97,33},{1,65},{33,97},{66,2}... | collective-permute-start | bytes 393224 | tf_op jit(solution)/shard_map/ppermute | solution.py:361
  74.5 0.7 collective-permute-start.22
  75.1 3.7 %collective-permute-done.20.refs_1_ = bf16[32,2048]{1,0:T(8,128)(2,1)S(1)} collective-permute-done((bf16[32,2048]{1,0:T(8,128)(2,1)S(1)}, bf16[32,2048]{1,0:T(8,128)(2,1)S(1)}, u32[]{:S(2)}, u32[]{:S(2)}) %collective-permute-start.20) | collective-permute-done | bytes 131104 | tf_op jit(solution)/shard_map/ppermute | solution.py:361
  78.9 2.0 %collective-permute-done.21.refs_2_ = bf16[32,2048]{1,0:T(8,128)(2,1)S(1)} collective-permute-done((bf16[32,2048]{1,0:T(8,128)(2,1)S(1)}, bf16[32,2048]{1,0:T(8,128)(2,1)S(1)}, u32[]{:S(2)}, u32[]{:S(2)}) %collective-permute-start.21) | collective-permute-done | bytes 131104 | tf_op jit(solution)/shard_map/ppermute | solution.py:361
  80.8 0.6 collective-permute-done.22.refs_3_
  81.4 3.0 %project.1 = (bf16[32,1792]{1,0:T(8,128)(2,1)S(1)}, bf16[32,1792]{1,0:T(8,128)(2,1)S(1)}, bf16[32,1792]{1,0:T(8,128)(2,1)S(1)}, bf16[32,1792]{1,0:T(8,128)(2,1)S(1)}) custom-call(s32[5]{0:T(128)S(1)} %stack.23.ids, bf16[32,2048]{1,0:T(8,128)(2,1)S(1)} %get-tuple-element.61.refs_0_, bf16[32,2048]{1,0:T(8,128)(2,1)S(1)} %collective-permute-done.20.refs_1_, ...), custom_call_target="tpu_custom_call" | custom-call | tf_op jit(solution)/shard_map/project/pallas_call | solution.py:349
  84.4 3.3 %collective-permute-start.25 = (bf16[32,1792]{1,0:T(8,128)(2,1)S(1)}, bf16[32,1792]{1,0:T(8,128)(2,1)S(1)}, u32[]{:S(2)}, u32[]{:S(2)}) collective-permute-start(bf16[32,1792]{1,0:T(8,128)(2,1)S(1)} %get-tuple-element.66), channel_id=1, source_target_pairs={{0,4},{4,8},{8,12},{12,0},{1,5},{5,9},{9,13},{13,1},{2,6},{6,10},{... | collective-permute-start | bytes 344072 | tf_op jit(solution)/shard_map/ppermute | solution.py:442
  87.7 5.2 %collective-permute-start.26 = (bf16[32,1792]{1,0:T(8,128)(2,1)S(1)}, bf16[32,1792]{1,0:T(8,128)(2,1)S(1)}, u32[]{:S(2)}, u32[]{:S(2)}) collective-permute-start(bf16[32,1792]{1,0:T(8,128)(2,1)S(1)} %get-tuple-element.67), channel_id=1, source_target_pairs={{0,8},{4,12},{8,0},{12,4},{1,9},{5,13},{9,1},{13,5},{2,10},{6,14},... | collective-permute-start | bytes 344072 | tf_op jit(solution)/shard_map/ppermute | solution.py:442
  92.9 2.7 %collective-permute-start.27 = (bf16[32,1792]{1,0:T(8,128)(2,1)S(1)}, bf16[32,1792]{1,0:T(8,128)(2,1)S(1)}, u32[]{:S(2)}, u32[]{:S(2)}) collective-permute-start(bf16[32,1792]{1,0:T(8,128)(2,1)S(1)} %get-tuple-element.68), channel_id=1, source_target_pairs={{0,12},{4,0},{8,4},{12,8},{1,13},{5,1},{9,5},{13,9},{2,14},{6,2},{... | collective-permute-start | bytes 344072 | tf_op jit(solution)/shard_map/ppermute | solution.py:442
  95.6 5.0 %collective-permute-done.26.refs_2_ = bf16[32,1792]{1,0:T(8,128)(2,1)S(1)} collective-permute-done((bf16[32,1792]{1,0:T(8,128)(2,1)S(1)}, bf16[32,1792]{1,0:T(8,128)(2,1)S(1)}, u32[]{:S(2)}, u32[]{:S(2)}) %collective-permute-start.26) | collective-permute-done | bytes 114720 | tf_op jit(solution)/shard_map/ppermute | solution.py:442
  100.6 2.3 %collective-permute-done.27.refs_3_ = bf16[32,1792]{1,0:T(8,128)(2,1)S(1)} collective-permute-done((bf16[32,1792]{1,0:T(8,128)(2,1)S(1)}, bf16[32,1792]{1,0:T(8,128)(2,1)S(1)}, u32[]{:S(2)}, u32[]{:S(2)}) %collective-permute-start.27) | collective-permute-done | bytes 114720 | tf_op jit(solution)/shard_map/ppermute | solution.py:442
  102.9 0.1 share.1
  103.0 3.8 %collective-permute-start.28 = (f32[8,1792]{1,0:T(8,128)S(1)}, f32[8,1792]{1,0:T(8,128)S(1)}, u32[]{:S(2)}, u32[]{:S(2)}) collective-permute-start(f32[8,1792]{1,0:T(8,128)S(1)} %get-tuple-element.70), channel_id=1, source_target_pairs={{0,32},{32,64},{64,96},{96,0},{1,33},{33,65},{65,97},{97,1},{2,34}... | collective-permute-start | bytes 172040 | tf_op jit(solution)/shard_map/ppermute | solution.py:446
  106.7 0.2 collective-permute-start.29
  106.9 0.8 collective-permute-start.30
  107.7 1.7 %collective-permute-done.28.refs_1_ = f32[8,1792]{1,0:T(8,128)S(1)} collective-permute-done((f32[8,1792]{1,0:T(8,128)S(1)}, f32[8,1792]{1,0:T(8,128)S(1)}, u32[]{:S(2)}, u32[]{:S(2)}) %collective-permute-start.28) | collective-permute-done | bytes 57376 | tf_op jit(solution)/shard_map/ppermute | solution.py:446
  109.3 3.1 %collective-permute-done.29.refs_2_ = f32[8,1792]{1,0:T(8,128)S(1)} collective-permute-done((f32[8,1792]{1,0:T(8,128)S(1)}, f32[8,1792]{1,0:T(8,128)S(1)}, u32[]{:S(2)}, u32[]{:S(2)}) %collective-permute-start.29) | collective-permute-done | bytes 57376 | tf_op jit(solution)/shard_map/ppermute | solution.py:446
  112.5 0.4 collective-permute-done.30.refs_3_
  112.9 1.3 %place.1 = bf16[8,7168]{1,0:T(8,128)(2,1)} custom-call(s32[5]{0:T(128)S(1)} %stack.23.ids, f32[8,1792]{1,0:T(8,128)S(1)} %get-tuple-element.69.refs_0_, f32[8,1792]{1,0:T(8,128)S(1)} %collective-permute-done.28.refs_1_, f32[8,1792]{1,0:T(8,128)S(1)} %collective-permute-done.29.refs_2_, f32[8,1792]{1,0:T(8,128)S(1)} %collective-permute-done.30.refs_3_), custom_call_target="tpu_custom_call" | custom-call | tf_op jit(solution)/shard_map/place/pallas_call | solution.py:349
  (39 shorter events, 0.2 us)
Async XLA Ops:
  0.0 0.8 copy-start
  0.0 3.6 %copy-start.3 = (bf16[512,448]{0,1:T(8,128)(2,1)S(1)}, bf16[512,448]{0,1:T(8,128)(2,1)}, u32[]{:S(2)}) copy-start(bf16[512,448]{0,1:T(8,128)(2,1)} %param.21) | copy-start | bytes 1376260
  0.0 5.5 %copy-start.8 = (bf16[128,512]{1,0:T(8,128)(2,1)S(1)}, bf16[128,512]{1,0:T(8,128)(2,1)}, u32[]{:S(2)}) copy-start(bf16[128,512]{1,0:T(8,128)(2,1)} %param.11) | copy-start | bytes 393220
  0.0 5.5 %copy-start.9 = (bf16[128,256]{1,0:T(8,128)(2,1)S(1)}, bf16[128,256]{1,0:T(8,128)(2,1)}, u32[]{:S(2)}) copy-start(bf16[128,256]{1,0:T(8,128)(2,1)} %param.12) | copy-start | bytes 196612
  0.0 17.7 %copy-start.6 = (s32[16,32]{1,0:T(8,128)S(1)}, s32[16,32]{1,0:T(8,128)}, u32[]{:S(2)}) copy-start(s32[16,32]{1,0:T(8,128)} %table.1) | copy-start | bytes 6148
  0.0 17.7 %copy-start.7 = (s32[16]{0:T(128)S(1)}, s32[16]{0:T(128)}, u32[]{:S(2)}) copy-start(s32[16]{0:T(128)} %lens.1) | copy-start | bytes 196
  0.0 17.7 %copy-start.2 = (bf16[4,128,512]{2,1,0:T(8,128)(2,1)S(1)}, bf16[4,128,512]{2,1,0:T(8,128)(2,1)}, u32[]{:S(2)}) copy-start(bf16[4,128,512]{2,1,0:T(8,128)(2,1)} %refs_4_.3) | copy-start | bytes 1572868
  1.9 19.0 %collective-permute-start.3 = (bf16[576,512]{1,0:T(8,128)(2,1)S(1)}, bf16[576,512]{1,0:T(8,128)(2,1)S(1)}, u32[]{:S(2)}, u32[]{:S(2)}) collective-permute-start(bf16[576,512]{1,0:T(8,128)(2,1)S(1)} %pad_maximum_fusion.refs_0_), channel_id=1, source_target_pairs={{0,128},{128,0},{1,129},{129,1},{2,130},{130,2},{3,131},{131,3},{4... | collective-permute-start | bytes 1769480 | tf_op jit(solution)/shard_map/ppermute | solution.py:365
  3.6 17.3 %collective-permute-start.4 = (bf16[448,512]{1,0:T(8,128)(2,1)S(1)}, bf16[448,512]{1,0:T(8,128)(2,1)S(1)}, u32[]{:S(2)}, u32[]{:S(2)}) collective-permute-start(bf16[448,512]{1,0:T(8,128)(2,1)S(1)} %bitcast.18), channel_id=1, source_target_pairs={{0,2},{2,0},{1,3},{3,1},{4,6},{6,4},{5,7},{7,5},{8,10},{10,8},{9,1... | collective-permute-start | bytes 1376264 | tf_op jit(solution)/shard_map/ppermute | solution.py:365
  5.6 11.6 %collective-permute-start = (bf16[128,768]{1,0:T(8,128)(2,1)S(1)}, bf16[128,768]{1,0:T(8,128)(2,1)S(1)}, u32[]{:S(2)}, u32[]{:S(2)}) collective-permute-start(bf16[128,768]{1,0:T(8,128)(2,1)S(1)} %constant_dynamic-update-slice_fusion.refs_0_), channel_id=1, source_target_pairs={{32,0},{64,32},{96,64},{0,96},{33,1},{65,33},{97,65},{1,97},{34,2}... | collective-permute-start | bytes 589832 | tf_op jit(solution)/shard_map/ppermute | solution.py:361
  6.5 10.7 %collective-permute-start.1 = (bf16[128,768]{1,0:T(8,128)(2,1)S(1)}, bf16[128,768]{1,0:T(8,128)(2,1)S(1)}, u32[]{:S(2)}, u32[]{:S(2)}) collective-permute-start(bf16[128,768]{1,0:T(8,128)(2,1)S(1)} %constant_dynamic-update-slice_fusion.refs_0_), channel_id=1, source_target_pairs={{64,0},{96,32},{0,64},{32,96},{65,1},{97,33},{1,65},{33,97},{66,2}... | collective-permute-start | bytes 589832 | tf_op jit(solution)/shard_map/ppermute | solution.py:361
  7.6 10.2 %collective-permute-start.2 = (bf16[128,768]{1,0:T(8,128)(2,1)S(1)}, bf16[128,768]{1,0:T(8,128)(2,1)S(1)}, u32[]{:S(2)}, u32[]{:S(2)}) collective-permute-start(bf16[128,768]{1,0:T(8,128)(2,1)S(1)} %constant_dynamic-update-slice_fusion.refs_0_), channel_id=1, source_target_pairs={{96,0},{0,32},{32,64},{64,96},{97,1},{1,33},{33,65},{65,97},{98,2}... | collective-permute-start | bytes 589832 | tf_op jit(solution)/shard_map/ppermute | solution.py:361
  21.0 6.5 %copy-start.1 = (bf16[4,512,128]{2,1,0:T(8,128)(2,1)S(1)}, bf16[4,512,128]{2,1,0:T(8,128)(2,1)}, u32[]{:S(2)}) copy-start(bf16[4,512,128]{2,1,0:T(8,128)(2,1)} %refs_4_.5) | copy-start | bytes 1572868
  21.0 5.7 %collective-permute-start.6 = (bf16[2,448,512]{2,1,0:T(8,128)(2,1)S(1)}, bf16[2,448,512]{2,1,0:T(8,128)(2,1)S(1)}, u32[]{:S(2)}, u32[]{:S(2)}) collective-permute-start(bf16[2,448,512]{2,1,0:T(8,128)(2,1)S(1)} %pair.1.refs_4_), channel_id=1, source_target_pairs={{0,16},{16,0},{1,17},{17,1},{2,18},{18,2},{3,19},{19,3},{4,20},{20... | collective-permute-start | bytes 2752520 | tf_op jit(solution)/shard_map/ppermute | solution.py:365
  21.1 22.8 %collective-permute-start.8 = (bf16[2,448,512]{2,1,0:T(8,128)(2,1)S(1)}, bf16[2,448,512]{2,1,0:T(8,128)(2,1)S(1)}, u32[]{:S(2)}, u32[]{:S(2)}) collective-permute-start(bf16[2,448,512]{2,1,0:T(8,128)(2,1)S(1)} %pair.1.refs_4_), channel_id=1, source_target_pairs={{0,128},{1,129},{128,0},{129,1},{2,130},{3,131},{130,2},{131,3},{4... | collective-permute-start | bytes 2752520 | tf_op jit(solution)/shard_map/ppermute | solution.py:365
  21.4 23.9 %collective-permute-start.9 = (bf16[2,448,512]{2,1,0:T(8,128)(2,1)S(1)}, bf16[2,448,512]{2,1,0:T(8,128)(2,1)S(1)}, u32[]{:S(2)}, u32[]{:S(2)}) collective-permute-start(bf16[2,448,512]{2,1,0:T(8,128)(2,1)S(1)} %pair.1.refs_4_), channel_id=1, source_target_pairs={{0,129},{1,128},{128,1},{129,0},{2,131},{3,130},{130,3},{131,2},{4... | collective-permute-start | bytes 2752520 | tf_op jit(solution)/shard_map/ppermute | solution.py:365
  24.6 2.0 %collective-permute-start.5 = (bf16[576,512]{1,0:T(8,128)(2,1)S(1)}, bf16[576,512]{1,0:T(8,128)(2,1)S(1)}, u32[]{:S(2)}, u32[]{:S(2)}) collective-permute-start(bf16[576,512]{1,0:T(8,128)(2,1)S(1)} %get-tuple-element.43.refs_0_), channel_id=1, source_target_pairs={{0,16},{16,0},{1,17},{17,1},{2,18},{18,2},{3,19},{19,3},{4,20},{20... | collective-permute-start | bytes 1769480 | tf_op jit(solution)/shard_map/ppermute | solution.py:365
  24.7 2.8 %collective-permute-start.7 = (bf16[576,512]{1,0:T(8,128)(2,1)S(1)}, bf16[576,512]{1,0:T(8,128)(2,1)S(1)}, u32[]{:S(2)}, u32[]{:S(2)}) collective-permute-start(bf16[576,512]{1,0:T(8,128)(2,1)S(1)} %get-tuple-element.44.refs_1_), channel_id=1, source_target_pairs={{0,16},{16,0},{1,17},{17,1},{2,18},{18,2},{3,19},{19,3},{4,20},{20... | collective-permute-start | bytes 1769480 | tf_op jit(solution)/shard_map/ppermute | solution.py:365
  45.3 6.7 %copy-start.4 = (bf16[128,512]{1,0:T(8,128)(2,1)S(1)}, bf16[128,512]{1,0:T(8,128)(2,1)}, u32[]{:S(2)}) copy-start(bf16[128,512]{1,0:T(8,128)(2,1)} %refs_5_.1) | copy-start | bytes 393220
  45.3 6.7 %copy-start.5 = (bf16[1,64,128]{2,1,0:T(8,128)(2,1)S(1)}, bf16[1,64,128]{2,1,0:T(8,128)(2,1)}, u32[]{:S(2)}) copy-start(bf16[1,64,128]{2,1,0:T(8,128)(2,1)} %param.14) | copy-start | bytes 49156
  45.4 15.4 %collective-permute-start.16 = (bf16[448,512]{1,0:T(8,128)(2,1)S(1)}, bf16[448,512]{1,0:T(8,128)(2,1)S(1)}, u32[]{:S(2)}, u32[]{:S(2)}) collective-permute-start(bf16[448,512]{1,0:T(8,128)(2,1)S(1)} %slice_bitcast_fusion.1), channel_id=1, source_target_pairs={{0,128},{1,129},{128,0},{129,1},{2,130},{3,131},{130,2},{131,3},{4... | collective-permute-start | bytes 1376264 | tf_op jit(solution)/shard_map/ppermute | solution.py:365
  45.8 15.0 %collective-permute-start.17 = (bf16[448,512]{1,0:T(8,128)(2,1)S(1)}, bf16[448,512]{1,0:T(8,128)(2,1)S(1)}, u32[]{:S(2)}, u32[]{:S(2)}) collective-permute-start(bf16[448,512]{1,0:T(8,128)(2,1)S(1)} %slice_bitcast_fusion), channel_id=1, source_target_pairs={{0,129},{1,128},{128,1},{129,0},{2,131},{3,130},{130,3},{131,2},{4... | collective-permute-start | bytes 1376264 | tf_op jit(solution)/shard_map/ppermute | solution.py:365
  48.5 8.8 %collective-permute-start.10 = (bf16[128,640]{1,0:T(8,128)(2,1)S(1)}, bf16[128,640]{1,0:T(8,128)(2,1)S(1)}, u32[]{:S(2)}, u32[]{:S(2)}) collective-permute-start(bf16[128,640]{1,0:T(8,128)(2,1)S(1)} %get-tuple-element.50), channel_id=1, source_target_pairs={{0,32},{32,64},{64,96},{96,0},{1,33},{33,65},{65,97},{97,1},{2,34}... | collective-permute-start | bytes 491528 | tf_op jit(solution)/shard_map/ppermute | solution.py:416
  51.2 8.2 %collective-permute-start.11 = (bf16[128,640]{1,0:T(8,128)(2,1)S(1)}, bf16[128,640]{1,0:T(8,128)(2,1)S(1)}, u32[]{:S(2)}, u32[]{:S(2)}) collective-permute-start(bf16[128,640]{1,0:T(8,128)(2,1)S(1)} %get-tuple-element.51), channel_id=1, source_target_pairs={{0,64},{32,96},{64,0},{96,32},{1,65},{33,97},{65,1},{97,33},{2,66}... | collective-permute-start | bytes 491528 | tf_op jit(solution)/shard_map/ppermute | solution.py:416
  51.4 9.4 %collective-permute-start.12 = (bf16[128,640]{1,0:T(8,128)(2,1)S(1)}, bf16[128,640]{1,0:T(8,128)(2,1)S(1)}, u32[]{:S(2)}, u32[]{:S(2)}) collective-permute-start(bf16[128,640]{1,0:T(8,128)(2,1)S(1)} %get-tuple-element.52), channel_id=1, source_target_pairs={{0,96},{32,0},{64,32},{96,64},{1,97},{33,1},{65,33},{97,65},{2,98}... | collective-permute-start | bytes 491528 | tf_op jit(solution)/shard_map/ppermute | solution.py:416
  60.8 9.9 %collective-permute-start.18 = (bf16[2,448,512]{2,1,0:T(8,128)(2,1)S(1)}, bf16[2,448,512]{2,1,0:T(8,128)(2,1)S(1)}, u32[]{:S(2)}, u32[]{:S(2)}) collective-permute-start(bf16[2,448,512]{2,1,0:T(8,128)(2,1)S(1)} %get-tuple-element.59.refs_5_), channel_id=1, source_target_pairs={{0,16},{16,0},{1,17},{17,1},{2,18},{18,2},{3,19},{19,3},{4,20},{20... | collective-permute-start | bytes 2752520 | tf_op jit(solution)/shard_map/ppermute | solution.py:365
  60.9 9.8 %collective-permute-start.19 = (bf16[2,448,512]{2,1,0:T(8,128)(2,1)S(1)}, bf16[2,448,512]{2,1,0:T(8,128)(2,1)S(1)}, u32[]{:S(2)}, u32[]{:S(2)}) collective-permute-start(bf16[2,448,512]{2,1,0:T(8,128)(2,1)S(1)} %get-tuple-element.60.refs_6_), channel_id=1, source_target_pairs={{0,16},{16,0},{1,17},{17,1},{2,18},{18,2},{3,19},{19,3},{4,20},{20... | collective-permute-start | bytes 2752520 | tf_op jit(solution)/shard_map/ppermute | solution.py:365
  62.4 5.5 %collective-permute-start.13 = (bf16[32,512]{1,0:T(8,128)(2,1)S(1)}, bf16[32,512]{1,0:T(8,128)(2,1)S(1)}, u32[]{:S(2)}, u32[]{:S(2)}) collective-permute-start(bf16[32,512]{1,0:T(8,128)(2,1)S(1)} %get-tuple-element.54), channel_id=1, source_target_pairs={{0,1},{1,0},{2,3},{3,2},{4,5},{5,4},{6,7},{7,6},{8,9},{9,8},{10,11... | collective-permute-start | bytes 98312 | tf_op jit(solution)/shard_map/ppermute | solution.py:365
  64.1 4.0 %collective-permute-start.14 = (bf16[32,512]{1,0:T(8,128)(2,1)S(1)}, bf16[32,512]{1,0:T(8,128)(2,1)S(1)}, u32[]{:S(2)}, u32[]{:S(2)}) collective-permute-start(bf16[32,512]{1,0:T(8,128)(2,1)S(1)} %get-tuple-element.55), channel_id=1, source_target_pairs={{0,2},{1,3},{2,0},{3,1},{4,6},{5,7},{6,4},{7,5},{8,10},{9,11},{10,... | collective-permute-start | bytes 98312 | tf_op jit(solution)/shard_map/ppermute | solution.py:365
  64.3 6.3 %collective-permute-start.15 = (bf16[32,512]{1,0:T(8,128)(2,1)S(1)}, bf16[32,512]{1,0:T(8,128)(2,1)S(1)}, u32[]{:S(2)}, u32[]{:S(2)}) collective-permute-start(bf16[32,512]{1,0:T(8,128)(2,1)S(1)} %get-tuple-element.56), channel_id=1, source_target_pairs={{0,3},{1,2},{2,1},{3,0},{4,7},{5,6},{6,5},{7,4},{8,11},{9,10},{10,... | collective-permute-start | bytes 98312 | tf_op jit(solution)/shard_map/ppermute | solution.py:365
  70.7 10.7 %collective-permute-start.23 = (bf16[448,512]{1,0:T(8,128)(2,1)S(1)}, bf16[448,512]{1,0:T(8,128)(2,1)S(1)}, u32[]{:S(2)}, u32[]{:S(2)}) collective-permute-start(bf16[448,512]{1,0:T(8,128)(2,1)S(1)} %get-tuple-element.62.refs_7_), channel_id=1, source_target_pairs={{0,16},{16,0},{1,17},{17,1},{2,18},{18,2},{3,19},{19,3},{4,20},{20... | collective-permute-start | bytes 1376264 | tf_op jit(solution)/shard_map/ppermute | solution.py:365
  70.8 10.6 %collective-permute-start.24 = (bf16[448,512]{1,0:T(8,128)(2,1)S(1)}, bf16[448,512]{1,0:T(8,128)(2,1)S(1)}, u32[]{:S(2)}, u32[]{:S(2)}) collective-permute-start(bf16[448,512]{1,0:T(8,128)(2,1)S(1)} %get-tuple-element.63.refs_8_), channel_id=1, source_target_pairs={{0,16},{16,0},{1,17},{17,1},{2,18},{18,2},{3,19},{19,3},{4,20},{20... | collective-permute-start | bytes 1376264 | tf_op jit(solution)/shard_map/ppermute | solution.py:365
  71.3 7.6 %collective-permute-start.20 = (bf16[32,2048]{1,0:T(8,128)(2,1)S(1)}, bf16[32,2048]{1,0:T(8,128)(2,1)S(1)}, u32[]{:S(2)}, u32[]{:S(2)}) collective-permute-start(bf16[32,2048]{1,0:T(8,128)(2,1)S(1)} %get-tuple-element.61.refs_0_), channel_id=1, source_target_pairs={{32,0},{64,32},{96,64},{0,96},{33,1},{65,33},{97,65},{1,97},{34,2}... | collective-permute-start | bytes 393224 | tf_op jit(solution)/shard_map/ppermute | solution.py:361
  72.5 8.4 %collective-permute-start.21 = (bf16[32,2048]{1,0:T(8,128)(2,1)S(1)}, bf16[32,2048]{1,0:T(8,128)(2,1)S(1)}, u32[]{:S(2)}, u32[]{:S(2)}) collective-permute-start(bf16[32,2048]{1,0:T(8,128)(2,1)S(1)} %get-tuple-element.61.refs_0_), channel_id=1, source_target_pairs={{64,0},{96,32},{0,64},{32,96},{65,1},{97,33},{1,65},{33,97},{66,2}... | collective-permute-start | bytes 393224 | tf_op jit(solution)/shard_map/ppermute | solution.py:361
  74.5 6.9 %collective-permute-start.22 = (bf16[32,2048]{1,0:T(8,128)(2,1)S(1)}, bf16[32,2048]{1,0:T(8,128)(2,1)S(1)}, u32[]{:S(2)}, u32[]{:S(2)}) collective-permute-start(bf16[32,2048]{1,0:T(8,128)(2,1)S(1)} %get-tuple-element.61.refs_0_), channel_id=1, source_target_pairs={{96,0},{0,32},{32,64},{64,96},{97,1},{1,33},{33,65},{65,97},{98,2}... | collective-permute-start | bytes 393224 | tf_op jit(solution)/shard_map/ppermute | solution.py:361
  84.4 11.2 %collective-permute-start.25 = (bf16[32,1792]{1,0:T(8,128)(2,1)S(1)}, bf16[32,1792]{1,0:T(8,128)(2,1)S(1)}, u32[]{:S(2)}, u32[]{:S(2)}) collective-permute-start(bf16[32,1792]{1,0:T(8,128)(2,1)S(1)} %get-tuple-element.66), channel_id=1, source_target_pairs={{0,4},{4,8},{8,12},{12,0},{1,5},{5,9},{9,13},{13,1},{2,6},{6,10},{... | collective-permute-start | bytes 344072 | tf_op jit(solution)/shard_map/ppermute | solution.py:442
  87.7 12.8 %collective-permute-start.26 = (bf16[32,1792]{1,0:T(8,128)(2,1)S(1)}, bf16[32,1792]{1,0:T(8,128)(2,1)S(1)}, u32[]{:S(2)}, u32[]{:S(2)}) collective-permute-start(bf16[32,1792]{1,0:T(8,128)(2,1)S(1)} %get-tuple-element.67), channel_id=1, source_target_pairs={{0,8},{4,12},{8,0},{12,4},{1,9},{5,13},{9,1},{13,5},{2,10},{6,14},... | collective-permute-start | bytes 344072 | tf_op jit(solution)/shard_map/ppermute | solution.py:442
  92.9 10.0 %collective-permute-start.27 = (bf16[32,1792]{1,0:T(8,128)(2,1)S(1)}, bf16[32,1792]{1,0:T(8,128)(2,1)S(1)}, u32[]{:S(2)}, u32[]{:S(2)}) collective-permute-start(bf16[32,1792]{1,0:T(8,128)(2,1)S(1)} %get-tuple-element.68), channel_id=1, source_target_pairs={{0,12},{4,0},{8,4},{12,8},{1,13},{5,1},{9,5},{13,9},{2,14},{6,2},{... | collective-permute-start | bytes 344072 | tf_op jit(solution)/shard_map/ppermute | solution.py:442
  103.0 6.4 %collective-permute-start.28 = (f32[8,1792]{1,0:T(8,128)S(1)}, f32[8,1792]{1,0:T(8,128)S(1)}, u32[]{:S(2)}, u32[]{:S(2)}) collective-permute-start(f32[8,1792]{1,0:T(8,128)S(1)} %get-tuple-element.70), channel_id=1, source_target_pairs={{0,32},{32,64},{64,96},{96,0},{1,33},{33,65},{65,97},{97,1},{2,34}... | collective-permute-start | bytes 172040 | tf_op jit(solution)/shard_map/ppermute | solution.py:446
  106.7 5.7 %collective-permute-start.29 = (f32[8,1792]{1,0:T(8,128)S(1)}, f32[8,1792]{1,0:T(8,128)S(1)}, u32[]{:S(2)}, u32[]{:S(2)}) collective-permute-start(f32[8,1792]{1,0:T(8,128)S(1)} %get-tuple-element.71), channel_id=1, source_target_pairs={{0,64},{32,96},{64,0},{96,32},{1,65},{33,97},{65,1},{97,33},{2,66}... | collective-permute-start | bytes 172040 | tf_op jit(solution)/shard_map/ppermute | solution.py:446
  106.9 6.0 %collective-permute-start.30 = (f32[8,1792]{1,0:T(8,128)S(1)}, f32[8,1792]{1,0:T(8,128)S(1)}, u32[]{:S(2)}, u32[]{:S(2)}) collective-permute-start(f32[8,1792]{1,0:T(8,128)S(1)} %get-tuple-element.72), channel_id=1, source_target_pairs={{0,96},{32,0},{64,32},{96,64},{1,97},{33,1},{65,33},{97,65},{2,98}... | collective-permute-start | bytes 172040 | tf_op jit(solution)/shard_map/ppermute | solution.py:446

commit v6 on v5

--- a/solution.py
+++ b/solution.py
@@ -35,12 +35,8 @@
     return lax.dot_general(a, b, (((1,), (1,)), ((), ())), preferred_element_type=jnp.float32)
 
 
-def prepare_kernel(ids, table, lens, *refs):
-    queries = refs[:SLOTS]
-    weight, q_lat, q_rot, lists, counts, w_uk, sem = refs[SLOTS:]
+def plan_kernel(ids, table, lens, lists, counts):
     yl, x, k = ids[0], ids[1], ids[2]
-    load = pltpu.make_async_copy(weight, w_uk, sem)
-    load.start()
     for s in range(SLOTS):
         limit = lens[yl * 8 + ((x + s) % 4) * 2 + k]
 
@@ -62,7 +58,23 @@
         found, valid = lax.fori_loop(0, blocks, scan, (jnp.int32(0), jnp.int32(0)))
         counts[s] = found
         counts[SLOTS + s] = valid
-    load.wait()
+
+
+def plan(ids, table, lens):
+    scalar = pl.BlockSpec(memory_space=SMEM)
+    return pl.pallas_call(
+        plan_kernel,
+        out_shape=[jax.ShapeDtypeStruct((SLOTS * 16,), jnp.int32), jax.ShapeDtypeStruct((2 * SLOTS,), jnp.int32)],
+        in_specs=[scalar] * 3,
+        out_specs=[scalar] * 2,
+        compiler_params=pltpu.CompilerParams(vmem_limit_bytes=2**20),
+        name="plan",
+    )(ids, table, lens)
+
+
+def prepare_kernel(counts, *refs):
+    queries = refs[:SLOTS]
+    w_uk, q_lat, q_rot = refs[SLOTS : SLOTS + 3]
     for h in range(HEADS):
         rows = slice(h * TOK, (h + 1) * TOK)
         part = jnp.concatenate([q[:, h * NOPE : (h + 1) * NOPE] for q in queries], axis=0)
@@ -71,25 +83,6 @@
         for s in range(SLOTS):
             q_lat[s, rows, :] = part[s * TOK : (s + 1) * TOK]
             q_rot[s, rows, :] = queries[s][:, first : first + ROPE]
-
-
-def prepare(ids, table, lens, queries, w_uk):
-    full = pl.BlockSpec(memory_space=VMEM)
-    scalar = pl.BlockSpec(memory_space=SMEM)
-    return pl.pallas_call(
-        prepare_kernel,
-        out_shape=[
-            jax.ShapeDtypeStruct((SLOTS, ROWS, LAT), jnp.bfloat16),
-            jax.ShapeDtypeStruct((SLOTS, ROWS, ROPE), jnp.bfloat16),
-            jax.ShapeDtypeStruct((SLOTS * 16,), jnp.int32),
-            jax.ShapeDtypeStruct((2 * SLOTS,), jnp.int32),
-        ],
-        in_specs=[scalar] * 3 + [full] * SLOTS + [pl.BlockSpec(memory_space=pltpu.HBM)],
-        out_specs=[full, full, scalar, scalar],
-        scratch_shapes=[pltpu.VMEM((HEADS, NOPE, LAT), jnp.bfloat16), pltpu.SemaphoreType.DMA],
-        compiler_params=pltpu.CompilerParams(vmem_limit_bytes=16 * 2**20),
-        name="prepare",
-    )(ids, table, lens, *queries, w_uk)
 
 
 def attention_kernel(slots, own, lists, counts, q_lat, q_rot, *refs):
@@ -287,9 +280,17 @@
     out[1] = two[...]
 
 
+def rest_kernel(*refs):
+    out = refs[4]
+    for i in range(4):
+        out[i] = refs[i // 2][i % 2]
+    out[4] = refs[2][...]
+    out[5] = refs[3][...]
+
+
 def project_kernel(ids, *refs):
-    heads, mine, other = refs[:4], refs[4:9], refs[9:14]
-    outs, total = refs[14:18], refs[18]
+    heads, mine, other = refs[:4], refs[4:6], refs[6:8]
+    outs, total = refs[8:12], refs[12]
     zb = ids[3]
     rows = jnp.concatenate([h[...] for h in heads], axis=0)
     for side_y in range(2):
@@ -298,7 +299,7 @@
             value = None
             for d in range(4):
                 m, dz = side_y * 2 + (d & 1), d >> 1
-                weight = pieces[3 + dz][...] if m == 1 else pieces[max(m - 1, 0)][dz]
+                weight = pieces[0][dz] if m == 0 else pieces[1][(0, 4, 0, 2)[m] + dz]
                 part = dot_nt(rows[:, d * 512 : (d + 1) * 512], weight)
                 value = part if value is None else value + part
             sides.append(value)
@@ -396,7 +397,16 @@
     queries = [query] + [turn(query, "x", 4, s) for s in (1, 2, 3)]
     pool_y = flip(pool, "yl", 2, 1)
     weight_z = flip(weight, "z0", 2, 1)
-    q_lat, q_rot, lists, counts = prepare(ids, block_table, prefix_len, queries, w_uk)
+    lists, counts = plan(ids, block_table, prefix_len)
+    q_lat, q_rot = simple(
+        prepare_kernel,
+        "prepare",
+        [
+            jax.ShapeDtypeStruct((SLOTS, ROWS, LAT), jnp.bfloat16),
+            jax.ShapeDtypeStruct((SLOTS, ROWS, ROPE), jnp.bfloat16),
+        ],
+        [counts, *queries, w_uk],
+    )
     pool, pool_y, weight_z = tie([pool, pool_y, weight_z], [q_lat])
     pool_k = flip(pool, "k", 2, 1)
     pool_yk = flip(pool_y, "k", 2, 1)
@@ -410,14 +420,12 @@
     pools = [pool, pool_y, pool_k, pool_yk]
 
     away = attention((1, 2, 3), False, lists, counts, q_lat, q_rot, pools, w_uv, ())
-    *away, mine[1], mine[2] = tie([*away, mine[1], mine[2]], [])
-    far = [flip(mine[2][0], ring, 4, 2), flip(mine[1][1], ring, 4, 3)]
     came = [
         lax.ppermute(part, "x", [(i, (i + s) % 4) for i in range(4)]) for s, part in zip((1, 2, 3), away)
     ]
     (home,) = attention((0,), True, lists, counts, q_lat, q_rot, pools, w_uv, (new_latent, new_rope[0]))
-    mine[1], mine[2] = tie([mine[1], mine[2]], [*came, *far, home])
-    other += [flip(m, "k", 2, 1) for m in mine[1:]]
+    mine[1], mine[2] = tie([mine[1], mine[2]], [*came, home])
+    far = [flip(mine[2][0], ring, 4, 2), flip(mine[1][1], ring, 4, 3)]
     heads = simple(
         combine_kernel,
         "combine",
@@ -427,9 +435,11 @@
     )
     heads = [heads[0]] + [flip(heads[d], ("z0", "yh"), 4, d) for d in (1, 2, 3)]
     heads = simple(join_kernel, "join", jax.ShapeDtypeStruct((32, 2048), jnp.bfloat16), heads)
-    heads, *far = tie([heads, *far], other[1:])
-    mine += far
-    other += [flip(f, "k", 2, 1) for f in far]
+    rest = simple(
+        rest_kernel, "rest", jax.ShapeDtypeStruct((6, 448, 512), jnp.bfloat16), tie([*mine[1:], *far], [heads])
+    )
+    mine = [pair, rest]
+    other.append(flip(rest, "k", 2, 1))
     heads = [heads] + [turn(heads, "x", 4, s) for s in (1, 2, 3)]
     partial = simple(
         project_kernel,

time: 114 us -> 110 us (0.965)
  waiting for transfers between devices: 45.6 us -> 37 us
  local copies, waits for them, and re-layouts: 1 us -> 5.09 us
    ppermute x3, starting transfers between devices: 3.49 us -> 7.1 us  [local(): lax.ppermute(part, 'x', [(i, (i + s) % 4) for i in range(4)])]
    ppermute x6, waiting for transfers between devices: 14.3 us -> 10.8 us  [turn(): lax.ppermute(value, axis, [((i + shift) % size, i) for i in range(size)])]
    unnamed x21 -> x17, local copies, waits for them, and re-layouts: 0.84 us -> 4.09 us
    ppermute x16 -> x13, waiting for transfers between devices: 13.8 us -> 10.8 us  [flip(): return lax.ppermute(value, axis, [(i, i ^ bits) for i in range(size)])]
    ppermute x3, waiting for transfers between devices: 4.97 us -> 2.33 us  [local(): lax.ppermute(part, 'x', [(i, (i + s) % 4) for i in range(4)])]
    ppermute x16 -> x13, starting transfers between devices: 17.1 us -> 15 us  [flip(): return lax.ppermute(value, axis, [(i, i ^ bits) for i in range(size)])]
    pallas_call x2, Pallas kernels: 13.2 us -> 11.6 us  [attention(): pl.pallas_call(functools.partial(attention_kernel, slots, own), out_shape...]
    pallas_call x6 -> x8, Pallas kernels: 5.45 us -> 6.91 us  [simple(): pl.pallas_call(kernel, out_shape=out_shape, in_specs=[pl.BlockSpec(memory...]
  transfers between devices with their start and end apart: 31 -> 28, of which waited for: 20 -> 15; matrix products, arithmetic and copies ran while one was open for 0% -> 2% of each run, Pallas kernels for 15% -> 15%
where the time goes in v6:
time: 110 us; the launch traced here: 109 us
  starting transfers between devices  45 us (41%)
  waiting for transfers between devices  37 us (34%)
  Pallas kernels  20.9 us (19%)
  local copies, waits for them, and re-layouts  5.09 us (5%)
    ppermute x13, starting transfers between devices, flip(): return lax.ppermute(value, axis, [(i, i ^ bits) for i in range(size)])  15 us
    pallas_call x2, Pallas kernels, attention(): pl.pallas_call(functools.partial(attention_kernel, slots, own), out_shape...  11.6 us
    ppermute x13, waiting for transfers between devices, flip(): return lax.ppermute(value, axis, [(i, i ^ bits) for i in range(size)])  10.8 us
    ppermute x6, waiting for transfers between devices, turn(): lax.ppermute(value, axis, [((i + shift) % size, i) for i in range(size)])  10.8 us
    ppermute x3, starting transfers between devices, local(): lax.ppermute(partial[d], 'zb', [(i, (i + d) % 4) for i in range(4)])  10.5 us
    ppermute x6, starting transfers between devices, turn(): lax.ppermute(value, axis, [((i + shift) % size, i) for i in range(size)])  8.91 us
    ppermute x3, waiting for transfers between devices, local(): lax.ppermute(partial[d], 'zb', [(i, (i + d) % 4) for i in range(4)])  7.96 us
    ppermute x3, starting transfers between devices, local(): lax.ppermute(part, 'x', [(i, (i + s) % 4) for i in range(4)])  7.1 us
  transfers between devices with their start and end apart: 28, of which 15 were waited for; matrix products, arithmetic and copies ran while one was open for 2% of the time, Pallas kernels for 15%

profile of v6, /device:TPU:6, one launch (start us, length us, event | category | flops | bytes accessed | tf_op | source)
XLA Modules:
  0.0 109.3 jit_solution(5229498709746302340)
XLA Ops:
  0.0 0.8 copy-done
  0.9 1.1 pad_maximum_fusion.refs_0_
  1.9 1.7 %collective-permute-start.3 = (bf16[576,512]{1,0:T(8,128)(2,1)S(1)}, bf16[576,512]{1,0:T(8,128)(2,1)S(1)}, u32[]{:S(2)}, u32[]{:S(2)}) collective-permute-start(bf16[576,512]{1,0:T(8,128)(2,1)S(1)} %pad_maximum_fusion.refs_0_), channel_id=1, source_target_pairs={{0,128},{128,0},{1,129},{129,1},{2,130},{130,2},{3,131},{131,3},{4... | collective-permute-start | bytes 1769480 | tf_op jit(solution)/shard_map/ppermute | solution.py:366
  3.6 1.9 %collective-permute-start.4 = (bf16[448,512]{1,0:T(8,128)(2,1)}, bf16[448,512]{1,0:T(8,128)(2,1)S(1)}, u32[]{:S(2)}, u32[]{:S(2)}) collective-permute-start(bf16[448,512]{1,0:T(8,128)(2,1)} %bitcast.18), channel_id=1, source_target_pairs={{0,2},{2,0},{1,3},{3,1},{4,6},{6,4},{5,7},{7,5},{8,10},{10,8},{9,1... | collective-permute-start | bytes 1376264 | tf_op jit(solution)/shard_map/ppermute | solution.py:366
  5.5 0.9 constant_dynamic-update-slice_fusion.1
  6.4 0.8 constant_dynamic-update-slice_fusion.refs_0_
  7.3 0.8 collective-permute-start
  8.1 1.1 %collective-permute-start.1 = (bf16[128,768]{1,0:T(8,128)(2,1)S(1)}, bf16[128,768]{1,0:T(8,128)(2,1)S(1)}, u32[]{:S(2)}, u32[]{:S(2)}) collective-permute-start(bf16[128,768]{1,0:T(8,128)(2,1)S(1)} %constant_dynamic-update-slice_fusion.refs_0_), channel_id=1, source_target_pairs={{64,0},{96,32},{0,64},{32,96},{65,1},{97,33},{1,65},{33,97},{66,2}... | collective-permute-start | bytes 589832 | tf_op jit(solution)/shard_map/ppermute | solution.py:362
  9.2 2.1 %collective-permute-start.2 = (bf16[128,768]{1,0:T(8,128)(2,1)S(1)}, bf16[128,768]{1,0:T(8,128)(2,1)S(1)}, u32[]{:S(2)}, u32[]{:S(2)}) collective-permute-start(bf16[128,768]{1,0:T(8,128)(2,1)S(1)} %constant_dynamic-update-slice_fusion.refs_0_), channel_id=1, source_target_pairs={{96,0},{0,32},{32,64},{64,96},{97,1},{1,33},{33,65},{65,97},{98,2}... | collective-permute-start | bytes 589832 | tf_op jit(solution)/shard_map/ppermute | solution.py:362
  11.3 0.1 stack.23.ids
  11.4 0.7 copy-done.6
  12.1 0.7 copy-done.7
  12.8 2.4 %plan.1 = (s32[64]{0:T(128)S(1)}, s32[8]{0:T(128)S(1)}) custom-call(s32[5]{0:T(128)S(1)} %stack.23.ids, s32[16,32]{1,0:T(8,128)S(1)} %copy-done.6, s32[16]{0:T(128)S(1)} %copy-done.7), custom_call_target="tpu_custom_call" | custom-call | tf_op jit(solution)/shard_map/plan/pallas_call | solution.py:65
  15.2 3.6 %collective-permute-done.refs_1_ = bf16[128,768]{1,0:T(8,128)(2,1)S(1)} collective-permute-done((bf16[128,768]{1,0:T(8,128)(2,1)S(1)}, bf16[128,768]{1,0:T(8,128)(2,1)S(1)}, u32[]{:S(2)}, u32[]{:S(2)}) %collective-permute-start) | collective-permute-done | bytes 196640 | tf_op jit(solution)/shard_map/ppermute | solution.py:362
  18.8 0.6 collective-permute-done.2.refs_3_
  19.4 1.3 %prepare.1 = (bf16[4,512,512]{2,1,0:T(8,128)(2,1)S(1)}, bf16[4,512,64]{2,1,0:T(8,128)(2,1)S(1)}) custom-call(s32[8]{0:T(128)S(1)} %get-tuple-element.36.counts, bf16[128,768]{1,0:T(8,128)(2,1)S(1)} %constant_dynamic-update-slice_fusion.refs_0_, bf16[128,768]{1,0:T(8,128)(2,1)S(1)} %collective-permute-done.refs_1_, ...), custom_call_target="tpu_custom_call" | custom-call | tf_op jit(solution)/shard_map/prepare/pallas_call | solution.py:350
  20.7 0.0 copy-start.3
  20.7 0.0 collective-permute-done.4.refs_2_
  20.7 0.0 collective-permute-done.3.refs_1_
  20.7 0.0 copy-start.1
  20.8 1.0 copy-done.3
  21.7 0.1 pair.1.refs_4_
  21.8 0.1 collective-permute-start.6
  21.9 0.5 collective-permute-start.17
  22.4 3.0 %collective-permute-start.18 = (bf16[2,448,512]{2,1,0:T(8,128)(2,1)S(1)}, bf16[2,448,512]{2,1,0:T(8,128)(2,1)S(1)}, u32[]{:S(2)}, u32[]{:S(2)}) collective-permute-start(bf16[2,448,512]{2,1,0:T(8,128)(2,1)S(1)} %pair.1.refs_4_), channel_id=1, source_target_pairs={{0,129},{1,128},{128,1},{129,0},{2,131},{3,130},{130,3},{131,2},{4... | collective-permute-start | bytes 2752520 | tf_op jit(solution)/shard_map/ppermute | solution.py:366
  25.4 0.0 collective-permute-start.5
  25.4 0.5 collective-permute-start.7
  26.0 1.5 %collective-permute-done.5.refs_0_ = bf16[576,512]{1,0:T(8,128)(2,1)S(1)} collective-permute-done((bf16[576,512]{1,0:T(8,128)(2,1)S(1)}, bf16[576,512]{1,0:T(8,128)(2,1)S(1)}, u32[]{:S(2)}, u32[]{:S(2)}) %collective-permute-start.5) | collective-permute-done | bytes 589856 | tf_op jit(solution)/shard_map/ppermute | solution.py:366
  27.4 0.0 collective-permute-done.6.refs_1_
  27.5 0.8 collective-permute-done.7.refs_3_
  28.3 7.9 %attend.3 = (bf16[128,640]{1,0:T(8,128)(2,1)S(1)}, bf16[128,640]{1,0:T(8,128)(2,1)S(1)}, bf16[128,640]{1,0:T(8,128)(2,1)S(1)}) custom-call(s32[64]{0:T(128)S(1)} %get-tuple-element.35.lists, s32[8]{0:T(128)S(1)} %get-tuple-element.36.counts, bf16[4,512,512]{2,1,0:T(8,128)(2,1)S(1)} %get-tuple-element.37.refs_3_.q_lat, ...), custom_call_target="tpu_custom_call" | custom-call | tf_op jit(solution)/shard_map/attend/pallas_call | solution.py:225
  36.2 4.1 %collective-permute-start.10 = (bf16[128,640]{1,0:T(8,128)(2,1)S(1)}, bf16[128,640]{1,0:T(8,128)(2,1)S(1)}, u32[]{:S(2)}, u32[]{:S(2)}) collective-permute-start(bf16[128,640]{1,0:T(8,128)(2,1)S(1)} %get-tuple-element.45), channel_id=1, source_target_pairs={{0,96},{32,0},{64,32},{96,64},{1,97},{33,1},{65,33},{97,65},{2,98}... | collective-permute-start | bytes 491528 | tf_op jit(solution)/shard_map/ppermute | solution.py:424
  40.2 0.5 collective-permute-start.8
  40.8 2.5 %collective-permute-start.9 = (bf16[128,640]{1,0:T(8,128)(2,1)S(1)}, bf16[128,640]{1,0:T(8,128)(2,1)S(1)}, u32[]{:S(2)}, u32[]{:S(2)}) collective-permute-start(bf16[128,640]{1,0:T(8,128)(2,1)S(1)} %get-tuple-element.44), channel_id=1, source_target_pairs={{0,64},{32,96},{64,0},{96,32},{1,65},{33,97},{65,1},{97,33},{2,66}... | collective-permute-start | bytes 491528 | tf_op jit(solution)/shard_map/ppermute | solution.py:424
  43.3 3.7 %attend.2.refs_0_.refs_5_ = bf16[128,640]{1,0:T(8,128)(2,1)S(1)} custom-call(s32[64]{0:T(128)S(1)} %get-tuple-element.35.lists, s32[8]{0:T(128)S(1)} %get-tuple-element.36.counts, bf16[4,512,512]{2,1,0:T(8,128)(2,1)S(1)} %get-tuple-element.37.refs_3_.q_lat, bf16[4,512,64]{2,1,0:T(8,128)(2,1)S(1)} %get-tuple-element.38.q_rot, ...), custom_call_target="tpu_custom_call" | custom-call | tf_op jit(solution)/shard_map/attend/pallas_call | solution.py:225
  47.0 0.3 collective-permute-done.8.refs_1_.refs_2_
  47.3 2.0 %collective-permute-done.9.refs_2_.refs_3_ = bf16[128,640]{1,0:T(8,128)(2,1)S(1)} collective-permute-done((bf16[128,640]{1,0:T(8,128)(2,1)S(1)}, bf16[128,640]{1,0:T(8,128)(2,1)S(1)}, u32[]{:S(2)}, u32[]{:S(2)}) %collective-permute-start.9) | collective-permute-done | bytes 163872 | tf_op jit(solution)/shard_map/ppermute | solution.py:424
  49.4 0.9 collective-permute-start.19
  50.3 0.5 collective-permute-start.20
  50.8 1.1 combine.1
  51.9 3.0 %collective-permute-start.11 = (bf16[32,512]{1,0:T(8,128)(2,1)S(1)}, bf16[32,512]{1,0:T(8,128)(2,1)S(1)}, u32[]{:S(2)}, u32[]{:S(2)}) collective-permute-start(bf16[32,512]{1,0:T(8,128)(2,1)S(1)} %get-tuple-element.47), channel_id=1, source_target_pairs={{0,1},{1,0},{2,3},{3,2},{4,5},{5,4},{6,7},{7,6},{8,9},{9,8},{10,11... | collective-permute-start | bytes 98312 | tf_op jit(solution)/shard_map/ppermute | solution.py:366
  54.9 0.3 collective-permute-start.12
  55.1 1.8 %collective-permute-start.13 = (bf16[32,512]{1,0:T(8,128)(2,1)S(1)}, bf16[32,512]{1,0:T(8,128)(2,1)S(1)}, u32[]{:S(2)}, u32[]{:S(2)}) collective-permute-start(bf16[32,512]{1,0:T(8,128)(2,1)S(1)} %get-tuple-element.49), channel_id=1, source_target_pairs={{0,3},{1,2},{2,1},{3,0},{4,7},{5,6},{6,5},{7,4},{8,11},{9,10},{10,... | collective-permute-start | bytes 98312 | tf_op jit(solution)/shard_map/ppermute | solution.py:366
  57.0 6.4 %collective-permute-done.11.refs_1_ = bf16[32,512]{1,0:T(8,128)(2,1)S(1)} collective-permute-done((bf16[32,512]{1,0:T(8,128)(2,1)S(1)}, bf16[32,512]{1,0:T(8,128)(2,1)S(1)}, u32[]{:S(2)}, u32[]{:S(2)}) %collective-permute-start.11) | collective-permute-done | bytes 32800 | tf_op jit(solution)/shard_map/ppermute | solution.py:366
  63.4 2.1 %collective-permute-done.20.refs_3_ = bf16[448,512]{1,0:T(8,128)(2,1)S(1)} collective-permute-done((bf16[448,512]{1,0:T(8,128)(2,1)S(1)}, bf16[448,512]{1,0:T(8,128)(2,1)S(1)}, u32[]{:S(2)}, u32[]{:S(2)}) %collective-permute-start.20) | collective-permute-done | bytes 458784 | tf_op jit(solution)/shard_map/ppermute | solution.py:366
  65.5 0.2 rest.1.refs_5_
  65.7 0.8 collective-permute-start.21
  66.5 0.8 collective-permute-start.14
  67.3 4.1 %collective-permute-start.15 = (bf16[32,2048]{1,0:T(8,128)(2,1)S(1)}, bf16[32,2048]{1,0:T(8,128)(2,1)S(1)}, u32[]{:S(2)}, u32[]{:S(2)}) collective-permute-start(bf16[32,2048]{1,0:T(8,128)(2,1)S(1)} %join.1.refs_4_.refs_0_), channel_id=1, source_target_pairs={{64,0},{96,32},{0,64},{32,96},{65,1},{97,33},{1,65},{33,97},{66,2}... | collective-permute-start | bytes 393224 | tf_op jit(solution)/shard_map/ppermute | solution.py:362
  71.4 2.6 %collective-permute-done.14.refs_1_ = bf16[32,2048]{1,0:T(8,128)(2,1)S(1)} collective-permute-done((bf16[32,2048]{1,0:T(8,128)(2,1)S(1)}, bf16[32,2048]{1,0:T(8,128)(2,1)S(1)}, u32[]{:S(2)}, u32[]{:S(2)}) %collective-permute-start.14) | collective-permute-done | bytes 131104 | tf_op jit(solution)/shard_map/ppermute | solution.py:362
  74.0 4.0 %collective-permute-done.15.refs_2_ = bf16[32,2048]{1,0:T(8,128)(2,1)S(1)} collective-permute-done((bf16[32,2048]{1,0:T(8,128)(2,1)S(1)}, bf16[32,2048]{1,0:T(8,128)(2,1)S(1)}, u32[]{:S(2)}, u32[]{:S(2)}) %collective-permute-start.15) | collective-permute-done | bytes 131104 | tf_op jit(solution)/shard_map/ppermute | solution.py:362
  78.0 3.0 %project.1 = (bf16[32,1792]{1,0:T(8,128)(2,1)S(1)}, bf16[32,1792]{1,0:T(8,128)(2,1)S(1)}, bf16[32,1792]{1,0:T(8,128)(2,1)S(1)}, bf16[32,1792]{1,0:T(8,128)(2,1)S(1)}) custom-call(s32[5]{0:T(128)S(1)} %stack.23.ids, bf16[32,2048]{1,0:T(8,128)(2,1)S(1)} %join.1.refs_4_.refs_0_, bf16[32,2048]{1,0:T(8,128)(2,1)S(1)} %collective-permute-done.14.refs_1_, ...), custom_call_target="tpu_custom_call" | custom-call | tf_op jit(solution)/shard_map/project/pallas_call | solution.py:350
  80.9 3.4 %collective-permute-start.22 = (bf16[32,1792]{1,0:T(8,128)(2,1)S(1)}, bf16[32,1792]{1,0:T(8,128)(2,1)S(1)}, u32[]{:S(2)}, u32[]{:S(2)}) collective-permute-start(bf16[32,1792]{1,0:T(8,128)(2,1)S(1)} %get-tuple-element.58), channel_id=1, source_target_pairs={{0,4},{4,8},{8,12},{12,0},{1,5},{5,9},{9,13},{13,1},{2,6},{6,10},{... | collective-permute-start | bytes 344072 | tf_op jit(solution)/shard_map/ppermute | solution.py:452
  84.3 4.5 %collective-permute-start.23 = (bf16[32,1792]{1,0:T(8,128)(2,1)S(1)}, bf16[32,1792]{1,0:T(8,128)(2,1)S(1)}, u32[]{:S(2)}, u32[]{:S(2)}) collective-permute-start(bf16[32,1792]{1,0:T(8,128)(2,1)S(1)} %get-tuple-element.59), channel_id=1, source_target_pairs={{0,8},{4,12},{8,0},{12,4},{1,9},{5,13},{9,1},{13,5},{2,10},{6,14},... | collective-permute-start | bytes 344072 | tf_op jit(solution)/shard_map/ppermute | solution.py:452
  88.8 2.7 %collective-permute-start.24 = (bf16[32,1792]{1,0:T(8,128)(2,1)S(1)}, bf16[32,1792]{1,0:T(8,128)(2,1)S(1)}, u32[]{:S(2)}, u32[]{:S(2)}) collective-permute-start(bf16[32,1792]{1,0:T(8,128)(2,1)S(1)} %get-tuple-element.60), channel_id=1, source_target_pairs={{0,12},{4,0},{8,4},{12,8},{1,13},{5,1},{9,5},{13,9},{2,14},{6,2},{... | collective-permute-start | bytes 344072 | tf_op jit(solution)/shard_map/ppermute | solution.py:452
  91.5 4.9 %collective-permute-done.23.refs_2_ = bf16[32,1792]{1,0:T(8,128)(2,1)S(1)} collective-permute-done((bf16[32,1792]{1,0:T(8,128)(2,1)S(1)}, bf16[32,1792]{1,0:T(8,128)(2,1)S(1)}, u32[]{:S(2)}, u32[]{:S(2)}) %collective-permute-start.23) | collective-permute-done | bytes 114720 | tf_op jit(solution)/shard_map/ppermute | solution.py:452
  96.3 3.1 %collective-permute-done.24.refs_3_ = bf16[32,1792]{1,0:T(8,128)(2,1)S(1)} collective-permute-done((bf16[32,1792]{1,0:T(8,128)(2,1)S(1)}, bf16[32,1792]{1,0:T(8,128)(2,1)S(1)}, u32[]{:S(2)}, u32[]{:S(2)}) %collective-permute-start.24) | collective-permute-done | bytes 114720 | tf_op jit(solution)/shard_map/ppermute | solution.py:452
  99.4 0.1 share.1
  99.5 2.5 %collective-permute-start.25 = (f32[8,1792]{1,0:T(8,128)S(1)}, f32[8,1792]{1,0:T(8,128)S(1)}, u32[]{:S(2)}, u32[]{:S(2)}) collective-permute-start(f32[8,1792]{1,0:T(8,128)S(1)} %get-tuple-element.62), channel_id=1, source_target_pairs={{0,32},{32,64},{64,96},{96,0},{1,33},{33,65},{65,97},{97,1},{2,34}... | collective-permute-start | bytes 172040 | tf_op jit(solution)/shard_map/ppermute | solution.py:456
  102.0 1.0 collective-permute-start.27
  103.0 1.2 %collective-permute-done.25.refs_1_ = f32[8,1792]{1,0:T(8,128)S(1)} collective-permute-done((f32[8,1792]{1,0:T(8,128)S(1)}, f32[8,1792]{1,0:T(8,128)S(1)}, u32[]{:S(2)}, u32[]{:S(2)}) %collective-permute-start.25) | collective-permute-done | bytes 57376 | tf_op jit(solution)/shard_map/ppermute | solution.py:456
  104.1 3.7 %collective-permute-done.26.refs_2_ = f32[8,1792]{1,0:T(8,128)S(1)} collective-permute-done((f32[8,1792]{1,0:T(8,128)S(1)}, f32[8,1792]{1,0:T(8,128)S(1)}, u32[]{:S(2)}, u32[]{:S(2)}) %collective-permute-start.26) | collective-permute-done | bytes 57376 | tf_op jit(solution)/shard_map/ppermute | solution.py:456
  107.8 0.2 collective-permute-done.27.refs_3_
  108.0 1.3 %place.1 = bf16[8,7168]{1,0:T(8,128)(2,1)} custom-call(s32[5]{0:T(128)S(1)} %stack.23.ids, f32[8,1792]{1,0:T(8,128)S(1)} %get-tuple-element.61.refs_0_, f32[8,1792]{1,0:T(8,128)S(1)} %collective-permute-done.25.refs_1_, f32[8,1792]{1,0:T(8,128)S(1)} %collective-permute-done.26.refs_2_, f32[8,1792]{1,0:T(8,128)S(1)} %collective-permute-done.27.refs_3_), custom_call_target="tpu_custom_call" | custom-call | tf_op jit(solution)/shard_map/place/pallas_call | solution.py:350
  (30 shorter events, 0.1 us)
Async XLA Ops:
  0.0 0.8 copy-start
  0.0 19.4 %copy-start.2 = (bf16[4,128,512]{2,1,0:T(8,128)(2,1)S(1)}, bf16[4,128,512]{2,1,0:T(8,128)(2,1)}, u32[]{:S(2)}) copy-start(bf16[4,128,512]{2,1,0:T(8,128)(2,1)} %refs_4_.3) | copy-start | bytes 1572868
  1.9 18.8 %collective-permute-start.3 = (bf16[576,512]{1,0:T(8,128)(2,1)S(1)}, bf16[576,512]{1,0:T(8,128)(2,1)S(1)}, u32[]{:S(2)}, u32[]{:S(2)}) collective-permute-start(bf16[576,512]{1,0:T(8,128)(2,1)S(1)} %pad_maximum_fusion.refs_0_), channel_id=1, source_target_pairs={{0,128},{128,0},{1,129},{129,1},{2,130},{130,2},{3,131},{131,3},{4... | collective-permute-start | bytes 1769480 | tf_op jit(solution)/shard_map/ppermute | solution.py:366
  3.6 17.1 %collective-permute-start.4 = (bf16[448,512]{1,0:T(8,128)(2,1)}, bf16[448,512]{1,0:T(8,128)(2,1)S(1)}, u32[]{:S(2)}, u32[]{:S(2)}) collective-permute-start(bf16[448,512]{1,0:T(8,128)(2,1)} %bitcast.18), channel_id=1, source_target_pairs={{0,2},{2,0},{1,3},{3,1},{4,6},{6,4},{5,7},{7,5},{8,10},{10,8},{9,1... | collective-permute-start | bytes 1376264 | tf_op jit(solution)/shard_map/ppermute | solution.py:366
  7.3 11.5 %collective-permute-start = (bf16[128,768]{1,0:T(8,128)(2,1)S(1)}, bf16[128,768]{1,0:T(8,128)(2,1)S(1)}, u32[]{:S(2)}, u32[]{:S(2)}) collective-permute-start(bf16[128,768]{1,0:T(8,128)(2,1)S(1)} %constant_dynamic-update-slice_fusion.refs_0_), channel_id=1, source_target_pairs={{32,0},{64,32},{96,64},{0,96},{33,1},{65,33},{97,65},{1,97},{34,2}... | collective-permute-start | bytes 589832 | tf_op jit(solution)/shard_map/ppermute | solution.py:362
  8.1 10.7 %collective-permute-start.1 = (bf16[128,768]{1,0:T(8,128)(2,1)S(1)}, bf16[128,768]{1,0:T(8,128)(2,1)S(1)}, u32[]{:S(2)}, u32[]{:S(2)}) collective-permute-start(bf16[128,768]{1,0:T(8,128)(2,1)S(1)} %constant_dynamic-update-slice_fusion.refs_0_), channel_id=1, source_target_pairs={{64,0},{96,32},{0,64},{32,96},{65,1},{97,33},{1,65},{33,97},{66,2}... | collective-permute-start | bytes 589832 | tf_op jit(solution)/shard_map/ppermute | solution.py:362
  9.2 10.2 %collective-permute-start.2 = (bf16[128,768]{1,0:T(8,128)(2,1)S(1)}, bf16[128,768]{1,0:T(8,128)(2,1)S(1)}, u32[]{:S(2)}, u32[]{:S(2)}) collective-permute-start(bf16[128,768]{1,0:T(8,128)(2,1)S(1)} %constant_dynamic-update-slice_fusion.refs_0_), channel_id=1, source_target_pairs={{96,0},{0,32},{32,64},{64,96},{97,1},{1,33},{33,65},{65,97},{98,2}... | collective-permute-start | bytes 589832 | tf_op jit(solution)/shard_map/ppermute | solution.py:362
  11.4 0.7 copy-start.6
  12.1 0.7 copy-start.7
  20.7 1.0 copy-start.3
  20.7 7.5 %copy-start.1 = (bf16[4,512,128]{2,1,0:T(8,128)(2,1)S(1)}, bf16[4,512,128]{2,1,0:T(8,128)(2,1)}, u32[]{:S(2)}) copy-start(bf16[4,512,128]{2,1,0:T(8,128)(2,1)} %refs_4_.5) | copy-start | bytes 1572868
  21.8 5.7 %collective-permute-start.6 = (bf16[2,448,512]{2,1,0:T(8,128)(2,1)S(1)}, bf16[2,448,512]{2,1,0:T(8,128)(2,1)S(1)}, u32[]{:S(2)}, u32[]{:S(2)}) collective-permute-start(bf16[2,448,512]{2,1,0:T(8,128)(2,1)S(1)} %pair.1.refs_4_), channel_id=1, source_target_pairs={{0,16},{16,0},{1,17},{17,1},{2,18},{18,2},{3,19},{19,3},{4,20},{20... | collective-permute-start | bytes 2752520 | tf_op jit(solution)/shard_map/ppermute | solution.py:366
  21.9 25.1 %collective-permute-start.17 = (bf16[2,448,512]{2,1,0:T(8,128)(2,1)S(1)}, bf16[2,448,512]{2,1,0:T(8,128)(2,1)S(1)}, u32[]{:S(2)}, u32[]{:S(2)}) collective-permute-start(bf16[2,448,512]{2,1,0:T(8,128)(2,1)S(1)} %pair.1.refs_4_), channel_id=1, source_target_pairs={{0,128},{1,129},{128,0},{129,1},{2,130},{3,131},{130,2},{131,3},{4... | collective-permute-start | bytes 2752520 | tf_op jit(solution)/shard_map/ppermute | solution.py:366
  22.4 24.6 %collective-permute-start.18 = (bf16[2,448,512]{2,1,0:T(8,128)(2,1)S(1)}, bf16[2,448,512]{2,1,0:T(8,128)(2,1)S(1)}, u32[]{:S(2)}, u32[]{:S(2)}) collective-permute-start(bf16[2,448,512]{2,1,0:T(8,128)(2,1)S(1)} %pair.1.refs_4_), channel_id=1, source_target_pairs={{0,129},{1,128},{128,1},{129,0},{2,131},{3,130},{130,3},{131,2},{4... | collective-permute-start | bytes 2752520 | tf_op jit(solution)/shard_map/ppermute | solution.py:366
  25.4 2.0 %collective-permute-start.5 = (bf16[576,512]{1,0:T(8,128)(2,1)S(1)}, bf16[576,512]{1,0:T(8,128)(2,1)S(1)}, u32[]{:S(2)}, u32[]{:S(2)}) collective-permute-start(bf16[576,512]{1,0:T(8,128)(2,1)S(1)} %get-tuple-element.39.refs_0_), channel_id=1, source_target_pairs={{0,16},{16,0},{1,17},{17,1},{2,18},{18,2},{3,19},{19,3},{4,20},{20... | collective-permute-start | bytes 1769480 | tf_op jit(solution)/shard_map/ppermute | solution.py:366
  25.4 2.8 %collective-permute-start.7 = (bf16[576,512]{1,0:T(8,128)(2,1)S(1)}, bf16[576,512]{1,0:T(8,128)(2,1)S(1)}, u32[]{:S(2)}, u32[]{:S(2)}) collective-permute-start(bf16[576,512]{1,0:T(8,128)(2,1)S(1)} %get-tuple-element.40.refs_1_), channel_id=1, source_target_pairs={{0,16},{16,0},{1,17},{17,1},{2,18},{18,2},{3,19},{19,3},{4,20},{20... | collective-permute-start | bytes 1769480 | tf_op jit(solution)/shard_map/ppermute | solution.py:366
  28.3 15.0 %copy-start.4 = (bf16[128,512]{1,0:T(8,128)(2,1)S(1)}, bf16[128,512]{1,0:T(8,128)(2,1)}, u32[]{:S(2)}) copy-start(bf16[128,512]{1,0:T(8,128)(2,1)} %refs_5_.1) | copy-start | bytes 393220
  28.3 15.0 %copy-start.5 = (bf16[1,64,128]{2,1,0:T(8,128)(2,1)S(1)}, bf16[1,64,128]{2,1,0:T(8,128)(2,1)}, u32[]{:S(2)}) copy-start(bf16[1,64,128]{2,1,0:T(8,128)(2,1)} %param.14) | copy-start | bytes 49156
  36.2 10.9 %collective-permute-start.10 = (bf16[128,640]{1,0:T(8,128)(2,1)S(1)}, bf16[128,640]{1,0:T(8,128)(2,1)S(1)}, u32[]{:S(2)}, u32[]{:S(2)}) collective-permute-start(bf16[128,640]{1,0:T(8,128)(2,1)S(1)} %get-tuple-element.45), channel_id=1, source_target_pairs={{0,96},{32,0},{64,32},{96,64},{1,97},{33,1},{65,33},{97,65},{2,98}... | collective-permute-start | bytes 491528 | tf_op jit(solution)/shard_map/ppermute | solution.py:424
  40.2 7.1 %collective-permute-start.8 = (bf16[128,640]{1,0:T(8,128)(2,1)S(1)}, bf16[128,640]{1,0:T(8,128)(2,1)S(1)}, u32[]{:S(2)}, u32[]{:S(2)}) collective-permute-start(bf16[128,640]{1,0:T(8,128)(2,1)S(1)} %get-tuple-element.43), channel_id=1, source_target_pairs={{0,32},{32,64},{64,96},{96,0},{1,33},{33,65},{65,97},{97,1},{2,34}... | collective-permute-start | bytes 491528 | tf_op jit(solution)/shard_map/ppermute | solution.py:424
  40.8 8.6 %collective-permute-start.9 = (bf16[128,640]{1,0:T(8,128)(2,1)S(1)}, bf16[128,640]{1,0:T(8,128)(2,1)S(1)}, u32[]{:S(2)}, u32[]{:S(2)}) collective-permute-start(bf16[128,640]{1,0:T(8,128)(2,1)S(1)} %get-tuple-element.44), channel_id=1, source_target_pairs={{0,64},{32,96},{64,0},{96,32},{1,65},{33,97},{65,1},{97,33},{2,66}... | collective-permute-start | bytes 491528 | tf_op jit(solution)/shard_map/ppermute | solution.py:424
  49.4 14.0 %collective-permute-start.19 = (bf16[448,512]{1,0:T(8,128)(2,1)S(1)}, bf16[448,512]{1,0:T(8,128)(2,1)S(1)}, u32[]{:S(2)}, u32[]{:S(2)}) collective-permute-start(bf16[448,512]{1,0:T(8,128)(2,1)S(1)} %slice_bitcast_fusion.1), channel_id=1, source_target_pairs={{0,128},{1,129},{128,0},{129,1},{2,130},{3,131},{130,2},{131,3},{4... | collective-permute-start | bytes 1376264 | tf_op jit(solution)/shard_map/ppermute | solution.py:366
  50.3 15.2 %collective-permute-start.20 = (bf16[448,512]{1,0:T(8,128)(2,1)S(1)}, bf16[448,512]{1,0:T(8,128)(2,1)S(1)}, u32[]{:S(2)}, u32[]{:S(2)}) collective-permute-start(bf16[448,512]{1,0:T(8,128)(2,1)S(1)} %slice_bitcast_fusion), channel_id=1, source_target_pairs={{0,129},{1,128},{128,1},{129,0},{2,131},{3,130},{130,3},{131,2},{4... | collective-permute-start | bytes 1376264 | tf_op jit(solution)/shard_map/ppermute | solution.py:366
  51.9 11.5 %collective-permute-start.11 = (bf16[32,512]{1,0:T(8,128)(2,1)S(1)}, bf16[32,512]{1,0:T(8,128)(2,1)S(1)}, u32[]{:S(2)}, u32[]{:S(2)}) collective-permute-start(bf16[32,512]{1,0:T(8,128)(2,1)S(1)} %get-tuple-element.47), channel_id=1, source_target_pairs={{0,1},{1,0},{2,3},{3,2},{4,5},{5,4},{6,7},{7,6},{8,9},{9,8},{10,11... | collective-permute-start | bytes 98312 | tf_op jit(solution)/shard_map/ppermute | solution.py:366
  54.9 8.5 %collective-permute-start.12 = (bf16[32,512]{1,0:T(8,128)(2,1)S(1)}, bf16[32,512]{1,0:T(8,128)(2,1)S(1)}, u32[]{:S(2)}, u32[]{:S(2)}) collective-permute-start(bf16[32,512]{1,0:T(8,128)(2,1)S(1)} %get-tuple-element.48), channel_id=1, source_target_pairs={{0,2},{1,3},{2,0},{3,1},{4,6},{5,7},{6,4},{7,5},{8,10},{9,11},{10,... | collective-permute-start | bytes 98312 | tf_op jit(solution)/shard_map/ppermute | solution.py:366
  55.1 8.2 %collective-permute-start.13 = (bf16[32,512]{1,0:T(8,128)(2,1)S(1)}, bf16[32,512]{1,0:T(8,128)(2,1)S(1)}, u32[]{:S(2)}, u32[]{:S(2)}) collective-permute-start(bf16[32,512]{1,0:T(8,128)(2,1)S(1)} %get-tuple-element.49), channel_id=1, source_target_pairs={{0,3},{1,2},{2,1},{3,0},{4,7},{5,6},{6,5},{7,4},{8,11},{9,10},{10,... | collective-permute-start | bytes 98312 | tf_op jit(solution)/shard_map/ppermute | solution.py:366
  65.7 12.3 %collective-permute-start.21 = (bf16[6,448,512]{2,1,0:T(8,128)(2,1)S(1)}, bf16[6,448,512]{2,1,0:T(8,128)(2,1)S(1)}, u32[]{:S(2)}, u32[]{:S(2)}) collective-permute-start(bf16[6,448,512]{2,1,0:T(8,128)(2,1)S(1)} %rest.1.refs_5_), channel_id=1, source_target_pairs={{0,16},{16,0},{1,17},{17,1},{2,18},{18,2},{3,19},{19,3},{4,20},{20... | collective-permute-start | bytes 8257544 | tf_op jit(solution)/shard_map/ppermute | solution.py:366
  66.5 7.5 %collective-permute-start.14 = (bf16[32,2048]{1,0:T(8,128)(2,1)S(1)}, bf16[32,2048]{1,0:T(8,128)(2,1)S(1)}, u32[]{:S(2)}, u32[]{:S(2)}) collective-permute-start(bf16[32,2048]{1,0:T(8,128)(2,1)S(1)} %join.1.refs_4_.refs_0_), channel_id=1, source_target_pairs={{32,0},{64,32},{96,64},{0,96},{33,1},{65,33},{97,65},{1,97},{34,2}... | collective-permute-start | bytes 393224 | tf_op jit(solution)/shard_map/ppermute | solution.py:362
  67.3 10.7 %collective-permute-start.15 = (bf16[32,2048]{1,0:T(8,128)(2,1)S(1)}, bf16[32,2048]{1,0:T(8,128)(2,1)S(1)}, u32[]{:S(2)}, u32[]{:S(2)}) collective-permute-start(bf16[32,2048]{1,0:T(8,128)(2,1)S(1)} %join.1.refs_4_.refs_0_), channel_id=1, source_target_pairs={{64,0},{96,32},{0,64},{32,96},{65,1},{97,33},{1,65},{33,97},{66,2}... | collective-permute-start | bytes 393224 | tf_op jit(solution)/shard_map/ppermute | solution.py:362
  71.4 6.6 %collective-permute-start.16 = (bf16[32,2048]{1,0:T(8,128)(2,1)S(1)}, bf16[32,2048]{1,0:T(8,128)(2,1)S(1)}, u32[]{:S(2)}, u32[]{:S(2)}) collective-permute-start(bf16[32,2048]{1,0:T(8,128)(2,1)S(1)} %join.1.refs_4_.refs_0_), channel_id=1, source_target_pairs={{96,0},{0,32},{32,64},{64,96},{97,1},{1,33},{33,65},{65,97},{98,2}... | collective-permute-start | bytes 393224 | tf_op jit(solution)/shard_map/ppermute | solution.py:362
  80.9 10.5 %collective-permute-start.22 = (bf16[32,1792]{1,0:T(8,128)(2,1)S(1)}, bf16[32,1792]{1,0:T(8,128)(2,1)S(1)}, u32[]{:S(2)}, u32[]{:S(2)}) collective-permute-start(bf16[32,1792]{1,0:T(8,128)(2,1)S(1)} %get-tuple-element.58), channel_id=1, source_target_pairs={{0,4},{4,8},{8,12},{12,0},{1,5},{5,9},{9,13},{13,1},{2,6},{6,10},{... | collective-permute-start | bytes 344072 | tf_op jit(solution)/shard_map/ppermute | solution.py:452
  84.3 12.0 %collective-permute-start.23 = (bf16[32,1792]{1,0:T(8,128)(2,1)S(1)}, bf16[32,1792]{1,0:T(8,128)(2,1)S(1)}, u32[]{:S(2)}, u32[]{:S(2)}) collective-permute-start(bf16[32,1792]{1,0:T(8,128)(2,1)S(1)} %get-tuple-element.59), channel_id=1, source_target_pairs={{0,8},{4,12},{8,0},{12,4},{1,9},{5,13},{9,1},{13,5},{2,10},{6,14},... | collective-permute-start | bytes 344072 | tf_op jit(solution)/shard_map/ppermute | solution.py:452
  88.8 10.6 %collective-permute-start.24 = (bf16[32,1792]{1,0:T(8,128)(2,1)S(1)}, bf16[32,1792]{1,0:T(8,128)(2,1)S(1)}, u32[]{:S(2)}, u32[]{:S(2)}) collective-permute-start(bf16[32,1792]{1,0:T(8,128)(2,1)S(1)} %get-tuple-element.60), channel_id=1, source_target_pairs={{0,12},{4,0},{8,4},{12,8},{1,13},{5,1},{9,5},{13,9},{2,14},{6,2},{... | collective-permute-start | bytes 344072 | tf_op jit(solution)/shard_map/ppermute | solution.py:452
  99.5 4.6 %collective-permute-start.25 = (f32[8,1792]{1,0:T(8,128)S(1)}, f32[8,1792]{1,0:T(8,128)S(1)}, u32[]{:S(2)}, u32[]{:S(2)}) collective-permute-start(f32[8,1792]{1,0:T(8,128)S(1)} %get-tuple-element.62), channel_id=1, source_target_pairs={{0,32},{32,64},{64,96},{96,0},{1,33},{33,65},{65,97},{97,1},{2,34}... | collective-permute-start | bytes 172040 | tf_op jit(solution)/shard_map/ppermute | solution.py:456
  102.0 5.8 %collective-permute-start.26 = (f32[8,1792]{1,0:T(8,128)S(1)}, f32[8,1792]{1,0:T(8,128)S(1)}, u32[]{:S(2)}, u32[]{:S(2)}) collective-permute-start(f32[8,1792]{1,0:T(8,128)S(1)} %get-tuple-element.63), channel_id=1, source_target_pairs={{0,64},{32,96},{64,0},{96,32},{1,65},{33,97},{65,1},{97,33},{2,66}... | collective-permute-start | bytes 172040 | tf_op jit(solution)/shard_map/ppermute | solution.py:456
  102.0 6.0 %collective-permute-start.27 = (f32[8,1792]{1,0:T(8,128)S(1)}, f32[8,1792]{1,0:T(8,128)S(1)}, u32[]{:S(2)}, u32[]{:S(2)}) collective-permute-start(f32[8,1792]{1,0:T(8,128)S(1)} %get-tuple-element.64), channel_id=1, source_target_pairs={{0,96},{32,0},{64,32},{96,64},{1,97},{33,1},{65,33},{97,65},{2,98}... | collective-permute-start | bytes 172040 | tf_op jit(solution)/shard_map/ppermute | solution.py:456

commit v7 on v6

--- a/solution.py
+++ b/solution.py
@@ -95,54 +95,12 @@
         return got
 
     pools = take(4)
-    (weight,) = take(1)
+    (w_uv,) = take(1)
     new_latent, new_rope = take(2) if own else (None, None)
     outs = take(count)
-    w_uv, keys, rots, sems, weight_sem, acc, top, tot, latents, levels = refs
-    load = pltpu.make_async_copy(weight, w_uv, weight_sem)
-
-    def fetch(s, src, i, at):
-        chunk, part = at // STEP, pl.multiple_of((at % STEP) * BLOCK, BLOCK)
-        return (
-            pltpu.make_async_copy(
-                src.at[pl.ds(pl.multiple_of(i * BLOCK, BLOCK), BLOCK), :],
-                keys.at[s, chunk, pl.ds(part, BLOCK), :],
-                sems.at[s, at, 0],
-            ),
-            pltpu.make_async_copy(
-                src.at[pl.ds(4 * BLOCK, ROPE), pl.ds(pl.multiple_of(i * BLOCK, BLOCK), BLOCK)],
-                rots.at[s, chunk, :, pl.ds(part, BLOCK)],
-                sems.at[s, at, 1],
-            ),
-        )
-
-    for s, slot in enumerate(slots):
-
-        def bring(at, carry):
-            code = lists[slot * 16 + at]
-            for j in range(4):
-
-                @pl.when((code >> 2) == j)
-                def _():
-                    for copy in fetch(s, pools[j], code & 3, at):
-                        copy.start()
-
-            return carry
-
-        lax.fori_loop(0, counts[slot], bring, 0)
-        if s == 0:
-            load.start()
-
-    for s, slot in enumerate(slots):
-        found = counts[slot]
-        for extra in range(STEP):
-            at = found + extra
-
-            @pl.when(at < jnp.maximum((found + STEP - 1) // STEP, 1) * STEP)
-            def _():
-                part = pl.multiple_of((at % STEP) * BLOCK, BLOCK)
-                keys[s, at // STEP, pl.ds(part, BLOCK), :] = jnp.zeros((BLOCK, LAT), jnp.bfloat16)
-                rots[s, at // STEP, :, pl.ds(part, BLOCK)] = jnp.zeros((ROPE, BLOCK), jnp.bfloat16)
+    keys, rots, acc, top, tot, latents, levels = refs
+    keys[...] = jnp.zeros_like(keys)
+    rots[...] = jnp.zeros_like(rots)
 
     def wide(value, times):
         return jnp.concatenate([value] * times, axis=1)
@@ -155,15 +113,19 @@
         tot[...] = sum(weight[:, i * 128 : (i + 1) * 128] for i in range(times))
         acc[...] = dot_nn(weight.astype(jnp.bfloat16), latent)
 
-    def scores(s, found, valid, q, r, chunk):
+    def scores(slot, found, valid, q, r, chunk):
         for b in range(STEP):
-
-            @pl.when(chunk * STEP + b < found)
-            def _():
-                for copy in fetch(s, pools[0], 0, chunk * STEP + b):
-                    copy.wait()
-
-        score = dot_nt(q, keys[s, chunk]) + dot_nn(r, rots[s, chunk])
+            part = slice(b * BLOCK, (b + 1) * BLOCK)
+            code = lists[slot * 16 + chunk * STEP + b]
+            first = pl.multiple_of((code & 3) * BLOCK, BLOCK)
+            for j in range(4):
+
+                @pl.when(jnp.logical_and(chunk * STEP + b < found, (code >> 2) == j))
+                def _():
+                    keys[part, :] = pools[j][pl.ds(first, BLOCK), :]
+                    rots[:, part] = pools[j][4 * BLOCK :, pl.ds(first, BLOCK)]
+
+        score = dot_nt(q, keys[...]) + dot_nn(r, rots[...])
         seen = lax.broadcasted_iota(jnp.int32, score.shape, 1) < valid - chunk * STEP * BLOCK
         return jnp.where(seen, score, LOW)
 
@@ -177,17 +139,17 @@
             seen = lax.broadcasted_iota(jnp.int32, score.shape, 1) <= at
             begin(jnp.where(seen, score, LOW), new_latent[...])
         else:
-            begin(scores(s, found, valid, q, r, 0), keys[s, 0])
+            begin(scores(slot, found, valid, q, r, 0), keys[...])
 
         def step(chunk, inner):
-            score = scores(s, found, valid, q_lat[slot], q_rot[slot], chunk)
+            score = scores(slot, found, valid, q_lat[slot], q_rot[slot], chunk)
             before = top[...]
             best = jnp.maximum(before, jnp.max(score, axis=1, keepdims=True))
             keep = jnp.exp2((before - best) * SCALE2)
             weight = jnp.exp2((score - wide(best, STEP)) * SCALE2)
             top[...] = best
             tot[...] = tot[...] * keep + sum(weight[:, i * 128 : (i + 1) * 128] for i in range(STEP))
-            acc[...] = acc[...] * wide(keep, 4) + dot_nn(weight.astype(jnp.bfloat16), keys[s, chunk])
+            acc[...] = acc[...] * wide(keep, 4) + dot_nn(weight.astype(jnp.bfloat16), keys[...])
             return inner
 
         lax.fori_loop(0 if own else 1, (found + STEP - 1) // STEP, step, 0)
@@ -198,7 +160,6 @@
         return carry
 
     lax.fori_loop(0, count, one_slot, 0)
-    load.wait()
     lane = lax.broadcasted_iota(jnp.int32, (TOK, 128), 1)
     for h in range(HEADS):
         rows = slice(h * TOK, (h + 1) * TOK)
@@ -221,22 +182,14 @@
     count = len(slots)
     full = pl.BlockSpec(memory_space=VMEM)
     scalar = pl.BlockSpec(memory_space=SMEM)
-    chunks = 16 // STEP
     return pl.pallas_call(
         functools.partial(attention_kernel, slots, own),
         out_shape=[jax.ShapeDtypeStruct((TOK, MSG), jnp.bfloat16)] * count,
-        in_specs=[scalar] * 2
-        + [full] * 2
-        + [pl.BlockSpec(memory_space=pl.ANY)] * 4
-        + [pl.BlockSpec(memory_space=pltpu.HBM)]
-        + [full] * (2 if own else 0),
+        in_specs=[scalar] * 2 + [full] * (9 if own else 7),
         out_specs=[full] * count,
         scratch_shapes=[
-            pltpu.VMEM((HEADS, LAT, VD), jnp.bfloat16),
-            pltpu.VMEM((count, chunks, STEP * BLOCK, LAT), jnp.bfloat16),
-            pltpu.VMEM((count, chunks, ROPE, STEP * BLOCK), jnp.bfloat16),
-            pltpu.SemaphoreType.DMA((count, 16, 2)),
-            pltpu.SemaphoreType.DMA,
+            pltpu.VMEM((STEP * BLOCK, LAT), jnp.bfloat16),
+            pltpu.VMEM((ROPE, STEP * BLOCK), jnp.bfloat16),
             pltpu.VMEM((ROWS, LAT), jnp.float32),
             pltpu.VMEM((ROWS, 128), jnp.float32),
             pltpu.VMEM((ROWS, 128), jnp.float32),
@@ -398,6 +351,7 @@
     pool_y = flip(pool, "yl", 2, 1)
     weight_z = flip(weight, "z0", 2, 1)
     lists, counts = plan(ids, block_table, prefix_len)
+    pool, pool_y, counts, weight_z = tie([pool, pool_y, counts, weight_z], queries[1:])
     q_lat, q_rot = simple(
         prepare_kernel,
         "prepare",
@@ -407,7 +361,6 @@
         ],
         [counts, *queries, w_uk],
     )
-    pool, pool_y, weight_z = tie([pool, pool_y, weight_z], [q_lat])
     pool_k = flip(pool, "k", 2, 1)
     pool_yk = flip(pool_y, "k", 2, 1)
     pair = simple(

time: 110 us -> 104 us (0.945)
  waiting for transfers between devices: 37 us -> 32.2 us
    ppermute x13, waiting for transfers between devices: 10.8 us -> 7.35 us  [flip(): return lax.ppermute(value, axis, [(i, i ^ bits) for i in range(size)])]
  transfers between devices with their start and end apart: 28 -> 28, of which waited for: 15 -> 13; matrix products, arithmetic and copies ran while one was open for 2% -> 2% of each run, Pallas kernels for 15% -> 16%
where the time goes in v7:
time: 104 us; the launch traced here: 103 us
  starting transfers between devices  44.6 us (43%)
  waiting for transfers between devices  32.2 us (31%)
  Pallas kernels  20.7 us (20%)
  local copies, waits for them, and re-layouts  4.12 us (4%)
  other arithmetic  1.08 us (1%)
    ppermute x13, starting transfers between devices, flip(): return lax.ppermute(value, axis, [(i, i ^ bits) for i in range(size)])  14.7 us
    pallas_call x2, Pallas kernels, attention(): pl.pallas_call(functools.partial(attention_kernel, slots, own), out_shape...  11.1 us
    ppermute x6, waiting for transfers between devices, turn(): lax.ppermute(value, axis, [((i + shift) % size, i) for i in range(size)])  10.6 us
    ppermute x3, starting transfers between devices, local(): lax.ppermute(partial[d], 'zb', [(i, (i + d) % 4) for i in range(4)])  10.5 us
    ppermute x6, starting transfers between devices, turn(): lax.ppermute(value, axis, [((i + shift) % size, i) for i in range(size)])  9.19 us
    ppermute x3, waiting for transfers between devices, local(): lax.ppermute(partial[d], 'zb', [(i, (i + d) % 4) for i in range(4)])  7.97 us
    ppermute x13, waiting for transfers between devices, flip(): return lax.ppermute(value, axis, [(i, i ^ bits) for i in range(size)])  7.35 us
    pallas_call x8, Pallas kernels, simple(): pl.pallas_call(kernel, out_shape=out_shape, in_specs=[pl.BlockSpec(memory...  6.92 us
  transfers between devices with their start and end apart: 28, of which 13 were waited for; matrix products, arithmetic and copies ran while one was open for 2% of the time, Pallas kernels for 16%

profile of v7, /device:TPU:6, one launch (start us, length us, event | category | flops | bytes accessed | tf_op | source)
XLA Modules:
  0.0 103.0 jit_solution(3761110230444705602)
XLA Ops:
  0.0 0.8 copy-done
  0.9 1.1 %pad_maximum_fusion.refs_0_ = bf16[576,512]{1,0:T(8,128)(2,1)S(1)} fusion(bf16[64,512]{1,0:T(8,128)(2,1)S(1)} %copy_bitcast_fusion, bf16[512,512]{1,0:T(8,128)(2,1)} %bitcast.21), kind=kLoop, calls=%fused_computation | loop fusion | flops 1179648 | bytes 1179648 | tf_op jit(solution)/shard_map/concatenate | solution.py:345
  1.9 1.7 %collective-permute-start = (bf16[576,512]{1,0:T(8,128)(2,1)S(1)}, bf16[576,512]{1,0:T(8,128)(2,1)S(1)}, u32[]{:S(2)}, u32[]{:S(2)}) collective-permute-start(bf16[576,512]{1,0:T(8,128)(2,1)S(1)} %pad_maximum_fusion.refs_0_), channel_id=1, source_target_pairs={{0,128},{128,0},{1,129},{129,1},{2,130},{130,2},{3,131},{131,3},{4... | collective-permute-start | bytes 1769480 | tf_op jit(solution)/shard_map/ppermute | solution.py:319
  3.6 1.9 %collective-permute-start.1 = (bf16[448,512]{1,0:T(8,128)(2,1)}, bf16[448,512]{1,0:T(8,128)(2,1)S(1)}, u32[]{:S(2)}, u32[]{:S(2)}) collective-permute-start(bf16[448,512]{1,0:T(8,128)(2,1)} %bitcast.18), channel_id=1, source_target_pairs={{0,2},{2,0},{1,3},{3,1},{4,6},{6,4},{5,7},{7,5},{8,10},{10,8},{9,1... | collective-permute-start | bytes 1376264 | tf_op jit(solution)/shard_map/ppermute | solution.py:319
  5.5 0.9 constant_dynamic-update-slice_fusion.1
  6.4 0.8 constant_dynamic-update-slice_fusion.refs_0_
  7.3 0.8 collective-permute-start.2
  8.1 1.1 %collective-permute-start.3 = (bf16[128,768]{1,0:T(8,128)(2,1)S(1)}, bf16[128,768]{1,0:T(8,128)(2,1)S(1)}, u32[]{:S(2)}, u32[]{:S(2)}) collective-permute-start(bf16[128,768]{1,0:T(8,128)(2,1)S(1)} %constant_dynamic-update-slice_fusion.refs_0_), channel_id=1, source_target_pairs={{64,0},{96,32},{0,64},{32,96},{65,1},{97,33},{1,65},{33,97},{66,2}... | collective-permute-start | bytes 589832 | tf_op jit(solution)/shard_map/ppermute | solution.py:315
  9.2 2.1 %collective-permute-start.4 = (bf16[128,768]{1,0:T(8,128)(2,1)S(1)}, bf16[128,768]{1,0:T(8,128)(2,1)S(1)}, u32[]{:S(2)}, u32[]{:S(2)}) collective-permute-start(bf16[128,768]{1,0:T(8,128)(2,1)S(1)} %constant_dynamic-update-slice_fusion.refs_0_), channel_id=1, source_target_pairs={{96,0},{0,32},{32,64},{64,96},{97,1},{1,33},{33,65},{65,97},{98,2}... | collective-permute-start | bytes 589832 | tf_op jit(solution)/shard_map/ppermute | solution.py:315
  11.3 0.1 stack.23.ids
  11.4 0.7 copy-done.6
  12.1 0.7 copy-done.7
  12.8 2.7 %plan.1 = (s32[64]{0:T(128)S(1)}, s32[8]{0:T(128)S(1)}) custom-call(s32[5]{0:T(128)S(1)} %stack.23.ids, s32[16,32]{1,0:T(8,128)S(1)} %copy-done.6, s32[16]{0:T(128)S(1)} %copy-done.7), custom_call_target="tpu_custom_call" | custom-call | tf_op jit(solution)/shard_map/plan/pallas_call | solution.py:65
  15.5 3.3 %collective-permute-done.2.refs_4_.refs_1_ = bf16[128,768]{1,0:T(8,128)(2,1)S(1)} collective-permute-done((bf16[128,768]{1,0:T(8,128)(2,1)S(1)}, bf16[128,768]{1,0:T(8,128)(2,1)S(1)}, u32[]{:S(2)}, u32[]{:S(2)}) %collective-permute-start.2) | collective-permute-done | bytes 196640 | tf_op jit(solution)/shard_map/ppermute | solution.py:315
  18.8 0.0 collective-permute-done.3.refs_5_.refs_2_
  18.8 0.6 collective-permute-done.4.refs_6_.refs_3_
  19.4 0.0 copy-start.1
  19.4 0.1 pair.1.refs_4_
  19.5 0.1 collective-permute-start.6
  19.6 0.5 collective-permute-start.17
  20.1 3.0 %collective-permute-start.18 = (bf16[2,448,512]{2,1,0:T(8,128)(2,1)S(1)}, bf16[2,448,512]{2,1,0:T(8,128)(2,1)S(1)}, u32[]{:S(2)}, u32[]{:S(2)}) collective-permute-start(bf16[2,448,512]{2,1,0:T(8,128)(2,1)S(1)} %pair.1.refs_4_), channel_id=1, source_target_pairs={{0,129},{1,128},{128,1},{129,0},{2,131},{3,130},{130,3},{131,2},{4... | collective-permute-start | bytes 2752520 | tf_op jit(solution)/shard_map/ppermute | solution.py:319
  23.2 0.5 collective-permute-start.7
  23.7 1.3 %prepare.1 = (bf16[4,512,512]{2,1,0:T(8,128)(2,1)S(1)}, bf16[4,512,64]{2,1,0:T(8,128)(2,1)S(1)}) custom-call(s32[8]{0:T(128)S(1)} %get-tuple-element.38.counts, bf16[128,768]{1,0:T(8,128)(2,1)S(1)} %constant_dynamic-update-slice_fusion.refs_0_, bf16[128,768]{1,0:T(8,128)(2,1)S(1)} %collective-permute-done.2.refs_4_.refs_1_, ...), custom_call_target="tpu_custom_call" | custom-call | tf_op jit(solution)/shard_map/prepare/pallas_call | solution.py:303
  25.0 0.2 collective-permute-done.5.refs_0_
  25.2 0.8 collective-permute-done.7.refs_3_
  26.0 7.2 %attend.3 = (bf16[128,640]{1,0:T(8,128)(2,1)S(1)}, bf16[128,640]{1,0:T(8,128)(2,1)S(1)}, bf16[128,640]{1,0:T(8,128)(2,1)S(1)}) custom-call(s32[64]{0:T(128)S(1)} %get-tuple-element.36.lists, s32[8]{0:T(128)S(1)} %get-tuple-element.38.counts, bf16[4,512,512]{2,1,0:T(8,128)(2,1)S(1)} %get-tuple-element.39.q_lat, ...), custom_call_target="tpu_custom_call" | custom-call | tf_op jit(solution)/shard_map/attend/pallas_call | solution.py:185
  33.2 2.0 %collective-permute-start.10 = (bf16[128,640]{1,0:T(8,128)(2,1)S(1)}, bf16[128,640]{1,0:T(8,128)(2,1)S(1)}, u32[]{:S(2)}, u32[]{:S(2)}) collective-permute-start(bf16[128,640]{1,0:T(8,128)(2,1)S(1)} %get-tuple-element.47), channel_id=1, source_target_pairs={{0,96},{32,0},{64,32},{96,64},{1,97},{33,1},{65,33},{97,65},{2,98}... | collective-permute-start | bytes 491528 | tf_op jit(solution)/shard_map/ppermute | solution.py:377
  35.2 1.3 %collective-permute-start.8 = (bf16[128,640]{1,0:T(8,128)(2,1)S(1)}, bf16[128,640]{1,0:T(8,128)(2,1)S(1)}, u32[]{:S(2)}, u32[]{:S(2)}) collective-permute-start(bf16[128,640]{1,0:T(8,128)(2,1)S(1)} %get-tuple-element.45), channel_id=1, source_target_pairs={{0,32},{32,64},{64,96},{96,0},{1,33},{33,65},{65,97},{97,1},{2,34}... | collective-permute-start | bytes 491528 | tf_op jit(solution)/shard_map/ppermute | solution.py:377
  36.6 3.5 %collective-permute-start.9 = (bf16[128,640]{1,0:T(8,128)(2,1)S(1)}, bf16[128,640]{1,0:T(8,128)(2,1)S(1)}, u32[]{:S(2)}, u32[]{:S(2)}) collective-permute-start(bf16[128,640]{1,0:T(8,128)(2,1)S(1)} %get-tuple-element.46), channel_id=1, source_target_pairs={{0,64},{32,96},{64,0},{96,32},{1,65},{33,97},{65,1},{97,33},{2,66}... | collective-permute-start | bytes 491528 | tf_op jit(solution)/shard_map/ppermute | solution.py:377
  40.0 3.9 %attend.2.refs_0_.refs_5_ = bf16[128,640]{1,0:T(8,128)(2,1)S(1)} custom-call(s32[64]{0:T(128)S(1)} %get-tuple-element.36.lists, s32[8]{0:T(128)S(1)} %get-tuple-element.38.counts, bf16[4,512,512]{2,1,0:T(8,128)(2,1)S(1)} %get-tuple-element.39.q_lat, bf16[4,512,64]{2,1,0:T(8,128)(2,1)S(1)} %get-tuple-element.40.q_rot, ...), custom_call_target="tpu_custom_call" | custom-call | tf_op jit(solution)/shard_map/attend/pallas_call | solution.py:185
  43.9 0.0 collective-permute-done.10.refs_3_.refs_4_
  43.9 0.0 collective-permute-done.8.refs_1_.refs_2_
  43.9 1.2 %collective-permute-done.9.refs_2_.refs_3_ = bf16[128,640]{1,0:T(8,128)(2,1)S(1)} collective-permute-done((bf16[128,640]{1,0:T(8,128)(2,1)S(1)}, bf16[128,640]{1,0:T(8,128)(2,1)S(1)}, u32[]{:S(2)}, u32[]{:S(2)}) %collective-permute-start.9) | collective-permute-done | bytes 163872 | tf_op jit(solution)/shard_map/ppermute | solution.py:377
  45.2 0.1 collective-permute-start.19
  45.3 1.7 %collective-permute-start.20 = (bf16[448,512]{1,0:T(8,128)(2,1)S(1)}, bf16[448,512]{1,0:T(8,128)(2,1)S(1)}, u32[]{:S(2)}, u32[]{:S(2)}) collective-permute-start(bf16[448,512]{1,0:T(8,128)(2,1)S(1)} %slice_bitcast_fusion), channel_id=1, source_target_pairs={{0,129},{1,128},{128,1},{129,0},{2,131},{3,130},{130,3},{131,2},{4... | collective-permute-start | bytes 1376264 | tf_op jit(solution)/shard_map/ppermute | solution.py:319
  47.1 1.1 %combine.1 = (bf16[32,512]{1,0:T(8,128)(2,1)S(1)}, bf16[32,512]{1,0:T(8,128)(2,1)S(1)}, bf16[32,512]{1,0:T(8,128)(2,1)S(1)}, bf16[32,512]{1,0:T(8,128)(2,1)S(1)}) custom-call(s32[5]{0:T(128)S(1)} %stack.23.ids, bf16[128,640]{1,0:T(8,128)(2,1)S(1)} %attend.2.refs_0_.refs_5_, bf16[128,640]{1,0:T(8,128)(2,1)S(1)} %collective-permute-done.8.refs_1_.refs_2_, ...), custom_call_target="tpu_custom_call" | custom-call | tf_op jit(solution)/shard_map/combine/pallas_call | solution.py:303
  48.1 2.5 %collective-permute-start.11 = (bf16[32,512]{1,0:T(8,128)(2,1)S(1)}, bf16[32,512]{1,0:T(8,128)(2,1)S(1)}, u32[]{:S(2)}, u32[]{:S(2)}) collective-permute-start(bf16[32,512]{1,0:T(8,128)(2,1)S(1)} %get-tuple-element.49), channel_id=1, source_target_pairs={{0,1},{1,0},{2,3},{3,2},{4,5},{5,4},{6,7},{7,6},{8,9},{9,8},{10,11... | collective-permute-start | bytes 98312 | tf_op jit(solution)/shard_map/ppermute | solution.py:319
  50.7 0.3 collective-permute-start.12
  51.0 2.3 %collective-permute-start.13 = (bf16[32,512]{1,0:T(8,128)(2,1)S(1)}, bf16[32,512]{1,0:T(8,128)(2,1)S(1)}, u32[]{:S(2)}, u32[]{:S(2)}) collective-permute-start(bf16[32,512]{1,0:T(8,128)(2,1)S(1)} %get-tuple-element.51), channel_id=1, source_target_pairs={{0,3},{1,2},{2,1},{3,0},{4,7},{5,6},{6,5},{7,4},{8,11},{9,10},{10,... | collective-permute-start | bytes 98312 | tf_op jit(solution)/shard_map/ppermute | solution.py:319
  53.2 6.3 %collective-permute-done.11.refs_1_ = bf16[32,512]{1,0:T(8,128)(2,1)S(1)} collective-permute-done((bf16[32,512]{1,0:T(8,128)(2,1)S(1)}, bf16[32,512]{1,0:T(8,128)(2,1)S(1)}, u32[]{:S(2)}, u32[]{:S(2)}) %collective-permute-start.11) | collective-permute-done | bytes 32800 | tf_op jit(solution)/shard_map/ppermute | solution.py:319
  59.5 0.0 collective-permute-done.12.refs_2_
  59.5 0.0 collective-permute-done.13.refs_3_
  59.5 0.0 collective-permute-done.19.refs_2_
  59.6 0.2 rest.1.refs_5_
  59.8 0.1 collective-permute-start.21
  59.9 1.4 %collective-permute-start.14 = (bf16[32,2048]{1,0:T(8,128)(2,1)S(1)}, bf16[32,2048]{1,0:T(8,128)(2,1)S(1)}, u32[]{:S(2)}, u32[]{:S(2)}) collective-permute-start(bf16[32,2048]{1,0:T(8,128)(2,1)S(1)} %join.1.refs_4_.refs_0_), channel_id=1, source_target_pairs={{32,0},{64,32},{96,64},{0,96},{33,1},{65,33},{97,65},{1,97},{34,2}... | collective-permute-start | bytes 393224 | tf_op jit(solution)/shard_map/ppermute | solution.py:315
  61.3 3.7 %collective-permute-start.15 = (bf16[32,2048]{1,0:T(8,128)(2,1)S(1)}, bf16[32,2048]{1,0:T(8,128)(2,1)S(1)}, u32[]{:S(2)}, u32[]{:S(2)}) collective-permute-start(bf16[32,2048]{1,0:T(8,128)(2,1)S(1)} %join.1.refs_4_.refs_0_), channel_id=1, source_target_pairs={{64,0},{96,32},{0,64},{32,96},{65,1},{97,33},{1,65},{33,97},{66,2}... | collective-permute-start | bytes 393224 | tf_op jit(solution)/shard_map/ppermute | solution.py:315
  65.0 0.0 collective-permute-start.16
  65.0 2.6 %collective-permute-done.14.refs_1_ = bf16[32,2048]{1,0:T(8,128)(2,1)S(1)} collective-permute-done((bf16[32,2048]{1,0:T(8,128)(2,1)S(1)}, bf16[32,2048]{1,0:T(8,128)(2,1)S(1)}, u32[]{:S(2)}, u32[]{:S(2)}) %collective-permute-start.14) | collective-permute-done | bytes 131104 | tf_op jit(solution)/shard_map/ppermute | solution.py:315
  67.6 4.0 %collective-permute-done.15.refs_2_ = bf16[32,2048]{1,0:T(8,128)(2,1)S(1)} collective-permute-done((bf16[32,2048]{1,0:T(8,128)(2,1)S(1)}, bf16[32,2048]{1,0:T(8,128)(2,1)S(1)}, u32[]{:S(2)}, u32[]{:S(2)}) %collective-permute-start.15) | collective-permute-done | bytes 131104 | tf_op jit(solution)/shard_map/ppermute | solution.py:315
  71.6 0.0 collective-permute-done.21.refs_7_
  71.6 3.0 %project.1 = (bf16[32,1792]{1,0:T(8,128)(2,1)S(1)}, bf16[32,1792]{1,0:T(8,128)(2,1)S(1)}, bf16[32,1792]{1,0:T(8,128)(2,1)S(1)}, bf16[32,1792]{1,0:T(8,128)(2,1)S(1)}) custom-call(s32[5]{0:T(128)S(1)} %stack.23.ids, bf16[32,2048]{1,0:T(8,128)(2,1)S(1)} %join.1.refs_4_.refs_0_, bf16[32,2048]{1,0:T(8,128)(2,1)S(1)} %collective-permute-done.14.refs_1_, ...), custom_call_target="tpu_custom_call" | custom-call | tf_op jit(solution)/shard_map/project/pallas_call | solution.py:303
  74.6 3.3 %collective-permute-start.22 = (bf16[32,1792]{1,0:T(8,128)(2,1)S(1)}, bf16[32,1792]{1,0:T(8,128)(2,1)S(1)}, u32[]{:S(2)}, u32[]{:S(2)}) collective-permute-start(bf16[32,1792]{1,0:T(8,128)(2,1)S(1)} %get-tuple-element.60), channel_id=1, source_target_pairs={{0,4},{4,8},{8,12},{12,0},{1,5},{5,9},{9,13},{13,1},{2,6},{6,10},{... | collective-permute-start | bytes 344072 | tf_op jit(solution)/shard_map/ppermute | solution.py:405
  77.9 4.5 %collective-permute-start.23 = (bf16[32,1792]{1,0:T(8,128)(2,1)S(1)}, bf16[32,1792]{1,0:T(8,128)(2,1)S(1)}, u32[]{:S(2)}, u32[]{:S(2)}) collective-permute-start(bf16[32,1792]{1,0:T(8,128)(2,1)S(1)} %get-tuple-element.61), channel_id=1, source_target_pairs={{0,8},{4,12},{8,0},{12,4},{1,9},{5,13},{9,1},{13,5},{2,10},{6,14},... | collective-permute-start | bytes 344072 | tf_op jit(solution)/shard_map/ppermute | solution.py:405
  82.4 2.7 %collective-permute-start.24 = (bf16[32,1792]{1,0:T(8,128)(2,1)S(1)}, bf16[32,1792]{1,0:T(8,128)(2,1)S(1)}, u32[]{:S(2)}, u32[]{:S(2)}) collective-permute-start(bf16[32,1792]{1,0:T(8,128)(2,1)S(1)} %get-tuple-element.62), channel_id=1, source_target_pairs={{0,12},{4,0},{8,4},{12,8},{1,13},{5,1},{9,5},{13,9},{2,14},{6,2},{... | collective-permute-start | bytes 344072 | tf_op jit(solution)/shard_map/ppermute | solution.py:405
  85.1 4.8 %collective-permute-done.23.refs_2_ = bf16[32,1792]{1,0:T(8,128)(2,1)S(1)} collective-permute-done((bf16[32,1792]{1,0:T(8,128)(2,1)S(1)}, bf16[32,1792]{1,0:T(8,128)(2,1)S(1)}, u32[]{:S(2)}, u32[]{:S(2)}) %collective-permute-start.23) | collective-permute-done | bytes 114720 | tf_op jit(solution)/shard_map/ppermute | solution.py:405
  89.9 3.1 %collective-permute-done.24.refs_3_ = bf16[32,1792]{1,0:T(8,128)(2,1)S(1)} collective-permute-done((bf16[32,1792]{1,0:T(8,128)(2,1)S(1)}, bf16[32,1792]{1,0:T(8,128)(2,1)S(1)}, u32[]{:S(2)}, u32[]{:S(2)}) %collective-permute-start.24) | collective-permute-done | bytes 114720 | tf_op jit(solution)/shard_map/ppermute | solution.py:405
  93.1 0.1 share.1
  93.1 2.5 %collective-permute-start.25 = (f32[8,1792]{1,0:T(8,128)S(1)}, f32[8,1792]{1,0:T(8,128)S(1)}, u32[]{:S(2)}, u32[]{:S(2)}) collective-permute-start(f32[8,1792]{1,0:T(8,128)S(1)} %get-tuple-element.64), channel_id=1, source_target_pairs={{0,32},{32,64},{64,96},{96,0},{1,33},{33,65},{65,97},{97,1},{2,34}... | collective-permute-start | bytes 172040 | tf_op jit(solution)/shard_map/ppermute | solution.py:409
  95.7 1.0 collective-permute-start.27
  96.6 1.2 %collective-permute-done.25.refs_1_ = f32[8,1792]{1,0:T(8,128)S(1)} collective-permute-done((f32[8,1792]{1,0:T(8,128)S(1)}, f32[8,1792]{1,0:T(8,128)S(1)}, u32[]{:S(2)}, u32[]{:S(2)}) %collective-permute-start.25) | collective-permute-done | bytes 57376 | tf_op jit(solution)/shard_map/ppermute | solution.py:409
  97.8 3.7 %collective-permute-done.26.refs_2_ = f32[8,1792]{1,0:T(8,128)S(1)} collective-permute-done((f32[8,1792]{1,0:T(8,128)S(1)}, f32[8,1792]{1,0:T(8,128)S(1)}, u32[]{:S(2)}, u32[]{:S(2)}) %collective-permute-start.26) | collective-permute-done | bytes 57376 | tf_op jit(solution)/shard_map/ppermute | solution.py:409
  101.4 0.2 collective-permute-done.27.refs_3_
  101.7 1.3 %place.1 = bf16[8,7168]{1,0:T(8,128)(2,1)} custom-call(s32[5]{0:T(128)S(1)} %stack.23.ids, f32[8,1792]{1,0:T(8,128)S(1)} %get-tuple-element.63.refs_0_, f32[8,1792]{1,0:T(8,128)S(1)} %collective-permute-done.25.refs_1_, f32[8,1792]{1,0:T(8,128)S(1)} %collective-permute-done.26.refs_2_, f32[8,1792]{1,0:T(8,128)S(1)} %collective-permute-done.27.refs_3_), custom_call_target="tpu_custom_call" | custom-call | tf_op jit(solution)/shard_map/place/pallas_call | solution.py:303
  (30 shorter events, 0.1 us)
Async XLA Ops:
  0.0 0.8 copy-start
  0.0 19.4 %copy-start.3 = (bf16[512,448]{0,1:T(8,128)(2,1)S(1)}, bf16[512,448]{0,1:T(8,128)(2,1)}, u32[]{:S(2)}) copy-start(bf16[512,448]{0,1:T(8,128)(2,1)} %param.21) | copy-start | bytes 1376260
  1.9 17.5 %collective-permute-start = (bf16[576,512]{1,0:T(8,128)(2,1)S(1)}, bf16[576,512]{1,0:T(8,128)(2,1)S(1)}, u32[]{:S(2)}, u32[]{:S(2)}) collective-permute-start(bf16[576,512]{1,0:T(8,128)(2,1)S(1)} %pad_maximum_fusion.refs_0_), channel_id=1, source_target_pairs={{0,128},{128,0},{1,129},{129,1},{2,130},{130,2},{3,131},{131,3},{4... | collective-permute-start | bytes 1769480 | tf_op jit(solution)/shard_map/ppermute | solution.py:319
  3.6 15.8 %collective-permute-start.1 = (bf16[448,512]{1,0:T(8,128)(2,1)}, bf16[448,512]{1,0:T(8,128)(2,1)S(1)}, u32[]{:S(2)}, u32[]{:S(2)}) collective-permute-start(bf16[448,512]{1,0:T(8,128)(2,1)} %bitcast.18), channel_id=1, source_target_pairs={{0,2},{2,0},{1,3},{3,1},{4,6},{6,4},{5,7},{7,5},{8,10},{10,8},{9,1... | collective-permute-start | bytes 1376264 | tf_op jit(solution)/shard_map/ppermute | solution.py:319
  7.3 16.4 %copy-start.2 = (bf16[4,128,512]{2,1,0:T(8,128)(2,1)S(1)}, bf16[4,128,512]{2,1,0:T(8,128)(2,1)}, u32[]{:S(2)}) copy-start(bf16[4,128,512]{2,1,0:T(8,128)(2,1)} %refs_4_.3) | copy-start | bytes 1572868
  7.3 11.5 %collective-permute-start.2 = (bf16[128,768]{1,0:T(8,128)(2,1)S(1)}, bf16[128,768]{1,0:T(8,128)(2,1)S(1)}, u32[]{:S(2)}, u32[]{:S(2)}) collective-permute-start(bf16[128,768]{1,0:T(8,128)(2,1)S(1)} %constant_dynamic-update-slice_fusion.refs_0_), channel_id=1, source_target_pairs={{32,0},{64,32},{96,64},{0,96},{33,1},{65,33},{97,65},{1,97},{34,2}... | collective-permute-start | bytes 589832 | tf_op jit(solution)/shard_map/ppermute | solution.py:315
  8.1 10.7 %collective-permute-start.3 = (bf16[128,768]{1,0:T(8,128)(2,1)S(1)}, bf16[128,768]{1,0:T(8,128)(2,1)S(1)}, u32[]{:S(2)}, u32[]{:S(2)}) collective-permute-start(bf16[128,768]{1,0:T(8,128)(2,1)S(1)} %constant_dynamic-update-slice_fusion.refs_0_), channel_id=1, source_target_pairs={{64,0},{96,32},{0,64},{32,96},{65,1},{97,33},{1,65},{33,97},{66,2}... | collective-permute-start | bytes 589832 | tf_op jit(solution)/shard_map/ppermute | solution.py:315
  9.2 10.2 %collective-permute-start.4 = (bf16[128,768]{1,0:T(8,128)(2,1)S(1)}, bf16[128,768]{1,0:T(8,128)(2,1)S(1)}, u32[]{:S(2)}, u32[]{:S(2)}) collective-permute-start(bf16[128,768]{1,0:T(8,128)(2,1)S(1)} %constant_dynamic-update-slice_fusion.refs_0_), channel_id=1, source_target_pairs={{96,0},{0,32},{32,64},{64,96},{97,1},{1,33},{33,65},{65,97},{98,2}... | collective-permute-start | bytes 589832 | tf_op jit(solution)/shard_map/ppermute | solution.py:315
  11.4 0.7 copy-start.6
  12.1 0.7 copy-start.7
  19.4 6.6 %copy-start.1 = (bf16[4,512,128]{2,1,0:T(8,128)(2,1)S(1)}, bf16[4,512,128]{2,1,0:T(8,128)(2,1)}, u32[]{:S(2)}) copy-start(bf16[4,512,128]{2,1,0:T(8,128)(2,1)} %refs_4_.5) | copy-start | bytes 1572868
  19.5 5.7 %collective-permute-start.6 = (bf16[2,448,512]{2,1,0:T(8,128)(2,1)S(1)}, bf16[2,448,512]{2,1,0:T(8,128)(2,1)S(1)}, u32[]{:S(2)}, u32[]{:S(2)}) collective-permute-start(bf16[2,448,512]{2,1,0:T(8,128)(2,1)S(1)} %pair.1.refs_4_), channel_id=1, source_target_pairs={{0,16},{16,0},{1,17},{17,1},{2,18},{18,2},{3,19},{19,3},{4,20},{20... | collective-permute-start | bytes 2752520 | tf_op jit(solution)/shard_map/ppermute | solution.py:319
  19.6 24.3 %collective-permute-start.17 = (bf16[2,448,512]{2,1,0:T(8,128)(2,1)S(1)}, bf16[2,448,512]{2,1,0:T(8,128)(2,1)S(1)}, u32[]{:S(2)}, u32[]{:S(2)}) collective-permute-start(bf16[2,448,512]{2,1,0:T(8,128)(2,1)S(1)} %pair.1.refs_4_), channel_id=1, source_target_pairs={{0,128},{1,129},{128,0},{129,1},{2,130},{3,131},{130,2},{131,3},{4... | collective-permute-start | bytes 2752520 | tf_op jit(solution)/shard_map/ppermute | solution.py:319
  20.1 23.8 %collective-permute-start.18 = (bf16[2,448,512]{2,1,0:T(8,128)(2,1)S(1)}, bf16[2,448,512]{2,1,0:T(8,128)(2,1)S(1)}, u32[]{:S(2)}, u32[]{:S(2)}) collective-permute-start(bf16[2,448,512]{2,1,0:T(8,128)(2,1)S(1)} %pair.1.refs_4_), channel_id=1, source_target_pairs={{0,129},{1,128},{128,1},{129,0},{2,131},{3,130},{130,3},{131,2},{4... | collective-permute-start | bytes 2752520 | tf_op jit(solution)/shard_map/ppermute | solution.py:319
  23.2 2.0 %collective-permute-start.5 = (bf16[576,512]{1,0:T(8,128)(2,1)S(1)}, bf16[576,512]{1,0:T(8,128)(2,1)S(1)}, u32[]{:S(2)}, u32[]{:S(2)}) collective-permute-start(bf16[576,512]{1,0:T(8,128)(2,1)S(1)} %get-tuple-element.41.refs_0_), channel_id=1, source_target_pairs={{0,16},{16,0},{1,17},{17,1},{2,18},{18,2},{3,19},{19,3},{4,20},{20... | collective-permute-start | bytes 1769480 | tf_op jit(solution)/shard_map/ppermute | solution.py:319
  23.2 2.8 %collective-permute-start.7 = (bf16[576,512]{1,0:T(8,128)(2,1)S(1)}, bf16[576,512]{1,0:T(8,128)(2,1)S(1)}, u32[]{:S(2)}, u32[]{:S(2)}) collective-permute-start(bf16[576,512]{1,0:T(8,128)(2,1)S(1)} %get-tuple-element.42.refs_1_), channel_id=1, source_target_pairs={{0,16},{16,0},{1,17},{17,1},{2,18},{18,2},{3,19},{19,3},{4,20},{20... | collective-permute-start | bytes 1769480 | tf_op jit(solution)/shard_map/ppermute | solution.py:319
  26.0 14.0 %copy-start.4 = (bf16[128,512]{1,0:T(8,128)(2,1)S(1)}, bf16[128,512]{1,0:T(8,128)(2,1)}, u32[]{:S(2)}) copy-start(bf16[128,512]{1,0:T(8,128)(2,1)} %refs_5_.1) | copy-start | bytes 393220
  26.0 14.0 %copy-start.5 = (bf16[1,64,128]{2,1,0:T(8,128)(2,1)S(1)}, bf16[1,64,128]{2,1,0:T(8,128)(2,1)}, u32[]{:S(2)}) copy-start(bf16[1,64,128]{2,1,0:T(8,128)(2,1)} %param.14) | copy-start | bytes 49156
  33.2 10.7 %collective-permute-start.10 = (bf16[128,640]{1,0:T(8,128)(2,1)S(1)}, bf16[128,640]{1,0:T(8,128)(2,1)S(1)}, u32[]{:S(2)}, u32[]{:S(2)}) collective-permute-start(bf16[128,640]{1,0:T(8,128)(2,1)S(1)} %get-tuple-element.47), channel_id=1, source_target_pairs={{0,96},{32,0},{64,32},{96,64},{1,97},{33,1},{65,33},{97,65},{2,98}... | collective-permute-start | bytes 491528 | tf_op jit(solution)/shard_map/ppermute | solution.py:377
  35.2 8.7 %collective-permute-start.8 = (bf16[128,640]{1,0:T(8,128)(2,1)S(1)}, bf16[128,640]{1,0:T(8,128)(2,1)S(1)}, u32[]{:S(2)}, u32[]{:S(2)}) collective-permute-start(bf16[128,640]{1,0:T(8,128)(2,1)S(1)} %get-tuple-element.45), channel_id=1, source_target_pairs={{0,32},{32,64},{64,96},{96,0},{1,33},{33,65},{65,97},{97,1},{2,34}... | collective-permute-start | bytes 491528 | tf_op jit(solution)/shard_map/ppermute | solution.py:377
  36.6 8.6 %collective-permute-start.9 = (bf16[128,640]{1,0:T(8,128)(2,1)S(1)}, bf16[128,640]{1,0:T(8,128)(2,1)S(1)}, u32[]{:S(2)}, u32[]{:S(2)}) collective-permute-start(bf16[128,640]{1,0:T(8,128)(2,1)S(1)} %get-tuple-element.46), channel_id=1, source_target_pairs={{0,64},{32,96},{64,0},{96,32},{1,65},{33,97},{65,1},{97,33},{2,66}... | collective-permute-start | bytes 491528 | tf_op jit(solution)/shard_map/ppermute | solution.py:377
  45.2 14.3 %collective-permute-start.19 = (bf16[448,512]{1,0:T(8,128)(2,1)S(1)}, bf16[448,512]{1,0:T(8,128)(2,1)S(1)}, u32[]{:S(2)}, u32[]{:S(2)}) collective-permute-start(bf16[448,512]{1,0:T(8,128)(2,1)S(1)} %slice_bitcast_fusion.1), channel_id=1, source_target_pairs={{0,128},{1,129},{128,0},{129,1},{2,130},{3,131},{130,2},{131,3},{4... | collective-permute-start | bytes 1376264 | tf_op jit(solution)/shard_map/ppermute | solution.py:319
  45.3 14.2 %collective-permute-start.20 = (bf16[448,512]{1,0:T(8,128)(2,1)S(1)}, bf16[448,512]{1,0:T(8,128)(2,1)S(1)}, u32[]{:S(2)}, u32[]{:S(2)}) collective-permute-start(bf16[448,512]{1,0:T(8,128)(2,1)S(1)} %slice_bitcast_fusion), channel_id=1, source_target_pairs={{0,129},{1,128},{128,1},{129,0},{2,131},{3,130},{130,3},{131,2},{4... | collective-permute-start | bytes 1376264 | tf_op jit(solution)/shard_map/ppermute | solution.py:319
  48.1 11.4 %collective-permute-start.11 = (bf16[32,512]{1,0:T(8,128)(2,1)S(1)}, bf16[32,512]{1,0:T(8,128)(2,1)S(1)}, u32[]{:S(2)}, u32[]{:S(2)}) collective-permute-start(bf16[32,512]{1,0:T(8,128)(2,1)S(1)} %get-tuple-element.49), channel_id=1, source_target_pairs={{0,1},{1,0},{2,3},{3,2},{4,5},{5,4},{6,7},{7,6},{8,9},{9,8},{10,11... | collective-permute-start | bytes 98312 | tf_op jit(solution)/shard_map/ppermute | solution.py:319
  50.7 8.8 %collective-permute-start.12 = (bf16[32,512]{1,0:T(8,128)(2,1)S(1)}, bf16[32,512]{1,0:T(8,128)(2,1)S(1)}, u32[]{:S(2)}, u32[]{:S(2)}) collective-permute-start(bf16[32,512]{1,0:T(8,128)(2,1)S(1)} %get-tuple-element.50), channel_id=1, source_target_pairs={{0,2},{1,3},{2,0},{3,1},{4,6},{5,7},{6,4},{7,5},{8,10},{9,11},{10,... | collective-permute-start | bytes 98312 | tf_op jit(solution)/shard_map/ppermute | solution.py:319
  51.0 8.5 %collective-permute-start.13 = (bf16[32,512]{1,0:T(8,128)(2,1)S(1)}, bf16[32,512]{1,0:T(8,128)(2,1)S(1)}, u32[]{:S(2)}, u32[]{:S(2)}) collective-permute-start(bf16[32,512]{1,0:T(8,128)(2,1)S(1)} %get-tuple-element.51), channel_id=1, source_target_pairs={{0,3},{1,2},{2,1},{3,0},{4,7},{5,6},{6,5},{7,4},{8,11},{9,10},{10,... | collective-permute-start | bytes 98312 | tf_op jit(solution)/shard_map/ppermute | solution.py:319
  59.8 11.9 %collective-permute-start.21 = (bf16[6,448,512]{2,1,0:T(8,128)(2,1)S(1)}, bf16[6,448,512]{2,1,0:T(8,128)(2,1)S(1)}, u32[]{:S(2)}, u32[]{:S(2)}) collective-permute-start(bf16[6,448,512]{2,1,0:T(8,128)(2,1)S(1)} %rest.1.refs_5_), channel_id=1, source_target_pairs={{0,16},{16,0},{1,17},{17,1},{2,18},{18,2},{3,19},{19,3},{4,20},{20... | collective-permute-start | bytes 8257544 | tf_op jit(solution)/shard_map/ppermute | solution.py:319
  59.9 7.8 %collective-permute-start.14 = (bf16[32,2048]{1,0:T(8,128)(2,1)S(1)}, bf16[32,2048]{1,0:T(8,128)(2,1)S(1)}, u32[]{:S(2)}, u32[]{:S(2)}) collective-permute-start(bf16[32,2048]{1,0:T(8,128)(2,1)S(1)} %join.1.refs_4_.refs_0_), channel_id=1, source_target_pairs={{32,0},{64,32},{96,64},{0,96},{33,1},{65,33},{97,65},{1,97},{34,2}... | collective-permute-start | bytes 393224 | tf_op jit(solution)/shard_map/ppermute | solution.py:315
  61.3 10.3 %collective-permute-start.15 = (bf16[32,2048]{1,0:T(8,128)(2,1)S(1)}, bf16[32,2048]{1,0:T(8,128)(2,1)S(1)}, u32[]{:S(2)}, u32[]{:S(2)}) collective-permute-start(bf16[32,2048]{1,0:T(8,128)(2,1)S(1)} %join.1.refs_4_.refs_0_), channel_id=1, source_target_pairs={{64,0},{96,32},{0,64},{32,96},{65,1},{97,33},{1,65},{33,97},{66,2}... | collective-permute-start | bytes 393224 | tf_op jit(solution)/shard_map/ppermute | solution.py:315
  65.0 6.6 %collective-permute-start.16 = (bf16[32,2048]{1,0:T(8,128)(2,1)S(1)}, bf16[32,2048]{1,0:T(8,128)(2,1)S(1)}, u32[]{:S(2)}, u32[]{:S(2)}) collective-permute-start(bf16[32,2048]{1,0:T(8,128)(2,1)S(1)} %join.1.refs_4_.refs_0_), channel_id=1, source_target_pairs={{96,0},{0,32},{32,64},{64,96},{97,1},{1,33},{33,65},{65,97},{98,2}... | collective-permute-start | bytes 393224 | tf_op jit(solution)/shard_map/ppermute | solution.py:315
  74.6 10.5 %collective-permute-start.22 = (bf16[32,1792]{1,0:T(8,128)(2,1)S(1)}, bf16[32,1792]{1,0:T(8,128)(2,1)S(1)}, u32[]{:S(2)}, u32[]{:S(2)}) collective-permute-start(bf16[32,1792]{1,0:T(8,128)(2,1)S(1)} %get-tuple-element.60), channel_id=1, source_target_pairs={{0,4},{4,8},{8,12},{12,0},{1,5},{5,9},{9,13},{13,1},{2,6},{6,10},{... | collective-permute-start | bytes 344072 | tf_op jit(solution)/shard_map/ppermute | solution.py:405
  77.9 12.0 %collective-permute-start.23 = (bf16[32,1792]{1,0:T(8,128)(2,1)S(1)}, bf16[32,1792]{1,0:T(8,128)(2,1)S(1)}, u32[]{:S(2)}, u32[]{:S(2)}) collective-permute-start(bf16[32,1792]{1,0:T(8,128)(2,1)S(1)} %get-tuple-element.61), channel_id=1, source_target_pairs={{0,8},{4,12},{8,0},{12,4},{1,9},{5,13},{9,1},{13,5},{2,10},{6,14},... | collective-permute-start | bytes 344072 | tf_op jit(solution)/shard_map/ppermute | solution.py:405
  82.4 10.6 %collective-permute-start.24 = (bf16[32,1792]{1,0:T(8,128)(2,1)S(1)}, bf16[32,1792]{1,0:T(8,128)(2,1)S(1)}, u32[]{:S(2)}, u32[]{:S(2)}) collective-permute-start(bf16[32,1792]{1,0:T(8,128)(2,1)S(1)} %get-tuple-element.62), channel_id=1, source_target_pairs={{0,12},{4,0},{8,4},{12,8},{1,13},{5,1},{9,5},{13,9},{2,14},{6,2},{... | collective-permute-start | bytes 344072 | tf_op jit(solution)/shard_map/ppermute | solution.py:405
  93.1 4.6 %collective-permute-start.25 = (f32[8,1792]{1,0:T(8,128)S(1)}, f32[8,1792]{1,0:T(8,128)S(1)}, u32[]{:S(2)}, u32[]{:S(2)}) collective-permute-start(f32[8,1792]{1,0:T(8,128)S(1)} %get-tuple-element.64), channel_id=1, source_target_pairs={{0,32},{32,64},{64,96},{96,0},{1,33},{33,65},{65,97},{97,1},{2,34}... | collective-permute-start | bytes 172040 | tf_op jit(solution)/shard_map/ppermute | solution.py:409
  95.7 5.8 %collective-permute-start.26 = (f32[8,1792]{1,0:T(8,128)S(1)}, f32[8,1792]{1,0:T(8,128)S(1)}, u32[]{:S(2)}, u32[]{:S(2)}) collective-permute-start(f32[8,1792]{1,0:T(8,128)S(1)} %get-tuple-element.65), channel_id=1, source_target_pairs={{0,64},{32,96},{64,0},{96,32},{1,65},{33,97},{65,1},{97,33},{2,66}... | collective-permute-start | bytes 172040 | tf_op jit(solution)/shard_map/ppermute | solution.py:409
  95.7 6.0 %collective-permute-start.27 = (f32[8,1792]{1,0:T(8,128)S(1)}, f32[8,1792]{1,0:T(8,128)S(1)}, u32[]{:S(2)}, u32[]{:S(2)}) collective-permute-start(f32[8,1792]{1,0:T(8,128)S(1)} %get-tuple-element.66), channel_id=1, source_target_pairs={{0,96},{32,0},{64,32},{96,64},{1,97},{33,1},{65,33},{97,65},{2,98}... | collective-permute-start | bytes 172040 | tf_op jit(solution)/shard_map/ppermute | solution.py:409

commit v8 on v7

--- a/solution.py
+++ b/solution.py
@@ -38,11 +38,11 @@
 def plan_kernel(ids, table, lens, lists, counts):
     yl, x, k = ids[0], ids[1], ids[2]
     for s in range(SLOTS):
-        limit = lens[yl * 8 + ((x + s) % 4) * 2 + k]
+        limit = lens[yl * 8 + (x ^ s) * 2 + k]
 
         def scan(m, carry):
             found, valid = carry
-            block = table[yl * 8 + ((x + s) % 4) * 2 + k, m]
+            block = table[yl * 8 + (x ^ s) * 2 + k, m]
             owner = block >> 2
             here = ((owner >> 1) & 3) == x
 
@@ -68,6 +68,7 @@
         in_specs=[scalar] * 3,
         out_specs=[scalar] * 2,
         compiler_params=pltpu.CompilerParams(vmem_limit_bytes=2**20),
+        cost_estimate=pl.CostEstimate(flops=1, bytes_accessed=1, transcendentals=0),
         name="plan",
     )(ids, table, lens)
 
@@ -197,6 +198,7 @@
             pltpu.VMEM((count, ROWS, 128), jnp.float32),
         ],
         compiler_params=pltpu.CompilerParams(vmem_limit_bytes=24 * 2**20),
+        cost_estimate=pl.CostEstimate(flops=1, bytes_accessed=1, transcendentals=0),
         name="attend",
     )(lists, counts, q_lat, q_rot, *pools, w_uv, *fresh)
 
@@ -258,7 +260,7 @@
             sides.append(value)
         total[:, side_y * 896 : (side_y + 1) * 896] = jnp.concatenate(sides, axis=1)
     for d in range(4):
-        first = pl.multiple_of(((zb + d) % 4) * 8, 8)
+        first = pl.multiple_of((zb ^ d) * 8, 8)
         parts = [total[pl.ds(first + s * 32, 8), :] for s in range(4)]
         outs[d][...] = jnp.concatenate(parts, axis=0).astype(jnp.bfloat16)
 
@@ -274,7 +276,7 @@
     yl, x, k = ids[0], ids[1], ids[2]
     for s in range(4):
         for side_y in range(2):
-            first = ((yl ^ side_y) * 4 + (x - s + 4) % 4) * 896
+            first = ((yl ^ side_y) * 4 + (x ^ s)) * 896
             columns = pl.ds(pl.multiple_of(first, 128), 896)
             value = parts[s][:, side_y * 896 : (side_y + 1) * 896]
             swapped = jnp.concatenate([value[:, 448:], value[:, :448]], axis=1)
@@ -294,6 +296,7 @@
         out_specs=[free] * len(values),
         input_output_aliases={i: i for i in range(len(values))},
         compiler_params=pltpu.CompilerParams(vmem_limit_bytes=2**20),
+        cost_estimate=pl.CostEstimate(flops=1, bytes_accessed=1, transcendentals=0),
         name="tie",
     )(*values, *others)
 
@@ -307,12 +310,9 @@
         out_specs=jax.tree.map(lambda _: full, out_shape),
         scratch_shapes=scratch,
         compiler_params=pltpu.CompilerParams(vmem_limit_bytes=16 * 2**20),
+        cost_estimate=pl.CostEstimate(flops=1, bytes_accessed=1, transcendentals=0),
         name=name,
     )(*args)
-
-
-def turn(value, axis, size, shift):
-    return lax.ppermute(value, axis, [((i + shift) % size, i) for i in range(size)])
 
 
 def flip(value, axis, size, bits):
@@ -347,11 +347,12 @@
     )
     weight = w_out.T
 
-    queries = [query] + [turn(query, "x", 4, s) for s in (1, 2, 3)]
+    queries = [query] + [flip(query, "x", 4, s) for s in (1, 2, 3)]
     pool_y = flip(pool, "yl", 2, 1)
     weight_z = flip(weight, "z0", 2, 1)
     lists, counts = plan(ids, block_table, prefix_len)
-    pool, pool_y, counts, weight_z = tie([pool, pool_y, counts, weight_z], queries[1:])
+    (weight_z,) = tie([weight_z], [counts])
+    pool, pool_y, counts = tie([pool, pool_y, counts], queries[1:])
     q_lat, q_rot = simple(
         prepare_kernel,
         "prepare",
@@ -373,9 +374,7 @@
     pools = [pool, pool_y, pool_k, pool_yk]
 
     away = attention((1, 2, 3), False, lists, counts, q_lat, q_rot, pools, w_uv, ())
-    came = [
-        lax.ppermute(part, "x", [(i, (i + s) % 4) for i in range(4)]) for s, part in zip((1, 2, 3), away)
-    ]
+    came = [flip(part, "x", 4, s) for s, part in zip((1, 2, 3), away)]
     (home,) = attention((0,), True, lists, counts, q_lat, q_rot, pools, w_uv, (new_latent, new_rope[0]))
     mine[1], mine[2] = tie([mine[1], mine[2]], [*came, home])
     far = [flip(mine[2][0], ring, 4, 2), flip(mine[1][1], ring, 4, 3)]
@@ -393,7 +392,7 @@
     )
     mine = [pair, rest]
     other.append(flip(rest, "k", 2, 1))
-    heads = [heads] + [turn(heads, "x", 4, s) for s in (1, 2, 3)]
+    heads = [heads] + [flip(heads, "x", 4, s) for s in (1, 2, 3)]
     partial = simple(
         project_kernel,
         "project",
@@ -401,13 +400,9 @@
         [ids, *heads, *mine, *other],
         scratch=[pltpu.VMEM((TOK, 1792), jnp.float32)],
     )
-    sums = [partial[0]] + [
-        lax.ppermute(partial[d], "zb", [(i, (i + d) % 4) for i in range(4)]) for d in (1, 2, 3)
-    ]
+    sums = [partial[0]] + [flip(partial[d], "zb", 4, d) for d in (1, 2, 3)]
     pieces = simple(share_kernel, "share", [jax.ShapeDtypeStruct((8, 1792), jnp.float32)] * 4, sums)
-    pieces = [pieces[0]] + [
-        lax.ppermute(pieces[s], "x", [(i, (i + s) % 4) for i in range(4)]) for s in (1, 2, 3)
-    ]
+    pieces = [pieces[0]] + [flip(pieces[s], "x", 4, s) for s in (1, 2, 3)]
     return simple(place_kernel, "place", jax.ShapeDtypeStruct((8, 7168), jnp.bfloat16), [ids, *pieces])
 
 

time: 104 us -> 106 us (1.019); the launches traced: 103 us -> 104 us
  waiting for transfers between devices: 32.2 us -> 36.2 us
  starting transfers between devices: 44.6 us -> 42.7 us
    ppermute x15 -> x0, starting transfers between devices: 29.9 us -> none  [the longest x3 10.5 us: local(): lax.ppermute(partial[d], 'zb', [(i, (i + d) % 4) for i in range(4)])]
    ppermute x13 -> x28, waiting for transfers between devices: 7.35 us -> 36.2 us  [flip(): return lax.ppermute(value, axis, [(i, i ^ bits) for i in range(size)])]
    ppermute x13 -> x28, starting transfers between devices: 14.7 us -> 42.7 us  [flip(): return lax.ppermute(value, axis, [(i, i ^ bits) for i in range(size)])]
    ppermute x15 -> x0, waiting for transfers between devices: 24.8 us -> none  [the longest x6 10.6 us: turn(): lax.ppermute(value, axis, [((i + shift) % size, i) for i in range(size)])]
  transfers between devices with their start and end apart: 28 -> 28, of which waited for: 13 -> 17; matrix products, arithmetic and copies ran while one was open for 2% -> 3% of each run, Pallas kernels for 16% -> 15%
where the time goes in v8:
time: 106 us; the launch traced here: 104 us
  starting transfers between devices  42.7 us (40%)
  waiting for transfers between devices  36.2 us (34%)
  Pallas kernels  20.4 us (19%)
  local copies, waits for them, and re-layouts  3.29 us (3%)
  other arithmetic  1.08 us (1%)
    ppermute x28, starting transfers between devices, flip(): return lax.ppermute(value, axis, [(i, i ^ bits) for i in range(size)])  42.7 us
    ppermute x28, waiting for transfers between devices, flip(): return lax.ppermute(value, axis, [(i, i ^ bits) for i in range(size)])  36.2 us
    pallas_call x2, Pallas kernels, attention(): pl.pallas_call(functools.partial(attention_kernel, slots, own), out_shape...  11.1 us
    pallas_call x8, Pallas kernels, simple(): pl.pallas_call(kernel, out_shape=out_shape, in_specs=[pl.BlockSpec(memory...  6.92 us
    pallas_call x1, Pallas kernels, plan(): pl.pallas_call(plan_kernel, out_shape=[jax.ShapeDtypeStruct((SLOTS * 16,)...  2.41 us
    unnamed x17, local copies, waits for them, and re-layouts  2.29 us
  transfers between devices with their start and end apart: 28, of which 17 were waited for; matrix products, arithmetic and copies ran while one was open for 3% of the time, Pallas kernels for 15%

profile of v8, /device:TPU:6, one launch (start us, length us, event | category | flops | bytes accessed | tf_op | source)
XLA Modules:
  0.0 103.9 jit_solution(11415511377312399656)
XLA Ops:
  0.0 1.9 %collective-permute-start.5 = (bf16[448,512]{1,0:T(8,128)(2,1)}, bf16[448,512]{1,0:T(8,128)(2,1)S(1)}, u32[]{:S(2)}, u32[]{:S(2)}) collective-permute-start(bf16[448,512]{1,0:T(8,128)(2,1)} %bitcast.18), channel_id=1, source_target_pairs={{0,2},{2,0},{1,3},{3,1},{4,6},{6,4},{5,7},{7,5},{8,10},{10,8},{9,1... | collective-permute-start | bytes 1376264 | tf_op jit(solution)/shard_map/ppermute | solution.py:319
  1.9 1.1 %pad_maximum_fusion.refs_0_ = bf16[576,512]{1,0:T(8,128)(2,1)S(1)} fusion(bf16[64,512]{1,0:T(8,128)(2,1)S(1)} %copy_bitcast_fusion, bf16[512,512]{1,0:T(8,128)(2,1)} %bitcast.21), kind=kLoop, calls=%fused_computation | loop fusion | flops 1179648 | bytes 1179648 | tf_op jit(solution)/shard_map/concatenate | solution.py:345
  3.0 1.7 %collective-permute-start = (bf16[576,512]{1,0:T(8,128)(2,1)S(1)}, bf16[576,512]{1,0:T(8,128)(2,1)S(1)}, u32[]{:S(2)}, u32[]{:S(2)}) collective-permute-start(bf16[576,512]{1,0:T(8,128)(2,1)S(1)} %pad_maximum_fusion.refs_0_), channel_id=1, source_target_pairs={{0,128},{128,0},{1,129},{129,1},{2,130},{130,2},{3,131},{131,3},{4... | collective-permute-start | bytes 1769480 | tf_op jit(solution)/shard_map/ppermute | solution.py:319
  4.7 0.9 constant_dynamic-update-slice_fusion.1
  5.6 0.8 constant_dynamic-update-slice_fusion.refs_0_
  6.5 0.8 collective-permute-start.1
  7.3 1.1 %collective-permute-start.2 = (bf16[128,768]{1,0:T(8,128)(2,1)S(1)}, bf16[128,768]{1,0:T(8,128)(2,1)S(1)}, u32[]{:S(2)}, u32[]{:S(2)}) collective-permute-start(bf16[128,768]{1,0:T(8,128)(2,1)S(1)} %constant_dynamic-update-slice_fusion.refs_0_), channel_id=1, source_target_pairs={{0,64},{32,96},{64,0},{96,32},{1,65},{33,97},{65,1},{97,33},{2,66}... | collective-permute-start | bytes 589832 | tf_op jit(solution)/shard_map/ppermute | solution.py:319
  8.4 0.1 stack.23.ids
  8.5 0.7 copy-done.6
  9.2 0.7 copy-done.7
  9.8 2.4 %plan.1 = (s32[64]{0:T(128)S(1)}, s32[8]{0:T(128)S(1)}) custom-call(s32[5]{0:T(128)S(1)} %stack.23.ids, s32[16,32]{1,0:T(8,128)S(1)} %copy-done.6, s32[16]{0:T(128)S(1)} %copy-done.7), custom_call_target="tpu_custom_call" | custom-call | flops 1 | bytes 1 | tf_op jit(solution)/shard_map/plan/pallas_call | solution.py:65
  12.2 0.4 collective-permute-done.5.refs_0_
  12.7 0.1 pair.1.refs_4_
  12.8 0.0 copy-start.1
  12.8 0.1 collective-permute-start.6
  12.9 2.5 %collective-permute-start.3 = (bf16[128,768]{1,0:T(8,128)(2,1)S(1)}, bf16[128,768]{1,0:T(8,128)(2,1)S(1)}, u32[]{:S(2)}, u32[]{:S(2)}) collective-permute-start(bf16[128,768]{1,0:T(8,128)(2,1)S(1)} %constant_dynamic-update-slice_fusion.refs_0_), channel_id=1, source_target_pairs={{0,96},{32,64},{64,32},{96,0},{1,97},{33,65},{65,33},{97,1},{2,98}... | collective-permute-start | bytes 589832 | tf_op jit(solution)/shard_map/ppermute | solution.py:319
  15.3 0.4 collective-permute-start.17
  15.8 0.9 collective-permute-done.2.refs_4_.refs_2_
  16.7 2.2 %collective-permute-start.18 = (bf16[2,448,512]{2,1,0:T(8,128)(2,1)S(1)}, bf16[2,448,512]{2,1,0:T(8,128)(2,1)S(1)}, u32[]{:S(2)}, u32[]{:S(2)}) collective-permute-start(bf16[2,448,512]{2,1,0:T(8,128)(2,1)S(1)} %pair.1.refs_4_), channel_id=1, source_target_pairs={{0,129},{1,128},{128,1},{129,0},{2,131},{3,130},{130,3},{131,2},{4... | collective-permute-start | bytes 2752520 | tf_op jit(solution)/shard_map/ppermute | solution.py:319
  18.8 2.6 %collective-permute-done.3.refs_5_.refs_3_ = bf16[128,768]{1,0:T(8,128)(2,1)S(1)} collective-permute-done((bf16[128,768]{1,0:T(8,128)(2,1)S(1)}, bf16[128,768]{1,0:T(8,128)(2,1)S(1)}, u32[]{:S(2)}, u32[]{:S(2)}) %collective-permute-start.3) | collective-permute-done | bytes 196640 | tf_op jit(solution)/shard_map/ppermute | solution.py:319
  21.4 0.0 collective-permute-done.refs_1_
  21.4 0.0 collective-permute-start.4
  21.4 0.5 collective-permute-start.7
  21.9 1.3 %prepare.1 = (bf16[4,512,512]{2,1,0:T(8,128)(2,1)S(1)}, bf16[4,512,64]{2,1,0:T(8,128)(2,1)S(1)}) custom-call(s32[8]{0:T(128)S(1)} %get-tuple-element.37.counts, bf16[128,768]{1,0:T(8,128)(2,1)S(1)} %constant_dynamic-update-slice_fusion.refs_0_, bf16[128,768]{1,0:T(8,128)(2,1)S(1)} %collective-permute-done.1.refs_3_.refs_1_, ...), custom_call_target="tpu_custom_call" | custom-call | flops 1 | bytes 1 | tf_op jit(solution)/shard_map/prepare/pallas_call | solution.py:306
  23.2 0.2 collective-permute-done.4.refs_0_
  23.4 0.0 collective-permute-done.6.refs_1_
  23.4 0.8 collective-permute-done.7.refs_3_
  24.3 7.2 %attend.3 = (bf16[128,640]{1,0:T(8,128)(2,1)S(1)}, bf16[128,640]{1,0:T(8,128)(2,1)S(1)}, bf16[128,640]{1,0:T(8,128)(2,1)S(1)}) custom-call(s32[64]{0:T(128)S(1)} %get-tuple-element.35.lists, s32[8]{0:T(128)S(1)} %get-tuple-element.37.counts, bf16[4,512,512]{2,1,0:T(8,128)(2,1)S(1)} %get-tuple-element.38.q_lat, ...), custom_call_target="tpu_custom_call" | custom-call | flops 1 | bytes 1 | tf_op jit(solution)/shard_map/attend/pallas_call | solution.py:186
  31.5 3.6 %collective-permute-start.10 = (bf16[128,640]{1,0:T(8,128)(2,1)S(1)}, bf16[128,640]{1,0:T(8,128)(2,1)S(1)}, u32[]{:S(2)}, u32[]{:S(2)}) collective-permute-start(bf16[128,640]{1,0:T(8,128)(2,1)S(1)} %get-tuple-element.45), channel_id=1, source_target_pairs={{0,96},{32,64},{64,32},{96,0},{1,97},{33,65},{65,33},{97,1},{2,98}... | collective-permute-start | bytes 491528 | tf_op jit(solution)/shard_map/ppermute | solution.py:319
  35.1 1.6 %collective-permute-start.9 = (bf16[128,640]{1,0:T(8,128)(2,1)S(1)}, bf16[128,640]{1,0:T(8,128)(2,1)S(1)}, u32[]{:S(2)}, u32[]{:S(2)}) collective-permute-start(bf16[128,640]{1,0:T(8,128)(2,1)S(1)} %get-tuple-element.44), channel_id=1, source_target_pairs={{0,64},{32,96},{64,0},{96,32},{1,65},{33,97},{65,1},{97,33},{2,66}... | collective-permute-start | bytes 491528 | tf_op jit(solution)/shard_map/ppermute | solution.py:319
  36.6 3.9 %attend.2.refs_0_.refs_5_ = bf16[128,640]{1,0:T(8,128)(2,1)S(1)} custom-call(s32[64]{0:T(128)S(1)} %get-tuple-element.35.lists, s32[8]{0:T(128)S(1)} %get-tuple-element.37.counts, bf16[4,512,512]{2,1,0:T(8,128)(2,1)S(1)} %get-tuple-element.38.q_lat, bf16[4,512,64]{2,1,0:T(8,128)(2,1)S(1)} %get-tuple-element.39.q_rot, ...), custom_call_target="tpu_custom_call" | custom-call | flops 1 | bytes 1 | tf_op jit(solution)/shard_map/attend/pallas_call | solution.py:186
  40.5 0.0 collective-permute-done.18.refs_1_
  40.5 0.0 collective-permute-done.10.refs_3_.refs_4_
  40.5 1.6 %collective-permute-done.8.refs_1_.refs_2_ = bf16[128,640]{1,0:T(8,128)(2,1)S(1)} collective-permute-done((bf16[128,640]{1,0:T(8,128)(2,1)S(1)}, bf16[128,640]{1,0:T(8,128)(2,1)S(1)}, u32[]{:S(2)}, u32[]{:S(2)}) %collective-permute-start.8) | collective-permute-done | bytes 163872 | tf_op jit(solution)/shard_map/ppermute | solution.py:319
  42.1 2.8 %collective-permute-done.9.refs_2_.refs_3_ = bf16[128,640]{1,0:T(8,128)(2,1)S(1)} collective-permute-done((bf16[128,640]{1,0:T(8,128)(2,1)S(1)}, bf16[128,640]{1,0:T(8,128)(2,1)S(1)}, u32[]{:S(2)}, u32[]{:S(2)}) %collective-permute-start.9) | collective-permute-done | bytes 163872 | tf_op jit(solution)/shard_map/ppermute | solution.py:319
  45.0 0.1 collective-permute-start.19
  45.1 3.5 %collective-permute-start.20 = (bf16[448,512]{1,0:T(8,128)(2,1)S(1)}, bf16[448,512]{1,0:T(8,128)(2,1)S(1)}, u32[]{:S(2)}, u32[]{:S(2)}) collective-permute-start(bf16[448,512]{1,0:T(8,128)(2,1)S(1)} %slice_bitcast_fusion), channel_id=1, source_target_pairs={{0,129},{1,128},{128,1},{129,0},{2,131},{3,130},{130,3},{131,2},{4... | collective-permute-start | bytes 1376264 | tf_op jit(solution)/shard_map/ppermute | solution.py:319
  48.6 1.1 %combine.1 = (bf16[32,512]{1,0:T(8,128)(2,1)S(1)}, bf16[32,512]{1,0:T(8,128)(2,1)S(1)}, bf16[32,512]{1,0:T(8,128)(2,1)S(1)}, bf16[32,512]{1,0:T(8,128)(2,1)S(1)}) custom-call(s32[5]{0:T(128)S(1)} %stack.23.ids, bf16[128,640]{1,0:T(8,128)(2,1)S(1)} %attend.2.refs_0_.refs_5_, bf16[128,640]{1,0:T(8,128)(2,1)S(1)} %collective-permute-done.8.refs_1_.refs_2_, ...), custom_call_target="tpu_custom_call" | custom-call | flops 1 | bytes 1 | tf_op jit(solution)/shard_map/combine/pallas_call | solution.py:306
  49.7 0.7 collective-permute-start.11
  50.4 1.5 %collective-permute-start.12 = (bf16[32,512]{1,0:T(8,128)(2,1)S(1)}, bf16[32,512]{1,0:T(8,128)(2,1)S(1)}, u32[]{:S(2)}, u32[]{:S(2)}) collective-permute-start(bf16[32,512]{1,0:T(8,128)(2,1)S(1)} %get-tuple-element.48), channel_id=1, source_target_pairs={{0,2},{1,3},{2,0},{3,1},{4,6},{5,7},{6,4},{7,5},{8,10},{9,11},{10,... | collective-permute-start | bytes 98312 | tf_op jit(solution)/shard_map/ppermute | solution.py:319
  51.9 2.9 %collective-permute-start.13 = (bf16[32,512]{1,0:T(8,128)(2,1)S(1)}, bf16[32,512]{1,0:T(8,128)(2,1)S(1)}, u32[]{:S(2)}, u32[]{:S(2)}) collective-permute-start(bf16[32,512]{1,0:T(8,128)(2,1)S(1)} %get-tuple-element.49), channel_id=1, source_target_pairs={{0,3},{1,2},{2,1},{3,0},{4,7},{5,6},{6,5},{7,4},{8,11},{9,10},{10,... | collective-permute-start | bytes 98312 | tf_op jit(solution)/shard_map/ppermute | solution.py:319
  54.8 5.4 %collective-permute-done.11.refs_1_ = bf16[32,512]{1,0:T(8,128)(2,1)S(1)} collective-permute-done((bf16[32,512]{1,0:T(8,128)(2,1)S(1)}, bf16[32,512]{1,0:T(8,128)(2,1)S(1)}, u32[]{:S(2)}, u32[]{:S(2)}) %collective-permute-start.11) | collective-permute-done | bytes 32800 | tf_op jit(solution)/shard_map/ppermute | solution.py:319
  60.2 0.0 collective-permute-done.12.refs_2_
  60.2 0.3 collective-permute-done.20.refs_3_
  60.6 0.2 rest.1.refs_5_
  60.8 0.1 collective-permute-start.21
  60.9 0.3 collective-permute-start.14
  61.2 4.6 %collective-permute-start.15 = (bf16[32,2048]{1,0:T(8,128)(2,1)S(1)}, bf16[32,2048]{1,0:T(8,128)(2,1)S(1)}, u32[]{:S(2)}, u32[]{:S(2)}) collective-permute-start(bf16[32,2048]{1,0:T(8,128)(2,1)S(1)} %join.1.refs_4_.refs_0_), channel_id=1, source_target_pairs={{0,64},{32,96},{64,0},{96,32},{1,65},{33,97},{65,1},{97,33},{2,66}... | collective-permute-start | bytes 393224 | tf_op jit(solution)/shard_map/ppermute | solution.py:319
  65.8 1.5 %collective-permute-done.14.refs_1_ = bf16[32,2048]{1,0:T(8,128)(2,1)S(1)} collective-permute-done((bf16[32,2048]{1,0:T(8,128)(2,1)S(1)}, bf16[32,2048]{1,0:T(8,128)(2,1)S(1)}, u32[]{:S(2)}, u32[]{:S(2)}) %collective-permute-start.14) | collective-permute-done | bytes 131104 | tf_op jit(solution)/shard_map/ppermute | solution.py:319
  67.2 5.2 %collective-permute-done.15.refs_2_ = bf16[32,2048]{1,0:T(8,128)(2,1)S(1)} collective-permute-done((bf16[32,2048]{1,0:T(8,128)(2,1)S(1)}, bf16[32,2048]{1,0:T(8,128)(2,1)S(1)}, u32[]{:S(2)}, u32[]{:S(2)}) %collective-permute-start.15) | collective-permute-done | bytes 131104 | tf_op jit(solution)/shard_map/ppermute | solution.py:319
  72.5 2.4 %collective-permute-done.16.refs_3_ = bf16[32,2048]{1,0:T(8,128)(2,1)S(1)} collective-permute-done((bf16[32,2048]{1,0:T(8,128)(2,1)S(1)}, bf16[32,2048]{1,0:T(8,128)(2,1)S(1)}, u32[]{:S(2)}, u32[]{:S(2)}) %collective-permute-start.16) | collective-permute-done | bytes 131104 | tf_op jit(solution)/shard_map/ppermute | solution.py:319
  74.9 3.0 %project.1 = (bf16[32,1792]{1,0:T(8,128)(2,1)S(1)}, bf16[32,1792]{1,0:T(8,128)(2,1)S(1)}, bf16[32,1792]{1,0:T(8,128)(2,1)S(1)}, bf16[32,1792]{1,0:T(8,128)(2,1)S(1)}) custom-call(s32[5]{0:T(128)S(1)} %stack.23.ids, bf16[32,2048]{1,0:T(8,128)(2,1)S(1)} %join.1.refs_4_.refs_0_, bf16[32,2048]{1,0:T(8,128)(2,1)S(1)} %collective-permute-done.14.refs_1_, ...), custom_call_target="tpu_custom_call" | custom-call | flops 1 | bytes 1 | tf_op jit(solution)/shard_map/project/pallas_call | solution.py:306
  77.8 3.4 %collective-permute-start.22 = (bf16[32,1792]{1,0:T(8,128)(2,1)S(1)}, bf16[32,1792]{1,0:T(8,128)(2,1)S(1)}, u32[]{:S(2)}, u32[]{:S(2)}) collective-permute-start(bf16[32,1792]{1,0:T(8,128)(2,1)S(1)} %get-tuple-element.58), channel_id=1, source_target_pairs={{0,4},{4,0},{8,12},{12,8},{1,5},{5,1},{9,13},{13,9},{2,6},{6,2},{1... | collective-permute-start | bytes 344072 | tf_op jit(solution)/shard_map/ppermute | solution.py:319
  81.2 4.5 %collective-permute-start.23 = (bf16[32,1792]{1,0:T(8,128)(2,1)S(1)}, bf16[32,1792]{1,0:T(8,128)(2,1)S(1)}, u32[]{:S(2)}, u32[]{:S(2)}) collective-permute-start(bf16[32,1792]{1,0:T(8,128)(2,1)S(1)} %get-tuple-element.59), channel_id=1, source_target_pairs={{0,8},{4,12},{8,0},{12,4},{1,9},{5,13},{9,1},{13,5},{2,10},{6,14},... | collective-permute-start | bytes 344072 | tf_op jit(solution)/shard_map/ppermute | solution.py:319
  85.7 1.0 collective-permute-done.22.refs_1_
  86.7 7.0 %collective-permute-done.23.refs_2_ = bf16[32,1792]{1,0:T(8,128)(2,1)S(1)} collective-permute-done((bf16[32,1792]{1,0:T(8,128)(2,1)S(1)}, bf16[32,1792]{1,0:T(8,128)(2,1)S(1)}, u32[]{:S(2)}, u32[]{:S(2)}) %collective-permute-start.23) | collective-permute-done | bytes 114720 | tf_op jit(solution)/shard_map/ppermute | solution.py:319
  93.7 1.5 %collective-permute-done.24.refs_3_ = bf16[32,1792]{1,0:T(8,128)(2,1)S(1)} collective-permute-done((bf16[32,1792]{1,0:T(8,128)(2,1)S(1)}, bf16[32,1792]{1,0:T(8,128)(2,1)S(1)}, u32[]{:S(2)}, u32[]{:S(2)}) %collective-permute-start.24) | collective-permute-done | bytes 114720 | tf_op jit(solution)/shard_map/ppermute | solution.py:319
  95.2 0.1 share.1
  95.3 0.1 collective-permute-start.25
  95.4 1.8 %collective-permute-start.26 = (f32[8,1792]{1,0:T(8,128)S(1)}, f32[8,1792]{1,0:T(8,128)S(1)}, u32[]{:S(2)}, u32[]{:S(2)}) collective-permute-start(f32[8,1792]{1,0:T(8,128)S(1)} %get-tuple-element.63), channel_id=1, source_target_pairs={{0,64},{32,96},{64,0},{96,32},{1,65},{33,97},{65,1},{97,33},{2,66}... | collective-permute-start | bytes 172040 | tf_op jit(solution)/shard_map/ppermute | solution.py:319
  97.2 2.9 %collective-permute-start.27 = (f32[8,1792]{1,0:T(8,128)S(1)}, f32[8,1792]{1,0:T(8,128)S(1)}, u32[]{:S(2)}, u32[]{:S(2)}) collective-permute-start(f32[8,1792]{1,0:T(8,128)S(1)} %get-tuple-element.64), channel_id=1, source_target_pairs={{0,96},{32,64},{64,32},{96,0},{1,97},{33,65},{65,33},{97,1},{2,98}... | collective-permute-start | bytes 172040 | tf_op jit(solution)/shard_map/ppermute | solution.py:319
  100.1 1.1 %collective-permute-done.26.refs_2_ = f32[8,1792]{1,0:T(8,128)S(1)} collective-permute-done((f32[8,1792]{1,0:T(8,128)S(1)}, f32[8,1792]{1,0:T(8,128)S(1)}, u32[]{:S(2)}, u32[]{:S(2)}) %collective-permute-start.26) | collective-permute-done | bytes 57376 | tf_op jit(solution)/shard_map/ppermute | solution.py:319
  101.2 1.4 %collective-permute-done.27.refs_3_ = f32[8,1792]{1,0:T(8,128)S(1)} collective-permute-done((f32[8,1792]{1,0:T(8,128)S(1)}, f32[8,1792]{1,0:T(8,128)S(1)}, u32[]{:S(2)}, u32[]{:S(2)}) %collective-permute-start.27) | collective-permute-done | bytes 57376 | tf_op jit(solution)/shard_map/ppermute | solution.py:319
  102.6 1.3 %place.1 = bf16[8,7168]{1,0:T(8,128)(2,1)} custom-call(s32[5]{0:T(128)S(1)} %stack.23.ids, f32[8,1792]{1,0:T(8,128)S(1)} %get-tuple-element.61.refs_0_, f32[8,1792]{1,0:T(8,128)S(1)} %collective-permute-done.25.refs_1_, f32[8,1792]{1,0:T(8,128)S(1)} %collective-permute-done.26.refs_2_, f32[8,1792]{1,0:T(8,128)S(1)} %collective-permute-done.27.refs_3_), custom_call_target="tpu_custom_call" | custom-call | flops 1 | bytes 1 | tf_op jit(solution)/shard_map/place/pallas_call | solution.py:306
  (31 shorter events, 0.1 us)
Async XLA Ops:
  0.0 1.9 %copy-start = (bf16[4,64,128]{2,1,0:T(8,128)(2,1)S(1)}, bf16[4,64,128]{2,1,0:T(8,128)(2,1)}, u32[]{:S(2)}) copy-start(bf16[4,64,128]{2,1,0:T(8,128)(2,1)} %param.16) | copy-start | bytes 196612
  0.0 12.7 %copy-start.3 = (bf16[512,448]{0,1:T(8,128)(2,1)S(1)}, bf16[512,448]{0,1:T(8,128)(2,1)}, u32[]{:S(2)}) copy-start(bf16[512,448]{0,1:T(8,128)(2,1)} %param.21) | copy-start | bytes 1376260
  0.0 12.7 %collective-permute-start.5 = (bf16[448,512]{1,0:T(8,128)(2,1)}, bf16[448,512]{1,0:T(8,128)(2,1)S(1)}, u32[]{:S(2)}, u32[]{:S(2)}) collective-permute-start(bf16[448,512]{1,0:T(8,128)(2,1)} %bitcast.18), channel_id=1, source_target_pairs={{0,2},{2,0},{1,3},{3,1},{4,6},{6,4},{5,7},{7,5},{8,10},{10,8},{9,1... | collective-permute-start | bytes 1376264 | tf_op jit(solution)/shard_map/ppermute | solution.py:319
  3.0 18.4 %collective-permute-start = (bf16[576,512]{1,0:T(8,128)(2,1)S(1)}, bf16[576,512]{1,0:T(8,128)(2,1)S(1)}, u32[]{:S(2)}, u32[]{:S(2)}) collective-permute-start(bf16[576,512]{1,0:T(8,128)(2,1)S(1)} %pad_maximum_fusion.refs_0_), channel_id=1, source_target_pairs={{0,128},{128,0},{1,129},{129,1},{2,130},{130,2},{3,131},{131,3},{4... | collective-permute-start | bytes 1769480 | tf_op jit(solution)/shard_map/ppermute | solution.py:319
  6.5 8.9 %collective-permute-start.1 = (bf16[128,768]{1,0:T(8,128)(2,1)S(1)}, bf16[128,768]{1,0:T(8,128)(2,1)S(1)}, u32[]{:S(2)}, u32[]{:S(2)}) collective-permute-start(bf16[128,768]{1,0:T(8,128)(2,1)S(1)} %constant_dynamic-update-slice_fusion.refs_0_), channel_id=1, source_target_pairs={{0,32},{32,0},{64,96},{96,64},{1,33},{33,1},{65,97},{97,65},{2,34}... | collective-permute-start | bytes 589832 | tf_op jit(solution)/shard_map/ppermute | solution.py:319
  7.3 9.4 %collective-permute-start.2 = (bf16[128,768]{1,0:T(8,128)(2,1)S(1)}, bf16[128,768]{1,0:T(8,128)(2,1)S(1)}, u32[]{:S(2)}, u32[]{:S(2)}) collective-permute-start(bf16[128,768]{1,0:T(8,128)(2,1)S(1)} %constant_dynamic-update-slice_fusion.refs_0_), channel_id=1, source_target_pairs={{0,64},{32,96},{64,0},{96,32},{1,65},{33,97},{65,1},{97,33},{2,66}... | collective-permute-start | bytes 589832 | tf_op jit(solution)/shard_map/ppermute | solution.py:319
  8.5 0.7 copy-start.6
  9.2 0.7 copy-start.7
  12.7 9.2 %copy-start.2 = (bf16[4,128,512]{2,1,0:T(8,128)(2,1)S(1)}, bf16[4,128,512]{2,1,0:T(8,128)(2,1)}, u32[]{:S(2)}) copy-start(bf16[4,128,512]{2,1,0:T(8,128)(2,1)} %refs_4_.3) | copy-start | bytes 1572868
  12.8 11.5 %copy-start.1 = (bf16[4,512,128]{2,1,0:T(8,128)(2,1)S(1)}, bf16[4,512,128]{2,1,0:T(8,128)(2,1)}, u32[]{:S(2)}) copy-start(bf16[4,512,128]{2,1,0:T(8,128)(2,1)} %refs_4_.5) | copy-start | bytes 1572868
  12.8 10.6 %collective-permute-start.6 = (bf16[2,448,512]{2,1,0:T(8,128)(2,1)S(1)}, bf16[2,448,512]{2,1,0:T(8,128)(2,1)S(1)}, u32[]{:S(2)}, u32[]{:S(2)}) collective-permute-start(bf16[2,448,512]{2,1,0:T(8,128)(2,1)S(1)} %pair.1.refs_4_), channel_id=1, source_target_pairs={{0,16},{16,0},{1,17},{17,1},{2,18},{18,2},{3,19},{19,3},{4,20},{20... | collective-permute-start | bytes 2752520 | tf_op jit(solution)/shard_map/ppermute | solution.py:319
  12.9 8.5 %collective-permute-start.3 = (bf16[128,768]{1,0:T(8,128)(2,1)S(1)}, bf16[128,768]{1,0:T(8,128)(2,1)S(1)}, u32[]{:S(2)}, u32[]{:S(2)}) collective-permute-start(bf16[128,768]{1,0:T(8,128)(2,1)S(1)} %constant_dynamic-update-slice_fusion.refs_0_), channel_id=1, source_target_pairs={{0,96},{32,64},{64,32},{96,0},{1,97},{33,65},{65,33},{97,1},{2,98}... | collective-permute-start | bytes 589832 | tf_op jit(solution)/shard_map/ppermute | solution.py:319
  15.3 25.2 %collective-permute-start.17 = (bf16[2,448,512]{2,1,0:T(8,128)(2,1)S(1)}, bf16[2,448,512]{2,1,0:T(8,128)(2,1)S(1)}, u32[]{:S(2)}, u32[]{:S(2)}) collective-permute-start(bf16[2,448,512]{2,1,0:T(8,128)(2,1)S(1)} %pair.1.refs_4_), channel_id=1, source_target_pairs={{0,128},{1,129},{128,0},{129,1},{2,130},{3,131},{130,2},{131,3},{4... | collective-permute-start | bytes 2752520 | tf_op jit(solution)/shard_map/ppermute | solution.py:319
  16.7 23.9 %collective-permute-start.18 = (bf16[2,448,512]{2,1,0:T(8,128)(2,1)S(1)}, bf16[2,448,512]{2,1,0:T(8,128)(2,1)S(1)}, u32[]{:S(2)}, u32[]{:S(2)}) collective-permute-start(bf16[2,448,512]{2,1,0:T(8,128)(2,1)S(1)} %pair.1.refs_4_), channel_id=1, source_target_pairs={{0,129},{1,128},{128,1},{129,0},{2,131},{3,130},{130,3},{131,2},{4... | collective-permute-start | bytes 2752520 | tf_op jit(solution)/shard_map/ppermute | solution.py:319
  21.4 2.0 %collective-permute-start.4 = (bf16[576,512]{1,0:T(8,128)(2,1)S(1)}, bf16[576,512]{1,0:T(8,128)(2,1)S(1)}, u32[]{:S(2)}, u32[]{:S(2)}) collective-permute-start(bf16[576,512]{1,0:T(8,128)(2,1)S(1)} %get-tuple-element.40.refs_0_), channel_id=1, source_target_pairs={{0,16},{16,0},{1,17},{17,1},{2,18},{18,2},{3,19},{19,3},{4,20},{20... | collective-permute-start | bytes 1769480 | tf_op jit(solution)/shard_map/ppermute | solution.py:319
  21.4 2.8 %collective-permute-start.7 = (bf16[576,512]{1,0:T(8,128)(2,1)S(1)}, bf16[576,512]{1,0:T(8,128)(2,1)S(1)}, u32[]{:S(2)}, u32[]{:S(2)}) collective-permute-start(bf16[576,512]{1,0:T(8,128)(2,1)S(1)} %get-tuple-element.41.refs_1_), channel_id=1, source_target_pairs={{0,16},{16,0},{1,17},{17,1},{2,18},{18,2},{3,19},{19,3},{4,20},{20... | collective-permute-start | bytes 1769480 | tf_op jit(solution)/shard_map/ppermute | solution.py:319
  24.3 12.4 %copy-start.4 = (bf16[128,512]{1,0:T(8,128)(2,1)S(1)}, bf16[128,512]{1,0:T(8,128)(2,1)}, u32[]{:S(2)}) copy-start(bf16[128,512]{1,0:T(8,128)(2,1)} %refs_5_.1) | copy-start | bytes 393220
  24.3 12.4 %copy-start.5 = (bf16[1,64,128]{2,1,0:T(8,128)(2,1)S(1)}, bf16[1,64,128]{2,1,0:T(8,128)(2,1)}, u32[]{:S(2)}) copy-start(bf16[1,64,128]{2,1,0:T(8,128)(2,1)} %param.14) | copy-start | bytes 49156
  31.5 9.0 %collective-permute-start.10 = (bf16[128,640]{1,0:T(8,128)(2,1)S(1)}, bf16[128,640]{1,0:T(8,128)(2,1)S(1)}, u32[]{:S(2)}, u32[]{:S(2)}) collective-permute-start(bf16[128,640]{1,0:T(8,128)(2,1)S(1)} %get-tuple-element.45), channel_id=1, source_target_pairs={{0,96},{32,64},{64,32},{96,0},{1,97},{33,65},{65,33},{97,1},{2,98}... | collective-permute-start | bytes 491528 | tf_op jit(solution)/shard_map/ppermute | solution.py:319
  35.1 7.1 %collective-permute-start.8 = (bf16[128,640]{1,0:T(8,128)(2,1)S(1)}, bf16[128,640]{1,0:T(8,128)(2,1)S(1)}, u32[]{:S(2)}, u32[]{:S(2)}) collective-permute-start(bf16[128,640]{1,0:T(8,128)(2,1)S(1)} %get-tuple-element.43), channel_id=1, source_target_pairs={{0,32},{32,0},{64,96},{96,64},{1,33},{33,1},{65,97},{97,65},{2,34}... | collective-permute-start | bytes 491528 | tf_op jit(solution)/shard_map/ppermute | solution.py:319
  35.1 9.8 %collective-permute-start.9 = (bf16[128,640]{1,0:T(8,128)(2,1)S(1)}, bf16[128,640]{1,0:T(8,128)(2,1)S(1)}, u32[]{:S(2)}, u32[]{:S(2)}) collective-permute-start(bf16[128,640]{1,0:T(8,128)(2,1)S(1)} %get-tuple-element.44), channel_id=1, source_target_pairs={{0,64},{32,96},{64,0},{96,32},{1,65},{33,97},{65,1},{97,33},{2,66}... | collective-permute-start | bytes 491528 | tf_op jit(solution)/shard_map/ppermute | solution.py:319
  45.0 15.3 %collective-permute-start.19 = (bf16[448,512]{1,0:T(8,128)(2,1)S(1)}, bf16[448,512]{1,0:T(8,128)(2,1)S(1)}, u32[]{:S(2)}, u32[]{:S(2)}) collective-permute-start(bf16[448,512]{1,0:T(8,128)(2,1)S(1)} %slice_bitcast_fusion.1), channel_id=1, source_target_pairs={{0,128},{1,129},{128,0},{129,1},{2,130},{3,131},{130,2},{131,3},{4... | collective-permute-start | bytes 1376264 | tf_op jit(solution)/shard_map/ppermute | solution.py:319
  45.1 15.5 %collective-permute-start.20 = (bf16[448,512]{1,0:T(8,128)(2,1)S(1)}, bf16[448,512]{1,0:T(8,128)(2,1)S(1)}, u32[]{:S(2)}, u32[]{:S(2)}) collective-permute-start(bf16[448,512]{1,0:T(8,128)(2,1)S(1)} %slice_bitcast_fusion), channel_id=1, source_target_pairs={{0,129},{1,128},{128,1},{129,0},{2,131},{3,130},{130,3},{131,2},{4... | collective-permute-start | bytes 1376264 | tf_op jit(solution)/shard_map/ppermute | solution.py:319
  49.7 10.5 %collective-permute-start.11 = (bf16[32,512]{1,0:T(8,128)(2,1)S(1)}, bf16[32,512]{1,0:T(8,128)(2,1)S(1)}, u32[]{:S(2)}, u32[]{:S(2)}) collective-permute-start(bf16[32,512]{1,0:T(8,128)(2,1)S(1)} %get-tuple-element.47), channel_id=1, source_target_pairs={{0,1},{1,0},{2,3},{3,2},{4,5},{5,4},{6,7},{7,6},{8,9},{9,8},{10,11... | collective-permute-start | bytes 98312 | tf_op jit(solution)/shard_map/ppermute | solution.py:319
  50.4 9.8 %collective-permute-start.12 = (bf16[32,512]{1,0:T(8,128)(2,1)S(1)}, bf16[32,512]{1,0:T(8,128)(2,1)S(1)}, u32[]{:S(2)}, u32[]{:S(2)}) collective-permute-start(bf16[32,512]{1,0:T(8,128)(2,1)S(1)} %get-tuple-element.48), channel_id=1, source_target_pairs={{0,2},{1,3},{2,0},{3,1},{4,6},{5,7},{6,4},{7,5},{8,10},{9,11},{10,... | collective-permute-start | bytes 98312 | tf_op jit(solution)/shard_map/ppermute | solution.py:319
  51.9 8.3 %collective-permute-start.13 = (bf16[32,512]{1,0:T(8,128)(2,1)S(1)}, bf16[32,512]{1,0:T(8,128)(2,1)S(1)}, u32[]{:S(2)}, u32[]{:S(2)}) collective-permute-start(bf16[32,512]{1,0:T(8,128)(2,1)S(1)} %get-tuple-element.49), channel_id=1, source_target_pairs={{0,3},{1,2},{2,1},{3,0},{4,7},{5,6},{6,5},{7,4},{8,11},{9,10},{10,... | collective-permute-start | bytes 98312 | tf_op jit(solution)/shard_map/ppermute | solution.py:319
  60.8 14.1 %collective-permute-start.21 = (bf16[6,448,512]{2,1,0:T(8,128)(2,1)S(1)}, bf16[6,448,512]{2,1,0:T(8,128)(2,1)S(1)}, u32[]{:S(2)}, u32[]{:S(2)}) collective-permute-start(bf16[6,448,512]{2,1,0:T(8,128)(2,1)S(1)} %rest.1.refs_5_), channel_id=1, source_target_pairs={{0,16},{16,0},{1,17},{17,1},{2,18},{18,2},{3,19},{19,3},{4,20},{20... | collective-permute-start | bytes 8257544 | tf_op jit(solution)/shard_map/ppermute | solution.py:319
  60.9 6.4 %collective-permute-start.14 = (bf16[32,2048]{1,0:T(8,128)(2,1)S(1)}, bf16[32,2048]{1,0:T(8,128)(2,1)S(1)}, u32[]{:S(2)}, u32[]{:S(2)}) collective-permute-start(bf16[32,2048]{1,0:T(8,128)(2,1)S(1)} %join.1.refs_4_.refs_0_), channel_id=1, source_target_pairs={{0,32},{32,0},{64,96},{96,64},{1,33},{33,1},{65,97},{97,65},{2,34}... | collective-permute-start | bytes 393224 | tf_op jit(solution)/shard_map/ppermute | solution.py:319
  61.2 11.3 %collective-permute-start.15 = (bf16[32,2048]{1,0:T(8,128)(2,1)S(1)}, bf16[32,2048]{1,0:T(8,128)(2,1)S(1)}, u32[]{:S(2)}, u32[]{:S(2)}) collective-permute-start(bf16[32,2048]{1,0:T(8,128)(2,1)S(1)} %join.1.refs_4_.refs_0_), channel_id=1, source_target_pairs={{0,64},{32,96},{64,0},{96,32},{1,65},{33,97},{65,1},{97,33},{2,66}... | collective-permute-start | bytes 393224 | tf_op jit(solution)/shard_map/ppermute | solution.py:319
  65.7 9.1 %collective-permute-start.16 = (bf16[32,2048]{1,0:T(8,128)(2,1)S(1)}, bf16[32,2048]{1,0:T(8,128)(2,1)S(1)}, u32[]{:S(2)}, u32[]{:S(2)}) collective-permute-start(bf16[32,2048]{1,0:T(8,128)(2,1)S(1)} %join.1.refs_4_.refs_0_), channel_id=1, source_target_pairs={{0,96},{32,64},{64,32},{96,0},{1,97},{33,65},{65,33},{97,1},{2,98}... | collective-permute-start | bytes 393224 | tf_op jit(solution)/shard_map/ppermute | solution.py:319
  77.8 8.9 %collective-permute-start.22 = (bf16[32,1792]{1,0:T(8,128)(2,1)S(1)}, bf16[32,1792]{1,0:T(8,128)(2,1)S(1)}, u32[]{:S(2)}, u32[]{:S(2)}) collective-permute-start(bf16[32,1792]{1,0:T(8,128)(2,1)S(1)} %get-tuple-element.58), channel_id=1, source_target_pairs={{0,4},{4,0},{8,12},{12,8},{1,5},{5,1},{9,13},{13,9},{2,6},{6,2},{1... | collective-permute-start | bytes 344072 | tf_op jit(solution)/shard_map/ppermute | solution.py:319
  81.2 12.5 %collective-permute-start.23 = (bf16[32,1792]{1,0:T(8,128)(2,1)S(1)}, bf16[32,1792]{1,0:T(8,128)(2,1)S(1)}, u32[]{:S(2)}, u32[]{:S(2)}) collective-permute-start(bf16[32,1792]{1,0:T(8,128)(2,1)S(1)} %get-tuple-element.59), channel_id=1, source_target_pairs={{0,8},{4,12},{8,0},{12,4},{1,9},{5,13},{9,1},{13,5},{2,10},{6,14},... | collective-permute-start | bytes 344072 | tf_op jit(solution)/shard_map/ppermute | solution.py:319
  85.7 9.5 %collective-permute-start.24 = (bf16[32,1792]{1,0:T(8,128)(2,1)S(1)}, bf16[32,1792]{1,0:T(8,128)(2,1)S(1)}, u32[]{:S(2)}, u32[]{:S(2)}) collective-permute-start(bf16[32,1792]{1,0:T(8,128)(2,1)S(1)} %get-tuple-element.60), channel_id=1, source_target_pairs={{0,12},{4,8},{8,4},{12,0},{1,13},{5,9},{9,5},{13,1},{2,14},{6,10},... | collective-permute-start | bytes 344072 | tf_op jit(solution)/shard_map/ppermute | solution.py:319
  95.3 4.8 %collective-permute-start.25 = (f32[8,1792]{1,0:T(8,128)S(1)}, f32[8,1792]{1,0:T(8,128)S(1)}, u32[]{:S(2)}, u32[]{:S(2)}) collective-permute-start(f32[8,1792]{1,0:T(8,128)S(1)} %get-tuple-element.62), channel_id=1, source_target_pairs={{0,32},{32,0},{64,96},{96,64},{1,33},{33,1},{65,97},{97,65},{2,34}... | collective-permute-start | bytes 172040 | tf_op jit(solution)/shard_map/ppermute | solution.py:319
  95.4 5.8 %collective-permute-start.26 = (f32[8,1792]{1,0:T(8,128)S(1)}, f32[8,1792]{1,0:T(8,128)S(1)}, u32[]{:S(2)}, u32[]{:S(2)}) collective-permute-start(f32[8,1792]{1,0:T(8,128)S(1)} %get-tuple-element.63), channel_id=1, source_target_pairs={{0,64},{32,96},{64,0},{96,32},{1,65},{33,97},{65,1},{97,33},{2,66}... | collective-permute-start | bytes 172040 | tf_op jit(solution)/shard_map/ppermute | solution.py:319
  97.2 5.4 %collective-permute-start.27 = (f32[8,1792]{1,0:T(8,128)S(1)}, f32[8,1792]{1,0:T(8,128)S(1)}, u32[]{:S(2)}, u32[]{:S(2)}) collective-permute-start(f32[8,1792]{1,0:T(8,128)S(1)} %get-tuple-element.64), channel_id=1, source_target_pairs={{0,96},{32,64},{64,32},{96,0},{1,97},{33,65},{65,33},{97,1},{2,98}... | collective-permute-start | bytes 172040 | tf_op jit(solution)/shard_map/ppermute | solution.py:319

commit v9 on v7

--- a/solution.py
+++ b/solution.py
@@ -228,6 +228,33 @@
         refs[4][:, d * 512 : (d + 1) * 512] = refs[d][...]
 
 
+def pack_kernel(q_nope, q_rope, pool_latent, pool_rope, query, pool, sems):
+    moves = [(q_nope, query.at[:, : HEADS * NOPE]), (q_rope, query.at[:, HEADS * NOPE :])]
+    for i in range(4):
+        moves.append((pool_latent.at[i], pool.at[i * BLOCK : (i + 1) * BLOCK, :]))
+        moves.append((pool_rope.at[i], pool.at[4 * BLOCK :, i * BLOCK : (i + 1) * BLOCK]))
+    copies = [pltpu.make_async_copy(src, dst, sems.at[i]) for i, (src, dst) in enumerate(moves)]
+    for copy in copies:
+        copy.start()
+    for copy in copies:
+        copy.wait()
+
+
+def pack(*args):
+    return pl.pallas_call(
+        pack_kernel,
+        out_shape=[
+            jax.ShapeDtypeStruct((TOK, HEADS * (NOPE + ROPE)), jnp.bfloat16),
+            jax.ShapeDtypeStruct((4 * BLOCK + ROPE, LAT), jnp.bfloat16),
+        ],
+        in_specs=[pl.BlockSpec(memory_space=pltpu.HBM)] * 4,
+        out_specs=[pl.BlockSpec(memory_space=VMEM)] * 2,
+        scratch_shapes=[pltpu.SemaphoreType.DMA((10,))],
+        compiler_params=pltpu.CompilerParams(vmem_limit_bytes=56 * 2**20),
+        name="pack",
+    )(*args)
+
+
 def pair_kernel(one, two, out):
     out[0] = one[...]
     out[1] = two[...]
@@ -253,10 +280,10 @@
             for d in range(4):
                 m, dz = side_y * 2 + (d & 1), d >> 1
                 weight = pieces[0][dz] if m == 0 else pieces[1][(0, 4, 0, 2)[m] + dz]
-                part = dot_nt(rows[:, d * 512 : (d + 1) * 512], weight)
+                part = dot_nt(weight, rows[:, d * 512 : (d + 1) * 512])
                 value = part if value is None else value + part
             sides.append(value)
-        total[:, side_y * 896 : (side_y + 1) * 896] = jnp.concatenate(sides, axis=1)
+        total[:, side_y * 896 : (side_y + 1) * 896] = jnp.concatenate(sides, axis=0).T
     for d in range(4):
         first = pl.multiple_of(((zb + d) % 4) * 8, 8)
         parts = [total[pl.ds(first + s * 32, 8), :] for s in range(4)]
@@ -341,17 +368,14 @@
             lax.axis_index("z0") * 2 + lax.axis_index("yh"),
         ]
     ).astype(jnp.int32)
-    query = jnp.concatenate([q_nope, q_rope], axis=1)
-    pool = jnp.concatenate(
-        [pool_latent.reshape(4 * BLOCK, LAT), jnp.transpose(pool_rope, (1, 0, 2)).reshape(ROPE, 4 * BLOCK)], axis=0
-    )
+    query, pool = pack(q_nope, q_rope, pool_latent, pool_rope)
     weight = w_out.T
 
     queries = [query] + [turn(query, "x", 4, s) for s in (1, 2, 3)]
     pool_y = flip(pool, "yl", 2, 1)
     weight_z = flip(weight, "z0", 2, 1)
     lists, counts = plan(ids, block_table, prefix_len)
-    pool, pool_y, counts, weight_z = tie([pool, pool_y, counts, weight_z], queries[1:])
+    pool_y, counts, weight_z = tie([pool_y, counts, weight_z], queries[1:])
     q_lat, q_rot = simple(
         prepare_kernel,
         "prepare",

time: 104 us -> 102 us (0.981)
  Pallas kernels: 20.7 us -> 23.9 us
  starting transfers between devices: 44.6 us -> 41.9 us
  local copies, waits for them, and re-layouts: 4.12 us -> 1.52 us
  waiting for transfers between devices: 32.2 us -> 34.3 us
  other arithmetic: 1.08 us -> 0 us
    ppermute x3, starting transfers between devices: 6.77 us -> 4.16 us  [local(): lax.ppermute(part, 'x', [(i, (i + s) % 4) for i in range(4)])]
    pallas_call x0 -> x1, Pallas kernels: none -> 2.27 us  [pack(): pl.pallas_call(pack_kernel, out_shape=[jax.ShapeDtypeStruct((TOK, HEADS *...]
    ppermute x13, waiting for transfers between devices: 7.35 us -> 9.5 us  [flip(): return lax.ppermute(value, axis, [(i, i ^ bits) for i in range(size)])]
    unnamed x17 -> x18, local copies, waits for them, and re-layouts: 3.12 us -> 1.38 us
    pallas_call x2, Pallas kernels: 11.1 us -> 12.2 us  [attention(): pl.pallas_call(functools.partial(attention_kernel, slots, own), out_shape...]
    concatenate x1 -> x0, other arithmetic: 1.08 us -> none  [local(): jnp.concatenate([pool_latent.reshape(4 * BLOCK, LAT), jnp.transpose(pool_...]
  transfers between devices with their start and end apart: 28 -> 28, of which waited for: 13 -> 15; matrix products, arithmetic and copies ran while one was open for 2% -> 0% of each run, Pallas kernels for 16% -> 17%
where the time goes in v9:
time: 102 us
  starting transfers between devices  41.9 us (41%)
  waiting for transfers between devices  34.3 us (34%)
  Pallas kernels  23.9 us (23%)
  local copies, waits for them, and re-layouts  1.52 us (1%)
    ppermute x13, starting transfers between devices, flip(): return lax.ppermute(value, axis, [(i, i ^ bits) for i in range(size)])  14.5 us
    pallas_call x2, Pallas kernels, attention(): pl.pallas_call(functools.partial(attention_kernel, slots, own), out_shape...  12.2 us
    ppermute x3, starting transfers between devices, local(): lax.ppermute(partial[d], 'zb', [(i, (i + d) % 4) for i in range(4)])  11.3 us
    ppermute x6, waiting for transfers between devices, turn(): lax.ppermute(value, axis, [((i + shift) % size, i) for i in range(size)])  10.4 us
    ppermute x13, waiting for transfers between devices, flip(): return lax.ppermute(value, axis, [(i, i ^ bits) for i in range(size)])  9.5 us
    ppermute x6, starting transfers between devices, turn(): lax.ppermute(value, axis, [((i + shift) % size, i) for i in range(size)])  8.31 us
    ppermute x3, waiting for transfers between devices, local(): lax.ppermute(partial[d], 'zb', [(i, (i + d) % 4) for i in range(4)])  7.93 us
    pallas_call x8, Pallas kernels, simple(): pl.pallas_call(kernel, out_shape=out_shape, in_specs=[pl.BlockSpec(memory...  6.71 us
  transfers between devices with their start and end apart: 28, of which 15 were waited for; matrix products, arithmetic and copies ran while one was open for 0% of the time, Pallas kernels for 17%

profile of v9, /device:TPU:6, one launch (start us, length us, event | category | flops | bytes accessed | tf_op | source)
XLA Modules:
  0.0 101.8 jit_solution(13122160296414602217)
XLA Ops:
  0.0 2.3 %pack.1 = (bf16[128,768]{1,0:T(8,128)(2,1)}, bf16[576,512]{1,0:T(8,128)(2,1)}) custom-call(bf16[128,512]{1,0:T(8,128)(2,1)} %q_nope.1, bf16[128,256]{1,0:T(8,128)(2,1)} %q_rope.1, bf16[4,128,512]{2,1,0:T(8,128)(2,1)} %pool_latent.1, bf16[4,64,128]{2,1,0:T(8,128)(2,1)} %pool_rope.1), custom_call_target="tpu_custom_call" | custom-call | tf_op jit(solution)/shard_map/pack/pallas_call | solution.py:244
  2.3 1.7 %collective-permute-start = (bf16[576,512]{1,0:T(8,128)(2,1)}, bf16[576,512]{1,0:T(8,128)(2,1)S(1)}, u32[]{:S(2)}, u32[]{:S(2)}) collective-permute-start(bf16[576,512]{1,0:T(8,128)(2,1)} %get-tuple-element.38.refs_0_), channel_id=1, source_target_pairs={{0,128},{128,0},{1,129},{129,1},{2,130},{130,2},{3,131},{131,3},{4... | collective-permute-start | bytes 1769480 | tf_op jit(solution)/shard_map/ppermute | solution.py:346
  4.0 1.9 %collective-permute-start.1 = (bf16[448,512]{1,0:T(8,128)(2,1)}, bf16[448,512]{1,0:T(8,128)(2,1)S(1)}, u32[]{:S(2)}, u32[]{:S(2)}) collective-permute-start(bf16[448,512]{1,0:T(8,128)(2,1)} %bitcast.11), channel_id=1, source_target_pairs={{0,2},{2,0},{1,3},{3,1},{4,6},{6,4},{5,7},{7,5},{8,10},{10,8},{9,1... | collective-permute-start | bytes 1376264 | tf_op jit(solution)/shard_map/ppermute | solution.py:346
  5.9 0.8 collective-permute-start.2
  6.7 1.1 %collective-permute-start.3 = (bf16[128,768]{1,0:T(8,128)(2,1)}, bf16[128,768]{1,0:T(8,128)(2,1)S(1)}, u32[]{:S(2)}, u32[]{:S(2)}) collective-permute-start(bf16[128,768]{1,0:T(8,128)(2,1)} %get-tuple-element.40.refs_0_), channel_id=1, source_target_pairs={{64,0},{96,32},{0,64},{32,96},{65,1},{97,33},{1,65},{33,97},{66,2}... | collective-permute-start | bytes 589832 | tf_op jit(solution)/shard_map/ppermute | solution.py:342
  7.8 2.1 %collective-permute-start.4 = (bf16[128,768]{1,0:T(8,128)(2,1)}, bf16[128,768]{1,0:T(8,128)(2,1)S(1)}, u32[]{:S(2)}, u32[]{:S(2)}) collective-permute-start(bf16[128,768]{1,0:T(8,128)(2,1)} %get-tuple-element.40.refs_0_), channel_id=1, source_target_pairs={{96,0},{0,32},{32,64},{64,96},{97,1},{1,33},{33,65},{65,97},{98,2}... | collective-permute-start | bytes 589832 | tf_op jit(solution)/shard_map/ppermute | solution.py:342
  9.9 0.1 stack.23.ids
  10.0 0.7 copy-done.7
  10.7 0.7 copy-done.8
  11.4 2.6 %plan.1 = (s32[64]{0:T(128)S(1)}, s32[8]{0:T(128)S(1)}) custom-call(s32[5]{0:T(128)S(1)} %stack.23.ids, s32[16,32]{1,0:T(8,128)S(1)} %copy-done.7, s32[16]{0:T(128)S(1)} %copy-done.8), custom_call_target="tpu_custom_call" | custom-call | tf_op jit(solution)/shard_map/plan/pallas_call | solution.py:65
  14.0 3.6 %collective-permute-done.2.refs_3_.refs_1_ = bf16[128,768]{1,0:T(8,128)(2,1)S(1)} collective-permute-done((bf16[128,768]{1,0:T(8,128)(2,1)}, bf16[128,768]{1,0:T(8,128)(2,1)S(1)}, u32[]{:S(2)}, u32[]{:S(2)}) %collective-permute-start.2) | collective-permute-done | bytes 196640 | tf_op jit(solution)/shard_map/ppermute | solution.py:342
  17.6 0.0 collective-permute-done.3.refs_4_.refs_2_
  17.6 0.6 collective-permute-done.4.refs_5_.refs_3_
  18.2 0.0 collective-permute-done.refs_0_
  18.3 0.1 pair.1.refs_4_
  18.3 0.1 collective-permute-start.6
  18.4 1.1 %collective-permute-start.17 = (bf16[2,448,512]{2,1,0:T(8,128)(2,1)S(1)}, bf16[2,448,512]{2,1,0:T(8,128)(2,1)S(1)}, u32[]{:S(2)}, u32[]{:S(2)}) collective-permute-start(bf16[2,448,512]{2,1,0:T(8,128)(2,1)S(1)} %pair.1.refs_4_), channel_id=1, source_target_pairs={{0,128},{1,129},{128,0},{129,1},{2,130},{3,131},{130,2},{131,3},{4... | collective-permute-start | bytes 2752520 | tf_op jit(solution)/shard_map/ppermute | solution.py:346
  19.5 2.5 %collective-permute-start.18 = (bf16[2,448,512]{2,1,0:T(8,128)(2,1)S(1)}, bf16[2,448,512]{2,1,0:T(8,128)(2,1)S(1)}, u32[]{:S(2)}, u32[]{:S(2)}) collective-permute-start(bf16[2,448,512]{2,1,0:T(8,128)(2,1)S(1)} %pair.1.refs_4_), channel_id=1, source_target_pairs={{0,129},{1,128},{128,1},{129,0},{2,131},{3,130},{130,3},{131,2},{4... | collective-permute-start | bytes 2752520 | tf_op jit(solution)/shard_map/ppermute | solution.py:346
  22.0 0.5 collective-permute-start.7
  22.5 1.3 %prepare.1 = (bf16[4,512,512]{2,1,0:T(8,128)(2,1)S(1)}, bf16[4,512,64]{2,1,0:T(8,128)(2,1)S(1)}) custom-call(s32[8]{0:T(128)S(1)} %get-tuple-element.41.counts, bf16[128,768]{1,0:T(8,128)(2,1)S(1)} %copy-done.4, bf16[128,768]{1,0:T(8,128)(2,1)S(1)} %collective-permute-done.2.refs_3_.refs_1_, bf16[128,768]{1,0:T(8,128)(2,1)S(1)} %collective-permute-done.3.refs_4_.refs_2_, ...), custom_call_target="tpu_custom_call" | custom-call | tf_op jit(solution)/shard_map/prepare/pallas_call | solution.py:330
  23.8 0.2 collective-permute-done.5.refs_0_
  24.0 0.8 collective-permute-done.7.refs_3_
  24.8 8.4 %attend.3 = (bf16[128,640]{1,0:T(8,128)(2,1)S(1)}, bf16[128,640]{1,0:T(8,128)(2,1)S(1)}, bf16[128,640]{1,0:T(8,128)(2,1)S(1)}) custom-call(s32[64]{0:T(128)S(1)} %get-tuple-element.37.lists, s32[8]{0:T(128)S(1)} %get-tuple-element.41.counts, bf16[4,512,512]{2,1,0:T(8,128)(2,1)S(1)} %get-tuple-element.42.q_lat, ...), custom_call_target="tpu_custom_call" | custom-call | tf_op jit(solution)/shard_map/attend/pallas_call | solution.py:185
  33.2 0.1 collective-permute-start.10
  33.3 3.2 %collective-permute-start.8 = (bf16[128,640]{1,0:T(8,128)(2,1)S(1)}, bf16[128,640]{1,0:T(8,128)(2,1)S(1)}, u32[]{:S(2)}, u32[]{:S(2)}) collective-permute-start(bf16[128,640]{1,0:T(8,128)(2,1)S(1)} %get-tuple-element.47), channel_id=1, source_target_pairs={{0,32},{32,64},{64,96},{96,0},{1,33},{33,65},{65,97},{97,1},{2,34}... | collective-permute-start | bytes 491528 | tf_op jit(solution)/shard_map/ppermute | solution.py:401
  36.5 0.9 collective-permute-start.9
  37.4 3.9 %attend.2.refs_0_.refs_5_ = bf16[128,640]{1,0:T(8,128)(2,1)S(1)} custom-call(s32[64]{0:T(128)S(1)} %get-tuple-element.37.lists, s32[8]{0:T(128)S(1)} %get-tuple-element.41.counts, bf16[4,512,512]{2,1,0:T(8,128)(2,1)S(1)} %get-tuple-element.42.q_lat, bf16[4,512,64]{2,1,0:T(8,128)(2,1)S(1)} %get-tuple-element.43.q_rot, bf16[576,512]{1,0:T(8,128)(2,1)S(1)} %copy-done, ...), custom_call_target="tpu_custom_call" | custom-call | tf_op jit(solution)/shard_map/attend/pallas_call | solution.py:185
  41.3 0.0 collective-permute-done.17.refs_0_
  41.3 1.8 %collective-permute-done.18.refs_1_ = bf16[2,448,512]{2,1,0:T(8,128)(2,1)S(1)} collective-permute-done((bf16[2,448,512]{2,1,0:T(8,128)(2,1)S(1)}, bf16[2,448,512]{2,1,0:T(8,128)(2,1)S(1)}, u32[]{:S(2)}, u32[]{:S(2)}) %collective-permute-start.18) | collective-permute-done | bytes 917536 | tf_op jit(solution)/shard_map/ppermute | solution.py:346
  43.1 1.1 %collective-permute-done.9.refs_2_.refs_3_ = bf16[128,640]{1,0:T(8,128)(2,1)S(1)} collective-permute-done((bf16[128,640]{1,0:T(8,128)(2,1)S(1)}, bf16[128,640]{1,0:T(8,128)(2,1)S(1)}, u32[]{:S(2)}, u32[]{:S(2)}) %collective-permute-start.9) | collective-permute-done | bytes 163872 | tf_op jit(solution)/shard_map/ppermute | solution.py:401
  44.2 0.1 collective-permute-start.19
  44.4 1.5 %collective-permute-start.20 = (bf16[448,512]{1,0:T(8,128)(2,1)S(1)}, bf16[448,512]{1,0:T(8,128)(2,1)S(1)}, u32[]{:S(2)}, u32[]{:S(2)}) collective-permute-start(bf16[448,512]{1,0:T(8,128)(2,1)S(1)} %slice_bitcast_fusion), channel_id=1, source_target_pairs={{0,129},{1,128},{128,1},{129,0},{2,131},{3,130},{130,3},{131,2},{4... | collective-permute-start | bytes 1376264 | tf_op jit(solution)/shard_map/ppermute | solution.py:346
  45.9 1.1 %combine.1 = (bf16[32,512]{1,0:T(8,128)(2,1)S(1)}, bf16[32,512]{1,0:T(8,128)(2,1)S(1)}, bf16[32,512]{1,0:T(8,128)(2,1)S(1)}, bf16[32,512]{1,0:T(8,128)(2,1)S(1)}) custom-call(s32[5]{0:T(128)S(1)} %stack.23.ids, bf16[128,640]{1,0:T(8,128)(2,1)S(1)} %attend.2.refs_0_.refs_5_, bf16[128,640]{1,0:T(8,128)(2,1)S(1)} %collective-permute-done.8.refs_1_.refs_2_, ...), custom_call_target="tpu_custom_call" | custom-call | tf_op jit(solution)/shard_map/combine/pallas_call | solution.py:330
  47.0 2.7 %collective-permute-start.11 = (bf16[32,512]{1,0:T(8,128)(2,1)S(1)}, bf16[32,512]{1,0:T(8,128)(2,1)S(1)}, u32[]{:S(2)}, u32[]{:S(2)}) collective-permute-start(bf16[32,512]{1,0:T(8,128)(2,1)S(1)} %get-tuple-element.51), channel_id=1, source_target_pairs={{0,1},{1,0},{2,3},{3,2},{4,5},{5,4},{6,7},{7,6},{8,9},{9,8},{10,11... | collective-permute-start | bytes 98312 | tf_op jit(solution)/shard_map/ppermute | solution.py:346
  49.7 0.9 collective-permute-start.12
  50.6 1.5 %collective-permute-start.13 = (bf16[32,512]{1,0:T(8,128)(2,1)S(1)}, bf16[32,512]{1,0:T(8,128)(2,1)S(1)}, u32[]{:S(2)}, u32[]{:S(2)}) collective-permute-start(bf16[32,512]{1,0:T(8,128)(2,1)S(1)} %get-tuple-element.53), channel_id=1, source_target_pairs={{0,3},{1,2},{2,1},{3,0},{4,7},{5,6},{6,5},{7,4},{8,11},{9,10},{10,... | collective-permute-start | bytes 98312 | tf_op jit(solution)/shard_map/ppermute | solution.py:346
  52.0 6.3 %collective-permute-done.11.refs_1_ = bf16[32,512]{1,0:T(8,128)(2,1)S(1)} collective-permute-done((bf16[32,512]{1,0:T(8,128)(2,1)S(1)}, bf16[32,512]{1,0:T(8,128)(2,1)S(1)}, u32[]{:S(2)}, u32[]{:S(2)}) %collective-permute-start.11) | collective-permute-done | bytes 32800 | tf_op jit(solution)/shard_map/ppermute | solution.py:346
  58.4 0.0 collective-permute-done.12.refs_2_
  58.4 0.0 collective-permute-done.13.refs_3_
  58.4 0.0 collective-permute-done.19.refs_2_
  58.4 0.3 collective-permute-done.20.refs_3_
  58.7 0.2 rest.1.refs_5_
  58.9 0.1 collective-permute-start.21
  59.0 1.5 %collective-permute-start.14 = (bf16[32,2048]{1,0:T(8,128)(2,1)S(1)}, bf16[32,2048]{1,0:T(8,128)(2,1)S(1)}, u32[]{:S(2)}, u32[]{:S(2)}) collective-permute-start(bf16[32,2048]{1,0:T(8,128)(2,1)S(1)} %join.1.refs_4_.refs_0_), channel_id=1, source_target_pairs={{32,0},{64,32},{96,64},{0,96},{33,1},{65,33},{97,65},{1,97},{34,2}... | collective-permute-start | bytes 393224 | tf_op jit(solution)/shard_map/ppermute | solution.py:342
  60.5 2.4 %collective-permute-start.15 = (bf16[32,2048]{1,0:T(8,128)(2,1)S(1)}, bf16[32,2048]{1,0:T(8,128)(2,1)S(1)}, u32[]{:S(2)}, u32[]{:S(2)}) collective-permute-start(bf16[32,2048]{1,0:T(8,128)(2,1)S(1)} %join.1.refs_4_.refs_0_), channel_id=1, source_target_pairs={{64,0},{96,32},{0,64},{32,96},{65,1},{97,33},{1,65},{33,97},{66,2}... | collective-permute-start | bytes 393224 | tf_op jit(solution)/shard_map/ppermute | solution.py:342
  62.8 0.4 collective-permute-start.16
  63.2 2.9 %collective-permute-done.14.refs_1_ = bf16[32,2048]{1,0:T(8,128)(2,1)S(1)} collective-permute-done((bf16[32,2048]{1,0:T(8,128)(2,1)S(1)}, bf16[32,2048]{1,0:T(8,128)(2,1)S(1)}, u32[]{:S(2)}, u32[]{:S(2)}) %collective-permute-start.14) | collective-permute-done | bytes 131104 | tf_op jit(solution)/shard_map/ppermute | solution.py:342
  66.1 3.4 %collective-permute-done.15.refs_2_ = bf16[32,2048]{1,0:T(8,128)(2,1)S(1)} collective-permute-done((bf16[32,2048]{1,0:T(8,128)(2,1)S(1)}, bf16[32,2048]{1,0:T(8,128)(2,1)S(1)}, u32[]{:S(2)}, u32[]{:S(2)}) %collective-permute-start.15) | collective-permute-done | bytes 131104 | tf_op jit(solution)/shard_map/ppermute | solution.py:342
  69.5 0.0 collective-permute-done.16.refs_3_
  69.5 0.0 collective-permute-done.21.refs_7_
  69.5 2.8 %project.1 = (bf16[32,1792]{1,0:T(8,128)(2,1)S(1)}, bf16[32,1792]{1,0:T(8,128)(2,1)S(1)}, bf16[32,1792]{1,0:T(8,128)(2,1)S(1)}, bf16[32,1792]{1,0:T(8,128)(2,1)S(1)}) custom-call(s32[5]{0:T(128)S(1)} %stack.23.ids, bf16[32,2048]{1,0:T(8,128)(2,1)S(1)} %join.1.refs_4_.refs_0_, bf16[32,2048]{1,0:T(8,128)(2,1)S(1)} %collective-permute-done.14.refs_1_, ...), custom_call_target="tpu_custom_call" | custom-call | tf_op jit(solution)/shard_map/project/pallas_call | solution.py:330
  72.2 3.4 %collective-permute-start.22 = (bf16[32,1792]{1,0:T(8,128)(2,1)S(1)}, bf16[32,1792]{1,0:T(8,128)(2,1)S(1)}, u32[]{:S(2)}, u32[]{:S(2)}) collective-permute-start(bf16[32,1792]{1,0:T(8,128)(2,1)S(1)} %get-tuple-element.62), channel_id=1, source_target_pairs={{0,4},{4,8},{8,12},{12,0},{1,5},{5,9},{9,13},{13,1},{2,6},{6,10},{... | collective-permute-start | bytes 344072 | tf_op jit(solution)/shard_map/ppermute | solution.py:429
  75.6 5.3 %collective-permute-start.23 = (bf16[32,1792]{1,0:T(8,128)(2,1)S(1)}, bf16[32,1792]{1,0:T(8,128)(2,1)S(1)}, u32[]{:S(2)}, u32[]{:S(2)}) collective-permute-start(bf16[32,1792]{1,0:T(8,128)(2,1)S(1)} %get-tuple-element.63), channel_id=1, source_target_pairs={{0,8},{4,12},{8,0},{12,4},{1,9},{5,13},{9,1},{13,5},{2,10},{6,14},... | collective-permute-start | bytes 344072 | tf_op jit(solution)/shard_map/ppermute | solution.py:429
  80.9 2.7 %collective-permute-start.24 = (bf16[32,1792]{1,0:T(8,128)(2,1)S(1)}, bf16[32,1792]{1,0:T(8,128)(2,1)S(1)}, u32[]{:S(2)}, u32[]{:S(2)}) collective-permute-start(bf16[32,1792]{1,0:T(8,128)(2,1)S(1)} %get-tuple-element.64), channel_id=1, source_target_pairs={{0,12},{4,0},{8,4},{12,8},{1,13},{5,1},{9,5},{13,9},{2,14},{6,2},{... | collective-permute-start | bytes 344072 | tf_op jit(solution)/shard_map/ppermute | solution.py:429
  83.6 5.1 %collective-permute-done.23.refs_2_ = bf16[32,1792]{1,0:T(8,128)(2,1)S(1)} collective-permute-done((bf16[32,1792]{1,0:T(8,128)(2,1)S(1)}, bf16[32,1792]{1,0:T(8,128)(2,1)S(1)}, u32[]{:S(2)}, u32[]{:S(2)}) %collective-permute-start.23) | collective-permute-done | bytes 114720 | tf_op jit(solution)/shard_map/ppermute | solution.py:429
  88.6 2.9 %collective-permute-done.24.refs_3_ = bf16[32,1792]{1,0:T(8,128)(2,1)S(1)} collective-permute-done((bf16[32,1792]{1,0:T(8,128)(2,1)S(1)}, bf16[32,1792]{1,0:T(8,128)(2,1)S(1)}, u32[]{:S(2)}, u32[]{:S(2)}) %collective-permute-start.24) | collective-permute-done | bytes 114720 | tf_op jit(solution)/shard_map/ppermute | solution.py:429
  91.5 0.1 share.1
  91.6 2.6 %collective-permute-start.25 = (f32[8,1792]{1,0:T(8,128)S(1)}, f32[8,1792]{1,0:T(8,128)S(1)}, u32[]{:S(2)}, u32[]{:S(2)}) collective-permute-start(f32[8,1792]{1,0:T(8,128)S(1)} %get-tuple-element.66), channel_id=1, source_target_pairs={{0,32},{32,64},{64,96},{96,0},{1,33},{33,65},{65,97},{97,1},{2,34}... | collective-permute-start | bytes 172040 | tf_op jit(solution)/shard_map/ppermute | solution.py:433
  94.2 0.8 collective-permute-start.26
  94.9 0.2 collective-permute-start.27
  95.1 1.7 %collective-permute-done.25.refs_1_ = f32[8,1792]{1,0:T(8,128)S(1)} collective-permute-done((f32[8,1792]{1,0:T(8,128)S(1)}, f32[8,1792]{1,0:T(8,128)S(1)}, u32[]{:S(2)}, u32[]{:S(2)}) %collective-permute-start.25) | collective-permute-done | bytes 57376 | tf_op jit(solution)/shard_map/ppermute | solution.py:433
  96.8 3.1 %collective-permute-done.26.refs_2_ = f32[8,1792]{1,0:T(8,128)S(1)} collective-permute-done((f32[8,1792]{1,0:T(8,128)S(1)}, f32[8,1792]{1,0:T(8,128)S(1)}, u32[]{:S(2)}, u32[]{:S(2)}) %collective-permute-start.26) | collective-permute-done | bytes 57376 | tf_op jit(solution)/shard_map/ppermute | solution.py:433
  99.9 0.6 collective-permute-done.27.refs_3_
  100.5 1.3 %place.1 = bf16[8,7168]{1,0:T(8,128)(2,1)} custom-call(s32[5]{0:T(128)S(1)} %stack.23.ids, f32[8,1792]{1,0:T(8,128)S(1)} %get-tuple-element.65.refs_0_, f32[8,1792]{1,0:T(8,128)S(1)} %collective-permute-done.25.refs_1_, f32[8,1792]{1,0:T(8,128)S(1)} %collective-permute-done.26.refs_2_, f32[8,1792]{1,0:T(8,128)S(1)} %collective-permute-done.27.refs_3_), custom_call_target="tpu_custom_call" | custom-call | tf_op jit(solution)/shard_map/place/pallas_call | solution.py:330
  (29 shorter events, 0.1 us)
Async XLA Ops:
  0.0 18.2 %copy-start.3 = (bf16[512,448]{0,1:T(8,128)(2,1)S(1)}, bf16[512,448]{0,1:T(8,128)(2,1)}, u32[]{:S(2)}) copy-start(bf16[512,448]{0,1:T(8,128)(2,1)} %param.21) | copy-start | bytes 1376260
  0.0 22.5 %copy-start.2 = (bf16[4,128,512]{2,1,0:T(8,128)(2,1)S(1)}, bf16[4,128,512]{2,1,0:T(8,128)(2,1)}, u32[]{:S(2)}) copy-start(bf16[4,128,512]{2,1,0:T(8,128)(2,1)} %refs_4_.3) | copy-start | bytes 1572868
  2.3 19.7 %copy-start = (bf16[576,512]{1,0:T(8,128)(2,1)S(1)}, bf16[576,512]{1,0:T(8,128)(2,1)}, u32[]{:S(2)}) copy-start(bf16[576,512]{1,0:T(8,128)(2,1)} %get-tuple-element.38.refs_0_) | copy-start | bytes 1769476
  2.3 20.2 %copy-start.4 = (bf16[128,768]{1,0:T(8,128)(2,1)S(1)}, bf16[128,768]{1,0:T(8,128)(2,1)}, u32[]{:S(2)}) copy-start(bf16[128,768]{1,0:T(8,128)(2,1)} %get-tuple-element.40.refs_0_) | copy-start | bytes 589828
  2.3 15.9 %collective-permute-start = (bf16[576,512]{1,0:T(8,128)(2,1)}, bf16[576,512]{1,0:T(8,128)(2,1)S(1)}, u32[]{:S(2)}, u32[]{:S(2)}) collective-permute-start(bf16[576,512]{1,0:T(8,128)(2,1)} %get-tuple-element.38.refs_0_), channel_id=1, source_target_pairs={{0,128},{128,0},{1,129},{129,1},{2,130},{130,2},{3,131},{131,3},{4... | collective-permute-start | bytes 1769480 | tf_op jit(solution)/shard_map/ppermute | solution.py:346
  4.0 14.3 %collective-permute-start.1 = (bf16[448,512]{1,0:T(8,128)(2,1)}, bf16[448,512]{1,0:T(8,128)(2,1)S(1)}, u32[]{:S(2)}, u32[]{:S(2)}) collective-permute-start(bf16[448,512]{1,0:T(8,128)(2,1)} %bitcast.11), channel_id=1, source_target_pairs={{0,2},{2,0},{1,3},{3,1},{4,6},{6,4},{5,7},{7,5},{8,10},{10,8},{9,1... | collective-permute-start | bytes 1376264 | tf_op jit(solution)/shard_map/ppermute | solution.py:346
  5.9 11.7 %collective-permute-start.2 = (bf16[128,768]{1,0:T(8,128)(2,1)}, bf16[128,768]{1,0:T(8,128)(2,1)S(1)}, u32[]{:S(2)}, u32[]{:S(2)}) collective-permute-start(bf16[128,768]{1,0:T(8,128)(2,1)} %get-tuple-element.40.refs_0_), channel_id=1, source_target_pairs={{32,0},{64,32},{96,64},{0,96},{33,1},{65,33},{97,65},{1,97},{34,2}... | collective-permute-start | bytes 589832 | tf_op jit(solution)/shard_map/ppermute | solution.py:342
  6.7 10.9 %collective-permute-start.3 = (bf16[128,768]{1,0:T(8,128)(2,1)}, bf16[128,768]{1,0:T(8,128)(2,1)S(1)}, u32[]{:S(2)}, u32[]{:S(2)}) collective-permute-start(bf16[128,768]{1,0:T(8,128)(2,1)} %get-tuple-element.40.refs_0_), channel_id=1, source_target_pairs={{64,0},{96,32},{0,64},{32,96},{65,1},{97,33},{1,65},{33,97},{66,2}... | collective-permute-start | bytes 589832 | tf_op jit(solution)/shard_map/ppermute | solution.py:342
  7.8 10.4 %collective-permute-start.4 = (bf16[128,768]{1,0:T(8,128)(2,1)}, bf16[128,768]{1,0:T(8,128)(2,1)S(1)}, u32[]{:S(2)}, u32[]{:S(2)}) collective-permute-start(bf16[128,768]{1,0:T(8,128)(2,1)} %get-tuple-element.40.refs_0_), channel_id=1, source_target_pairs={{96,0},{0,32},{32,64},{64,96},{97,1},{1,33},{33,65},{65,97},{98,2}... | collective-permute-start | bytes 589832 | tf_op jit(solution)/shard_map/ppermute | solution.py:342
  10.0 0.7 copy-start.7
  10.7 0.7 copy-start.8
  18.2 6.6 %copy-start.1 = (bf16[4,512,128]{2,1,0:T(8,128)(2,1)S(1)}, bf16[4,512,128]{2,1,0:T(8,128)(2,1)}, u32[]{:S(2)}) copy-start(bf16[4,512,128]{2,1,0:T(8,128)(2,1)} %refs_4_.5) | copy-start | bytes 1572868
  18.3 5.7 %collective-permute-start.6 = (bf16[2,448,512]{2,1,0:T(8,128)(2,1)S(1)}, bf16[2,448,512]{2,1,0:T(8,128)(2,1)S(1)}, u32[]{:S(2)}, u32[]{:S(2)}) collective-permute-start(bf16[2,448,512]{2,1,0:T(8,128)(2,1)S(1)} %pair.1.refs_4_), channel_id=1, source_target_pairs={{0,16},{16,0},{1,17},{17,1},{2,18},{18,2},{3,19},{19,3},{4,20},{20... | collective-permute-start | bytes 2752520 | tf_op jit(solution)/shard_map/ppermute | solution.py:346
  18.4 22.8 %collective-permute-start.17 = (bf16[2,448,512]{2,1,0:T(8,128)(2,1)S(1)}, bf16[2,448,512]{2,1,0:T(8,128)(2,1)S(1)}, u32[]{:S(2)}, u32[]{:S(2)}) collective-permute-start(bf16[2,448,512]{2,1,0:T(8,128)(2,1)S(1)} %pair.1.refs_4_), channel_id=1, source_target_pairs={{0,128},{1,129},{128,0},{129,1},{2,130},{3,131},{130,2},{131,3},{4... | collective-permute-start | bytes 2752520 | tf_op jit(solution)/shard_map/ppermute | solution.py:346
  19.5 23.6 %collective-permute-start.18 = (bf16[2,448,512]{2,1,0:T(8,128)(2,1)S(1)}, bf16[2,448,512]{2,1,0:T(8,128)(2,1)S(1)}, u32[]{:S(2)}, u32[]{:S(2)}) collective-permute-start(bf16[2,448,512]{2,1,0:T(8,128)(2,1)S(1)} %pair.1.refs_4_), channel_id=1, source_target_pairs={{0,129},{1,128},{128,1},{129,0},{2,131},{3,130},{130,3},{131,2},{4... | collective-permute-start | bytes 2752520 | tf_op jit(solution)/shard_map/ppermute | solution.py:346
  22.0 2.0 %collective-permute-start.5 = (bf16[576,512]{1,0:T(8,128)(2,1)S(1)}, bf16[576,512]{1,0:T(8,128)(2,1)S(1)}, u32[]{:S(2)}, u32[]{:S(2)}) collective-permute-start(bf16[576,512]{1,0:T(8,128)(2,1)S(1)} %copy-done), channel_id=1, source_target_pairs={{0,16},{16,0},{1,17},{17,1},{2,18},{18,2},{3,19},{19,3},{4,20},{20... | collective-permute-start | bytes 1769480 | tf_op jit(solution)/shard_map/ppermute | solution.py:346
  22.0 2.8 %collective-permute-start.7 = (bf16[576,512]{1,0:T(8,128)(2,1)S(1)}, bf16[576,512]{1,0:T(8,128)(2,1)S(1)}, u32[]{:S(2)}, u32[]{:S(2)}) collective-permute-start(bf16[576,512]{1,0:T(8,128)(2,1)S(1)} %get-tuple-element.44.refs_1_), channel_id=1, source_target_pairs={{0,16},{16,0},{1,17},{17,1},{2,18},{18,2},{3,19},{19,3},{4,20},{20... | collective-permute-start | bytes 1769480 | tf_op jit(solution)/shard_map/ppermute | solution.py:346
  24.8 12.6 %copy-start.5 = (bf16[128,512]{1,0:T(8,128)(2,1)S(1)}, bf16[128,512]{1,0:T(8,128)(2,1)}, u32[]{:S(2)}) copy-start(bf16[128,512]{1,0:T(8,128)(2,1)} %refs_5_.1) | copy-start | bytes 393220
  24.8 12.6 %copy-start.6 = (bf16[1,64,128]{2,1,0:T(8,128)(2,1)S(1)}, bf16[1,64,128]{2,1,0:T(8,128)(2,1)}, u32[]{:S(2)}) copy-start(bf16[1,64,128]{2,1,0:T(8,128)(2,1)} %param.14) | copy-start | bytes 49156
  33.2 9.9 %collective-permute-start.10 = (bf16[128,640]{1,0:T(8,128)(2,1)S(1)}, bf16[128,640]{1,0:T(8,128)(2,1)S(1)}, u32[]{:S(2)}, u32[]{:S(2)}) collective-permute-start(bf16[128,640]{1,0:T(8,128)(2,1)S(1)} %get-tuple-element.49), channel_id=1, source_target_pairs={{0,96},{32,0},{64,32},{96,64},{1,97},{33,1},{65,33},{97,65},{2,98}... | collective-permute-start | bytes 491528 | tf_op jit(solution)/shard_map/ppermute | solution.py:401
  33.3 9.8 %collective-permute-start.8 = (bf16[128,640]{1,0:T(8,128)(2,1)S(1)}, bf16[128,640]{1,0:T(8,128)(2,1)S(1)}, u32[]{:S(2)}, u32[]{:S(2)}) collective-permute-start(bf16[128,640]{1,0:T(8,128)(2,1)S(1)} %get-tuple-element.47), channel_id=1, source_target_pairs={{0,32},{32,64},{64,96},{96,0},{1,33},{33,65},{65,97},{97,1},{2,34}... | collective-permute-start | bytes 491528 | tf_op jit(solution)/shard_map/ppermute | solution.py:401
  36.5 7.7 %collective-permute-start.9 = (bf16[128,640]{1,0:T(8,128)(2,1)S(1)}, bf16[128,640]{1,0:T(8,128)(2,1)S(1)}, u32[]{:S(2)}, u32[]{:S(2)}) collective-permute-start(bf16[128,640]{1,0:T(8,128)(2,1)S(1)} %get-tuple-element.48), channel_id=1, source_target_pairs={{0,64},{32,96},{64,0},{96,32},{1,65},{33,97},{65,1},{97,33},{2,66}... | collective-permute-start | bytes 491528 | tf_op jit(solution)/shard_map/ppermute | solution.py:401
  44.2 14.2 %collective-permute-start.19 = (bf16[448,512]{1,0:T(8,128)(2,1)S(1)}, bf16[448,512]{1,0:T(8,128)(2,1)S(1)}, u32[]{:S(2)}, u32[]{:S(2)}) collective-permute-start(bf16[448,512]{1,0:T(8,128)(2,1)S(1)} %slice_bitcast_fusion.1), channel_id=1, source_target_pairs={{0,128},{1,129},{128,0},{129,1},{2,130},{3,131},{130,2},{131,3},{4... | collective-permute-start | bytes 1376264 | tf_op jit(solution)/shard_map/ppermute | solution.py:346
  44.4 14.3 %collective-permute-start.20 = (bf16[448,512]{1,0:T(8,128)(2,1)S(1)}, bf16[448,512]{1,0:T(8,128)(2,1)S(1)}, u32[]{:S(2)}, u32[]{:S(2)}) collective-permute-start(bf16[448,512]{1,0:T(8,128)(2,1)S(1)} %slice_bitcast_fusion), channel_id=1, source_target_pairs={{0,129},{1,128},{128,1},{129,0},{2,131},{3,130},{130,3},{131,2},{4... | collective-permute-start | bytes 1376264 | tf_op jit(solution)/shard_map/ppermute | solution.py:346
  47.0 11.4 %collective-permute-start.11 = (bf16[32,512]{1,0:T(8,128)(2,1)S(1)}, bf16[32,512]{1,0:T(8,128)(2,1)S(1)}, u32[]{:S(2)}, u32[]{:S(2)}) collective-permute-start(bf16[32,512]{1,0:T(8,128)(2,1)S(1)} %get-tuple-element.51), channel_id=1, source_target_pairs={{0,1},{1,0},{2,3},{3,2},{4,5},{5,4},{6,7},{7,6},{8,9},{9,8},{10,11... | collective-permute-start | bytes 98312 | tf_op jit(solution)/shard_map/ppermute | solution.py:346
  49.7 8.7 %collective-permute-start.12 = (bf16[32,512]{1,0:T(8,128)(2,1)S(1)}, bf16[32,512]{1,0:T(8,128)(2,1)S(1)}, u32[]{:S(2)}, u32[]{:S(2)}) collective-permute-start(bf16[32,512]{1,0:T(8,128)(2,1)S(1)} %get-tuple-element.52), channel_id=1, source_target_pairs={{0,2},{1,3},{2,0},{3,1},{4,6},{5,7},{6,4},{7,5},{8,10},{9,11},{10,... | collective-permute-start | bytes 98312 | tf_op jit(solution)/shard_map/ppermute | solution.py:346
  50.6 7.8 %collective-permute-start.13 = (bf16[32,512]{1,0:T(8,128)(2,1)S(1)}, bf16[32,512]{1,0:T(8,128)(2,1)S(1)}, u32[]{:S(2)}, u32[]{:S(2)}) collective-permute-start(bf16[32,512]{1,0:T(8,128)(2,1)S(1)} %get-tuple-element.53), channel_id=1, source_target_pairs={{0,3},{1,2},{2,1},{3,0},{4,7},{5,6},{6,5},{7,4},{8,11},{9,10},{10,... | collective-permute-start | bytes 98312 | tf_op jit(solution)/shard_map/ppermute | solution.py:346
  58.9 10.6 %collective-permute-start.21 = (bf16[6,448,512]{2,1,0:T(8,128)(2,1)S(1)}, bf16[6,448,512]{2,1,0:T(8,128)(2,1)S(1)}, u32[]{:S(2)}, u32[]{:S(2)}) collective-permute-start(bf16[6,448,512]{2,1,0:T(8,128)(2,1)S(1)} %rest.1.refs_5_), channel_id=1, source_target_pairs={{0,16},{16,0},{1,17},{17,1},{2,18},{18,2},{3,19},{19,3},{4,20},{20... | collective-permute-start | bytes 8257544 | tf_op jit(solution)/shard_map/ppermute | solution.py:346
  59.0 7.1 %collective-permute-start.14 = (bf16[32,2048]{1,0:T(8,128)(2,1)S(1)}, bf16[32,2048]{1,0:T(8,128)(2,1)S(1)}, u32[]{:S(2)}, u32[]{:S(2)}) collective-permute-start(bf16[32,2048]{1,0:T(8,128)(2,1)S(1)} %join.1.refs_4_.refs_0_), channel_id=1, source_target_pairs={{32,0},{64,32},{96,64},{0,96},{33,1},{65,33},{97,65},{1,97},{34,2}... | collective-permute-start | bytes 393224 | tf_op jit(solution)/shard_map/ppermute | solution.py:342
  60.5 9.0 %collective-permute-start.15 = (bf16[32,2048]{1,0:T(8,128)(2,1)S(1)}, bf16[32,2048]{1,0:T(8,128)(2,1)S(1)}, u32[]{:S(2)}, u32[]{:S(2)}) collective-permute-start(bf16[32,2048]{1,0:T(8,128)(2,1)S(1)} %join.1.refs_4_.refs_0_), channel_id=1, source_target_pairs={{64,0},{96,32},{0,64},{32,96},{65,1},{97,33},{1,65},{33,97},{66,2}... | collective-permute-start | bytes 393224 | tf_op jit(solution)/shard_map/ppermute | solution.py:342
  62.8 6.6 %collective-permute-start.16 = (bf16[32,2048]{1,0:T(8,128)(2,1)S(1)}, bf16[32,2048]{1,0:T(8,128)(2,1)S(1)}, u32[]{:S(2)}, u32[]{:S(2)}) collective-permute-start(bf16[32,2048]{1,0:T(8,128)(2,1)S(1)} %join.1.refs_4_.refs_0_), channel_id=1, source_target_pairs={{96,0},{0,32},{32,64},{64,96},{97,1},{1,33},{33,65},{65,97},{98,2}... | collective-permute-start | bytes 393224 | tf_op jit(solution)/shard_map/ppermute | solution.py:342
  72.2 11.3 %collective-permute-start.22 = (bf16[32,1792]{1,0:T(8,128)(2,1)S(1)}, bf16[32,1792]{1,0:T(8,128)(2,1)S(1)}, u32[]{:S(2)}, u32[]{:S(2)}) collective-permute-start(bf16[32,1792]{1,0:T(8,128)(2,1)S(1)} %get-tuple-element.62), channel_id=1, source_target_pairs={{0,4},{4,8},{8,12},{12,0},{1,5},{5,9},{9,13},{13,1},{2,6},{6,10},{... | collective-permute-start | bytes 344072 | tf_op jit(solution)/shard_map/ppermute | solution.py:429
  75.6 13.0 %collective-permute-start.23 = (bf16[32,1792]{1,0:T(8,128)(2,1)S(1)}, bf16[32,1792]{1,0:T(8,128)(2,1)S(1)}, u32[]{:S(2)}, u32[]{:S(2)}) collective-permute-start(bf16[32,1792]{1,0:T(8,128)(2,1)S(1)} %get-tuple-element.63), channel_id=1, source_target_pairs={{0,8},{4,12},{8,0},{12,4},{1,9},{5,13},{9,1},{13,5},{2,10},{6,14},... | collective-permute-start | bytes 344072 | tf_op jit(solution)/shard_map/ppermute | solution.py:429
  80.9 10.6 %collective-permute-start.24 = (bf16[32,1792]{1,0:T(8,128)(2,1)S(1)}, bf16[32,1792]{1,0:T(8,128)(2,1)S(1)}, u32[]{:S(2)}, u32[]{:S(2)}) collective-permute-start(bf16[32,1792]{1,0:T(8,128)(2,1)S(1)} %get-tuple-element.64), channel_id=1, source_target_pairs={{0,12},{4,0},{8,4},{12,8},{1,13},{5,1},{9,5},{13,9},{2,14},{6,2},{... | collective-permute-start | bytes 344072 | tf_op jit(solution)/shard_map/ppermute | solution.py:429
  91.6 5.2 %collective-permute-start.25 = (f32[8,1792]{1,0:T(8,128)S(1)}, f32[8,1792]{1,0:T(8,128)S(1)}, u32[]{:S(2)}, u32[]{:S(2)}) collective-permute-start(f32[8,1792]{1,0:T(8,128)S(1)} %get-tuple-element.66), channel_id=1, source_target_pairs={{0,32},{32,64},{64,96},{96,0},{1,33},{33,65},{65,97},{97,1},{2,34}... | collective-permute-start | bytes 172040 | tf_op jit(solution)/shard_map/ppermute | solution.py:433
  94.2 5.7 %collective-permute-start.26 = (f32[8,1792]{1,0:T(8,128)S(1)}, f32[8,1792]{1,0:T(8,128)S(1)}, u32[]{:S(2)}, u32[]{:S(2)}) collective-permute-start(f32[8,1792]{1,0:T(8,128)S(1)} %get-tuple-element.67), channel_id=1, source_target_pairs={{0,64},{32,96},{64,0},{96,32},{1,65},{33,97},{65,1},{97,33},{2,66}... | collective-permute-start | bytes 172040 | tf_op jit(solution)/shard_map/ppermute | solution.py:433
  94.9 5.5 %collective-permute-start.27 = (f32[8,1792]{1,0:T(8,128)S(1)}, f32[8,1792]{1,0:T(8,128)S(1)}, u32[]{:S(2)}, u32[]{:S(2)}) collective-permute-start(f32[8,1792]{1,0:T(8,128)S(1)} %get-tuple-element.68), channel_id=1, source_target_pairs={{0,96},{32,0},{64,32},{96,64},{1,97},{33,1},{65,33},{97,65},{2,98}... | collective-permute-start | bytes 172040 | tf_op jit(solution)/shard_map/ppermute | solution.py:433

commit v10 on v9

--- a/solution.py
+++ b/solution.py
@@ -260,40 +260,44 @@
     out[1] = two[...]
 
 
-def rest_kernel(*refs):
-    out = refs[4]
-    for i in range(4):
-        out[i] = refs[i // 2][i % 2]
-    out[4] = refs[2][...]
-    out[5] = refs[3][...]
-
-
-def project_kernel(ids, *refs):
-    heads, mine, other = refs[:4], refs[4:6], refs[6:8]
-    outs, total = refs[8:12], refs[12]
+def stack_kernel(*refs):
+    for s in range(4):
+        refs[4][s] = refs[s][...]
+
+
+def project_kernel(ids, own, other, pair, near, next_, far_one, far_two, *refs):
+    outs, total = refs[:4], refs[4]
     zb = ids[3]
-    rows = jnp.concatenate([h[...] for h in heads], axis=0)
+    rows = jnp.concatenate([own[...].reshape(TOK, 2048), other[...].reshape(TOK, 2048)], axis=0)
+    sides = []
     for side_y in range(2):
-        sides = []
-        for pieces in (mine, other):
-            value = None
-            for d in range(4):
-                m, dz = side_y * 2 + (d & 1), d >> 1
-                weight = pieces[0][dz] if m == 0 else pieces[1][(0, 4, 0, 2)[m] + dz]
-                part = dot_nt(weight, rows[:, d * 512 : (d + 1) * 512])
-                value = part if value is None else value + part
-            sides.append(value)
-        total[:, side_y * 896 : (side_y + 1) * 896] = jnp.concatenate(sides, axis=0).T
+        value = None
+        for d in range(4):
+            dz = d >> 1
+            if side_y == 0:
+                weight = pair[dz] if d & 1 == 0 else (far_one, far_two)[dz][...]
+            else:
+                weight = (near, next_)[d & 1][dz]
+            part = dot_nt(weight, rows[:, d * 512 : (d + 1) * 512])
+            value = part if value is None else value + part
+        sides.append(value)
+    total[...] = jnp.concatenate(sides, axis=0).T
     for d in range(4):
         first = pl.multiple_of(((zb + d) % 4) * 8, 8)
-        parts = [total[pl.ds(first + s * 32, 8), :] for s in range(4)]
+        parts = [total[pl.ds(first + s * 32, 8), :] for s in range(8)]
         outs[d][...] = jnp.concatenate(parts, axis=0).astype(jnp.bfloat16)
 
 
 def share_kernel(*refs):
     total = sum(p[...].astype(jnp.float32) for p in refs[:4])
+    refs[4][...] = total[:32]
+    refs[5][...] = total[32:]
+
+
+def merge_kernel(keep, got, *outs):
     for s in range(4):
-        refs[4 + s][...] = total[s * 8 : (s + 1) * 8]
+        outs[s][:, :896] = keep[s * 8 : (s + 1) * 8, :]
+        outs[s][:, 896:] = got[s * 8 : (s + 1) * 8, :]
 
 
 def place_kernel(ids, *refs):
@@ -303,9 +307,12 @@
         for side_y in range(2):
             first = ((yl ^ side_y) * 4 + (x - s + 4) % 4) * 896
             columns = pl.ds(pl.multiple_of(first, 128), 896)
-            value = parts[s][:, side_y * 896 : (side_y + 1) * 896]
-            swapped = jnp.concatenate([value[:, 448:], value[:, :448]], axis=1)
-            out[:, columns] = jnp.where(k == 0, value, swapped).astype(jnp.bfloat16)
+            mine = parts[s][:, side_y * 448 : (side_y + 1) * 448]
+            other = parts[s][:, 896 + side_y * 448 : 896 + (side_y + 1) * 448]
+            value = jnp.where(
+                k == 0, jnp.concatenate([mine, other], axis=1), jnp.concatenate([other, mine], axis=1)
+            )
+            out[:, columns] = value.astype(jnp.bfloat16)
 
 
 def tie_kernel(*refs):
@@ -392,8 +399,6 @@
     )
     ring = ("yl", "yh")
     mine = [pair, flip(pair, ring, 4, 2), flip(pair, ring, 4, 3)]
-    other = [flip(pair, "k", 2, 1)]
-    pool_k, other[0] = tie([pool_k, other[0]], [])
     pools = [pool, pool_y, pool_k, pool_yk]
 
     away = attention((1, 2, 3), False, lists, counts, q_lat, q_rot, pools, w_uv, ())
@@ -401,8 +406,6 @@
         lax.ppermute(part, "x", [(i, (i + s) % 4) for i in range(4)]) for s, part in zip((1, 2, 3), away)
     ]
     (home,) = attention((0,), True, lists, counts, q_lat, q_rot, pools, w_uv, (new_latent, new_rope[0]))
-    mine[1], mine[2] = tie([mine[1], mine[2]], [*came, home])
-    far = [flip(mine[2][0], ring, 4, 2), flip(mine[1][1], ring, 4, 3)]
     heads = simple(
         combine_kernel,
         "combine",
@@ -412,23 +415,28 @@
     )
     heads = [heads[0]] + [flip(heads[d], ("z0", "yh"), 4, d) for d in (1, 2, 3)]
     heads = simple(join_kernel, "join", jax.ShapeDtypeStruct((32, 2048), jnp.bfloat16), heads)
-    rest = simple(
-        rest_kernel, "rest", jax.ShapeDtypeStruct((6, 448, 512), jnp.bfloat16), tie([*mine[1:], *far], [heads])
-    )
-    mine = [pair, rest]
-    other.append(flip(rest, "k", 2, 1))
+    heads, mine[1], mine[2] = tie([heads, mine[1], mine[2]], [])
+    far = [flip(mine[2][0], ring, 4, 2), flip(mine[1][1], ring, 4, 3)]
     heads = [heads] + [turn(heads, "x", 4, s) for s in (1, 2, 3)]
+    heads[3], *far = tie([heads[3], *far], [])
+    heads = simple(stack_kernel, "stack", jax.ShapeDtypeStruct((4, 32, 2048), jnp.bfloat16), heads)
     partial = simple(
         project_kernel,
         "project",
-        [jax.ShapeDtypeStruct((32, 1792), jnp.bfloat16)] * 4,
-        [ids, *heads, *mine, *other],
-        scratch=[pltpu.VMEM((TOK, 1792), jnp.float32)],
+        [jax.ShapeDtypeStruct((64, 896), jnp.bfloat16)] * 4,
+        [ids, heads, flip(heads, "k", 2, 1), *mine, *far],
+        scratch=[pltpu.VMEM((256, 896), jnp.float32)],
     )
     sums = [partial[0]] + [
         lax.ppermute(partial[d], "zb", [(i, (i + d) % 4) for i in range(4)]) for d in (1, 2, 3)
     ]
-    pieces = simple(share_kernel, "share", [jax.ShapeDtypeStruct((8, 1792), jnp.float32)] * 4, sums)
+    keep, give = simple(share_kernel, "share", [jax.ShapeDtypeStruct((32, 896), jnp.float32)] * 2, sums)
+    pieces = simple(
+        merge_kernel,
+        "merge",
+        [jax.ShapeDtypeStruct((8, 1792), jnp.float32)] * 4,
+        [keep, flip(give, "k", 2, 1)],
+    )
     pieces = [pieces[0]] + [
         lax.ppermute(pieces[s], "x", [(i, (i + s) % 4) for i in range(4)]) for s in (1, 2, 3)
     ]

time: 102 us -> 102 us (level)
  starting transfers between devices: 41.9 us -> 38.9 us
  waiting for transfers between devices: 34.3 us -> 36.2 us
  Pallas kernels: 23.9 us -> 25.1 us
    ppermute x3, waiting for transfers between devices: 1.06 us -> 4.3 us  [local(): lax.ppermute(part, 'x', [(i, (i + s) % 4) for i in range(4)])]
    ppermute x6, waiting for transfers between devices: 10.4 us -> 7.42 us  [turn(): lax.ppermute(value, axis, [((i + shift) % size, i) for i in range(size)])]
    pallas_call x2, Pallas kernels: 12.2 us -> 14.4 us  [attention(): pl.pallas_call(functools.partial(attention_kernel, slots, own), out_shape...]
    ppermute x3, starting transfers between devices: 4.16 us -> 2.09 us  [local(): lax.ppermute(part, 'x', [(i, (i + s) % 4) for i in range(4)])]
    ppermute x13, starting transfers between devices: 14.5 us -> 16.5 us  [flip(): return lax.ppermute(value, axis, [(i, i ^ bits) for i in range(size)])]
    ppermute x6, starting transfers between devices: 8.31 us -> 6.57 us  [turn(): lax.ppermute(value, axis, [((i + shift) % size, i) for i in range(size)])]
    ppermute x13, waiting for transfers between devices: 9.5 us -> 10.8 us  [flip(): return lax.ppermute(value, axis, [(i, i ^ bits) for i in range(size)])]
    pallas_call x8 -> x9, Pallas kernels: 6.71 us -> 5.76 us  [simple(): pl.pallas_call(kernel, out_shape=out_shape, in_specs=[pl.BlockSpec(memory...]
  transfers between devices with their start and end apart: 28 -> 28, of which waited for: 15 -> 20; matrix products, arithmetic and copies ran while one was open for 0% -> 0% of each run, Pallas kernels for 17% -> 19%
where the time goes in v10:
time: 102 us
  starting transfers between devices  38.9 us (38%)
  waiting for transfers between devices  36.2 us (35%)
  Pallas kernels  25.1 us (25%)
  local copies, waits for them, and re-layouts  1.52 us (1%)
    ppermute x13, starting transfers between devices, flip(): return lax.ppermute(value, axis, [(i, i ^ bits) for i in range(size)])  16.5 us
    pallas_call x2, Pallas kernels, attention(): pl.pallas_call(functools.partial(attention_kernel, slots, own), out_shape...  14.4 us
    ppermute x13, waiting for transfers between devices, flip(): return lax.ppermute(value, axis, [(i, i ^ bits) for i in range(size)])  10.8 us
    ppermute x3, starting transfers between devices, local(): lax.ppermute(partial[d], 'zb', [(i, (i + d) % 4) for i in range(4)])  10.5 us
    ppermute x3, waiting for transfers between devices, local(): lax.ppermute(partial[d], 'zb', [(i, (i + d) % 4) for i in range(4)])  8.45 us
    ppermute x6, waiting for transfers between devices, turn(): lax.ppermute(value, axis, [((i + shift) % size, i) for i in range(size)])  7.42 us
    ppermute x6, starting transfers between devices, turn(): lax.ppermute(value, axis, [((i + shift) % size, i) for i in range(size)])  6.57 us
    pallas_call x9, Pallas kernels, simple(): pl.pallas_call(kernel, out_shape=out_shape, in_specs=[pl.BlockSpec(memory...  5.76 us
  transfers between devices with their start and end apart: 28, of which 20 were waited for; matrix products, arithmetic and copies ran while one was open for 0% of the time, Pallas kernels for 19%

profile of v10, /device:TPU:6, one launch (start us, length us, event | category | flops | bytes accessed | tf_op | source)
XLA Modules:
  0.0 101.9 jit_solution(11090590203152028916)
XLA Ops:
  0.0 2.3 %pack.1 = (bf16[128,768]{1,0:T(8,128)(2,1)}, bf16[576,512]{1,0:T(8,128)(2,1)}) custom-call(bf16[128,512]{1,0:T(8,128)(2,1)} %q_nope.1, bf16[128,256]{1,0:T(8,128)(2,1)} %q_rope.1, bf16[4,128,512]{2,1,0:T(8,128)(2,1)} %pool_latent.1, bf16[4,64,128]{2,1,0:T(8,128)(2,1)} %pool_rope.1), custom_call_target="tpu_custom_call" | custom-call | tf_op jit(solution)/shard_map/pack/pallas_call | solution.py:244
  2.3 1.7 %collective-permute-start = (bf16[576,512]{1,0:T(8,128)(2,1)}, bf16[576,512]{1,0:T(8,128)(2,1)S(1)}, u32[]{:S(2)}, u32[]{:S(2)}) collective-permute-start(bf16[576,512]{1,0:T(8,128)(2,1)} %get-tuple-element.38.refs_0_), channel_id=1, source_target_pairs={{0,128},{128,0},{1,129},{129,1},{2,130},{130,2},{3,131},{131,3},{4... | collective-permute-start | bytes 1769480 | tf_op jit(solution)/shard_map/ppermute | solution.py:353
  4.0 1.9 %collective-permute-start.1 = (bf16[448,512]{1,0:T(8,128)(2,1)}, bf16[448,512]{1,0:T(8,128)(2,1)S(1)}, u32[]{:S(2)}, u32[]{:S(2)}) collective-permute-start(bf16[448,512]{1,0:T(8,128)(2,1)} %bitcast.11), channel_id=1, source_target_pairs={{0,2},{2,0},{1,3},{3,1},{4,6},{6,4},{5,7},{7,5},{8,10},{10,8},{9,1... | collective-permute-start | bytes 1376264 | tf_op jit(solution)/shard_map/ppermute | solution.py:353
  5.9 0.8 collective-permute-start.2
  6.7 1.1 %collective-permute-start.3 = (bf16[128,768]{1,0:T(8,128)(2,1)}, bf16[128,768]{1,0:T(8,128)(2,1)S(1)}, u32[]{:S(2)}, u32[]{:S(2)}) collective-permute-start(bf16[128,768]{1,0:T(8,128)(2,1)} %get-tuple-element.40.refs_0_), channel_id=1, source_target_pairs={{64,0},{96,32},{0,64},{32,96},{65,1},{97,33},{1,65},{33,97},{66,2}... | collective-permute-start | bytes 589832 | tf_op jit(solution)/shard_map/ppermute | solution.py:349
  7.8 2.1 %collective-permute-start.4 = (bf16[128,768]{1,0:T(8,128)(2,1)}, bf16[128,768]{1,0:T(8,128)(2,1)S(1)}, u32[]{:S(2)}, u32[]{:S(2)}) collective-permute-start(bf16[128,768]{1,0:T(8,128)(2,1)} %get-tuple-element.40.refs_0_), channel_id=1, source_target_pairs={{96,0},{0,32},{32,64},{64,96},{97,1},{1,33},{33,65},{65,97},{98,2}... | collective-permute-start | bytes 589832 | tf_op jit(solution)/shard_map/ppermute | solution.py:349
  9.9 0.1 stack.24.ids
  10.0 0.7 copy-done.7
  10.7 0.7 copy-done.8
  11.4 2.6 %plan.1 = (s32[64]{0:T(128)S(1)}, s32[8]{0:T(128)S(1)}) custom-call(s32[5]{0:T(128)S(1)} %stack.24.ids, s32[16,32]{1,0:T(8,128)S(1)} %copy-done.7, s32[16]{0:T(128)S(1)} %copy-done.8), custom_call_target="tpu_custom_call" | custom-call | tf_op jit(solution)/shard_map/plan/pallas_call | solution.py:65
  14.0 3.6 %collective-permute-done.2.refs_3_.refs_1_ = bf16[128,768]{1,0:T(8,128)(2,1)S(1)} collective-permute-done((bf16[128,768]{1,0:T(8,128)(2,1)}, bf16[128,768]{1,0:T(8,128)(2,1)S(1)}, u32[]{:S(2)}, u32[]{:S(2)}) %collective-permute-start.2) | collective-permute-done | bytes 196640 | tf_op jit(solution)/shard_map/ppermute | solution.py:349
  17.6 0.0 collective-permute-done.3.refs_4_.refs_2_
  17.6 0.6 collective-permute-done.4.refs_5_.refs_3_
  18.2 0.0 collective-permute-done.1.refs_2_
  18.2 0.0 collective-permute-done.refs_0_
  18.3 0.1 pair.1
  18.3 1.1 %collective-permute-start.13 = (bf16[2,448,512]{2,1,0:T(8,128)(2,1)S(1)}, bf16[2,448,512]{2,1,0:T(8,128)(2,1)S(1)}, u32[]{:S(2)}, u32[]{:S(2)}) collective-permute-start(bf16[2,448,512]{2,1,0:T(8,128)(2,1)S(1)} %pair.1), channel_id=1, source_target_pairs={{0,128},{1,129},{128,0},{129,1},{2,130},{3,131},{130,2},{131,3},{4... | collective-permute-start | bytes 2752520 | tf_op jit(solution)/shard_map/ppermute | solution.py:353
  19.4 2.5 %collective-permute-start.14 = (bf16[2,448,512]{2,1,0:T(8,128)(2,1)S(1)}, bf16[2,448,512]{2,1,0:T(8,128)(2,1)S(1)}, u32[]{:S(2)}, u32[]{:S(2)}) collective-permute-start(bf16[2,448,512]{2,1,0:T(8,128)(2,1)S(1)} %pair.1), channel_id=1, source_target_pairs={{0,129},{1,128},{128,1},{129,0},{2,131},{3,130},{130,3},{131,2},{4... | collective-permute-start | bytes 2752520 | tf_op jit(solution)/shard_map/ppermute | solution.py:353
  21.9 0.5 collective-permute-start.6
  22.4 1.3 %prepare.1 = (bf16[4,512,512]{2,1,0:T(8,128)(2,1)S(1)}, bf16[4,512,64]{2,1,0:T(8,128)(2,1)S(1)}) custom-call(s32[8]{0:T(128)S(1)} %get-tuple-element.41.counts, bf16[128,768]{1,0:T(8,128)(2,1)S(1)} %copy-done.4, bf16[128,768]{1,0:T(8,128)(2,1)S(1)} %collective-permute-done.2.refs_3_.refs_1_, bf16[128,768]{1,0:T(8,128)(2,1)S(1)} %collective-permute-done.3.refs_4_.refs_2_, ...), custom_call_target="tpu_custom_call" | custom-call | tf_op jit(solution)/shard_map/prepare/pallas_call | solution.py:337
  23.7 0.2 collective-permute-done.5.refs_2_
  23.9 0.8 collective-permute-done.6.refs_3_
  24.7 10.6 %attend.3 = (bf16[128,640]{1,0:T(8,128)(2,1)S(1)}, bf16[128,640]{1,0:T(8,128)(2,1)S(1)}, bf16[128,640]{1,0:T(8,128)(2,1)S(1)}) custom-call(s32[64]{0:T(128)S(1)} %get-tuple-element.37.lists, s32[8]{0:T(128)S(1)} %get-tuple-element.41.counts, bf16[4,512,512]{2,1,0:T(8,128)(2,1)S(1)} %get-tuple-element.42.q_lat, ...), custom_call_target="tpu_custom_call" | custom-call | tf_op jit(solution)/shard_map/attend/pallas_call | solution.py:185
  35.3 0.1 collective-permute-start.7
  35.4 0.1 collective-permute-start.8
  35.5 1.9 %collective-permute-start.9 = (bf16[128,640]{1,0:T(8,128)(2,1)S(1)}, bf16[128,640]{1,0:T(8,128)(2,1)S(1)}, u32[]{:S(2)}, u32[]{:S(2)}) collective-permute-start(bf16[128,640]{1,0:T(8,128)(2,1)S(1)} %get-tuple-element.47), channel_id=1, source_target_pairs={{0,96},{32,0},{64,32},{96,64},{1,97},{33,1},{65,33},{97,65},{2,98}... | collective-permute-start | bytes 491528 | tf_op jit(solution)/shard_map/ppermute | solution.py:406
  37.4 3.9 %attend.2.refs_0_ = bf16[128,640]{1,0:T(8,128)(2,1)S(1)} custom-call(s32[64]{0:T(128)S(1)} %get-tuple-element.37.lists, s32[8]{0:T(128)S(1)} %get-tuple-element.41.counts, bf16[4,512,512]{2,1,0:T(8,128)(2,1)S(1)} %get-tuple-element.42.q_lat, bf16[4,512,64]{2,1,0:T(8,128)(2,1)S(1)} %get-tuple-element.43.q_rot, bf16[576,512]{1,0:T(8,128)(2,1)S(1)} %copy-done, ...), custom_call_target="tpu_custom_call" | custom-call | tf_op jit(solution)/shard_map/attend/pallas_call | solution.py:185
  41.3 0.9 collective-permute-done.7.refs_1_
  42.2 1.8 %collective-permute-done.8.refs_2_ = bf16[128,640]{1,0:T(8,128)(2,1)S(1)} collective-permute-done((bf16[128,640]{1,0:T(8,128)(2,1)S(1)}, bf16[128,640]{1,0:T(8,128)(2,1)S(1)}, u32[]{:S(2)}, u32[]{:S(2)}) %collective-permute-start.8) | collective-permute-done | bytes 163872 | tf_op jit(solution)/shard_map/ppermute | solution.py:406
  44.1 1.5 %collective-permute-done.9.refs_3_ = bf16[128,640]{1,0:T(8,128)(2,1)S(1)} collective-permute-done((bf16[128,640]{1,0:T(8,128)(2,1)S(1)}, bf16[128,640]{1,0:T(8,128)(2,1)S(1)}, u32[]{:S(2)}, u32[]{:S(2)}) %collective-permute-start.9) | collective-permute-done | bytes 163872 | tf_op jit(solution)/shard_map/ppermute | solution.py:406
  45.6 1.1 %combine.1 = (bf16[32,512]{1,0:T(8,128)(2,1)S(1)}, bf16[32,512]{1,0:T(8,128)(2,1)S(1)}, bf16[32,512]{1,0:T(8,128)(2,1)S(1)}, bf16[32,512]{1,0:T(8,128)(2,1)S(1)}) custom-call(s32[5]{0:T(128)S(1)} %stack.24.ids, bf16[128,640]{1,0:T(8,128)(2,1)S(1)} %attend.2.refs_0_, bf16[128,640]{1,0:T(8,128)(2,1)S(1)} %collective-permute-done.7.refs_1_, ...), custom_call_target="tpu_custom_call" | custom-call | tf_op jit(solution)/shard_map/combine/pallas_call | solution.py:337
  46.7 0.7 collective-permute-start.10
  47.4 1.7 %collective-permute-start.11 = (bf16[32,512]{1,0:T(8,128)(2,1)S(1)}, bf16[32,512]{1,0:T(8,128)(2,1)S(1)}, u32[]{:S(2)}, u32[]{:S(2)}) collective-permute-start(bf16[32,512]{1,0:T(8,128)(2,1)S(1)} %get-tuple-element.50), channel_id=1, source_target_pairs={{0,2},{1,3},{2,0},{3,1},{4,6},{5,7},{6,4},{7,5},{8,10},{9,11},{10,... | collective-permute-start | bytes 98312 | tf_op jit(solution)/shard_map/ppermute | solution.py:353
  49.1 2.6 %collective-permute-start.12 = (bf16[32,512]{1,0:T(8,128)(2,1)S(1)}, bf16[32,512]{1,0:T(8,128)(2,1)S(1)}, u32[]{:S(2)}, u32[]{:S(2)}) collective-permute-start(bf16[32,512]{1,0:T(8,128)(2,1)S(1)} %get-tuple-element.51), channel_id=1, source_target_pairs={{0,3},{1,2},{2,1},{3,0},{4,7},{5,6},{6,5},{7,4},{8,11},{9,10},{10,... | collective-permute-start | bytes 98312 | tf_op jit(solution)/shard_map/ppermute | solution.py:353
  51.8 0.4 collective-permute-done.10.refs_1_
  52.2 3.2 %collective-permute-done.12.refs_3_ = bf16[32,512]{1,0:T(8,128)(2,1)S(1)} collective-permute-done((bf16[32,512]{1,0:T(8,128)(2,1)S(1)}, bf16[32,512]{1,0:T(8,128)(2,1)S(1)}, u32[]{:S(2)}, u32[]{:S(2)}) %collective-permute-start.12) | collective-permute-done | bytes 32800 | tf_op jit(solution)/shard_map/ppermute | solution.py:353
  55.5 0.0 collective-permute-done.14.refs_2_
  55.5 0.3 collective-permute-start.18
  55.8 3.4 %collective-permute-start.19 = (bf16[448,512]{1,0:T(8,128)(2,1)S(1)}, bf16[448,512]{1,0:T(8,128)(2,1)S(1)}, u32[]{:S(2)}, u32[]{:S(2)}) collective-permute-start(bf16[448,512]{1,0:T(8,128)(2,1)S(1)} %slice_bitcast_fusion), channel_id=1, source_target_pairs={{0,129},{1,128},{128,1},{129,0},{2,131},{3,130},{130,3},{131,2},{4... | collective-permute-start | bytes 1376264 | tf_op jit(solution)/shard_map/ppermute | solution.py:353
  59.2 1.1 %collective-permute-start.17 = (bf16[32,2048]{1,0:T(8,128)(2,1)S(1)}, bf16[32,2048]{1,0:T(8,128)(2,1)S(1)}, u32[]{:S(2)}, u32[]{:S(2)}) collective-permute-start(bf16[32,2048]{1,0:T(8,128)(2,1)S(1)} %get-tuple-element.53.refs_0_), channel_id=1, source_target_pairs={{96,0},{0,32},{32,64},{64,96},{97,1},{1,33},{33,65},{65,97},{98,2}... | collective-permute-start | bytes 393224 | tf_op jit(solution)/shard_map/ppermute | solution.py:349
  60.3 1.0 collective-permute-start.15
  61.2 0.5 collective-permute-start.16
  61.7 2.4 %collective-permute-done.17.refs_0_ = bf16[32,2048]{1,0:T(8,128)(2,1)S(1)} collective-permute-done((bf16[32,2048]{1,0:T(8,128)(2,1)S(1)}, bf16[32,2048]{1,0:T(8,128)(2,1)S(1)}, u32[]{:S(2)}, u32[]{:S(2)}) %collective-permute-start.17) | collective-permute-done | bytes 131104 | tf_op jit(solution)/shard_map/ppermute | solution.py:349
  64.2 1.5 %collective-permute-done.18.refs_1_ = bf16[448,512]{1,0:T(8,128)(2,1)S(1)} collective-permute-done((bf16[448,512]{1,0:T(8,128)(2,1)S(1)}, bf16[448,512]{1,0:T(8,128)(2,1)S(1)}, u32[]{:S(2)}, u32[]{:S(2)}) %collective-permute-start.18) | collective-permute-done | bytes 458784 | tf_op jit(solution)/shard_map/ppermute | solution.py:353
  65.6 1.5 %collective-permute-done.19.refs_2_ = bf16[448,512]{1,0:T(8,128)(2,1)S(1)} collective-permute-done((bf16[448,512]{1,0:T(8,128)(2,1)S(1)}, bf16[448,512]{1,0:T(8,128)(2,1)S(1)}, u32[]{:S(2)}, u32[]{:S(2)}) %collective-permute-start.19) | collective-permute-done | bytes 458784 | tf_op jit(solution)/shard_map/ppermute | solution.py:353
  67.1 0.8 collective-permute-done.15.refs_1_
  67.9 0.1 collective-permute-start.20
  68.0 1.9 %collective-permute-done.20.other = bf16[4,32,2048]{2,1,0:T(8,128)(2,1)S(1)} collective-permute-done((bf16[4,32,2048]{2,1,0:T(8,128)(2,1)S(1)}, bf16[4,32,2048]{2,1,0:T(8,128)(2,1)S(1)}, u32[]{:S(2)}, u32[]{:S(2)}) %collective-permute-start.20) | collective-permute-done | bytes 524320 | tf_op jit(solution)/shard_map/ppermute | solution.py:353
  69.9 1.9 %project.1 = (bf16[64,896]{1,0:T(8,128)(2,1)S(1)}, bf16[64,896]{1,0:T(8,128)(2,1)S(1)}, bf16[64,896]{1,0:T(8,128)(2,1)S(1)}, bf16[64,896]{1,0:T(8,128)(2,1)S(1)}) custom-call(s32[5]{0:T(128)S(1)} %stack.24.ids, bf16[4,32,2048]{2,1,0:T(8,128)(2,1)S(1)} %stack.25.own, bf16[4,32,2048]{2,1,0:T(8,128)(2,1)S(1)} %collective-permute-done.20.other, ...), custom_call_target="tpu_custom_call" | custom-call | tf_op jit(solution)/shard_map/project/pallas_call | solution.py:337
  71.8 3.4 %collective-permute-start.21 = (bf16[64,896]{1,0:T(8,128)(2,1)S(1)}, bf16[64,896]{1,0:T(8,128)(2,1)S(1)}, u32[]{:S(2)}, u32[]{:S(2)}) collective-permute-start(bf16[64,896]{1,0:T(8,128)(2,1)S(1)} %get-tuple-element.60), channel_id=1, source_target_pairs={{0,4},{4,8},{8,12},{12,0},{1,5},{5,9},{9,13},{13,1},{2,6},{6,10},{... | collective-permute-start | bytes 344072 | tf_op jit(solution)/shard_map/ppermute | solution.py:431
  75.2 4.5 %collective-permute-start.22 = (bf16[64,896]{1,0:T(8,128)(2,1)S(1)}, bf16[64,896]{1,0:T(8,128)(2,1)S(1)}, u32[]{:S(2)}, u32[]{:S(2)}) collective-permute-start(bf16[64,896]{1,0:T(8,128)(2,1)S(1)} %get-tuple-element.61), channel_id=1, source_target_pairs={{0,8},{4,12},{8,0},{12,4},{1,9},{5,13},{9,1},{13,5},{2,10},{6,14},... | collective-permute-start | bytes 344072 | tf_op jit(solution)/shard_map/ppermute | solution.py:431
  79.7 2.7 %collective-permute-start.23 = (bf16[64,896]{1,0:T(8,128)(2,1)S(1)}, bf16[64,896]{1,0:T(8,128)(2,1)S(1)}, u32[]{:S(2)}, u32[]{:S(2)}) collective-permute-start(bf16[64,896]{1,0:T(8,128)(2,1)S(1)} %get-tuple-element.62), channel_id=1, source_target_pairs={{0,12},{4,0},{8,4},{12,8},{1,13},{5,1},{9,5},{13,9},{2,14},{6,2},{... | collective-permute-start | bytes 344072 | tf_op jit(solution)/shard_map/ppermute | solution.py:431
  82.3 5.6 %collective-permute-done.22.refs_2_ = bf16[64,896]{1,0:T(8,128)(2,1)S(1)} collective-permute-done((bf16[64,896]{1,0:T(8,128)(2,1)S(1)}, bf16[64,896]{1,0:T(8,128)(2,1)S(1)}, u32[]{:S(2)}, u32[]{:S(2)}) %collective-permute-start.22) | collective-permute-done | bytes 114720 | tf_op jit(solution)/shard_map/ppermute | solution.py:431
  88.0 2.8 %collective-permute-done.23.refs_3_ = bf16[64,896]{1,0:T(8,128)(2,1)S(1)} collective-permute-done((bf16[64,896]{1,0:T(8,128)(2,1)S(1)}, bf16[64,896]{1,0:T(8,128)(2,1)S(1)}, u32[]{:S(2)}, u32[]{:S(2)}) %collective-permute-start.23) | collective-permute-done | bytes 114720 | tf_op jit(solution)/shard_map/ppermute | solution.py:431
  90.8 0.1 share.1
  90.9 0.1 collective-permute-start.24
  91.0 1.3 %collective-permute-done.24.got = f32[32,896]{1,0:T(8,128)S(1)} collective-permute-done((f32[32,896]{1,0:T(8,128)S(1)}, f32[32,896]{1,0:T(8,128)S(1)}, u32[]{:S(2)}, u32[]{:S(2)}) %collective-permute-start.24) | collective-permute-done | bytes 114720 | tf_op jit(solution)/shard_map/ppermute | solution.py:353
  92.3 2.2 %collective-permute-start.25 = (f32[8,1792]{1,0:T(8,128)S(1)}, f32[8,1792]{1,0:T(8,128)S(1)}, u32[]{:S(2)}, u32[]{:S(2)}) collective-permute-start(f32[8,1792]{1,0:T(8,128)S(1)} %get-tuple-element.66), channel_id=1, source_target_pairs={{0,32},{32,64},{64,96},{96,0},{1,33},{33,65},{65,97},{97,1},{2,34}... | collective-permute-start | bytes 172040 | tf_op jit(solution)/shard_map/ppermute | solution.py:441
  94.5 0.0 collective-permute-start.26
  94.5 1.0 collective-permute-start.27
  95.4 1.8 %collective-permute-done.25.refs_1_ = f32[8,1792]{1,0:T(8,128)S(1)} collective-permute-done((f32[8,1792]{1,0:T(8,128)S(1)}, f32[8,1792]{1,0:T(8,128)S(1)}, u32[]{:S(2)}, u32[]{:S(2)}) %collective-permute-start.25) | collective-permute-done | bytes 57376 | tf_op jit(solution)/shard_map/ppermute | solution.py:441
  97.2 3.1 %collective-permute-done.26.refs_2_ = f32[8,1792]{1,0:T(8,128)S(1)} collective-permute-done((f32[8,1792]{1,0:T(8,128)S(1)}, f32[8,1792]{1,0:T(8,128)S(1)}, u32[]{:S(2)}, u32[]{:S(2)}) %collective-permute-start.26) | collective-permute-done | bytes 57376 | tf_op jit(solution)/shard_map/ppermute | solution.py:441
  100.3 0.3 collective-permute-done.27.refs_3_
  100.6 1.3 %place.1 = bf16[8,7168]{1,0:T(8,128)(2,1)} custom-call(s32[5]{0:T(128)S(1)} %stack.24.ids, f32[8,1792]{1,0:T(8,128)S(1)} %get-tuple-element.65.refs_0_, f32[8,1792]{1,0:T(8,128)S(1)} %collective-permute-done.25.refs_1_, f32[8,1792]{1,0:T(8,128)S(1)} %collective-permute-done.26.refs_2_, f32[8,1792]{1,0:T(8,128)S(1)} %collective-permute-done.27.refs_3_), custom_call_target="tpu_custom_call" | custom-call | tf_op jit(solution)/shard_map/place/pallas_call | solution.py:337
  (29 shorter events, 0.2 us)
Async XLA Ops:
  0.0 18.2 %copy-start.3 = (bf16[512,448]{0,1:T(8,128)(2,1)S(1)}, bf16[512,448]{0,1:T(8,128)(2,1)}, u32[]{:S(2)}) copy-start(bf16[512,448]{0,1:T(8,128)(2,1)} %param.21) | copy-start | bytes 1376260
  0.0 22.4 %copy-start.2 = (bf16[4,128,512]{2,1,0:T(8,128)(2,1)S(1)}, bf16[4,128,512]{2,1,0:T(8,128)(2,1)}, u32[]{:S(2)}) copy-start(bf16[4,128,512]{2,1,0:T(8,128)(2,1)} %refs_4_.3) | copy-start | bytes 1572868
  2.3 19.6 %copy-start = (bf16[576,512]{1,0:T(8,128)(2,1)S(1)}, bf16[576,512]{1,0:T(8,128)(2,1)}, u32[]{:S(2)}) copy-start(bf16[576,512]{1,0:T(8,128)(2,1)} %get-tuple-element.38.refs_0_) | copy-start | bytes 1769476
  2.3 20.1 %copy-start.4 = (bf16[128,768]{1,0:T(8,128)(2,1)S(1)}, bf16[128,768]{1,0:T(8,128)(2,1)}, u32[]{:S(2)}) copy-start(bf16[128,768]{1,0:T(8,128)(2,1)} %get-tuple-element.40.refs_0_) | copy-start | bytes 589828
  2.3 15.9 %collective-permute-start = (bf16[576,512]{1,0:T(8,128)(2,1)}, bf16[576,512]{1,0:T(8,128)(2,1)S(1)}, u32[]{:S(2)}, u32[]{:S(2)}) collective-permute-start(bf16[576,512]{1,0:T(8,128)(2,1)} %get-tuple-element.38.refs_0_), channel_id=1, source_target_pairs={{0,128},{128,0},{1,129},{129,1},{2,130},{130,2},{3,131},{131,3},{4... | collective-permute-start | bytes 1769480 | tf_op jit(solution)/shard_map/ppermute | solution.py:353
  4.0 14.3 %collective-permute-start.1 = (bf16[448,512]{1,0:T(8,128)(2,1)}, bf16[448,512]{1,0:T(8,128)(2,1)S(1)}, u32[]{:S(2)}, u32[]{:S(2)}) collective-permute-start(bf16[448,512]{1,0:T(8,128)(2,1)} %bitcast.11), channel_id=1, source_target_pairs={{0,2},{2,0},{1,3},{3,1},{4,6},{6,4},{5,7},{7,5},{8,10},{10,8},{9,1... | collective-permute-start | bytes 1376264 | tf_op jit(solution)/shard_map/ppermute | solution.py:353
  5.9 11.7 %collective-permute-start.2 = (bf16[128,768]{1,0:T(8,128)(2,1)}, bf16[128,768]{1,0:T(8,128)(2,1)S(1)}, u32[]{:S(2)}, u32[]{:S(2)}) collective-permute-start(bf16[128,768]{1,0:T(8,128)(2,1)} %get-tuple-element.40.refs_0_), channel_id=1, source_target_pairs={{32,0},{64,32},{96,64},{0,96},{33,1},{65,33},{97,65},{1,97},{34,2}... | collective-permute-start | bytes 589832 | tf_op jit(solution)/shard_map/ppermute | solution.py:349
  6.7 10.9 %collective-permute-start.3 = (bf16[128,768]{1,0:T(8,128)(2,1)}, bf16[128,768]{1,0:T(8,128)(2,1)S(1)}, u32[]{:S(2)}, u32[]{:S(2)}) collective-permute-start(bf16[128,768]{1,0:T(8,128)(2,1)} %get-tuple-element.40.refs_0_), channel_id=1, source_target_pairs={{64,0},{96,32},{0,64},{32,96},{65,1},{97,33},{1,65},{33,97},{66,2}... | collective-permute-start | bytes 589832 | tf_op jit(solution)/shard_map/ppermute | solution.py:349
  7.8 10.4 %collective-permute-start.4 = (bf16[128,768]{1,0:T(8,128)(2,1)}, bf16[128,768]{1,0:T(8,128)(2,1)S(1)}, u32[]{:S(2)}, u32[]{:S(2)}) collective-permute-start(bf16[128,768]{1,0:T(8,128)(2,1)} %get-tuple-element.40.refs_0_), channel_id=1, source_target_pairs={{96,0},{0,32},{32,64},{64,96},{97,1},{1,33},{33,65},{65,97},{98,2}... | collective-permute-start | bytes 589832 | tf_op jit(solution)/shard_map/ppermute | solution.py:349
  10.0 0.7 copy-start.7
  10.7 0.7 copy-start.8
  18.2 6.5 %copy-start.1 = (bf16[4,512,128]{2,1,0:T(8,128)(2,1)S(1)}, bf16[4,512,128]{2,1,0:T(8,128)(2,1)}, u32[]{:S(2)}) copy-start(bf16[4,512,128]{2,1,0:T(8,128)(2,1)} %refs_4_.5) | copy-start | bytes 1572868
  18.3 37.1 %collective-permute-start.13 = (bf16[2,448,512]{2,1,0:T(8,128)(2,1)S(1)}, bf16[2,448,512]{2,1,0:T(8,128)(2,1)S(1)}, u32[]{:S(2)}, u32[]{:S(2)}) collective-permute-start(bf16[2,448,512]{2,1,0:T(8,128)(2,1)S(1)} %pair.1), channel_id=1, source_target_pairs={{0,128},{1,129},{128,0},{129,1},{2,130},{3,131},{130,2},{131,3},{4... | collective-permute-start | bytes 2752520 | tf_op jit(solution)/shard_map/ppermute | solution.py:353
  19.4 36.1 %collective-permute-start.14 = (bf16[2,448,512]{2,1,0:T(8,128)(2,1)S(1)}, bf16[2,448,512]{2,1,0:T(8,128)(2,1)S(1)}, u32[]{:S(2)}, u32[]{:S(2)}) collective-permute-start(bf16[2,448,512]{2,1,0:T(8,128)(2,1)S(1)} %pair.1), channel_id=1, source_target_pairs={{0,129},{1,128},{128,1},{129,0},{2,131},{3,130},{130,3},{131,2},{4... | collective-permute-start | bytes 2752520 | tf_op jit(solution)/shard_map/ppermute | solution.py:353
  21.9 2.0 %collective-permute-start.5 = (bf16[576,512]{1,0:T(8,128)(2,1)S(1)}, bf16[576,512]{1,0:T(8,128)(2,1)S(1)}, u32[]{:S(2)}, u32[]{:S(2)}) collective-permute-start(bf16[576,512]{1,0:T(8,128)(2,1)S(1)} %copy-done), channel_id=1, source_target_pairs={{0,16},{16,0},{1,17},{17,1},{2,18},{18,2},{3,19},{19,3},{4,20},{20... | collective-permute-start | bytes 1769480 | tf_op jit(solution)/shard_map/ppermute | solution.py:353
  21.9 2.8 %collective-permute-start.6 = (bf16[576,512]{1,0:T(8,128)(2,1)S(1)}, bf16[576,512]{1,0:T(8,128)(2,1)S(1)}, u32[]{:S(2)}, u32[]{:S(2)}) collective-permute-start(bf16[576,512]{1,0:T(8,128)(2,1)S(1)} %get-tuple-element.44.refs_1_), channel_id=1, source_target_pairs={{0,16},{16,0},{1,17},{17,1},{2,18},{18,2},{3,19},{19,3},{4,20},{20... | collective-permute-start | bytes 1769480 | tf_op jit(solution)/shard_map/ppermute | solution.py:353
  24.7 12.7 %copy-start.5 = (bf16[128,512]{1,0:T(8,128)(2,1)S(1)}, bf16[128,512]{1,0:T(8,128)(2,1)}, u32[]{:S(2)}) copy-start(bf16[128,512]{1,0:T(8,128)(2,1)} %refs_5_.1) | copy-start | bytes 393220
  24.7 12.7 %copy-start.6 = (bf16[1,64,128]{2,1,0:T(8,128)(2,1)S(1)}, bf16[1,64,128]{2,1,0:T(8,128)(2,1)}, u32[]{:S(2)}) copy-start(bf16[1,64,128]{2,1,0:T(8,128)(2,1)} %param.14) | copy-start | bytes 49156
  35.3 6.9 %collective-permute-start.7 = (bf16[128,640]{1,0:T(8,128)(2,1)S(1)}, bf16[128,640]{1,0:T(8,128)(2,1)S(1)}, u32[]{:S(2)}, u32[]{:S(2)}) collective-permute-start(bf16[128,640]{1,0:T(8,128)(2,1)S(1)} %get-tuple-element.45), channel_id=1, source_target_pairs={{0,32},{32,64},{64,96},{96,0},{1,33},{33,65},{65,97},{97,1},{2,34}... | collective-permute-start | bytes 491528 | tf_op jit(solution)/shard_map/ppermute | solution.py:406
  35.4 8.7 %collective-permute-start.8 = (bf16[128,640]{1,0:T(8,128)(2,1)S(1)}, bf16[128,640]{1,0:T(8,128)(2,1)S(1)}, u32[]{:S(2)}, u32[]{:S(2)}) collective-permute-start(bf16[128,640]{1,0:T(8,128)(2,1)S(1)} %get-tuple-element.46), channel_id=1, source_target_pairs={{0,64},{32,96},{64,0},{96,32},{1,65},{33,97},{65,1},{97,33},{2,66}... | collective-permute-start | bytes 491528 | tf_op jit(solution)/shard_map/ppermute | solution.py:406
  35.5 10.1 %collective-permute-start.9 = (bf16[128,640]{1,0:T(8,128)(2,1)S(1)}, bf16[128,640]{1,0:T(8,128)(2,1)S(1)}, u32[]{:S(2)}, u32[]{:S(2)}) collective-permute-start(bf16[128,640]{1,0:T(8,128)(2,1)S(1)} %get-tuple-element.47), channel_id=1, source_target_pairs={{0,96},{32,0},{64,32},{96,64},{1,97},{33,1},{65,33},{97,65},{2,98}... | collective-permute-start | bytes 491528 | tf_op jit(solution)/shard_map/ppermute | solution.py:406
  46.7 5.5 %collective-permute-start.10 = (bf16[32,512]{1,0:T(8,128)(2,1)S(1)}, bf16[32,512]{1,0:T(8,128)(2,1)S(1)}, u32[]{:S(2)}, u32[]{:S(2)}) collective-permute-start(bf16[32,512]{1,0:T(8,128)(2,1)S(1)} %get-tuple-element.49), channel_id=1, source_target_pairs={{0,1},{1,0},{2,3},{3,2},{4,5},{5,4},{6,7},{7,6},{8,9},{9,8},{10,11... | collective-permute-start | bytes 98312 | tf_op jit(solution)/shard_map/ppermute | solution.py:353
  47.4 4.8 %collective-permute-start.11 = (bf16[32,512]{1,0:T(8,128)(2,1)S(1)}, bf16[32,512]{1,0:T(8,128)(2,1)S(1)}, u32[]{:S(2)}, u32[]{:S(2)}) collective-permute-start(bf16[32,512]{1,0:T(8,128)(2,1)S(1)} %get-tuple-element.50), channel_id=1, source_target_pairs={{0,2},{1,3},{2,0},{3,1},{4,6},{5,7},{6,4},{7,5},{8,10},{9,11},{10,... | collective-permute-start | bytes 98312 | tf_op jit(solution)/shard_map/ppermute | solution.py:353
  49.1 6.3 %collective-permute-start.12 = (bf16[32,512]{1,0:T(8,128)(2,1)S(1)}, bf16[32,512]{1,0:T(8,128)(2,1)S(1)}, u32[]{:S(2)}, u32[]{:S(2)}) collective-permute-start(bf16[32,512]{1,0:T(8,128)(2,1)S(1)} %get-tuple-element.51), channel_id=1, source_target_pairs={{0,3},{1,2},{2,1},{3,0},{4,7},{5,6},{6,5},{7,4},{8,11},{9,10},{10,... | collective-permute-start | bytes 98312 | tf_op jit(solution)/shard_map/ppermute | solution.py:353
  55.5 10.1 %collective-permute-start.18 = (bf16[448,512]{1,0:T(8,128)(2,1)S(1)}, bf16[448,512]{1,0:T(8,128)(2,1)S(1)}, u32[]{:S(2)}, u32[]{:S(2)}) collective-permute-start(bf16[448,512]{1,0:T(8,128)(2,1)S(1)} %slice_bitcast_fusion.1), channel_id=1, source_target_pairs={{0,128},{1,129},{128,0},{129,1},{2,130},{3,131},{130,2},{131,3},{4... | collective-permute-start | bytes 1376264 | tf_op jit(solution)/shard_map/ppermute | solution.py:353
  55.8 11.2 %collective-permute-start.19 = (bf16[448,512]{1,0:T(8,128)(2,1)S(1)}, bf16[448,512]{1,0:T(8,128)(2,1)S(1)}, u32[]{:S(2)}, u32[]{:S(2)}) collective-permute-start(bf16[448,512]{1,0:T(8,128)(2,1)S(1)} %slice_bitcast_fusion), channel_id=1, source_target_pairs={{0,129},{1,128},{128,1},{129,0},{2,131},{3,130},{130,3},{131,2},{4... | collective-permute-start | bytes 1376264 | tf_op jit(solution)/shard_map/ppermute | solution.py:353
  59.2 5.0 %collective-permute-start.17 = (bf16[32,2048]{1,0:T(8,128)(2,1)S(1)}, bf16[32,2048]{1,0:T(8,128)(2,1)S(1)}, u32[]{:S(2)}, u32[]{:S(2)}) collective-permute-start(bf16[32,2048]{1,0:T(8,128)(2,1)S(1)} %get-tuple-element.53.refs_0_), channel_id=1, source_target_pairs={{96,0},{0,32},{32,64},{64,96},{97,1},{1,33},{33,65},{65,97},{98,2}... | collective-permute-start | bytes 393224 | tf_op jit(solution)/shard_map/ppermute | solution.py:349
  60.3 7.6 %collective-permute-start.15 = (bf16[32,2048]{1,0:T(8,128)(2,1)S(1)}, bf16[32,2048]{1,0:T(8,128)(2,1)S(1)}, u32[]{:S(2)}, u32[]{:S(2)}) collective-permute-start(bf16[32,2048]{1,0:T(8,128)(2,1)S(1)} %get-tuple-element.53.refs_0_), channel_id=1, source_target_pairs={{32,0},{64,32},{96,64},{0,96},{33,1},{65,33},{97,65},{1,97},{34,2}... | collective-permute-start | bytes 393224 | tf_op jit(solution)/shard_map/ppermute | solution.py:349
  61.2 6.6 %collective-permute-start.16 = (bf16[32,2048]{1,0:T(8,128)(2,1)S(1)}, bf16[32,2048]{1,0:T(8,128)(2,1)S(1)}, u32[]{:S(2)}, u32[]{:S(2)}) collective-permute-start(bf16[32,2048]{1,0:T(8,128)(2,1)S(1)} %get-tuple-element.53.refs_0_), channel_id=1, source_target_pairs={{64,0},{96,32},{0,64},{32,96},{65,1},{97,33},{1,65},{33,97},{66,2}... | collective-permute-start | bytes 393224 | tf_op jit(solution)/shard_map/ppermute | solution.py:349
  67.9 2.0 %collective-permute-start.20 = (bf16[4,32,2048]{2,1,0:T(8,128)(2,1)S(1)}, bf16[4,32,2048]{2,1,0:T(8,128)(2,1)S(1)}, u32[]{:S(2)}, u32[]{:S(2)}) collective-permute-start(bf16[4,32,2048]{2,1,0:T(8,128)(2,1)S(1)} %stack.25.own), channel_id=1, source_target_pairs={{0,16},{16,0},{1,17},{17,1},{2,18},{18,2},{3,19},{19,3},{4,20},{20... | collective-permute-start | bytes 1572872 | tf_op jit(solution)/shard_map/ppermute | solution.py:353
  71.8 10.5 %collective-permute-start.21 = (bf16[64,896]{1,0:T(8,128)(2,1)S(1)}, bf16[64,896]{1,0:T(8,128)(2,1)S(1)}, u32[]{:S(2)}, u32[]{:S(2)}) collective-permute-start(bf16[64,896]{1,0:T(8,128)(2,1)S(1)} %get-tuple-element.60), channel_id=1, source_target_pairs={{0,4},{4,8},{8,12},{12,0},{1,5},{5,9},{9,13},{13,1},{2,6},{6,10},{... | collective-permute-start | bytes 344072 | tf_op jit(solution)/shard_map/ppermute | solution.py:431
  75.2 12.8 %collective-permute-start.22 = (bf16[64,896]{1,0:T(8,128)(2,1)S(1)}, bf16[64,896]{1,0:T(8,128)(2,1)S(1)}, u32[]{:S(2)}, u32[]{:S(2)}) collective-permute-start(bf16[64,896]{1,0:T(8,128)(2,1)S(1)} %get-tuple-element.61), channel_id=1, source_target_pairs={{0,8},{4,12},{8,0},{12,4},{1,9},{5,13},{9,1},{13,5},{2,10},{6,14},... | collective-permute-start | bytes 344072 | tf_op jit(solution)/shard_map/ppermute | solution.py:431
  79.7 11.1 %collective-permute-start.23 = (bf16[64,896]{1,0:T(8,128)(2,1)S(1)}, bf16[64,896]{1,0:T(8,128)(2,1)S(1)}, u32[]{:S(2)}, u32[]{:S(2)}) collective-permute-start(bf16[64,896]{1,0:T(8,128)(2,1)S(1)} %get-tuple-element.62), channel_id=1, source_target_pairs={{0,12},{4,0},{8,4},{12,8},{1,13},{5,1},{9,5},{13,9},{2,14},{6,2},{... | collective-permute-start | bytes 344072 | tf_op jit(solution)/shard_map/ppermute | solution.py:431
  90.9 1.4 %collective-permute-start.24 = (f32[32,896]{1,0:T(8,128)S(1)}, f32[32,896]{1,0:T(8,128)S(1)}, u32[]{:S(2)}, u32[]{:S(2)}) collective-permute-start(f32[32,896]{1,0:T(8,128)S(1)} %get-tuple-element.64), channel_id=1, source_target_pairs={{0,16},{16,0},{1,17},{17,1},{2,18},{18,2},{3,19},{19,3},{4,20},{20... | collective-permute-start | bytes 344072 | tf_op jit(solution)/shard_map/ppermute | solution.py:353
  92.3 5.0 %collective-permute-start.25 = (f32[8,1792]{1,0:T(8,128)S(1)}, f32[8,1792]{1,0:T(8,128)S(1)}, u32[]{:S(2)}, u32[]{:S(2)}) collective-permute-start(f32[8,1792]{1,0:T(8,128)S(1)} %get-tuple-element.66), channel_id=1, source_target_pairs={{0,32},{32,64},{64,96},{96,0},{1,33},{33,65},{65,97},{97,1},{2,34}... | collective-permute-start | bytes 172040 | tf_op jit(solution)/shard_map/ppermute | solution.py:441
  94.5 5.9 %collective-permute-start.26 = (f32[8,1792]{1,0:T(8,128)S(1)}, f32[8,1792]{1,0:T(8,128)S(1)}, u32[]{:S(2)}, u32[]{:S(2)}) collective-permute-start(f32[8,1792]{1,0:T(8,128)S(1)} %get-tuple-element.67), channel_id=1, source_target_pairs={{0,64},{32,96},{64,0},{96,32},{1,65},{33,97},{65,1},{97,33},{2,66}... | collective-permute-start | bytes 172040 | tf_op jit(solution)/shard_map/ppermute | solution.py:441
  94.5 6.1 %collective-permute-start.27 = (f32[8,1792]{1,0:T(8,128)S(1)}, f32[8,1792]{1,0:T(8,128)S(1)}, u32[]{:S(2)}, u32[]{:S(2)}) collective-permute-start(f32[8,1792]{1,0:T(8,128)S(1)} %get-tuple-element.68), channel_id=1, source_target_pairs={{0,96},{32,0},{64,32},{96,64},{1,97},{33,1},{65,33},{97,65},{2,98}... | collective-permute-start | bytes 172040 | tf_op jit(solution)/shard_map/ppermute | solution.py:441

commit v11 on v10

--- a/solution.py
+++ b/solution.py
@@ -248,7 +248,7 @@
             jax.ShapeDtypeStruct((4 * BLOCK + ROPE, LAT), jnp.bfloat16),
         ],
         in_specs=[pl.BlockSpec(memory_space=pltpu.HBM)] * 4,
-        out_specs=[pl.BlockSpec(memory_space=VMEM)] * 2,
+        out_specs=[pl.BlockSpec(memory_space=pltpu.HBM)] * 2,
         scratch_shapes=[pltpu.SemaphoreType.DMA((10,))],
         compiler_params=pltpu.CompilerParams(vmem_limit_bytes=56 * 2**20),
         name="pack",
@@ -260,15 +260,12 @@
     out[1] = two[...]
 
 
-def stack_kernel(*refs):
-    for s in range(4):
-        refs[4][s] = refs[s][...]
-
-
-def project_kernel(ids, own, other, pair, near, next_, far_one, far_two, *refs):
-    outs, total = refs[:4], refs[4]
+def project_kernel(ids, *refs):
+    heads = refs[:8]
+    pair, near, next_, far_one, far_two = refs[8:13]
+    outs, total = refs[13:17], refs[17]
     zb = ids[3]
-    rows = jnp.concatenate([own[...].reshape(TOK, 2048), other[...].reshape(TOK, 2048)], axis=0)
+    rows = jnp.concatenate([h[...] for h in heads], axis=0)
     sides = []
     for side_y in range(2):
         value = None
@@ -418,13 +415,12 @@
     heads, mine[1], mine[2] = tie([heads, mine[1], mine[2]], [])
     far = [flip(mine[2][0], ring, 4, 2), flip(mine[1][1], ring, 4, 3)]
     heads = [heads] + [turn(heads, "x", 4, s) for s in (1, 2, 3)]
-    heads[3], *far = tie([heads[3], *far], [])
-    heads = simple(stack_kernel, "stack", jax.ShapeDtypeStruct((4, 32, 2048), jnp.bfloat16), heads)
+    heads[1], *far = tie([heads[1], *far], [])
     partial = simple(
         project_kernel,
         "project",
         [jax.ShapeDtypeStruct((64, 896), jnp.bfloat16)] * 4,
-        [ids, heads, flip(heads, "k", 2, 1), *mine, *far],
+        [ids, *heads, *[flip(h, "k", 2, 1) for h in heads], *mine, *far],
         scratch=[pltpu.VMEM((256, 896), jnp.float32)],
     )
     sums = [partial[0]] + [

time: 102 us -> 125 us (1.23)
  Pallas kernels: 25.1 us -> 42 us
  starting transfers between devices: 38.9 us -> 46.3 us
  waiting for transfers between devices: 36.2 us -> 34.3 us
    pallas_call x1, Pallas kernels: 2.27 us -> 25 us  [pack(): pl.pallas_call(pack_kernel, out_shape=[jax.ShapeDtypeStruct((TOK, HEADS *...]
    pallas_call x2, Pallas kernels: 14.4 us -> 8.9 us  [attention(): pl.pallas_call(functools.partial(attention_kernel, slots, own), out_shape...]
    ppermute x13 -> x16, waiting for transfers between devices: 10.8 us -> 7.98 us  [flip(): return lax.ppermute(value, axis, [(i, i ^ bits) for i in range(size)])]
    ppermute x3, starting transfers between devices: 2.09 us -> 4.76 us  [local(): lax.ppermute(part, 'x', [(i, (i + s) % 4) for i in range(4)])]
    ppermute x13 -> x16, starting transfers between devices: 16.5 us -> 18.5 us  [flip(): return lax.ppermute(value, axis, [(i, i ^ bits) for i in range(size)])]
    ppermute x6, starting transfers between devices: 6.57 us -> 8.52 us  [turn(): lax.ppermute(value, axis, [((i + shift) % size, i) for i in range(size)])]
    pallas_call x9 -> x8, Pallas kernels: 5.76 us -> 5.73 us  [simple(): pl.pallas_call(kernel, out_shape=out_shape, in_specs=[pl.BlockSpec(memory...]
  transfers between devices with their start and end apart: 28 -> 31, of which waited for: 20 -> 19; matrix products, arithmetic and copies ran while one was open for 0% -> 0% of each run, Pallas kernels for 19% -> 11%
where the time goes in v11:
time: 125 us; the launch traced here: 124 us
  starting transfers between devices  46.3 us (37%)
  Pallas kernels  42 us (34%)
  waiting for transfers between devices  34.3 us (27%)
  local copies, waits for them, and re-layouts  1.52 us (1%)
    pallas_call x1, Pallas kernels, pack(): pl.pallas_call(pack_kernel, out_shape=[jax.ShapeDtypeStruct((TOK, HEADS *...  25 us
    ppermute x16, starting transfers between devices, flip(): return lax.ppermute(value, axis, [(i, i ^ bits) for i in range(size)])  18.5 us
    ppermute x3, starting transfers between devices, local(): lax.ppermute(partial[d], 'zb', [(i, (i + d) % 4) for i in range(4)])  11.5 us
    pallas_call x2, Pallas kernels, attention(): pl.pallas_call(functools.partial(attention_kernel, slots, own), out_shape...  8.9 us
    ppermute x6, starting transfers between devices, turn(): lax.ppermute(value, axis, [((i + shift) % size, i) for i in range(size)])  8.52 us
    ppermute x3, waiting for transfers between devices, local(): lax.ppermute(partial[d], 'zb', [(i, (i + d) % 4) for i in range(4)])  8.48 us
    ppermute x16, waiting for transfers between devices, flip(): return lax.ppermute(value, axis, [(i, i ^ bits) for i in range(size)])  7.98 us
    ppermute x6, waiting for transfers between devices, turn(): lax.ppermute(value, axis, [((i + shift) % size, i) for i in range(size)])  7.93 us
  transfers between devices with their start and end apart: 31, of which 19 were waited for; matrix products, arithmetic and copies ran while one was open for 0% of the time, Pallas kernels for 11%

profile of v11, /device:TPU:6, one launch (start us, length us, event | category | flops | bytes accessed | tf_op | source)
XLA Modules:
  0.0 124.3 jit_solution(18440202448001082260)
XLA Ops:
  0.0 25.0 %pack.1 = (bf16[128,768]{1,0:T(8,128)(2,1)}, bf16[576,512]{1,0:T(8,128)(2,1)}) custom-call(bf16[128,512]{1,0:T(8,128)(2,1)} %q_nope.1, bf16[128,256]{1,0:T(8,128)(2,1)} %q_rope.1, bf16[4,128,512]{2,1,0:T(8,128)(2,1)} %pool_latent.1, bf16[4,64,128]{2,1,0:T(8,128)(2,1)} %pool_rope.1), custom_call_target="tpu_custom_call" | custom-call | tf_op jit(solution)/shard_map/pack/pallas_call | solution.py:244
  25.0 1.7 %collective-permute-start = (bf16[576,512]{1,0:T(8,128)(2,1)}, bf16[576,512]{1,0:T(8,128)(2,1)S(1)}, u32[]{:S(2)}, u32[]{:S(2)}) collective-permute-start(bf16[576,512]{1,0:T(8,128)(2,1)} %get-tuple-element.38.refs_0_), channel_id=1, source_target_pairs={{0,128},{128,0},{1,129},{129,1},{2,130},{130,2},{3,131},{131,3},{4... | collective-permute-start | bytes 1769480 | tf_op jit(solution)/shard_map/ppermute | solution.py:350
  26.7 1.9 %collective-permute-start.1 = (bf16[448,512]{1,0:T(8,128)(2,1)}, bf16[448,512]{1,0:T(8,128)(2,1)S(1)}, u32[]{:S(2)}, u32[]{:S(2)}) collective-permute-start(bf16[448,512]{1,0:T(8,128)(2,1)} %bitcast.11), channel_id=1, source_target_pairs={{0,2},{2,0},{1,3},{3,1},{4,6},{6,4},{5,7},{7,5},{8,10},{10,8},{9,1... | collective-permute-start | bytes 1376264 | tf_op jit(solution)/shard_map/ppermute | solution.py:350
  28.6 0.8 collective-permute-start.2
  29.5 1.1 collective-permute-start.3
  30.6 2.1 %collective-permute-start.4 = (bf16[128,768]{1,0:T(8,128)(2,1)}, bf16[128,768]{1,0:T(8,128)(2,1)S(1)}, u32[]{:S(2)}, u32[]{:S(2)}) collective-permute-start(bf16[128,768]{1,0:T(8,128)(2,1)} %get-tuple-element.40.refs_0_), channel_id=1, source_target_pairs={{96,0},{0,32},{32,64},{64,96},{97,1},{1,33},{33,65},{65,97},{98,2}... | collective-permute-start | bytes 589832 | tf_op jit(solution)/shard_map/ppermute | solution.py:346
  32.7 0.1 stack.23.ids
  32.7 0.7 copy-done.7
  33.4 0.7 copy-done.8
  34.1 2.4 %plan.1 = (s32[64]{0:T(128)S(1)}, s32[8]{0:T(128)S(1)}) custom-call(s32[5]{0:T(128)S(1)} %stack.23.ids, s32[16,32]{1,0:T(8,128)S(1)} %copy-done.7, s32[16]{0:T(128)S(1)} %copy-done.8), custom_call_target="tpu_custom_call" | custom-call | tf_op jit(solution)/shard_map/plan/pallas_call | solution.py:65
  36.5 3.9 %collective-permute-done.2.refs_3_.refs_1_ = bf16[128,768]{1,0:T(8,128)(2,1)S(1)} collective-permute-done((bf16[128,768]{1,0:T(8,128)(2,1)}, bf16[128,768]{1,0:T(8,128)(2,1)S(1)}, u32[]{:S(2)}, u32[]{:S(2)}) %collective-permute-start.2) | collective-permute-done | bytes 196640 | tf_op jit(solution)/shard_map/ppermute | solution.py:346
  40.3 0.0 collective-permute-done.3.refs_4_.refs_2_
  40.3 0.6 collective-permute-done.4.refs_5_.refs_3_
  41.0 0.0 collective-permute-done.1.refs_2_
  41.0 0.0 collective-permute-done.refs_0_
  41.0 0.1 pair.1.refs_8_
  41.1 1.1 collective-permute-start.13
  42.1 2.5 %collective-permute-start.14 = (bf16[2,448,512]{2,1,0:T(8,128)(2,1)S(1)}, bf16[2,448,512]{2,1,0:T(8,128)(2,1)S(1)}, u32[]{:S(2)}, u32[]{:S(2)}) collective-permute-start(bf16[2,448,512]{2,1,0:T(8,128)(2,1)S(1)} %pair.1.refs_8_), channel_id=1, source_target_pairs={{0,129},{1,128},{128,1},{129,0},{2,131},{3,130},{130,3},{131,2},{4... | collective-permute-start | bytes 2752520 | tf_op jit(solution)/shard_map/ppermute | solution.py:350
  44.6 0.0 collective-permute-start.5
  44.6 0.5 collective-permute-start.6
  45.1 1.3 %prepare.1 = (bf16[4,512,512]{2,1,0:T(8,128)(2,1)S(1)}, bf16[4,512,64]{2,1,0:T(8,128)(2,1)S(1)}) custom-call(s32[8]{0:T(128)S(1)} %get-tuple-element.41.counts, bf16[128,768]{1,0:T(8,128)(2,1)S(1)} %copy-done.4, bf16[128,768]{1,0:T(8,128)(2,1)S(1)} %collective-permute-done.2.refs_3_.refs_1_, bf16[128,768]{1,0:T(8,128)(2,1)S(1)} %collective-permute-done.3.refs_4_.refs_2_, ...), custom_call_target="tpu_custom_call" | custom-call | tf_op jit(solution)/shard_map/prepare/pallas_call | solution.py:334
  46.4 0.2 collective-permute-done.5.refs_2_
  46.6 0.8 collective-permute-done.6.refs_3_
  47.5 6.1 %attend.3 = (bf16[128,640]{1,0:T(8,128)(2,1)S(1)}, bf16[128,640]{1,0:T(8,128)(2,1)S(1)}, bf16[128,640]{1,0:T(8,128)(2,1)S(1)}) custom-call(s32[64]{0:T(128)S(1)} %get-tuple-element.37.lists, s32[8]{0:T(128)S(1)} %get-tuple-element.41.counts, bf16[4,512,512]{2,1,0:T(8,128)(2,1)S(1)} %get-tuple-element.42.q_lat, ...), custom_call_target="tpu_custom_call" | custom-call | tf_op jit(solution)/shard_map/attend/pallas_call | solution.py:185
  53.6 3.8 %collective-permute-start.7 = (bf16[128,640]{1,0:T(8,128)(2,1)S(1)}, bf16[128,640]{1,0:T(8,128)(2,1)S(1)}, u32[]{:S(2)}, u32[]{:S(2)}) collective-permute-start(bf16[128,640]{1,0:T(8,128)(2,1)S(1)} %get-tuple-element.45), channel_id=1, source_target_pairs={{0,32},{32,64},{64,96},{96,0},{1,33},{33,65},{65,97},{97,1},{2,34}... | collective-permute-start | bytes 491528 | tf_op jit(solution)/shard_map/ppermute | solution.py:403
  57.4 0.2 collective-permute-start.8
  57.6 0.7 collective-permute-start.9
  58.4 2.8 %attend.2.refs_0_ = bf16[128,640]{1,0:T(8,128)(2,1)S(1)} custom-call(s32[64]{0:T(128)S(1)} %get-tuple-element.37.lists, s32[8]{0:T(128)S(1)} %get-tuple-element.41.counts, bf16[4,512,512]{2,1,0:T(8,128)(2,1)S(1)} %get-tuple-element.42.q_lat, bf16[4,512,64]{2,1,0:T(8,128)(2,1)S(1)} %get-tuple-element.43.q_rot, bf16[576,512]{1,0:T(8,128)(2,1)S(1)} %copy-done, ...), custom_call_target="tpu_custom_call" | custom-call | tf_op jit(solution)/shard_map/attend/pallas_call | solution.py:185
  61.2 1.4 %collective-permute-done.7.refs_1_ = bf16[128,640]{1,0:T(8,128)(2,1)S(1)} collective-permute-done((bf16[128,640]{1,0:T(8,128)(2,1)S(1)}, bf16[128,640]{1,0:T(8,128)(2,1)S(1)}, u32[]{:S(2)}, u32[]{:S(2)}) %collective-permute-start.7) | collective-permute-done | bytes 163872 | tf_op jit(solution)/shard_map/ppermute | solution.py:403
  62.6 2.0 %collective-permute-done.8.refs_2_ = bf16[128,640]{1,0:T(8,128)(2,1)S(1)} collective-permute-done((bf16[128,640]{1,0:T(8,128)(2,1)S(1)}, bf16[128,640]{1,0:T(8,128)(2,1)S(1)}, u32[]{:S(2)}, u32[]{:S(2)}) %collective-permute-start.8) | collective-permute-done | bytes 163872 | tf_op jit(solution)/shard_map/ppermute | solution.py:403
  64.6 1.7 %collective-permute-done.9.refs_3_ = bf16[128,640]{1,0:T(8,128)(2,1)S(1)} collective-permute-done((bf16[128,640]{1,0:T(8,128)(2,1)S(1)}, bf16[128,640]{1,0:T(8,128)(2,1)S(1)}, u32[]{:S(2)}, u32[]{:S(2)}) %collective-permute-start.9) | collective-permute-done | bytes 163872 | tf_op jit(solution)/shard_map/ppermute | solution.py:403
  66.2 1.1 combine.1
  67.3 0.7 collective-permute-start.10
  68.0 0.8 collective-permute-start.11
  68.8 3.6 %collective-permute-start.12 = (bf16[32,512]{1,0:T(8,128)(2,1)S(1)}, bf16[32,512]{1,0:T(8,128)(2,1)S(1)}, u32[]{:S(2)}, u32[]{:S(2)}) collective-permute-start(bf16[32,512]{1,0:T(8,128)(2,1)S(1)} %get-tuple-element.51), channel_id=1, source_target_pairs={{0,3},{1,2},{2,1},{3,0},{4,7},{5,6},{6,5},{7,4},{8,11},{9,10},{10,... | collective-permute-start | bytes 98312 | tf_op jit(solution)/shard_map/ppermute | solution.py:350
  72.4 0.4 collective-permute-done.10.refs_1_
  72.8 0.0 collective-permute-done.11.refs_2_
  72.8 2.3 %collective-permute-done.12.refs_3_ = bf16[32,512]{1,0:T(8,128)(2,1)S(1)} collective-permute-done((bf16[32,512]{1,0:T(8,128)(2,1)S(1)}, bf16[32,512]{1,0:T(8,128)(2,1)S(1)}, u32[]{:S(2)}, u32[]{:S(2)}) %collective-permute-start.12) | collective-permute-done | bytes 32800 | tf_op jit(solution)/shard_map/ppermute | solution.py:350
  75.2 3.4 %collective-permute-start.16 = (bf16[448,512]{1,0:T(8,128)(2,1)S(1)}, bf16[448,512]{1,0:T(8,128)(2,1)S(1)}, u32[]{:S(2)}, u32[]{:S(2)}) collective-permute-start(bf16[448,512]{1,0:T(8,128)(2,1)S(1)} %slice_bitcast_fusion.1), channel_id=1, source_target_pairs={{0,128},{1,129},{128,0},{129,1},{2,130},{3,131},{130,2},{131,3},{4... | collective-permute-start | bytes 1376264 | tf_op jit(solution)/shard_map/ppermute | solution.py:350
  78.6 1.8 %collective-permute-start.17 = (bf16[448,512]{1,0:T(8,128)(2,1)S(1)}, bf16[448,512]{1,0:T(8,128)(2,1)S(1)}, u32[]{:S(2)}, u32[]{:S(2)}) collective-permute-start(bf16[448,512]{1,0:T(8,128)(2,1)S(1)} %slice_bitcast_fusion), channel_id=1, source_target_pairs={{0,129},{1,128},{128,1},{129,0},{2,131},{3,130},{130,3},{131,2},{4... | collective-permute-start | bytes 1376264 | tf_op jit(solution)/shard_map/ppermute | solution.py:350
  80.4 0.7 collective-permute-start.15
  81.1 1.4 %collective-permute-start.18 = (bf16[32,2048]{1,0:T(8,128)(2,1)S(1)}, bf16[32,2048]{1,0:T(8,128)(2,1)S(1)}, u32[]{:S(2)}, u32[]{:S(2)}) collective-permute-start(bf16[32,2048]{1,0:T(8,128)(2,1)S(1)} %get-tuple-element.53.refs_0_), channel_id=1, source_target_pairs={{64,0},{96,32},{0,64},{32,96},{65,1},{97,33},{1,65},{33,97},{66,2}... | collective-permute-start | bytes 393224 | tf_op jit(solution)/shard_map/ppermute | solution.py:346
  82.5 2.3 %collective-permute-start.19 = (bf16[32,2048]{1,0:T(8,128)(2,1)S(1)}, bf16[32,2048]{1,0:T(8,128)(2,1)S(1)}, u32[]{:S(2)}, u32[]{:S(2)}) collective-permute-start(bf16[32,2048]{1,0:T(8,128)(2,1)S(1)} %get-tuple-element.53.refs_0_), channel_id=1, source_target_pairs={{96,0},{0,32},{32,64},{64,96},{97,1},{1,33},{33,65},{65,97},{98,2}... | collective-permute-start | bytes 393224 | tf_op jit(solution)/shard_map/ppermute | solution.py:346
  84.9 3.1 %collective-permute-done.15.refs_0_ = bf16[32,2048]{1,0:T(8,128)(2,1)S(1)} collective-permute-done((bf16[32,2048]{1,0:T(8,128)(2,1)S(1)}, bf16[32,2048]{1,0:T(8,128)(2,1)S(1)}, u32[]{:S(2)}, u32[]{:S(2)}) %collective-permute-start.15) | collective-permute-done | bytes 131104 | tf_op jit(solution)/shard_map/ppermute | solution.py:346
  88.0 0.5 collective-permute-start.22
  88.5 0.3 collective-permute-done.19.refs_3_
  88.9 1.6 %collective-permute-done.17.refs_2_ = bf16[448,512]{1,0:T(8,128)(2,1)S(1)} collective-permute-done((bf16[448,512]{1,0:T(8,128)(2,1)S(1)}, bf16[448,512]{1,0:T(8,128)(2,1)S(1)}, u32[]{:S(2)}, u32[]{:S(2)}) %collective-permute-start.17) | collective-permute-done | bytes 458784 | tf_op jit(solution)/shard_map/ppermute | solution.py:350
  90.4 1.3 %collective-permute-done.21.refs_5_ = bf16[32,2048]{1,0:T(8,128)(2,1)S(1)} collective-permute-done((bf16[32,2048]{1,0:T(8,128)(2,1)S(1)}, bf16[32,2048]{1,0:T(8,128)(2,1)S(1)}, u32[]{:S(2)}, u32[]{:S(2)}) %collective-permute-start.21) | collective-permute-done | bytes 131104 | tf_op jit(solution)/shard_map/ppermute | solution.py:350
  91.8 1.9 %project.1 = (bf16[64,896]{1,0:T(8,128)(2,1)S(1)}, bf16[64,896]{1,0:T(8,128)(2,1)S(1)}, bf16[64,896]{1,0:T(8,128)(2,1)S(1)}, bf16[64,896]{1,0:T(8,128)(2,1)S(1)}) custom-call(s32[5]{0:T(128)S(1)} %stack.23.ids, bf16[32,2048]{1,0:T(8,128)(2,1)S(1)} %get-tuple-element.53.refs_0_, bf16[32,2048]{1,0:T(8,128)(2,1)S(1)} %get-tuple-element.56.refs_1_, ...), custom_call_target="tpu_custom_call" | custom-call | tf_op jit(solution)/shard_map/project/pallas_call | solution.py:334
  93.7 3.3 %collective-permute-start.24 = (bf16[64,896]{1,0:T(8,128)(2,1)S(1)}, bf16[64,896]{1,0:T(8,128)(2,1)S(1)}, u32[]{:S(2)}, u32[]{:S(2)}) collective-permute-start(bf16[64,896]{1,0:T(8,128)(2,1)S(1)} %get-tuple-element.60), channel_id=1, source_target_pairs={{0,4},{4,8},{8,12},{12,0},{1,5},{5,9},{9,13},{13,1},{2,6},{6,10},{... | collective-permute-start | bytes 344072 | tf_op jit(solution)/shard_map/ppermute | solution.py:427
  97.0 5.5 %collective-permute-start.25 = (bf16[64,896]{1,0:T(8,128)(2,1)S(1)}, bf16[64,896]{1,0:T(8,128)(2,1)S(1)}, u32[]{:S(2)}, u32[]{:S(2)}) collective-permute-start(bf16[64,896]{1,0:T(8,128)(2,1)S(1)} %get-tuple-element.61), channel_id=1, source_target_pairs={{0,8},{4,12},{8,0},{12,4},{1,9},{5,13},{9,1},{13,5},{2,10},{6,14},... | collective-permute-start | bytes 344072 | tf_op jit(solution)/shard_map/ppermute | solution.py:427
  102.5 2.7 %collective-permute-start.26 = (bf16[64,896]{1,0:T(8,128)(2,1)S(1)}, bf16[64,896]{1,0:T(8,128)(2,1)S(1)}, u32[]{:S(2)}, u32[]{:S(2)}) collective-permute-start(bf16[64,896]{1,0:T(8,128)(2,1)S(1)} %get-tuple-element.62), channel_id=1, source_target_pairs={{0,12},{4,0},{8,4},{12,8},{1,13},{5,1},{9,5},{13,9},{2,14},{6,2},{... | collective-permute-start | bytes 344072 | tf_op jit(solution)/shard_map/ppermute | solution.py:427
  105.2 5.6 %collective-permute-done.25.refs_2_ = bf16[64,896]{1,0:T(8,128)(2,1)S(1)} collective-permute-done((bf16[64,896]{1,0:T(8,128)(2,1)S(1)}, bf16[64,896]{1,0:T(8,128)(2,1)S(1)}, u32[]{:S(2)}, u32[]{:S(2)}) %collective-permute-start.25) | collective-permute-done | bytes 114720 | tf_op jit(solution)/shard_map/ppermute | solution.py:427
  110.8 2.9 %collective-permute-done.26.refs_3_ = bf16[64,896]{1,0:T(8,128)(2,1)S(1)} collective-permute-done((bf16[64,896]{1,0:T(8,128)(2,1)S(1)}, bf16[64,896]{1,0:T(8,128)(2,1)S(1)}, u32[]{:S(2)}, u32[]{:S(2)}) %collective-permute-start.26) | collective-permute-done | bytes 114720 | tf_op jit(solution)/shard_map/ppermute | solution.py:427
  113.7 0.1 share.1
  113.7 0.1 collective-permute-start.27
  113.8 1.3 %collective-permute-done.27.got = f32[32,896]{1,0:T(8,128)S(1)} collective-permute-done((f32[32,896]{1,0:T(8,128)S(1)}, f32[32,896]{1,0:T(8,128)S(1)}, u32[]{:S(2)}, u32[]{:S(2)}) %collective-permute-start.27) | collective-permute-done | bytes 114720 | tf_op jit(solution)/shard_map/ppermute | solution.py:350
  115.2 1.3 %collective-permute-start.28 = (f32[8,1792]{1,0:T(8,128)S(1)}, f32[8,1792]{1,0:T(8,128)S(1)}, u32[]{:S(2)}, u32[]{:S(2)}) collective-permute-start(f32[8,1792]{1,0:T(8,128)S(1)} %get-tuple-element.66), channel_id=1, source_target_pairs={{0,32},{32,64},{64,96},{96,0},{1,33},{33,65},{65,97},{97,1},{2,34}... | collective-permute-start | bytes 172040 | tf_op jit(solution)/shard_map/ppermute | solution.py:437
  116.4 0.9 collective-permute-start.29
  117.4 0.8 collective-permute-start.30
  118.2 1.7 %collective-permute-done.28.refs_1_ = f32[8,1792]{1,0:T(8,128)S(1)} collective-permute-done((f32[8,1792]{1,0:T(8,128)S(1)}, f32[8,1792]{1,0:T(8,128)S(1)}, u32[]{:S(2)}, u32[]{:S(2)}) %collective-permute-start.28) | collective-permute-done | bytes 57376 | tf_op jit(solution)/shard_map/ppermute | solution.py:437
  119.9 2.8 %collective-permute-done.29.refs_2_ = f32[8,1792]{1,0:T(8,128)S(1)} collective-permute-done((f32[8,1792]{1,0:T(8,128)S(1)}, f32[8,1792]{1,0:T(8,128)S(1)}, u32[]{:S(2)}, u32[]{:S(2)}) %collective-permute-start.29) | collective-permute-done | bytes 57376 | tf_op jit(solution)/shard_map/ppermute | solution.py:437
  122.7 0.4 collective-permute-done.30.refs_3_
  123.0 1.3 %place.1 = bf16[8,7168]{1,0:T(8,128)(2,1)} custom-call(s32[5]{0:T(128)S(1)} %stack.23.ids, f32[8,1792]{1,0:T(8,128)S(1)} %get-tuple-element.65.refs_0_, f32[8,1792]{1,0:T(8,128)S(1)} %collective-permute-done.28.refs_1_, f32[8,1792]{1,0:T(8,128)S(1)} %collective-permute-done.29.refs_2_, f32[8,1792]{1,0:T(8,128)S(1)} %collective-permute-done.30.refs_3_), custom_call_target="tpu_custom_call" | custom-call | tf_op jit(solution)/shard_map/place/pallas_call | solution.py:334
  (34 shorter events, 0.2 us)
Async XLA Ops:
  0.0 41.0 %copy-start.3 = (bf16[512,448]{0,1:T(8,128)(2,1)S(1)}, bf16[512,448]{0,1:T(8,128)(2,1)}, u32[]{:S(2)}) copy-start(bf16[512,448]{0,1:T(8,128)(2,1)} %param.21) | copy-start | bytes 1376260
  0.0 45.1 %copy-start.2 = (bf16[4,128,512]{2,1,0:T(8,128)(2,1)S(1)}, bf16[4,128,512]{2,1,0:T(8,128)(2,1)}, u32[]{:S(2)}) copy-start(bf16[4,128,512]{2,1,0:T(8,128)(2,1)} %refs_4_.3) | copy-start | bytes 1572868
  25.0 19.6 %copy-start = (bf16[576,512]{1,0:T(8,128)(2,1)S(1)}, bf16[576,512]{1,0:T(8,128)(2,1)}, u32[]{:S(2)}) copy-start(bf16[576,512]{1,0:T(8,128)(2,1)} %get-tuple-element.38.refs_0_) | copy-start | bytes 1769476
  25.0 20.1 %copy-start.4 = (bf16[128,768]{1,0:T(8,128)(2,1)S(1)}, bf16[128,768]{1,0:T(8,128)(2,1)}, u32[]{:S(2)}) copy-start(bf16[128,768]{1,0:T(8,128)(2,1)} %get-tuple-element.40.refs_0_) | copy-start | bytes 589828
  25.0 15.9 %collective-permute-start = (bf16[576,512]{1,0:T(8,128)(2,1)}, bf16[576,512]{1,0:T(8,128)(2,1)S(1)}, u32[]{:S(2)}, u32[]{:S(2)}) collective-permute-start(bf16[576,512]{1,0:T(8,128)(2,1)} %get-tuple-element.38.refs_0_), channel_id=1, source_target_pairs={{0,128},{128,0},{1,129},{129,1},{2,130},{130,2},{3,131},{131,3},{4... | collective-permute-start | bytes 1769480 | tf_op jit(solution)/shard_map/ppermute | solution.py:350
  26.7 14.3 %collective-permute-start.1 = (bf16[448,512]{1,0:T(8,128)(2,1)}, bf16[448,512]{1,0:T(8,128)(2,1)S(1)}, u32[]{:S(2)}, u32[]{:S(2)}) collective-permute-start(bf16[448,512]{1,0:T(8,128)(2,1)} %bitcast.11), channel_id=1, source_target_pairs={{0,2},{2,0},{1,3},{3,1},{4,6},{6,4},{5,7},{7,5},{8,10},{10,8},{9,1... | collective-permute-start | bytes 1376264 | tf_op jit(solution)/shard_map/ppermute | solution.py:350
  28.6 11.7 %collective-permute-start.2 = (bf16[128,768]{1,0:T(8,128)(2,1)}, bf16[128,768]{1,0:T(8,128)(2,1)S(1)}, u32[]{:S(2)}, u32[]{:S(2)}) collective-permute-start(bf16[128,768]{1,0:T(8,128)(2,1)} %get-tuple-element.40.refs_0_), channel_id=1, source_target_pairs={{32,0},{64,32},{96,64},{0,96},{33,1},{65,33},{97,65},{1,97},{34,2}... | collective-permute-start | bytes 589832 | tf_op jit(solution)/shard_map/ppermute | solution.py:346
  29.5 10.9 %collective-permute-start.3 = (bf16[128,768]{1,0:T(8,128)(2,1)}, bf16[128,768]{1,0:T(8,128)(2,1)S(1)}, u32[]{:S(2)}, u32[]{:S(2)}) collective-permute-start(bf16[128,768]{1,0:T(8,128)(2,1)} %get-tuple-element.40.refs_0_), channel_id=1, source_target_pairs={{64,0},{96,32},{0,64},{32,96},{65,1},{97,33},{1,65},{33,97},{66,2}... | collective-permute-start | bytes 589832 | tf_op jit(solution)/shard_map/ppermute | solution.py:346
  30.6 10.4 %collective-permute-start.4 = (bf16[128,768]{1,0:T(8,128)(2,1)}, bf16[128,768]{1,0:T(8,128)(2,1)S(1)}, u32[]{:S(2)}, u32[]{:S(2)}) collective-permute-start(bf16[128,768]{1,0:T(8,128)(2,1)} %get-tuple-element.40.refs_0_), channel_id=1, source_target_pairs={{96,0},{0,32},{32,64},{64,96},{97,1},{1,33},{33,65},{65,97},{98,2}... | collective-permute-start | bytes 589832 | tf_op jit(solution)/shard_map/ppermute | solution.py:346
  32.7 0.7 copy-start.7
  33.4 0.7 copy-start.8
  41.0 6.5 %copy-start.1 = (bf16[4,512,128]{2,1,0:T(8,128)(2,1)S(1)}, bf16[4,512,128]{2,1,0:T(8,128)(2,1)}, u32[]{:S(2)}) copy-start(bf16[4,512,128]{2,1,0:T(8,128)(2,1)} %refs_4_.5) | copy-start | bytes 1572868
  41.1 34.0 %collective-permute-start.13 = (bf16[2,448,512]{2,1,0:T(8,128)(2,1)S(1)}, bf16[2,448,512]{2,1,0:T(8,128)(2,1)S(1)}, u32[]{:S(2)}, u32[]{:S(2)}) collective-permute-start(bf16[2,448,512]{2,1,0:T(8,128)(2,1)S(1)} %pair.1.refs_8_), channel_id=1, source_target_pairs={{0,128},{1,129},{128,0},{129,1},{2,130},{3,131},{130,2},{131,3},{4... | collective-permute-start | bytes 2752520 | tf_op jit(solution)/shard_map/ppermute | solution.py:350
  42.1 33.0 %collective-permute-start.14 = (bf16[2,448,512]{2,1,0:T(8,128)(2,1)S(1)}, bf16[2,448,512]{2,1,0:T(8,128)(2,1)S(1)}, u32[]{:S(2)}, u32[]{:S(2)}) collective-permute-start(bf16[2,448,512]{2,1,0:T(8,128)(2,1)S(1)} %pair.1.refs_8_), channel_id=1, source_target_pairs={{0,129},{1,128},{128,1},{129,0},{2,131},{3,130},{130,3},{131,2},{4... | collective-permute-start | bytes 2752520 | tf_op jit(solution)/shard_map/ppermute | solution.py:350
  44.6 2.0 %collective-permute-start.5 = (bf16[576,512]{1,0:T(8,128)(2,1)S(1)}, bf16[576,512]{1,0:T(8,128)(2,1)S(1)}, u32[]{:S(2)}, u32[]{:S(2)}) collective-permute-start(bf16[576,512]{1,0:T(8,128)(2,1)S(1)} %copy-done), channel_id=1, source_target_pairs={{0,16},{16,0},{1,17},{17,1},{2,18},{18,2},{3,19},{19,3},{4,20},{20... | collective-permute-start | bytes 1769480 | tf_op jit(solution)/shard_map/ppermute | solution.py:350
  44.6 2.8 %collective-permute-start.6 = (bf16[576,512]{1,0:T(8,128)(2,1)S(1)}, bf16[576,512]{1,0:T(8,128)(2,1)S(1)}, u32[]{:S(2)}, u32[]{:S(2)}) collective-permute-start(bf16[576,512]{1,0:T(8,128)(2,1)S(1)} %get-tuple-element.44.refs_1_), channel_id=1, source_target_pairs={{0,16},{16,0},{1,17},{17,1},{2,18},{18,2},{3,19},{19,3},{4,20},{20... | collective-permute-start | bytes 1769480 | tf_op jit(solution)/shard_map/ppermute | solution.py:350
  47.5 10.9 %copy-start.5 = (bf16[128,512]{1,0:T(8,128)(2,1)S(1)}, bf16[128,512]{1,0:T(8,128)(2,1)}, u32[]{:S(2)}) copy-start(bf16[128,512]{1,0:T(8,128)(2,1)} %refs_5_.1) | copy-start | bytes 393220
  47.5 10.9 %copy-start.6 = (bf16[1,64,128]{2,1,0:T(8,128)(2,1)S(1)}, bf16[1,64,128]{2,1,0:T(8,128)(2,1)}, u32[]{:S(2)}) copy-start(bf16[1,64,128]{2,1,0:T(8,128)(2,1)} %param.14) | copy-start | bytes 49156
  53.6 9.0 %collective-permute-start.7 = (bf16[128,640]{1,0:T(8,128)(2,1)S(1)}, bf16[128,640]{1,0:T(8,128)(2,1)S(1)}, u32[]{:S(2)}, u32[]{:S(2)}) collective-permute-start(bf16[128,640]{1,0:T(8,128)(2,1)S(1)} %get-tuple-element.45), channel_id=1, source_target_pairs={{0,32},{32,64},{64,96},{96,0},{1,33},{33,65},{65,97},{97,1},{2,34}... | collective-permute-start | bytes 491528 | tf_op jit(solution)/shard_map/ppermute | solution.py:403
  57.4 7.1 %collective-permute-start.8 = (bf16[128,640]{1,0:T(8,128)(2,1)S(1)}, bf16[128,640]{1,0:T(8,128)(2,1)S(1)}, u32[]{:S(2)}, u32[]{:S(2)}) collective-permute-start(bf16[128,640]{1,0:T(8,128)(2,1)S(1)} %get-tuple-element.46), channel_id=1, source_target_pairs={{0,64},{32,96},{64,0},{96,32},{1,65},{33,97},{65,1},{97,33},{2,66}... | collective-permute-start | bytes 491528 | tf_op jit(solution)/shard_map/ppermute | solution.py:403
  57.6 8.6 %collective-permute-start.9 = (bf16[128,640]{1,0:T(8,128)(2,1)S(1)}, bf16[128,640]{1,0:T(8,128)(2,1)S(1)}, u32[]{:S(2)}, u32[]{:S(2)}) collective-permute-start(bf16[128,640]{1,0:T(8,128)(2,1)S(1)} %get-tuple-element.47), channel_id=1, source_target_pairs={{0,96},{32,0},{64,32},{96,64},{1,97},{33,1},{65,33},{97,65},{2,98}... | collective-permute-start | bytes 491528 | tf_op jit(solution)/shard_map/ppermute | solution.py:403
  67.3 5.5 %collective-permute-start.10 = (bf16[32,512]{1,0:T(8,128)(2,1)S(1)}, bf16[32,512]{1,0:T(8,128)(2,1)S(1)}, u32[]{:S(2)}, u32[]{:S(2)}) collective-permute-start(bf16[32,512]{1,0:T(8,128)(2,1)S(1)} %get-tuple-element.49), channel_id=1, source_target_pairs={{0,1},{1,0},{2,3},{3,2},{4,5},{5,4},{6,7},{7,6},{8,9},{9,8},{10,11... | collective-permute-start | bytes 98312 | tf_op jit(solution)/shard_map/ppermute | solution.py:350
  68.0 4.8 %collective-permute-start.11 = (bf16[32,512]{1,0:T(8,128)(2,1)S(1)}, bf16[32,512]{1,0:T(8,128)(2,1)S(1)}, u32[]{:S(2)}, u32[]{:S(2)}) collective-permute-start(bf16[32,512]{1,0:T(8,128)(2,1)S(1)} %get-tuple-element.50), channel_id=1, source_target_pairs={{0,2},{1,3},{2,0},{3,1},{4,6},{5,7},{6,4},{7,5},{8,10},{9,11},{10,... | collective-permute-start | bytes 98312 | tf_op jit(solution)/shard_map/ppermute | solution.py:350
  68.8 6.3 %collective-permute-start.12 = (bf16[32,512]{1,0:T(8,128)(2,1)S(1)}, bf16[32,512]{1,0:T(8,128)(2,1)S(1)}, u32[]{:S(2)}, u32[]{:S(2)}) collective-permute-start(bf16[32,512]{1,0:T(8,128)(2,1)S(1)} %get-tuple-element.51), channel_id=1, source_target_pairs={{0,3},{1,2},{2,1},{3,0},{4,7},{5,6},{6,5},{7,4},{8,11},{9,10},{10,... | collective-permute-start | bytes 98312 | tf_op jit(solution)/shard_map/ppermute | solution.py:350
  75.2 13.7 %collective-permute-start.16 = (bf16[448,512]{1,0:T(8,128)(2,1)S(1)}, bf16[448,512]{1,0:T(8,128)(2,1)S(1)}, u32[]{:S(2)}, u32[]{:S(2)}) collective-permute-start(bf16[448,512]{1,0:T(8,128)(2,1)S(1)} %slice_bitcast_fusion.1), channel_id=1, source_target_pairs={{0,128},{1,129},{128,0},{129,1},{2,130},{3,131},{130,2},{131,3},{4... | collective-permute-start | bytes 1376264 | tf_op jit(solution)/shard_map/ppermute | solution.py:350
  78.6 11.8 %collective-permute-start.17 = (bf16[448,512]{1,0:T(8,128)(2,1)S(1)}, bf16[448,512]{1,0:T(8,128)(2,1)S(1)}, u32[]{:S(2)}, u32[]{:S(2)}) collective-permute-start(bf16[448,512]{1,0:T(8,128)(2,1)S(1)} %slice_bitcast_fusion), channel_id=1, source_target_pairs={{0,129},{1,128},{128,1},{129,0},{2,131},{3,130},{130,3},{131,2},{4... | collective-permute-start | bytes 1376264 | tf_op jit(solution)/shard_map/ppermute | solution.py:350
  80.4 7.6 %collective-permute-start.15 = (bf16[32,2048]{1,0:T(8,128)(2,1)S(1)}, bf16[32,2048]{1,0:T(8,128)(2,1)S(1)}, u32[]{:S(2)}, u32[]{:S(2)}) collective-permute-start(bf16[32,2048]{1,0:T(8,128)(2,1)S(1)} %get-tuple-element.53.refs_0_), channel_id=1, source_target_pairs={{32,0},{64,32},{96,64},{0,96},{33,1},{65,33},{97,65},{1,97},{34,2}... | collective-permute-start | bytes 393224 | tf_op jit(solution)/shard_map/ppermute | solution.py:346
  81.1 6.9 %collective-permute-start.18 = (bf16[32,2048]{1,0:T(8,128)(2,1)S(1)}, bf16[32,2048]{1,0:T(8,128)(2,1)S(1)}, u32[]{:S(2)}, u32[]{:S(2)}) collective-permute-start(bf16[32,2048]{1,0:T(8,128)(2,1)S(1)} %get-tuple-element.53.refs_0_), channel_id=1, source_target_pairs={{64,0},{96,32},{0,64},{32,96},{65,1},{97,33},{1,65},{33,97},{66,2}... | collective-permute-start | bytes 393224 | tf_op jit(solution)/shard_map/ppermute | solution.py:346
  82.5 6.3 %collective-permute-start.19 = (bf16[32,2048]{1,0:T(8,128)(2,1)S(1)}, bf16[32,2048]{1,0:T(8,128)(2,1)S(1)}, u32[]{:S(2)}, u32[]{:S(2)}) collective-permute-start(bf16[32,2048]{1,0:T(8,128)(2,1)S(1)} %get-tuple-element.53.refs_0_), channel_id=1, source_target_pairs={{96,0},{0,32},{32,64},{64,96},{97,1},{1,33},{33,65},{65,97},{98,2}... | collective-permute-start | bytes 393224 | tf_op jit(solution)/shard_map/ppermute | solution.py:346
  88.0 2.4 %collective-permute-start.20 = (bf16[32,2048]{1,0:T(8,128)(2,1)S(1)}, bf16[32,2048]{1,0:T(8,128)(2,1)S(1)}, u32[]{:S(2)}, u32[]{:S(2)}) collective-permute-start(bf16[32,2048]{1,0:T(8,128)(2,1)S(1)} %get-tuple-element.53.refs_0_), channel_id=1, source_target_pairs={{0,16},{16,0},{1,17},{17,1},{2,18},{18,2},{3,19},{19,3},{4,20},{20... | collective-permute-start | bytes 393224 | tf_op jit(solution)/shard_map/ppermute | solution.py:350
  88.0 2.4 %collective-permute-start.22 = (bf16[32,2048]{1,0:T(8,128)(2,1)S(1)}, bf16[32,2048]{1,0:T(8,128)(2,1)S(1)}, u32[]{:S(2)}, u32[]{:S(2)}) collective-permute-start(bf16[32,2048]{1,0:T(8,128)(2,1)S(1)} %collective-permute-done.18.refs_2_), channel_id=1, source_target_pairs={{0,16},{16,0},{1,17},{17,1},{2,18},{18,2},{3,19},{19,3},{4,20},{20... | collective-permute-start | bytes 393224 | tf_op jit(solution)/shard_map/ppermute | solution.py:350
  88.8 1.6 %collective-permute-start.23 = (bf16[32,2048]{1,0:T(8,128)(2,1)S(1)}, bf16[32,2048]{1,0:T(8,128)(2,1)S(1)}, u32[]{:S(2)}, u32[]{:S(2)}) collective-permute-start(bf16[32,2048]{1,0:T(8,128)(2,1)S(1)} %collective-permute-done.19.refs_3_), channel_id=1, source_target_pairs={{0,16},{16,0},{1,17},{17,1},{2,18},{18,2},{3,19},{19,3},{4,20},{20... | collective-permute-start | bytes 393224 | tf_op jit(solution)/shard_map/ppermute | solution.py:350
  90.4 1.3 %collective-permute-start.21 = (bf16[32,2048]{1,0:T(8,128)(2,1)S(1)}, bf16[32,2048]{1,0:T(8,128)(2,1)S(1)}, u32[]{:S(2)}, u32[]{:S(2)}) collective-permute-start(bf16[32,2048]{1,0:T(8,128)(2,1)S(1)} %get-tuple-element.56.refs_1_), channel_id=1, source_target_pairs={{0,16},{16,0},{1,17},{17,1},{2,18},{18,2},{3,19},{19,3},{4,20},{20... | collective-permute-start | bytes 393224 | tf_op jit(solution)/shard_map/ppermute | solution.py:350
  93.7 11.5 %collective-permute-start.24 = (bf16[64,896]{1,0:T(8,128)(2,1)S(1)}, bf16[64,896]{1,0:T(8,128)(2,1)S(1)}, u32[]{:S(2)}, u32[]{:S(2)}) collective-permute-start(bf16[64,896]{1,0:T(8,128)(2,1)S(1)} %get-tuple-element.60), channel_id=1, source_target_pairs={{0,4},{4,8},{8,12},{12,0},{1,5},{5,9},{9,13},{13,1},{2,6},{6,10},{... | collective-permute-start | bytes 344072 | tf_op jit(solution)/shard_map/ppermute | solution.py:427
  97.0 13.7 %collective-permute-start.25 = (bf16[64,896]{1,0:T(8,128)(2,1)S(1)}, bf16[64,896]{1,0:T(8,128)(2,1)S(1)}, u32[]{:S(2)}, u32[]{:S(2)}) collective-permute-start(bf16[64,896]{1,0:T(8,128)(2,1)S(1)} %get-tuple-element.61), channel_id=1, source_target_pairs={{0,8},{4,12},{8,0},{12,4},{1,9},{5,13},{9,1},{13,5},{2,10},{6,14},... | collective-permute-start | bytes 344072 | tf_op jit(solution)/shard_map/ppermute | solution.py:427
  102.5 11.1 %collective-permute-start.26 = (bf16[64,896]{1,0:T(8,128)(2,1)S(1)}, bf16[64,896]{1,0:T(8,128)(2,1)S(1)}, u32[]{:S(2)}, u32[]{:S(2)}) collective-permute-start(bf16[64,896]{1,0:T(8,128)(2,1)S(1)} %get-tuple-element.62), channel_id=1, source_target_pairs={{0,12},{4,0},{8,4},{12,8},{1,13},{5,1},{9,5},{13,9},{2,14},{6,2},{... | collective-permute-start | bytes 344072 | tf_op jit(solution)/shard_map/ppermute | solution.py:427
  113.7 1.4 %collective-permute-start.27 = (f32[32,896]{1,0:T(8,128)S(1)}, f32[32,896]{1,0:T(8,128)S(1)}, u32[]{:S(2)}, u32[]{:S(2)}) collective-permute-start(f32[32,896]{1,0:T(8,128)S(1)} %get-tuple-element.64), channel_id=1, source_target_pairs={{0,16},{16,0},{1,17},{17,1},{2,18},{18,2},{3,19},{19,3},{4,20},{20... | collective-permute-start | bytes 344072 | tf_op jit(solution)/shard_map/ppermute | solution.py:350
  115.2 4.7 %collective-permute-start.28 = (f32[8,1792]{1,0:T(8,128)S(1)}, f32[8,1792]{1,0:T(8,128)S(1)}, u32[]{:S(2)}, u32[]{:S(2)}) collective-permute-start(f32[8,1792]{1,0:T(8,128)S(1)} %get-tuple-element.66), channel_id=1, source_target_pairs={{0,32},{32,64},{64,96},{96,0},{1,33},{33,65},{65,97},{97,1},{2,34}... | collective-permute-start | bytes 172040 | tf_op jit(solution)/shard_map/ppermute | solution.py:437
  116.4 6.2 %collective-permute-start.29 = (f32[8,1792]{1,0:T(8,128)S(1)}, f32[8,1792]{1,0:T(8,128)S(1)}, u32[]{:S(2)}, u32[]{:S(2)}) collective-permute-start(f32[8,1792]{1,0:T(8,128)S(1)} %get-tuple-element.67), channel_id=1, source_target_pairs={{0,64},{32,96},{64,0},{96,32},{1,65},{33,97},{65,1},{97,33},{2,66}... | collective-permute-start | bytes 172040 | tf_op jit(solution)/shard_map/ppermute | solution.py:437
  117.4 5.6 %collective-permute-start.30 = (f32[8,1792]{1,0:T(8,128)S(1)}, f32[8,1792]{1,0:T(8,128)S(1)}, u32[]{:S(2)}, u32[]{:S(2)}) collective-permute-start(f32[8,1792]{1,0:T(8,128)S(1)} %get-tuple-element.68), channel_id=1, source_target_pairs={{0,96},{32,0},{64,32},{96,64},{1,97},{33,1},{65,33},{97,65},{2,98}... | collective-permute-start | bytes 172040 | tf_op jit(solution)/shard_map/ppermute | solution.py:437

commit v12 on v11

--- a/solution.py
+++ b/solution.py
@@ -248,7 +248,7 @@
             jax.ShapeDtypeStruct((4 * BLOCK + ROPE, LAT), jnp.bfloat16),
         ],
         in_specs=[pl.BlockSpec(memory_space=pltpu.HBM)] * 4,
-        out_specs=[pl.BlockSpec(memory_space=pltpu.HBM)] * 2,
+        out_specs=[pl.BlockSpec(memory_space=VMEM)] * 2,
         scratch_shapes=[pltpu.SemaphoreType.DMA((10,))],
         compiler_params=pltpu.CompilerParams(vmem_limit_bytes=56 * 2**20),
         name="pack",

time: 125 us -> 104 us (0.83)
  Pallas kernels: 42 us -> 22.9 us
  starting transfers between devices: 46.3 us -> 44.2 us
    pallas_call x1, Pallas kernels: 25 us -> 2.3 us  [pack(): pl.pallas_call(pack_kernel, out_shape=[jax.ShapeDtypeStruct((TOK, HEADS *...]
    pallas_call x2, Pallas kernels: 8.9 us -> 12.2 us  [attention(): pl.pallas_call(functools.partial(attention_kernel, slots, own), out_shape...]
    ppermute x3, starting transfers between devices: 4.76 us -> 2.86 us  [local(): lax.ppermute(part, 'x', [(i, (i + s) % 4) for i in range(4)])]
    ppermute x3, waiting for transfers between devices: 5.05 us -> 3.7 us  [local(): lax.ppermute(part, 'x', [(i, (i + s) % 4) for i in range(4)])]
  transfers between devices with their start and end apart: 31 -> 31, of which waited for: 19 -> 18; matrix products, arithmetic and copies ran while one was open for 0% -> 0% of each run, Pallas kernels for 11% -> 17%
where the time goes in v12:
time: 104 us; the launch traced here: 103 us
  starting transfers between devices  44.2 us (42%)
  waiting for transfers between devices  33.8 us (32%)
  Pallas kernels  22.9 us (22%)
  local copies, waits for them, and re-layouts  1.52 us (1%)
    ppermute x16, starting transfers between devices, flip(): return lax.ppermute(value, axis, [(i, i ^ bits) for i in range(size)])  18.5 us
    pallas_call x2, Pallas kernels, attention(): pl.pallas_call(functools.partial(attention_kernel, slots, own), out_shape...  12.2 us
    ppermute x3, starting transfers between devices, local(): lax.ppermute(partial[d], 'zb', [(i, (i + d) % 4) for i in range(4)])  11.5 us
    ppermute x16, waiting for transfers between devices, flip(): return lax.ppermute(value, axis, [(i, i ^ bits) for i in range(size)])  9 us
    ppermute x3, waiting for transfers between devices, local(): lax.ppermute(partial[d], 'zb', [(i, (i + d) % 4) for i in range(4)])  8.54 us
    ppermute x6, starting transfers between devices, turn(): lax.ppermute(value, axis, [((i + shift) % size, i) for i in range(size)])  8.41 us
    ppermute x6, waiting for transfers between devices, turn(): lax.ppermute(value, axis, [((i + shift) % size, i) for i in range(size)])  7.73 us
    pallas_call x8, Pallas kernels, simple(): pl.pallas_call(kernel, out_shape=out_shape, in_specs=[pl.BlockSpec(memory...  5.73 us
  transfers between devices with their start and end apart: 31, of which 18 were waited for; matrix products, arithmetic and copies ran while one was open for 0% of the time, Pallas kernels for 17%

profile of v12, /device:TPU:6, one launch (start us, length us, event | category | flops | bytes accessed | tf_op | source)
XLA Modules:
  0.0 102.7 jit_solution(3624160745603817296)
XLA Ops:
  0.0 2.3 %pack.1 = (bf16[128,768]{1,0:T(8,128)(2,1)}, bf16[576,512]{1,0:T(8,128)(2,1)}) custom-call(bf16[128,512]{1,0:T(8,128)(2,1)} %q_nope.1, bf16[128,256]{1,0:T(8,128)(2,1)} %q_rope.1, bf16[4,128,512]{2,1,0:T(8,128)(2,1)} %pool_latent.1, bf16[4,64,128]{2,1,0:T(8,128)(2,1)} %pool_rope.1), custom_call_target="tpu_custom_call" | custom-call | tf_op jit(solution)/shard_map/pack/pallas_call | solution.py:244
  2.3 1.7 %collective-permute-start = (bf16[576,512]{1,0:T(8,128)(2,1)}, bf16[576,512]{1,0:T(8,128)(2,1)S(1)}, u32[]{:S(2)}, u32[]{:S(2)}) collective-permute-start(bf16[576,512]{1,0:T(8,128)(2,1)} %get-tuple-element.38.refs_0_), channel_id=1, source_target_pairs={{0,128},{128,0},{1,129},{129,1},{2,130},{130,2},{3,131},{131,3},{4... | collective-permute-start | bytes 1769480 | tf_op jit(solution)/shard_map/ppermute | solution.py:350
  4.0 1.9 %collective-permute-start.1 = (bf16[448,512]{1,0:T(8,128)(2,1)}, bf16[448,512]{1,0:T(8,128)(2,1)S(1)}, u32[]{:S(2)}, u32[]{:S(2)}) collective-permute-start(bf16[448,512]{1,0:T(8,128)(2,1)} %bitcast.11), channel_id=1, source_target_pairs={{0,2},{2,0},{1,3},{3,1},{4,6},{6,4},{5,7},{7,5},{8,10},{10,8},{9,1... | collective-permute-start | bytes 1376264 | tf_op jit(solution)/shard_map/ppermute | solution.py:350
  5.9 0.8 collective-permute-start.2
  6.7 1.1 %collective-permute-start.3 = (bf16[128,768]{1,0:T(8,128)(2,1)}, bf16[128,768]{1,0:T(8,128)(2,1)S(1)}, u32[]{:S(2)}, u32[]{:S(2)}) collective-permute-start(bf16[128,768]{1,0:T(8,128)(2,1)} %get-tuple-element.40.refs_0_), channel_id=1, source_target_pairs={{64,0},{96,32},{0,64},{32,96},{65,1},{97,33},{1,65},{33,97},{66,2}... | collective-permute-start | bytes 589832 | tf_op jit(solution)/shard_map/ppermute | solution.py:346
  7.9 2.1 %collective-permute-start.4 = (bf16[128,768]{1,0:T(8,128)(2,1)}, bf16[128,768]{1,0:T(8,128)(2,1)S(1)}, u32[]{:S(2)}, u32[]{:S(2)}) collective-permute-start(bf16[128,768]{1,0:T(8,128)(2,1)} %get-tuple-element.40.refs_0_), channel_id=1, source_target_pairs={{96,0},{0,32},{32,64},{64,96},{97,1},{1,33},{33,65},{65,97},{98,2}... | collective-permute-start | bytes 589832 | tf_op jit(solution)/shard_map/ppermute | solution.py:346
  10.0 0.1 stack.23.ids
  10.0 0.7 copy-done.7
  10.7 0.7 copy-done.8
  11.4 2.7 %plan.1 = (s32[64]{0:T(128)S(1)}, s32[8]{0:T(128)S(1)}) custom-call(s32[5]{0:T(128)S(1)} %stack.23.ids, s32[16,32]{1,0:T(8,128)S(1)} %copy-done.7, s32[16]{0:T(128)S(1)} %copy-done.8), custom_call_target="tpu_custom_call" | custom-call | tf_op jit(solution)/shard_map/plan/pallas_call | solution.py:65
  14.1 3.6 %collective-permute-done.2.refs_3_.refs_1_ = bf16[128,768]{1,0:T(8,128)(2,1)S(1)} collective-permute-done((bf16[128,768]{1,0:T(8,128)(2,1)}, bf16[128,768]{1,0:T(8,128)(2,1)S(1)}, u32[]{:S(2)}, u32[]{:S(2)}) %collective-permute-start.2) | collective-permute-done | bytes 196640 | tf_op jit(solution)/shard_map/ppermute | solution.py:346
  17.6 0.0 collective-permute-done.3.refs_4_.refs_2_
  17.6 0.6 collective-permute-done.4.refs_5_.refs_3_
  18.3 0.0 collective-permute-done.1.refs_2_
  18.3 0.0 collective-permute-done.refs_0_
  18.3 0.1 pair.1.refs_8_
  18.4 1.1 %collective-permute-start.13 = (bf16[2,448,512]{2,1,0:T(8,128)(2,1)S(1)}, bf16[2,448,512]{2,1,0:T(8,128)(2,1)S(1)}, u32[]{:S(2)}, u32[]{:S(2)}) collective-permute-start(bf16[2,448,512]{2,1,0:T(8,128)(2,1)S(1)} %pair.1.refs_8_), channel_id=1, source_target_pairs={{0,128},{1,129},{128,0},{129,1},{2,130},{3,131},{130,2},{131,3},{4... | collective-permute-start | bytes 2752520 | tf_op jit(solution)/shard_map/ppermute | solution.py:350
  19.4 2.5 %collective-permute-start.14 = (bf16[2,448,512]{2,1,0:T(8,128)(2,1)S(1)}, bf16[2,448,512]{2,1,0:T(8,128)(2,1)S(1)}, u32[]{:S(2)}, u32[]{:S(2)}) collective-permute-start(bf16[2,448,512]{2,1,0:T(8,128)(2,1)S(1)} %pair.1.refs_8_), channel_id=1, source_target_pairs={{0,129},{1,128},{128,1},{129,0},{2,131},{3,130},{130,3},{131,2},{4... | collective-permute-start | bytes 2752520 | tf_op jit(solution)/shard_map/ppermute | solution.py:350
  21.9 0.0 collective-permute-start.5
  21.9 0.5 collective-permute-start.6
  22.4 1.3 %prepare.1 = (bf16[4,512,512]{2,1,0:T(8,128)(2,1)S(1)}, bf16[4,512,64]{2,1,0:T(8,128)(2,1)S(1)}) custom-call(s32[8]{0:T(128)S(1)} %get-tuple-element.41.counts, bf16[128,768]{1,0:T(8,128)(2,1)S(1)} %copy-done.4, bf16[128,768]{1,0:T(8,128)(2,1)S(1)} %collective-permute-done.2.refs_3_.refs_1_, bf16[128,768]{1,0:T(8,128)(2,1)S(1)} %collective-permute-done.3.refs_4_.refs_2_, ...), custom_call_target="tpu_custom_call" | custom-call | tf_op jit(solution)/shard_map/prepare/pallas_call | solution.py:334
  23.7 0.2 collective-permute-done.5.refs_2_
  23.9 0.8 collective-permute-done.6.refs_3_
  24.8 8.4 %attend.3 = (bf16[128,640]{1,0:T(8,128)(2,1)S(1)}, bf16[128,640]{1,0:T(8,128)(2,1)S(1)}, bf16[128,640]{1,0:T(8,128)(2,1)S(1)}) custom-call(s32[64]{0:T(128)S(1)} %get-tuple-element.37.lists, s32[8]{0:T(128)S(1)} %get-tuple-element.41.counts, bf16[4,512,512]{2,1,0:T(8,128)(2,1)S(1)} %get-tuple-element.42.q_lat, ...), custom_call_target="tpu_custom_call" | custom-call | tf_op jit(solution)/shard_map/attend/pallas_call | solution.py:185
  33.1 1.6 %collective-permute-start.7 = (bf16[128,640]{1,0:T(8,128)(2,1)S(1)}, bf16[128,640]{1,0:T(8,128)(2,1)S(1)}, u32[]{:S(2)}, u32[]{:S(2)}) collective-permute-start(bf16[128,640]{1,0:T(8,128)(2,1)S(1)} %get-tuple-element.45), channel_id=1, source_target_pairs={{0,32},{32,64},{64,96},{96,0},{1,33},{33,65},{65,97},{97,1},{2,34}... | collective-permute-start | bytes 491528 | tf_op jit(solution)/shard_map/ppermute | solution.py:403
  34.8 1.2 %collective-permute-start.8 = (bf16[128,640]{1,0:T(8,128)(2,1)S(1)}, bf16[128,640]{1,0:T(8,128)(2,1)S(1)}, u32[]{:S(2)}, u32[]{:S(2)}) collective-permute-start(bf16[128,640]{1,0:T(8,128)(2,1)S(1)} %get-tuple-element.46), channel_id=1, source_target_pairs={{0,64},{32,96},{64,0},{96,32},{1,65},{33,97},{65,1},{97,33},{2,66}... | collective-permute-start | bytes 491528 | tf_op jit(solution)/shard_map/ppermute | solution.py:403
  36.0 3.9 %attend.2.refs_0_ = bf16[128,640]{1,0:T(8,128)(2,1)S(1)} custom-call(s32[64]{0:T(128)S(1)} %get-tuple-element.37.lists, s32[8]{0:T(128)S(1)} %get-tuple-element.41.counts, bf16[4,512,512]{2,1,0:T(8,128)(2,1)S(1)} %get-tuple-element.42.q_lat, bf16[4,512,64]{2,1,0:T(8,128)(2,1)S(1)} %get-tuple-element.43.q_rot, bf16[576,512]{1,0:T(8,128)(2,1)S(1)} %copy-done, ...), custom_call_target="tpu_custom_call" | custom-call | tf_op jit(solution)/shard_map/attend/pallas_call | solution.py:185
  39.9 0.0 collective-permute-done.7.refs_1_
  39.9 2.0 %collective-permute-done.8.refs_2_ = bf16[128,640]{1,0:T(8,128)(2,1)S(1)} collective-permute-done((bf16[128,640]{1,0:T(8,128)(2,1)S(1)}, bf16[128,640]{1,0:T(8,128)(2,1)S(1)}, u32[]{:S(2)}, u32[]{:S(2)}) %collective-permute-start.8) | collective-permute-done | bytes 163872 | tf_op jit(solution)/shard_map/ppermute | solution.py:403
  41.9 1.7 %collective-permute-done.9.refs_3_ = bf16[128,640]{1,0:T(8,128)(2,1)S(1)} collective-permute-done((bf16[128,640]{1,0:T(8,128)(2,1)S(1)}, bf16[128,640]{1,0:T(8,128)(2,1)S(1)}, u32[]{:S(2)}, u32[]{:S(2)}) %collective-permute-start.9) | collective-permute-done | bytes 163872 | tf_op jit(solution)/shard_map/ppermute | solution.py:403
  43.6 1.1 %combine.1 = (bf16[32,512]{1,0:T(8,128)(2,1)S(1)}, bf16[32,512]{1,0:T(8,128)(2,1)S(1)}, bf16[32,512]{1,0:T(8,128)(2,1)S(1)}, bf16[32,512]{1,0:T(8,128)(2,1)S(1)}) custom-call(s32[5]{0:T(128)S(1)} %stack.23.ids, bf16[128,640]{1,0:T(8,128)(2,1)S(1)} %attend.2.refs_0_, bf16[128,640]{1,0:T(8,128)(2,1)S(1)} %collective-permute-done.7.refs_1_, ...), custom_call_target="tpu_custom_call" | custom-call | tf_op jit(solution)/shard_map/combine/pallas_call | solution.py:334
  44.7 0.7 collective-permute-start.10
  45.4 1.8 %collective-permute-start.11 = (bf16[32,512]{1,0:T(8,128)(2,1)S(1)}, bf16[32,512]{1,0:T(8,128)(2,1)S(1)}, u32[]{:S(2)}, u32[]{:S(2)}) collective-permute-start(bf16[32,512]{1,0:T(8,128)(2,1)S(1)} %get-tuple-element.50), channel_id=1, source_target_pairs={{0,2},{1,3},{2,0},{3,1},{4,6},{5,7},{6,4},{7,5},{8,10},{9,11},{10,... | collective-permute-start | bytes 98312 | tf_op jit(solution)/shard_map/ppermute | solution.py:350
  47.2 2.6 %collective-permute-start.12 = (bf16[32,512]{1,0:T(8,128)(2,1)S(1)}, bf16[32,512]{1,0:T(8,128)(2,1)S(1)}, u32[]{:S(2)}, u32[]{:S(2)}) collective-permute-start(bf16[32,512]{1,0:T(8,128)(2,1)S(1)} %get-tuple-element.51), channel_id=1, source_target_pairs={{0,3},{1,2},{2,1},{3,0},{4,7},{5,6},{6,5},{7,4},{8,11},{9,10},{10,... | collective-permute-start | bytes 98312 | tf_op jit(solution)/shard_map/ppermute | solution.py:350
  49.7 0.4 collective-permute-done.10.refs_1_
  50.2 0.0 collective-permute-done.11.refs_2_
  50.2 3.3 %collective-permute-done.12.refs_3_ = bf16[32,512]{1,0:T(8,128)(2,1)S(1)} collective-permute-done((bf16[32,512]{1,0:T(8,128)(2,1)S(1)}, bf16[32,512]{1,0:T(8,128)(2,1)S(1)}, u32[]{:S(2)}, u32[]{:S(2)}) %collective-permute-start.12) | collective-permute-done | bytes 32800 | tf_op jit(solution)/shard_map/ppermute | solution.py:350
  53.6 3.4 %collective-permute-start.16 = (bf16[448,512]{1,0:T(8,128)(2,1)S(1)}, bf16[448,512]{1,0:T(8,128)(2,1)S(1)}, u32[]{:S(2)}, u32[]{:S(2)}) collective-permute-start(bf16[448,512]{1,0:T(8,128)(2,1)S(1)} %slice_bitcast_fusion.1), channel_id=1, source_target_pairs={{0,128},{1,129},{128,0},{129,1},{2,130},{3,131},{130,2},{131,3},{4... | collective-permute-start | bytes 1376264 | tf_op jit(solution)/shard_map/ppermute | solution.py:350
  57.0 1.8 %collective-permute-start.17 = (bf16[448,512]{1,0:T(8,128)(2,1)S(1)}, bf16[448,512]{1,0:T(8,128)(2,1)S(1)}, u32[]{:S(2)}, u32[]{:S(2)}) collective-permute-start(bf16[448,512]{1,0:T(8,128)(2,1)S(1)} %slice_bitcast_fusion), channel_id=1, source_target_pairs={{0,129},{1,128},{128,1},{129,0},{2,131},{3,130},{130,3},{131,2},{4... | collective-permute-start | bytes 1376264 | tf_op jit(solution)/shard_map/ppermute | solution.py:350
  58.8 0.7 collective-permute-start.15
  59.5 1.4 %collective-permute-start.18 = (bf16[32,2048]{1,0:T(8,128)(2,1)S(1)}, bf16[32,2048]{1,0:T(8,128)(2,1)S(1)}, u32[]{:S(2)}, u32[]{:S(2)}) collective-permute-start(bf16[32,2048]{1,0:T(8,128)(2,1)S(1)} %get-tuple-element.53.refs_0_), channel_id=1, source_target_pairs={{64,0},{96,32},{0,64},{32,96},{65,1},{97,33},{1,65},{33,97},{66,2}... | collective-permute-start | bytes 393224 | tf_op jit(solution)/shard_map/ppermute | solution.py:346
  60.9 2.3 %collective-permute-start.19 = (bf16[32,2048]{1,0:T(8,128)(2,1)S(1)}, bf16[32,2048]{1,0:T(8,128)(2,1)S(1)}, u32[]{:S(2)}, u32[]{:S(2)}) collective-permute-start(bf16[32,2048]{1,0:T(8,128)(2,1)S(1)} %get-tuple-element.53.refs_0_), channel_id=1, source_target_pairs={{96,0},{0,32},{32,64},{64,96},{97,1},{1,33},{33,65},{65,97},{98,2}... | collective-permute-start | bytes 393224 | tf_op jit(solution)/shard_map/ppermute | solution.py:346
  63.2 3.2 %collective-permute-done.15.refs_0_ = bf16[32,2048]{1,0:T(8,128)(2,1)S(1)} collective-permute-done((bf16[32,2048]{1,0:T(8,128)(2,1)S(1)}, bf16[32,2048]{1,0:T(8,128)(2,1)S(1)}, u32[]{:S(2)}, u32[]{:S(2)}) %collective-permute-start.15) | collective-permute-done | bytes 131104 | tf_op jit(solution)/shard_map/ppermute | solution.py:346
  66.4 0.5 collective-permute-start.22
  66.9 0.3 collective-permute-done.19.refs_3_
  67.2 0.0 collective-permute-start.23
  67.2 1.6 %collective-permute-done.17.refs_2_ = bf16[448,512]{1,0:T(8,128)(2,1)S(1)} collective-permute-done((bf16[448,512]{1,0:T(8,128)(2,1)S(1)}, bf16[448,512]{1,0:T(8,128)(2,1)S(1)}, u32[]{:S(2)}, u32[]{:S(2)}) %collective-permute-start.17) | collective-permute-done | bytes 458784 | tf_op jit(solution)/shard_map/ppermute | solution.py:350
  68.8 1.3 %collective-permute-done.21.refs_5_ = bf16[32,2048]{1,0:T(8,128)(2,1)S(1)} collective-permute-done((bf16[32,2048]{1,0:T(8,128)(2,1)S(1)}, bf16[32,2048]{1,0:T(8,128)(2,1)S(1)}, u32[]{:S(2)}, u32[]{:S(2)}) %collective-permute-start.21) | collective-permute-done | bytes 131104 | tf_op jit(solution)/shard_map/ppermute | solution.py:350
  70.2 1.9 %project.1 = (bf16[64,896]{1,0:T(8,128)(2,1)S(1)}, bf16[64,896]{1,0:T(8,128)(2,1)S(1)}, bf16[64,896]{1,0:T(8,128)(2,1)S(1)}, bf16[64,896]{1,0:T(8,128)(2,1)S(1)}) custom-call(s32[5]{0:T(128)S(1)} %stack.23.ids, bf16[32,2048]{1,0:T(8,128)(2,1)S(1)} %get-tuple-element.53.refs_0_, bf16[32,2048]{1,0:T(8,128)(2,1)S(1)} %get-tuple-element.56.refs_1_, ...), custom_call_target="tpu_custom_call" | custom-call | tf_op jit(solution)/shard_map/project/pallas_call | solution.py:334
  72.1 3.3 %collective-permute-start.24 = (bf16[64,896]{1,0:T(8,128)(2,1)S(1)}, bf16[64,896]{1,0:T(8,128)(2,1)S(1)}, u32[]{:S(2)}, u32[]{:S(2)}) collective-permute-start(bf16[64,896]{1,0:T(8,128)(2,1)S(1)} %get-tuple-element.60), channel_id=1, source_target_pairs={{0,4},{4,8},{8,12},{12,0},{1,5},{5,9},{9,13},{13,1},{2,6},{6,10},{... | collective-permute-start | bytes 344072 | tf_op jit(solution)/shard_map/ppermute | solution.py:427
  75.4 5.4 %collective-permute-start.25 = (bf16[64,896]{1,0:T(8,128)(2,1)S(1)}, bf16[64,896]{1,0:T(8,128)(2,1)S(1)}, u32[]{:S(2)}, u32[]{:S(2)}) collective-permute-start(bf16[64,896]{1,0:T(8,128)(2,1)S(1)} %get-tuple-element.61), channel_id=1, source_target_pairs={{0,8},{4,12},{8,0},{12,4},{1,9},{5,13},{9,1},{13,5},{2,10},{6,14},... | collective-permute-start | bytes 344072 | tf_op jit(solution)/shard_map/ppermute | solution.py:427
  80.9 2.7 %collective-permute-start.26 = (bf16[64,896]{1,0:T(8,128)(2,1)S(1)}, bf16[64,896]{1,0:T(8,128)(2,1)S(1)}, u32[]{:S(2)}, u32[]{:S(2)}) collective-permute-start(bf16[64,896]{1,0:T(8,128)(2,1)S(1)} %get-tuple-element.62), channel_id=1, source_target_pairs={{0,12},{4,0},{8,4},{12,8},{1,13},{5,1},{9,5},{13,9},{2,14},{6,2},{... | collective-permute-start | bytes 344072 | tf_op jit(solution)/shard_map/ppermute | solution.py:427
  83.6 5.5 %collective-permute-done.25.refs_2_ = bf16[64,896]{1,0:T(8,128)(2,1)S(1)} collective-permute-done((bf16[64,896]{1,0:T(8,128)(2,1)S(1)}, bf16[64,896]{1,0:T(8,128)(2,1)S(1)}, u32[]{:S(2)}, u32[]{:S(2)}) %collective-permute-start.25) | collective-permute-done | bytes 114720 | tf_op jit(solution)/shard_map/ppermute | solution.py:427
  89.1 3.0 %collective-permute-done.26.refs_3_ = bf16[64,896]{1,0:T(8,128)(2,1)S(1)} collective-permute-done((bf16[64,896]{1,0:T(8,128)(2,1)S(1)}, bf16[64,896]{1,0:T(8,128)(2,1)S(1)}, u32[]{:S(2)}, u32[]{:S(2)}) %collective-permute-start.26) | collective-permute-done | bytes 114720 | tf_op jit(solution)/shard_map/ppermute | solution.py:427
  92.1 0.1 share.1
  92.2 0.1 collective-permute-start.27
  92.3 1.3 %collective-permute-done.27.got = f32[32,896]{1,0:T(8,128)S(1)} collective-permute-done((f32[32,896]{1,0:T(8,128)S(1)}, f32[32,896]{1,0:T(8,128)S(1)}, u32[]{:S(2)}, u32[]{:S(2)}) %collective-permute-start.27) | collective-permute-done | bytes 114720 | tf_op jit(solution)/shard_map/ppermute | solution.py:350
  93.6 1.3 %collective-permute-start.28 = (f32[8,1792]{1,0:T(8,128)S(1)}, f32[8,1792]{1,0:T(8,128)S(1)}, u32[]{:S(2)}, u32[]{:S(2)}) collective-permute-start(f32[8,1792]{1,0:T(8,128)S(1)} %get-tuple-element.66), channel_id=1, source_target_pairs={{0,32},{32,64},{64,96},{96,0},{1,33},{33,65},{65,97},{97,1},{2,34}... | collective-permute-start | bytes 172040 | tf_op jit(solution)/shard_map/ppermute | solution.py:437
  94.8 0.9 collective-permute-start.29
  95.7 0.8 collective-permute-start.30
  96.6 1.7 %collective-permute-done.28.refs_1_ = f32[8,1792]{1,0:T(8,128)S(1)} collective-permute-done((f32[8,1792]{1,0:T(8,128)S(1)}, f32[8,1792]{1,0:T(8,128)S(1)}, u32[]{:S(2)}, u32[]{:S(2)}) %collective-permute-start.28) | collective-permute-done | bytes 57376 | tf_op jit(solution)/shard_map/ppermute | solution.py:437
  98.3 2.8 %collective-permute-done.29.refs_2_ = f32[8,1792]{1,0:T(8,128)S(1)} collective-permute-done((f32[8,1792]{1,0:T(8,128)S(1)}, f32[8,1792]{1,0:T(8,128)S(1)}, u32[]{:S(2)}, u32[]{:S(2)}) %collective-permute-start.29) | collective-permute-done | bytes 57376 | tf_op jit(solution)/shard_map/ppermute | solution.py:437
  101.1 0.3 collective-permute-done.30.refs_3_
  101.4 1.3 %place.1 = bf16[8,7168]{1,0:T(8,128)(2,1)} custom-call(s32[5]{0:T(128)S(1)} %stack.23.ids, f32[8,1792]{1,0:T(8,128)S(1)} %get-tuple-element.65.refs_0_, f32[8,1792]{1,0:T(8,128)S(1)} %collective-permute-done.28.refs_1_, f32[8,1792]{1,0:T(8,128)S(1)} %collective-permute-done.29.refs_2_, f32[8,1792]{1,0:T(8,128)S(1)} %collective-permute-done.30.refs_3_), custom_call_target="tpu_custom_call" | custom-call | tf_op jit(solution)/shard_map/place/pallas_call | solution.py:334
  (34 shorter events, 0.2 us)
Async XLA Ops:
  0.0 18.3 %copy-start.3 = (bf16[512,448]{0,1:T(8,128)(2,1)S(1)}, bf16[512,448]{0,1:T(8,128)(2,1)}, u32[]{:S(2)}) copy-start(bf16[512,448]{0,1:T(8,128)(2,1)} %param.21) | copy-start | bytes 1376260
  0.0 22.4 %copy-start.2 = (bf16[4,128,512]{2,1,0:T(8,128)(2,1)S(1)}, bf16[4,128,512]{2,1,0:T(8,128)(2,1)}, u32[]{:S(2)}) copy-start(bf16[4,128,512]{2,1,0:T(8,128)(2,1)} %refs_4_.3) | copy-start | bytes 1572868
  2.3 19.6 %copy-start = (bf16[576,512]{1,0:T(8,128)(2,1)S(1)}, bf16[576,512]{1,0:T(8,128)(2,1)}, u32[]{:S(2)}) copy-start(bf16[576,512]{1,0:T(8,128)(2,1)} %get-tuple-element.38.refs_0_) | copy-start | bytes 1769476
  2.3 20.1 %copy-start.4 = (bf16[128,768]{1,0:T(8,128)(2,1)S(1)}, bf16[128,768]{1,0:T(8,128)(2,1)}, u32[]{:S(2)}) copy-start(bf16[128,768]{1,0:T(8,128)(2,1)} %get-tuple-element.40.refs_0_) | copy-start | bytes 589828
  2.3 15.9 %collective-permute-start = (bf16[576,512]{1,0:T(8,128)(2,1)}, bf16[576,512]{1,0:T(8,128)(2,1)S(1)}, u32[]{:S(2)}, u32[]{:S(2)}) collective-permute-start(bf16[576,512]{1,0:T(8,128)(2,1)} %get-tuple-element.38.refs_0_), channel_id=1, source_target_pairs={{0,128},{128,0},{1,129},{129,1},{2,130},{130,2},{3,131},{131,3},{4... | collective-permute-start | bytes 1769480 | tf_op jit(solution)/shard_map/ppermute | solution.py:350
  4.0 14.3 %collective-permute-start.1 = (bf16[448,512]{1,0:T(8,128)(2,1)}, bf16[448,512]{1,0:T(8,128)(2,1)S(1)}, u32[]{:S(2)}, u32[]{:S(2)}) collective-permute-start(bf16[448,512]{1,0:T(8,128)(2,1)} %bitcast.11), channel_id=1, source_target_pairs={{0,2},{2,0},{1,3},{3,1},{4,6},{6,4},{5,7},{7,5},{8,10},{10,8},{9,1... | collective-permute-start | bytes 1376264 | tf_op jit(solution)/shard_map/ppermute | solution.py:350
  5.9 11.7 %collective-permute-start.2 = (bf16[128,768]{1,0:T(8,128)(2,1)}, bf16[128,768]{1,0:T(8,128)(2,1)S(1)}, u32[]{:S(2)}, u32[]{:S(2)}) collective-permute-start(bf16[128,768]{1,0:T(8,128)(2,1)} %get-tuple-element.40.refs_0_), channel_id=1, source_target_pairs={{32,0},{64,32},{96,64},{0,96},{33,1},{65,33},{97,65},{1,97},{34,2}... | collective-permute-start | bytes 589832 | tf_op jit(solution)/shard_map/ppermute | solution.py:346
  6.7 10.9 %collective-permute-start.3 = (bf16[128,768]{1,0:T(8,128)(2,1)}, bf16[128,768]{1,0:T(8,128)(2,1)S(1)}, u32[]{:S(2)}, u32[]{:S(2)}) collective-permute-start(bf16[128,768]{1,0:T(8,128)(2,1)} %get-tuple-element.40.refs_0_), channel_id=1, source_target_pairs={{64,0},{96,32},{0,64},{32,96},{65,1},{97,33},{1,65},{33,97},{66,2}... | collective-permute-start | bytes 589832 | tf_op jit(solution)/shard_map/ppermute | solution.py:346
  7.9 10.4 %collective-permute-start.4 = (bf16[128,768]{1,0:T(8,128)(2,1)}, bf16[128,768]{1,0:T(8,128)(2,1)S(1)}, u32[]{:S(2)}, u32[]{:S(2)}) collective-permute-start(bf16[128,768]{1,0:T(8,128)(2,1)} %get-tuple-element.40.refs_0_), channel_id=1, source_target_pairs={{96,0},{0,32},{32,64},{64,96},{97,1},{1,33},{33,65},{65,97},{98,2}... | collective-permute-start | bytes 589832 | tf_op jit(solution)/shard_map/ppermute | solution.py:346
  10.0 0.7 copy-start.7
  10.7 0.7 copy-start.8
  18.3 6.5 %copy-start.1 = (bf16[4,512,128]{2,1,0:T(8,128)(2,1)S(1)}, bf16[4,512,128]{2,1,0:T(8,128)(2,1)}, u32[]{:S(2)}) copy-start(bf16[4,512,128]{2,1,0:T(8,128)(2,1)} %refs_4_.5) | copy-start | bytes 1572868
  18.4 35.1 %collective-permute-start.13 = (bf16[2,448,512]{2,1,0:T(8,128)(2,1)S(1)}, bf16[2,448,512]{2,1,0:T(8,128)(2,1)S(1)}, u32[]{:S(2)}, u32[]{:S(2)}) collective-permute-start(bf16[2,448,512]{2,1,0:T(8,128)(2,1)S(1)} %pair.1.refs_8_), channel_id=1, source_target_pairs={{0,128},{1,129},{128,0},{129,1},{2,130},{3,131},{130,2},{131,3},{4... | collective-permute-start | bytes 2752520 | tf_op jit(solution)/shard_map/ppermute | solution.py:350
  19.4 34.1 %collective-permute-start.14 = (bf16[2,448,512]{2,1,0:T(8,128)(2,1)S(1)}, bf16[2,448,512]{2,1,0:T(8,128)(2,1)S(1)}, u32[]{:S(2)}, u32[]{:S(2)}) collective-permute-start(bf16[2,448,512]{2,1,0:T(8,128)(2,1)S(1)} %pair.1.refs_8_), channel_id=1, source_target_pairs={{0,129},{1,128},{128,1},{129,0},{2,131},{3,130},{130,3},{131,2},{4... | collective-permute-start | bytes 2752520 | tf_op jit(solution)/shard_map/ppermute | solution.py:350
  21.9 2.0 %collective-permute-start.5 = (bf16[576,512]{1,0:T(8,128)(2,1)S(1)}, bf16[576,512]{1,0:T(8,128)(2,1)S(1)}, u32[]{:S(2)}, u32[]{:S(2)}) collective-permute-start(bf16[576,512]{1,0:T(8,128)(2,1)S(1)} %copy-done), channel_id=1, source_target_pairs={{0,16},{16,0},{1,17},{17,1},{2,18},{18,2},{3,19},{19,3},{4,20},{20... | collective-permute-start | bytes 1769480 | tf_op jit(solution)/shard_map/ppermute | solution.py:350
  21.9 2.8 %collective-permute-start.6 = (bf16[576,512]{1,0:T(8,128)(2,1)S(1)}, bf16[576,512]{1,0:T(8,128)(2,1)S(1)}, u32[]{:S(2)}, u32[]{:S(2)}) collective-permute-start(bf16[576,512]{1,0:T(8,128)(2,1)S(1)} %get-tuple-element.44.refs_1_), channel_id=1, source_target_pairs={{0,16},{16,0},{1,17},{17,1},{2,18},{18,2},{3,19},{19,3},{4,20},{20... | collective-permute-start | bytes 1769480 | tf_op jit(solution)/shard_map/ppermute | solution.py:350
  24.8 11.2 %copy-start.5 = (bf16[128,512]{1,0:T(8,128)(2,1)S(1)}, bf16[128,512]{1,0:T(8,128)(2,1)}, u32[]{:S(2)}) copy-start(bf16[128,512]{1,0:T(8,128)(2,1)} %refs_5_.1) | copy-start | bytes 393220
  24.8 11.2 %copy-start.6 = (bf16[1,64,128]{2,1,0:T(8,128)(2,1)S(1)}, bf16[1,64,128]{2,1,0:T(8,128)(2,1)}, u32[]{:S(2)}) copy-start(bf16[1,64,128]{2,1,0:T(8,128)(2,1)} %param.14) | copy-start | bytes 49156
  33.1 6.7 %collective-permute-start.7 = (bf16[128,640]{1,0:T(8,128)(2,1)S(1)}, bf16[128,640]{1,0:T(8,128)(2,1)S(1)}, u32[]{:S(2)}, u32[]{:S(2)}) collective-permute-start(bf16[128,640]{1,0:T(8,128)(2,1)S(1)} %get-tuple-element.45), channel_id=1, source_target_pairs={{0,32},{32,64},{64,96},{96,0},{1,33},{33,65},{65,97},{97,1},{2,34}... | collective-permute-start | bytes 491528 | tf_op jit(solution)/shard_map/ppermute | solution.py:403
  34.8 7.1 %collective-permute-start.8 = (bf16[128,640]{1,0:T(8,128)(2,1)S(1)}, bf16[128,640]{1,0:T(8,128)(2,1)S(1)}, u32[]{:S(2)}, u32[]{:S(2)}) collective-permute-start(bf16[128,640]{1,0:T(8,128)(2,1)S(1)} %get-tuple-element.46), channel_id=1, source_target_pairs={{0,64},{32,96},{64,0},{96,32},{1,65},{33,97},{65,1},{97,33},{2,66}... | collective-permute-start | bytes 491528 | tf_op jit(solution)/shard_map/ppermute | solution.py:403
  36.0 7.6 %collective-permute-start.9 = (bf16[128,640]{1,0:T(8,128)(2,1)S(1)}, bf16[128,640]{1,0:T(8,128)(2,1)S(1)}, u32[]{:S(2)}, u32[]{:S(2)}) collective-permute-start(bf16[128,640]{1,0:T(8,128)(2,1)S(1)} %get-tuple-element.47), channel_id=1, source_target_pairs={{0,96},{32,0},{64,32},{96,64},{1,97},{33,1},{65,33},{97,65},{2,98}... | collective-permute-start | bytes 491528 | tf_op jit(solution)/shard_map/ppermute | solution.py:403
  44.7 5.5 %collective-permute-start.10 = (bf16[32,512]{1,0:T(8,128)(2,1)S(1)}, bf16[32,512]{1,0:T(8,128)(2,1)S(1)}, u32[]{:S(2)}, u32[]{:S(2)}) collective-permute-start(bf16[32,512]{1,0:T(8,128)(2,1)S(1)} %get-tuple-element.49), channel_id=1, source_target_pairs={{0,1},{1,0},{2,3},{3,2},{4,5},{5,4},{6,7},{7,6},{8,9},{9,8},{10,11... | collective-permute-start | bytes 98312 | tf_op jit(solution)/shard_map/ppermute | solution.py:350
  45.4 4.8 %collective-permute-start.11 = (bf16[32,512]{1,0:T(8,128)(2,1)S(1)}, bf16[32,512]{1,0:T(8,128)(2,1)S(1)}, u32[]{:S(2)}, u32[]{:S(2)}) collective-permute-start(bf16[32,512]{1,0:T(8,128)(2,1)S(1)} %get-tuple-element.50), channel_id=1, source_target_pairs={{0,2},{1,3},{2,0},{3,1},{4,6},{5,7},{6,4},{7,5},{8,10},{9,11},{10,... | collective-permute-start | bytes 98312 | tf_op jit(solution)/shard_map/ppermute | solution.py:350
  47.2 6.3 %collective-permute-start.12 = (bf16[32,512]{1,0:T(8,128)(2,1)S(1)}, bf16[32,512]{1,0:T(8,128)(2,1)S(1)}, u32[]{:S(2)}, u32[]{:S(2)}) collective-permute-start(bf16[32,512]{1,0:T(8,128)(2,1)S(1)} %get-tuple-element.51), channel_id=1, source_target_pairs={{0,3},{1,2},{2,1},{3,0},{4,7},{5,6},{6,5},{7,4},{8,11},{9,10},{10,... | collective-permute-start | bytes 98312 | tf_op jit(solution)/shard_map/ppermute | solution.py:350
  53.6 13.7 %collective-permute-start.16 = (bf16[448,512]{1,0:T(8,128)(2,1)S(1)}, bf16[448,512]{1,0:T(8,128)(2,1)S(1)}, u32[]{:S(2)}, u32[]{:S(2)}) collective-permute-start(bf16[448,512]{1,0:T(8,128)(2,1)S(1)} %slice_bitcast_fusion.1), channel_id=1, source_target_pairs={{0,128},{1,129},{128,0},{129,1},{2,130},{3,131},{130,2},{131,3},{4... | collective-permute-start | bytes 1376264 | tf_op jit(solution)/shard_map/ppermute | solution.py:350
  57.0 11.8 %collective-permute-start.17 = (bf16[448,512]{1,0:T(8,128)(2,1)S(1)}, bf16[448,512]{1,0:T(8,128)(2,1)S(1)}, u32[]{:S(2)}, u32[]{:S(2)}) collective-permute-start(bf16[448,512]{1,0:T(8,128)(2,1)S(1)} %slice_bitcast_fusion), channel_id=1, source_target_pairs={{0,129},{1,128},{128,1},{129,0},{2,131},{3,130},{130,3},{131,2},{4... | collective-permute-start | bytes 1376264 | tf_op jit(solution)/shard_map/ppermute | solution.py:350
  58.8 7.6 %collective-permute-start.15 = (bf16[32,2048]{1,0:T(8,128)(2,1)S(1)}, bf16[32,2048]{1,0:T(8,128)(2,1)S(1)}, u32[]{:S(2)}, u32[]{:S(2)}) collective-permute-start(bf16[32,2048]{1,0:T(8,128)(2,1)S(1)} %get-tuple-element.53.refs_0_), channel_id=1, source_target_pairs={{32,0},{64,32},{96,64},{0,96},{33,1},{65,33},{97,65},{1,97},{34,2}... | collective-permute-start | bytes 393224 | tf_op jit(solution)/shard_map/ppermute | solution.py:346
  59.5 6.9 %collective-permute-start.18 = (bf16[32,2048]{1,0:T(8,128)(2,1)S(1)}, bf16[32,2048]{1,0:T(8,128)(2,1)S(1)}, u32[]{:S(2)}, u32[]{:S(2)}) collective-permute-start(bf16[32,2048]{1,0:T(8,128)(2,1)S(1)} %get-tuple-element.53.refs_0_), channel_id=1, source_target_pairs={{64,0},{96,32},{0,64},{32,96},{65,1},{97,33},{1,65},{33,97},{66,2}... | collective-permute-start | bytes 393224 | tf_op jit(solution)/shard_map/ppermute | solution.py:346
  60.9 6.4 %collective-permute-start.19 = (bf16[32,2048]{1,0:T(8,128)(2,1)S(1)}, bf16[32,2048]{1,0:T(8,128)(2,1)S(1)}, u32[]{:S(2)}, u32[]{:S(2)}) collective-permute-start(bf16[32,2048]{1,0:T(8,128)(2,1)S(1)} %get-tuple-element.53.refs_0_), channel_id=1, source_target_pairs={{96,0},{0,32},{32,64},{64,96},{97,1},{1,33},{33,65},{65,97},{98,2}... | collective-permute-start | bytes 393224 | tf_op jit(solution)/shard_map/ppermute | solution.py:346
  66.4 2.4 %collective-permute-start.20 = (bf16[32,2048]{1,0:T(8,128)(2,1)S(1)}, bf16[32,2048]{1,0:T(8,128)(2,1)S(1)}, u32[]{:S(2)}, u32[]{:S(2)}) collective-permute-start(bf16[32,2048]{1,0:T(8,128)(2,1)S(1)} %get-tuple-element.53.refs_0_), channel_id=1, source_target_pairs={{0,16},{16,0},{1,17},{17,1},{2,18},{18,2},{3,19},{19,3},{4,20},{20... | collective-permute-start | bytes 393224 | tf_op jit(solution)/shard_map/ppermute | solution.py:350
  66.4 2.4 %collective-permute-start.22 = (bf16[32,2048]{1,0:T(8,128)(2,1)S(1)}, bf16[32,2048]{1,0:T(8,128)(2,1)S(1)}, u32[]{:S(2)}, u32[]{:S(2)}) collective-permute-start(bf16[32,2048]{1,0:T(8,128)(2,1)S(1)} %collective-permute-done.18.refs_2_), channel_id=1, source_target_pairs={{0,16},{16,0},{1,17},{17,1},{2,18},{18,2},{3,19},{19,3},{4,20},{20... | collective-permute-start | bytes 393224 | tf_op jit(solution)/shard_map/ppermute | solution.py:350
  67.2 1.6 %collective-permute-start.23 = (bf16[32,2048]{1,0:T(8,128)(2,1)S(1)}, bf16[32,2048]{1,0:T(8,128)(2,1)S(1)}, u32[]{:S(2)}, u32[]{:S(2)}) collective-permute-start(bf16[32,2048]{1,0:T(8,128)(2,1)S(1)} %collective-permute-done.19.refs_3_), channel_id=1, source_target_pairs={{0,16},{16,0},{1,17},{17,1},{2,18},{18,2},{3,19},{19,3},{4,20},{20... | collective-permute-start | bytes 393224 | tf_op jit(solution)/shard_map/ppermute | solution.py:350
  68.8 1.3 %collective-permute-start.21 = (bf16[32,2048]{1,0:T(8,128)(2,1)S(1)}, bf16[32,2048]{1,0:T(8,128)(2,1)S(1)}, u32[]{:S(2)}, u32[]{:S(2)}) collective-permute-start(bf16[32,2048]{1,0:T(8,128)(2,1)S(1)} %get-tuple-element.56.refs_1_), channel_id=1, source_target_pairs={{0,16},{16,0},{1,17},{17,1},{2,18},{18,2},{3,19},{19,3},{4,20},{20... | collective-permute-start | bytes 393224 | tf_op jit(solution)/shard_map/ppermute | solution.py:350
  72.1 11.5 %collective-permute-start.24 = (bf16[64,896]{1,0:T(8,128)(2,1)S(1)}, bf16[64,896]{1,0:T(8,128)(2,1)S(1)}, u32[]{:S(2)}, u32[]{:S(2)}) collective-permute-start(bf16[64,896]{1,0:T(8,128)(2,1)S(1)} %get-tuple-element.60), channel_id=1, source_target_pairs={{0,4},{4,8},{8,12},{12,0},{1,5},{5,9},{9,13},{13,1},{2,6},{6,10},{... | collective-permute-start | bytes 344072 | tf_op jit(solution)/shard_map/ppermute | solution.py:427
  75.4 13.6 %collective-permute-start.25 = (bf16[64,896]{1,0:T(8,128)(2,1)S(1)}, bf16[64,896]{1,0:T(8,128)(2,1)S(1)}, u32[]{:S(2)}, u32[]{:S(2)}) collective-permute-start(bf16[64,896]{1,0:T(8,128)(2,1)S(1)} %get-tuple-element.61), channel_id=1, source_target_pairs={{0,8},{4,12},{8,0},{12,4},{1,9},{5,13},{9,1},{13,5},{2,10},{6,14},... | collective-permute-start | bytes 344072 | tf_op jit(solution)/shard_map/ppermute | solution.py:427
  80.9 11.2 %collective-permute-start.26 = (bf16[64,896]{1,0:T(8,128)(2,1)S(1)}, bf16[64,896]{1,0:T(8,128)(2,1)S(1)}, u32[]{:S(2)}, u32[]{:S(2)}) collective-permute-start(bf16[64,896]{1,0:T(8,128)(2,1)S(1)} %get-tuple-element.62), channel_id=1, source_target_pairs={{0,12},{4,0},{8,4},{12,8},{1,13},{5,1},{9,5},{13,9},{2,14},{6,2},{... | collective-permute-start | bytes 344072 | tf_op jit(solution)/shard_map/ppermute | solution.py:427
  92.2 1.4 %collective-permute-start.27 = (f32[32,896]{1,0:T(8,128)S(1)}, f32[32,896]{1,0:T(8,128)S(1)}, u32[]{:S(2)}, u32[]{:S(2)}) collective-permute-start(f32[32,896]{1,0:T(8,128)S(1)} %get-tuple-element.64), channel_id=1, source_target_pairs={{0,16},{16,0},{1,17},{17,1},{2,18},{18,2},{3,19},{19,3},{4,20},{20... | collective-permute-start | bytes 344072 | tf_op jit(solution)/shard_map/ppermute | solution.py:350
  93.6 4.7 %collective-permute-start.28 = (f32[8,1792]{1,0:T(8,128)S(1)}, f32[8,1792]{1,0:T(8,128)S(1)}, u32[]{:S(2)}, u32[]{:S(2)}) collective-permute-start(f32[8,1792]{1,0:T(8,128)S(1)} %get-tuple-element.66), channel_id=1, source_target_pairs={{0,32},{32,64},{64,96},{96,0},{1,33},{33,65},{65,97},{97,1},{2,34}... | collective-permute-start | bytes 172040 | tf_op jit(solution)/shard_map/ppermute | solution.py:437
  94.8 6.2 %collective-permute-start.29 = (f32[8,1792]{1,0:T(8,128)S(1)}, f32[8,1792]{1,0:T(8,128)S(1)}, u32[]{:S(2)}, u32[]{:S(2)}) collective-permute-start(f32[8,1792]{1,0:T(8,128)S(1)} %get-tuple-element.67), channel_id=1, source_target_pairs={{0,64},{32,96},{64,0},{96,32},{1,65},{33,97},{65,1},{97,33},{2,66}... | collective-permute-start | bytes 172040 | tf_op jit(solution)/shard_map/ppermute | solution.py:437
  95.7 5.7 %collective-permute-start.30 = (f32[8,1792]{1,0:T(8,128)S(1)}, f32[8,1792]{1,0:T(8,128)S(1)}, u32[]{:S(2)}, u32[]{:S(2)}) collective-permute-start(f32[8,1792]{1,0:T(8,128)S(1)} %get-tuple-element.68), channel_id=1, source_target_pairs={{0,96},{32,0},{64,32},{96,64},{1,97},{33,1},{65,33},{97,65},{2,98}... | collective-permute-start | bytes 172040 | tf_op jit(solution)/shard_map/ppermute | solution.py:437

commit v13 on v10

--- a/solution.py
+++ b/solution.py
@@ -290,29 +290,32 @@
 
 def share_kernel(*refs):
     total = sum(p[...].astype(jnp.float32) for p in refs[:4])
-    refs[4][...] = total[:32]
-    refs[5][...] = total[32:]
+    refs[4][...] = total[:32].astype(jnp.bfloat16)
+    refs[5][...] = total[32:].astype(jnp.bfloat16)
 
 
 def merge_kernel(keep, got, *outs):
+    own, other = keep[...].astype(jnp.float32), got[...].astype(jnp.float32)
     for s in range(4):
-        outs[s][:, :896] = keep[s * 8 : (s + 1) * 8, :]
-        outs[s][:, 896:] = got[s * 8 : (s + 1) * 8, :]
+        rows = slice(s * 8, (s + 1) * 8)
+        outs[s][...] = jnp.concatenate([own[rows], other[rows]], axis=0).astype(jnp.bfloat16)
 
 
 def place_kernel(ids, *refs):
     parts, out = refs[:4], refs[4]
     yl, x, k = ids[0], ids[1], ids[2]
-    for s in range(4):
-        for side_y in range(2):
-            first = ((yl ^ side_y) * 4 + (x - s + 4) % 4) * 896
-            columns = pl.ds(pl.multiple_of(first, 128), 896)
-            mine = parts[s][:, side_y * 448 : (side_y + 1) * 448]
-            other = parts[s][:, 896 + side_y * 448 : 896 + (side_y + 1) * 448]
-            value = jnp.where(
-                k == 0, jnp.concatenate([mine, other], axis=1), jnp.concatenate([other, mine], axis=1)
-            )
-            out[:, columns] = value.astype(jnp.bfloat16)
+    for core in range(2):
+
+        @pl.when(k == core)
+        def _():
+            for s in range(4):
+                value = parts[s][...].astype(jnp.float32)
+                pair = (value[:8], value[8:]) if core == 0 else (value[8:], value[:8])
+                for side_y in range(2):
+                    first = ((yl ^ side_y) * 4 + (x - s + 4) % 4) * 896
+                    cut = slice(side_y * 448, (side_y + 1) * 448)
+                    joined = jnp.concatenate([pair[0][:, cut], pair[1][:, cut]], axis=1)
+                    out[:, pl.ds(pl.multiple_of(first, 128), 896)] = joined.astype(jnp.bfloat16)
 
 
 def tie_kernel(*refs):
@@ -430,11 +433,11 @@
     sums = [partial[0]] + [
         lax.ppermute(partial[d], "zb", [(i, (i + d) % 4) for i in range(4)]) for d in (1, 2, 3)
     ]
-    keep, give = simple(share_kernel, "share", [jax.ShapeDtypeStruct((32, 896), jnp.float32)] * 2, sums)
+    keep, give = simple(share_kernel, "share", [jax.ShapeDtypeStruct((32, 896), jnp.bfloat16)] * 2, sums)
     pieces = simple(
         merge_kernel,
         "merge",
-        [jax.ShapeDtypeStruct((8, 1792), jnp.float32)] * 4,
+        [jax.ShapeDtypeStruct((16, 896), jnp.bfloat16)] * 4,
         [keep, flip(give, "k", 2, 1)],
     )
     pieces = [pieces[0]] + [

time: 102 us -> 103 us (level); the launches traced: 102 us -> 101 us
  Pallas kernels: 25.1 us -> 19.5 us
  starting transfers between devices: 38.9 us -> 43.2 us
    pallas_call x2, Pallas kernels: 14.4 us -> 8.96 us  [attention(): pl.pallas_call(functools.partial(attention_kernel, slots, own), out_shape...]
    ppermute x3, starting transfers between devices: 2.09 us -> 6.17 us  [local(): lax.ppermute(part, 'x', [(i, (i + s) % 4) for i in range(4)])]
    ppermute x3, waiting for transfers between devices: 4.3 us -> 6.57 us  [local(): lax.ppermute(part, 'x', [(i, (i + s) % 4) for i in range(4)])]
    ppermute x13, waiting for transfers between devices: 10.8 us -> 9.8 us  [flip(): return lax.ppermute(value, axis, [(i, i ^ bits) for i in range(size)])]
  transfers between devices with their start and end apart: 28 -> 28, of which waited for: 20 -> 18; matrix products, arithmetic and copies ran while one was open for 0% -> 0% of each run, Pallas kernels for 19% -> 14%
where the time goes in v13:
time: 103 us; the launch traced here: 101 us
  starting transfers between devices  43.2 us (42%)
  waiting for transfers between devices  36.8 us (36%)
  Pallas kernels  19.5 us (19%)
  local copies, waits for them, and re-layouts  1.52 us (1%)
    ppermute x13, starting transfers between devices, flip(): return lax.ppermute(value, axis, [(i, i ^ bits) for i in range(size)])  16.6 us
    ppermute x3, starting transfers between devices, local(): lax.ppermute(partial[d], 'zb', [(i, (i + d) % 4) for i in range(4)])  11.4 us
    ppermute x13, waiting for transfers between devices, flip(): return lax.ppermute(value, axis, [(i, i ^ bits) for i in range(size)])  9.8 us
    pallas_call x2, Pallas kernels, attention(): pl.pallas_call(functools.partial(attention_kernel, slots, own), out_shape...  8.96 us
    ppermute x3, waiting for transfers between devices, local(): lax.ppermute(partial[d], 'zb', [(i, (i + d) % 4) for i in range(4)])  8.47 us
    ppermute x6, waiting for transfers between devices, turn(): lax.ppermute(value, axis, [((i + shift) % size, i) for i in range(size)])  7.33 us
    ppermute x6, starting transfers between devices, turn(): lax.ppermute(value, axis, [((i + shift) % size, i) for i in range(size)])  6.64 us
    ppermute x3, waiting for transfers between devices, local(): lax.ppermute(part, 'x', [(i, (i + s) % 4) for i in range(4)])  6.57 us
  transfers between devices with their start and end apart: 28, of which 18 were waited for; matrix products, arithmetic and copies ran while one was open for 0% of the time, Pallas kernels for 14%

profile of v13, /device:TPU:6, one launch (start us, length us, event | category | flops | bytes accessed | tf_op | source)
XLA Modules:
  0.0 101.2 jit_solution(4411032681110088448)
XLA Ops:
  0.0 2.3 %pack.1 = (bf16[128,768]{1,0:T(8,128)(2,1)}, bf16[576,512]{1,0:T(8,128)(2,1)}) custom-call(bf16[128,512]{1,0:T(8,128)(2,1)} %q_nope.1, bf16[128,256]{1,0:T(8,128)(2,1)} %q_rope.1, bf16[4,128,512]{2,1,0:T(8,128)(2,1)} %pool_latent.1, bf16[4,64,128]{2,1,0:T(8,128)(2,1)} %pool_rope.1), custom_call_target="tpu_custom_call" | custom-call | tf_op jit(solution)/shard_map/pack/pallas_call | solution.py:244
  2.3 1.7 %collective-permute-start = (bf16[576,512]{1,0:T(8,128)(2,1)}, bf16[576,512]{1,0:T(8,128)(2,1)S(1)}, u32[]{:S(2)}, u32[]{:S(2)}) collective-permute-start(bf16[576,512]{1,0:T(8,128)(2,1)} %get-tuple-element.38.refs_0_), channel_id=1, source_target_pairs={{0,128},{128,0},{1,129},{129,1},{2,130},{130,2},{3,131},{131,3},{4... | collective-permute-start | bytes 1769480 | tf_op jit(solution)/shard_map/ppermute | solution.py:356
  4.0 1.9 %collective-permute-start.1 = (bf16[448,512]{1,0:T(8,128)(2,1)}, bf16[448,512]{1,0:T(8,128)(2,1)S(1)}, u32[]{:S(2)}, u32[]{:S(2)}) collective-permute-start(bf16[448,512]{1,0:T(8,128)(2,1)} %bitcast.11), channel_id=1, source_target_pairs={{0,2},{2,0},{1,3},{3,1},{4,6},{6,4},{5,7},{7,5},{8,10},{10,8},{9,1... | collective-permute-start | bytes 1376264 | tf_op jit(solution)/shard_map/ppermute | solution.py:356
  5.9 0.8 collective-permute-start.2
  6.7 1.1 %collective-permute-start.3 = (bf16[128,768]{1,0:T(8,128)(2,1)}, bf16[128,768]{1,0:T(8,128)(2,1)S(1)}, u32[]{:S(2)}, u32[]{:S(2)}) collective-permute-start(bf16[128,768]{1,0:T(8,128)(2,1)} %get-tuple-element.40.refs_0_), channel_id=1, source_target_pairs={{64,0},{96,32},{0,64},{32,96},{65,1},{97,33},{1,65},{33,97},{66,2}... | collective-permute-start | bytes 589832 | tf_op jit(solution)/shard_map/ppermute | solution.py:352
  7.8 2.1 %collective-permute-start.4 = (bf16[128,768]{1,0:T(8,128)(2,1)}, bf16[128,768]{1,0:T(8,128)(2,1)S(1)}, u32[]{:S(2)}, u32[]{:S(2)}) collective-permute-start(bf16[128,768]{1,0:T(8,128)(2,1)} %get-tuple-element.40.refs_0_), channel_id=1, source_target_pairs={{96,0},{0,32},{32,64},{64,96},{97,1},{1,33},{33,65},{65,97},{98,2}... | collective-permute-start | bytes 589832 | tf_op jit(solution)/shard_map/ppermute | solution.py:352
  9.9 0.1 stack.24.ids
  10.0 0.7 copy-done.7
  10.7 0.7 copy-done.8
  11.4 2.5 %plan.1 = (s32[64]{0:T(128)S(1)}, s32[8]{0:T(128)S(1)}) custom-call(s32[5]{0:T(128)S(1)} %stack.24.ids, s32[16,32]{1,0:T(8,128)S(1)} %copy-done.7, s32[16]{0:T(128)S(1)} %copy-done.8), custom_call_target="tpu_custom_call" | custom-call | tf_op jit(solution)/shard_map/plan/pallas_call | solution.py:65
  13.9 3.7 %collective-permute-done.2.refs_3_.refs_1_ = bf16[128,768]{1,0:T(8,128)(2,1)S(1)} collective-permute-done((bf16[128,768]{1,0:T(8,128)(2,1)}, bf16[128,768]{1,0:T(8,128)(2,1)S(1)}, u32[]{:S(2)}, u32[]{:S(2)}) %collective-permute-start.2) | collective-permute-done | bytes 196640 | tf_op jit(solution)/shard_map/ppermute | solution.py:352
  17.6 0.0 collective-permute-done.3.refs_4_.refs_2_
  17.6 0.6 collective-permute-done.4.refs_5_.refs_3_
  18.2 0.0 collective-permute-done.1.refs_2_
  18.3 0.1 pair.1
  18.3 1.1 %collective-permute-start.13 = (bf16[2,448,512]{2,1,0:T(8,128)(2,1)S(1)}, bf16[2,448,512]{2,1,0:T(8,128)(2,1)S(1)}, u32[]{:S(2)}, u32[]{:S(2)}) collective-permute-start(bf16[2,448,512]{2,1,0:T(8,128)(2,1)S(1)} %pair.1), channel_id=1, source_target_pairs={{0,128},{1,129},{128,0},{129,1},{2,130},{3,131},{130,2},{131,3},{4... | collective-permute-start | bytes 2752520 | tf_op jit(solution)/shard_map/ppermute | solution.py:356
  19.4 2.5 %collective-permute-start.14 = (bf16[2,448,512]{2,1,0:T(8,128)(2,1)S(1)}, bf16[2,448,512]{2,1,0:T(8,128)(2,1)S(1)}, u32[]{:S(2)}, u32[]{:S(2)}) collective-permute-start(bf16[2,448,512]{2,1,0:T(8,128)(2,1)S(1)} %pair.1), channel_id=1, source_target_pairs={{0,129},{1,128},{128,1},{129,0},{2,131},{3,130},{130,3},{131,2},{4... | collective-permute-start | bytes 2752520 | tf_op jit(solution)/shard_map/ppermute | solution.py:356
  21.9 0.0 collective-permute-start.5
  21.9 0.5 collective-permute-start.6
  22.4 1.3 %prepare.1 = (bf16[4,512,512]{2,1,0:T(8,128)(2,1)S(1)}, bf16[4,512,64]{2,1,0:T(8,128)(2,1)S(1)}) custom-call(s32[8]{0:T(128)S(1)} %get-tuple-element.41.counts, bf16[128,768]{1,0:T(8,128)(2,1)S(1)} %copy-done.4, bf16[128,768]{1,0:T(8,128)(2,1)S(1)} %collective-permute-done.2.refs_3_.refs_1_, bf16[128,768]{1,0:T(8,128)(2,1)S(1)} %collective-permute-done.3.refs_4_.refs_2_, ...), custom_call_target="tpu_custom_call" | custom-call | tf_op jit(solution)/shard_map/prepare/pallas_call | solution.py:340
  23.7 0.2 collective-permute-done.5.refs_2_
  23.9 0.8 collective-permute-done.6.refs_3_
  24.7 6.2 %attend.3 = (bf16[128,640]{1,0:T(8,128)(2,1)S(1)}, bf16[128,640]{1,0:T(8,128)(2,1)S(1)}, bf16[128,640]{1,0:T(8,128)(2,1)S(1)}) custom-call(s32[64]{0:T(128)S(1)} %get-tuple-element.37.lists, s32[8]{0:T(128)S(1)} %get-tuple-element.41.counts, bf16[4,512,512]{2,1,0:T(8,128)(2,1)S(1)} %get-tuple-element.42.q_lat, ...), custom_call_target="tpu_custom_call" | custom-call | tf_op jit(solution)/shard_map/attend/pallas_call | solution.py:185
  30.9 3.8 %collective-permute-start.7 = (bf16[128,640]{1,0:T(8,128)(2,1)S(1)}, bf16[128,640]{1,0:T(8,128)(2,1)S(1)}, u32[]{:S(2)}, u32[]{:S(2)}) collective-permute-start(bf16[128,640]{1,0:T(8,128)(2,1)S(1)} %get-tuple-element.45), channel_id=1, source_target_pairs={{0,32},{32,64},{64,96},{96,0},{1,33},{33,65},{65,97},{97,1},{2,34}... | collective-permute-start | bytes 491528 | tf_op jit(solution)/shard_map/ppermute | solution.py:409
  34.7 2.3 %collective-permute-start.8 = (bf16[128,640]{1,0:T(8,128)(2,1)S(1)}, bf16[128,640]{1,0:T(8,128)(2,1)S(1)}, u32[]{:S(2)}, u32[]{:S(2)}) collective-permute-start(bf16[128,640]{1,0:T(8,128)(2,1)S(1)} %get-tuple-element.46), channel_id=1, source_target_pairs={{0,64},{32,96},{64,0},{96,32},{1,65},{33,97},{65,1},{97,33},{2,66}... | collective-permute-start | bytes 491528 | tf_op jit(solution)/shard_map/ppermute | solution.py:409
  37.1 2.8 %attend.2.refs_0_ = bf16[128,640]{1,0:T(8,128)(2,1)S(1)} custom-call(s32[64]{0:T(128)S(1)} %get-tuple-element.37.lists, s32[8]{0:T(128)S(1)} %get-tuple-element.41.counts, bf16[4,512,512]{2,1,0:T(8,128)(2,1)S(1)} %get-tuple-element.42.q_lat, bf16[4,512,64]{2,1,0:T(8,128)(2,1)S(1)} %get-tuple-element.43.q_rot, bf16[576,512]{1,0:T(8,128)(2,1)S(1)} %copy-done, ...), custom_call_target="tpu_custom_call" | custom-call | tf_op jit(solution)/shard_map/attend/pallas_call | solution.py:185
  39.9 2.7 %collective-permute-done.7.refs_1_ = bf16[128,640]{1,0:T(8,128)(2,1)S(1)} collective-permute-done((bf16[128,640]{1,0:T(8,128)(2,1)S(1)}, bf16[128,640]{1,0:T(8,128)(2,1)S(1)}, u32[]{:S(2)}, u32[]{:S(2)}) %collective-permute-start.7) | collective-permute-done | bytes 163872 | tf_op jit(solution)/shard_map/ppermute | solution.py:409
  42.6 0.7 collective-permute-done.8.refs_2_
  43.4 3.1 %collective-permute-done.9.refs_3_ = bf16[128,640]{1,0:T(8,128)(2,1)S(1)} collective-permute-done((bf16[128,640]{1,0:T(8,128)(2,1)S(1)}, bf16[128,640]{1,0:T(8,128)(2,1)S(1)}, u32[]{:S(2)}, u32[]{:S(2)}) %collective-permute-start.9) | collective-permute-done | bytes 163872 | tf_op jit(solution)/shard_map/ppermute | solution.py:409
  46.5 1.1 %combine.1 = (bf16[32,512]{1,0:T(8,128)(2,1)S(1)}, bf16[32,512]{1,0:T(8,128)(2,1)S(1)}, bf16[32,512]{1,0:T(8,128)(2,1)S(1)}, bf16[32,512]{1,0:T(8,128)(2,1)S(1)}) custom-call(s32[5]{0:T(128)S(1)} %stack.24.ids, bf16[128,640]{1,0:T(8,128)(2,1)S(1)} %attend.2.refs_0_, bf16[128,640]{1,0:T(8,128)(2,1)S(1)} %collective-permute-done.7.refs_1_, ...), custom_call_target="tpu_custom_call" | custom-call | tf_op jit(solution)/shard_map/combine/pallas_call | solution.py:340
  47.5 0.7 collective-permute-start.10
  48.3 0.3 collective-permute-start.11
  48.5 4.1 %collective-permute-start.12 = (bf16[32,512]{1,0:T(8,128)(2,1)S(1)}, bf16[32,512]{1,0:T(8,128)(2,1)S(1)}, u32[]{:S(2)}, u32[]{:S(2)}) collective-permute-start(bf16[32,512]{1,0:T(8,128)(2,1)S(1)} %get-tuple-element.51), channel_id=1, source_target_pairs={{0,3},{1,2},{2,1},{3,0},{4,7},{5,6},{6,5},{7,4},{8,11},{9,10},{10,... | collective-permute-start | bytes 98312 | tf_op jit(solution)/shard_map/ppermute | solution.py:356
  52.6 0.8 collective-permute-done.10.refs_1_
  53.4 1.5 %collective-permute-done.12.refs_3_ = bf16[32,512]{1,0:T(8,128)(2,1)S(1)} collective-permute-done((bf16[32,512]{1,0:T(8,128)(2,1)S(1)}, bf16[32,512]{1,0:T(8,128)(2,1)S(1)}, u32[]{:S(2)}, u32[]{:S(2)}) %collective-permute-start.12) | collective-permute-done | bytes 32800 | tf_op jit(solution)/shard_map/ppermute | solution.py:356
  54.9 0.0 collective-permute-done.13.refs_1_
  54.9 0.9 collective-permute-start.18
  55.8 2.8 %collective-permute-start.19 = (bf16[448,512]{1,0:T(8,128)(2,1)S(1)}, bf16[448,512]{1,0:T(8,128)(2,1)S(1)}, u32[]{:S(2)}, u32[]{:S(2)}) collective-permute-start(bf16[448,512]{1,0:T(8,128)(2,1)S(1)} %slice_bitcast_fusion), channel_id=1, source_target_pairs={{0,129},{1,128},{128,1},{129,0},{2,131},{3,130},{130,3},{131,2},{4... | collective-permute-start | bytes 1376264 | tf_op jit(solution)/shard_map/ppermute | solution.py:356
  58.6 0.9 collective-permute-start.17
  59.5 1.1 %collective-permute-start.15 = (bf16[32,2048]{1,0:T(8,128)(2,1)S(1)}, bf16[32,2048]{1,0:T(8,128)(2,1)S(1)}, u32[]{:S(2)}, u32[]{:S(2)}) collective-permute-start(bf16[32,2048]{1,0:T(8,128)(2,1)S(1)} %get-tuple-element.53.refs_0_), channel_id=1, source_target_pairs={{32,0},{64,32},{96,64},{0,96},{33,1},{65,33},{97,65},{1,97},{34,2}... | collective-permute-start | bytes 393224 | tf_op jit(solution)/shard_map/ppermute | solution.py:352
  60.6 0.6 collective-permute-start.16
  61.2 3.0 %collective-permute-done.17.refs_0_ = bf16[32,2048]{1,0:T(8,128)(2,1)S(1)} collective-permute-done((bf16[32,2048]{1,0:T(8,128)(2,1)S(1)}, bf16[32,2048]{1,0:T(8,128)(2,1)S(1)}, u32[]{:S(2)}, u32[]{:S(2)}) %collective-permute-start.17) | collective-permute-done | bytes 131104 | tf_op jit(solution)/shard_map/ppermute | solution.py:352
  64.2 1.6 %collective-permute-done.18.refs_1_ = bf16[448,512]{1,0:T(8,128)(2,1)S(1)} collective-permute-done((bf16[448,512]{1,0:T(8,128)(2,1)S(1)}, bf16[448,512]{1,0:T(8,128)(2,1)S(1)}, u32[]{:S(2)}, u32[]{:S(2)}) %collective-permute-start.18) | collective-permute-done | bytes 458784 | tf_op jit(solution)/shard_map/ppermute | solution.py:356
  65.8 1.8 %collective-permute-done.19.refs_2_ = bf16[448,512]{1,0:T(8,128)(2,1)S(1)} collective-permute-done((bf16[448,512]{1,0:T(8,128)(2,1)S(1)}, bf16[448,512]{1,0:T(8,128)(2,1)S(1)}, u32[]{:S(2)}, u32[]{:S(2)}) %collective-permute-start.19) | collective-permute-done | bytes 458784 | tf_op jit(solution)/shard_map/ppermute | solution.py:356
  67.6 0.0 collective-permute-done.15.refs_1_
  67.6 0.0 collective-permute-done.16.refs_2_
  67.6 0.1 collective-permute-start.20
  67.7 1.9 %collective-permute-done.20.other = bf16[4,32,2048]{2,1,0:T(8,128)(2,1)S(1)} collective-permute-done((bf16[4,32,2048]{2,1,0:T(8,128)(2,1)S(1)}, bf16[4,32,2048]{2,1,0:T(8,128)(2,1)S(1)}, u32[]{:S(2)}, u32[]{:S(2)}) %collective-permute-start.20) | collective-permute-done | bytes 524320 | tf_op jit(solution)/shard_map/ppermute | solution.py:356
  69.6 1.9 %project.1 = (bf16[64,896]{1,0:T(8,128)(2,1)S(1)}, bf16[64,896]{1,0:T(8,128)(2,1)S(1)}, bf16[64,896]{1,0:T(8,128)(2,1)S(1)}, bf16[64,896]{1,0:T(8,128)(2,1)S(1)}) custom-call(s32[5]{0:T(128)S(1)} %stack.24.ids, bf16[4,32,2048]{2,1,0:T(8,128)(2,1)S(1)} %stack.25.own, bf16[4,32,2048]{2,1,0:T(8,128)(2,1)S(1)} %collective-permute-done.20.other, ...), custom_call_target="tpu_custom_call" | custom-call | tf_op jit(solution)/shard_map/project/pallas_call | solution.py:340
  71.6 3.3 %collective-permute-start.21 = (bf16[64,896]{1,0:T(8,128)(2,1)S(1)}, bf16[64,896]{1,0:T(8,128)(2,1)S(1)}, u32[]{:S(2)}, u32[]{:S(2)}) collective-permute-start(bf16[64,896]{1,0:T(8,128)(2,1)S(1)} %get-tuple-element.60), channel_id=1, source_target_pairs={{0,4},{4,8},{8,12},{12,0},{1,5},{5,9},{9,13},{13,1},{2,6},{6,10},{... | collective-permute-start | bytes 344072 | tf_op jit(solution)/shard_map/ppermute | solution.py:434
  74.9 5.4 %collective-permute-start.22 = (bf16[64,896]{1,0:T(8,128)(2,1)S(1)}, bf16[64,896]{1,0:T(8,128)(2,1)S(1)}, u32[]{:S(2)}, u32[]{:S(2)}) collective-permute-start(bf16[64,896]{1,0:T(8,128)(2,1)S(1)} %get-tuple-element.61), channel_id=1, source_target_pairs={{0,8},{4,12},{8,0},{12,4},{1,9},{5,13},{9,1},{13,5},{2,10},{6,14},... | collective-permute-start | bytes 344072 | tf_op jit(solution)/shard_map/ppermute | solution.py:434
  80.3 2.7 %collective-permute-start.23 = (bf16[64,896]{1,0:T(8,128)(2,1)S(1)}, bf16[64,896]{1,0:T(8,128)(2,1)S(1)}, u32[]{:S(2)}, u32[]{:S(2)}) collective-permute-start(bf16[64,896]{1,0:T(8,128)(2,1)S(1)} %get-tuple-element.62), channel_id=1, source_target_pairs={{0,12},{4,0},{8,4},{12,8},{1,13},{5,1},{9,5},{13,9},{2,14},{6,2},{... | collective-permute-start | bytes 344072 | tf_op jit(solution)/shard_map/ppermute | solution.py:434
  83.0 0.0 collective-permute-done.21.refs_1_
  83.0 5.5 %collective-permute-done.22.refs_2_ = bf16[64,896]{1,0:T(8,128)(2,1)S(1)} collective-permute-done((bf16[64,896]{1,0:T(8,128)(2,1)S(1)}, bf16[64,896]{1,0:T(8,128)(2,1)S(1)}, u32[]{:S(2)}, u32[]{:S(2)}) %collective-permute-start.22) | collective-permute-done | bytes 114720 | tf_op jit(solution)/shard_map/ppermute | solution.py:434
  88.5 2.9 %collective-permute-done.23.refs_3_ = bf16[64,896]{1,0:T(8,128)(2,1)S(1)} collective-permute-done((bf16[64,896]{1,0:T(8,128)(2,1)S(1)}, bf16[64,896]{1,0:T(8,128)(2,1)S(1)}, u32[]{:S(2)}, u32[]{:S(2)}) %collective-permute-start.23) | collective-permute-done | bytes 114720 | tf_op jit(solution)/shard_map/ppermute | solution.py:434
  91.5 0.1 share.1
  91.5 0.1 collective-permute-start.24
  91.6 1.2 %collective-permute-done.24.got = bf16[32,896]{1,0:T(8,128)(2,1)S(1)} collective-permute-done((bf16[32,896]{1,0:T(8,128)(2,1)S(1)}, bf16[32,896]{1,0:T(8,128)(2,1)S(1)}, u32[]{:S(2)}, u32[]{:S(2)}) %collective-permute-start.24) | collective-permute-done | bytes 57376 | tf_op jit(solution)/shard_map/ppermute | solution.py:356
  92.9 1.5 %collective-permute-start.25 = (bf16[16,896]{1,0:T(8,128)(2,1)S(1)}, bf16[16,896]{1,0:T(8,128)(2,1)S(1)}, u32[]{:S(2)}, u32[]{:S(2)}) collective-permute-start(bf16[16,896]{1,0:T(8,128)(2,1)S(1)} %get-tuple-element.66), channel_id=1, source_target_pairs={{0,32},{32,64},{64,96},{96,0},{1,33},{33,65},{65,97},{97,1},{2,34}... | collective-permute-start | bytes 86024 | tf_op jit(solution)/shard_map/ppermute | solution.py:444
  94.3 1.0 collective-permute-start.27
  95.3 1.5 %collective-permute-done.25.refs_1_ = bf16[16,896]{1,0:T(8,128)(2,1)S(1)} collective-permute-done((bf16[16,896]{1,0:T(8,128)(2,1)S(1)}, bf16[16,896]{1,0:T(8,128)(2,1)S(1)}, u32[]{:S(2)}, u32[]{:S(2)}) %collective-permute-start.25) | collective-permute-done | bytes 28704 | tf_op jit(solution)/shard_map/ppermute | solution.py:444
  96.8 3.1 %collective-permute-done.26.refs_2_ = bf16[16,896]{1,0:T(8,128)(2,1)S(1)} collective-permute-done((bf16[16,896]{1,0:T(8,128)(2,1)S(1)}, bf16[16,896]{1,0:T(8,128)(2,1)S(1)}, u32[]{:S(2)}, u32[]{:S(2)}) %collective-permute-start.26) | collective-permute-done | bytes 28704 | tf_op jit(solution)/shard_map/ppermute | solution.py:444
  99.9 0.0 collective-permute-done.27.refs_3_
  99.9 1.3 %place.1 = bf16[8,7168]{1,0:T(8,128)(2,1)} custom-call(s32[5]{0:T(128)S(1)} %stack.24.ids, bf16[16,896]{1,0:T(8,128)(2,1)S(1)} %get-tuple-element.65.refs_0_, bf16[16,896]{1,0:T(8,128)(2,1)S(1)} %collective-permute-done.25.refs_1_, bf16[16,896]{1,0:T(8,128)(2,1)S(1)} %collective-permute-done.26.refs_2_, bf16[16,896]{1,0:T(8,128)(2,1)S(1)} %collective-permute-done.27.refs_3_), custom_call_target="tpu_custom_call" | custom-call | tf_op jit(solution)/shard_map/place/pallas_call | solution.py:340
  (29 shorter events, 0.2 us)
Async XLA Ops:
  0.0 18.2 %copy-start.3 = (bf16[512,448]{0,1:T(8,128)(2,1)S(1)}, bf16[512,448]{0,1:T(8,128)(2,1)}, u32[]{:S(2)}) copy-start(bf16[512,448]{0,1:T(8,128)(2,1)} %param.21) | copy-start | bytes 1376260
  0.0 22.4 %copy-start.2 = (bf16[4,128,512]{2,1,0:T(8,128)(2,1)S(1)}, bf16[4,128,512]{2,1,0:T(8,128)(2,1)}, u32[]{:S(2)}) copy-start(bf16[4,128,512]{2,1,0:T(8,128)(2,1)} %refs_4_.3) | copy-start | bytes 1572868
  2.3 19.6 %copy-start = (bf16[576,512]{1,0:T(8,128)(2,1)S(1)}, bf16[576,512]{1,0:T(8,128)(2,1)}, u32[]{:S(2)}) copy-start(bf16[576,512]{1,0:T(8,128)(2,1)} %get-tuple-element.38.refs_0_) | copy-start | bytes 1769476
  2.3 20.1 %copy-start.4 = (bf16[128,768]{1,0:T(8,128)(2,1)S(1)}, bf16[128,768]{1,0:T(8,128)(2,1)}, u32[]{:S(2)}) copy-start(bf16[128,768]{1,0:T(8,128)(2,1)} %get-tuple-element.40.refs_0_) | copy-start | bytes 589828
  2.3 15.9 %collective-permute-start = (bf16[576,512]{1,0:T(8,128)(2,1)}, bf16[576,512]{1,0:T(8,128)(2,1)S(1)}, u32[]{:S(2)}, u32[]{:S(2)}) collective-permute-start(bf16[576,512]{1,0:T(8,128)(2,1)} %get-tuple-element.38.refs_0_), channel_id=1, source_target_pairs={{0,128},{128,0},{1,129},{129,1},{2,130},{130,2},{3,131},{131,3},{4... | collective-permute-start | bytes 1769480 | tf_op jit(solution)/shard_map/ppermute | solution.py:356
  4.0 14.3 %collective-permute-start.1 = (bf16[448,512]{1,0:T(8,128)(2,1)}, bf16[448,512]{1,0:T(8,128)(2,1)S(1)}, u32[]{:S(2)}, u32[]{:S(2)}) collective-permute-start(bf16[448,512]{1,0:T(8,128)(2,1)} %bitcast.11), channel_id=1, source_target_pairs={{0,2},{2,0},{1,3},{3,1},{4,6},{6,4},{5,7},{7,5},{8,10},{10,8},{9,1... | collective-permute-start | bytes 1376264 | tf_op jit(solution)/shard_map/ppermute | solution.py:356
  5.9 11.7 %collective-permute-start.2 = (bf16[128,768]{1,0:T(8,128)(2,1)}, bf16[128,768]{1,0:T(8,128)(2,1)S(1)}, u32[]{:S(2)}, u32[]{:S(2)}) collective-permute-start(bf16[128,768]{1,0:T(8,128)(2,1)} %get-tuple-element.40.refs_0_), channel_id=1, source_target_pairs={{32,0},{64,32},{96,64},{0,96},{33,1},{65,33},{97,65},{1,97},{34,2}... | collective-permute-start | bytes 589832 | tf_op jit(solution)/shard_map/ppermute | solution.py:352
  6.7 10.9 %collective-permute-start.3 = (bf16[128,768]{1,0:T(8,128)(2,1)}, bf16[128,768]{1,0:T(8,128)(2,1)S(1)}, u32[]{:S(2)}, u32[]{:S(2)}) collective-permute-start(bf16[128,768]{1,0:T(8,128)(2,1)} %get-tuple-element.40.refs_0_), channel_id=1, source_target_pairs={{64,0},{96,32},{0,64},{32,96},{65,1},{97,33},{1,65},{33,97},{66,2}... | collective-permute-start | bytes 589832 | tf_op jit(solution)/shard_map/ppermute | solution.py:352
  7.8 10.4 %collective-permute-start.4 = (bf16[128,768]{1,0:T(8,128)(2,1)}, bf16[128,768]{1,0:T(8,128)(2,1)S(1)}, u32[]{:S(2)}, u32[]{:S(2)}) collective-permute-start(bf16[128,768]{1,0:T(8,128)(2,1)} %get-tuple-element.40.refs_0_), channel_id=1, source_target_pairs={{96,0},{0,32},{32,64},{64,96},{97,1},{1,33},{33,65},{65,97},{98,2}... | collective-permute-start | bytes 589832 | tf_op jit(solution)/shard_map/ppermute | solution.py:352
  10.0 0.7 copy-start.7
  10.7 0.7 copy-start.8
  18.2 6.5 %copy-start.1 = (bf16[4,512,128]{2,1,0:T(8,128)(2,1)S(1)}, bf16[4,512,128]{2,1,0:T(8,128)(2,1)}, u32[]{:S(2)}) copy-start(bf16[4,512,128]{2,1,0:T(8,128)(2,1)} %refs_4_.5) | copy-start | bytes 1572868
  18.3 36.6 %collective-permute-start.13 = (bf16[2,448,512]{2,1,0:T(8,128)(2,1)S(1)}, bf16[2,448,512]{2,1,0:T(8,128)(2,1)S(1)}, u32[]{:S(2)}, u32[]{:S(2)}) collective-permute-start(bf16[2,448,512]{2,1,0:T(8,128)(2,1)S(1)} %pair.1), channel_id=1, source_target_pairs={{0,128},{1,129},{128,0},{129,1},{2,130},{3,131},{130,2},{131,3},{4... | collective-permute-start | bytes 2752520 | tf_op jit(solution)/shard_map/ppermute | solution.py:356
  19.4 35.5 %collective-permute-start.14 = (bf16[2,448,512]{2,1,0:T(8,128)(2,1)S(1)}, bf16[2,448,512]{2,1,0:T(8,128)(2,1)S(1)}, u32[]{:S(2)}, u32[]{:S(2)}) collective-permute-start(bf16[2,448,512]{2,1,0:T(8,128)(2,1)S(1)} %pair.1), channel_id=1, source_target_pairs={{0,129},{1,128},{128,1},{129,0},{2,131},{3,130},{130,3},{131,2},{4... | collective-permute-start | bytes 2752520 | tf_op jit(solution)/shard_map/ppermute | solution.py:356
  21.9 2.0 %collective-permute-start.5 = (bf16[576,512]{1,0:T(8,128)(2,1)S(1)}, bf16[576,512]{1,0:T(8,128)(2,1)S(1)}, u32[]{:S(2)}, u32[]{:S(2)}) collective-permute-start(bf16[576,512]{1,0:T(8,128)(2,1)S(1)} %copy-done), channel_id=1, source_target_pairs={{0,16},{16,0},{1,17},{17,1},{2,18},{18,2},{3,19},{19,3},{4,20},{20... | collective-permute-start | bytes 1769480 | tf_op jit(solution)/shard_map/ppermute | solution.py:356
  21.9 2.8 %collective-permute-start.6 = (bf16[576,512]{1,0:T(8,128)(2,1)S(1)}, bf16[576,512]{1,0:T(8,128)(2,1)S(1)}, u32[]{:S(2)}, u32[]{:S(2)}) collective-permute-start(bf16[576,512]{1,0:T(8,128)(2,1)S(1)} %get-tuple-element.44.refs_1_), channel_id=1, source_target_pairs={{0,16},{16,0},{1,17},{17,1},{2,18},{18,2},{3,19},{19,3},{4,20},{20... | collective-permute-start | bytes 1769480 | tf_op jit(solution)/shard_map/ppermute | solution.py:356
  24.7 12.4 %copy-start.5 = (bf16[128,512]{1,0:T(8,128)(2,1)S(1)}, bf16[128,512]{1,0:T(8,128)(2,1)}, u32[]{:S(2)}) copy-start(bf16[128,512]{1,0:T(8,128)(2,1)} %refs_5_.1) | copy-start | bytes 393220
  24.7 12.4 %copy-start.6 = (bf16[1,64,128]{2,1,0:T(8,128)(2,1)S(1)}, bf16[1,64,128]{2,1,0:T(8,128)(2,1)}, u32[]{:S(2)}) copy-start(bf16[1,64,128]{2,1,0:T(8,128)(2,1)} %param.14) | copy-start | bytes 49156
  30.9 11.7 %collective-permute-start.7 = (bf16[128,640]{1,0:T(8,128)(2,1)S(1)}, bf16[128,640]{1,0:T(8,128)(2,1)S(1)}, u32[]{:S(2)}, u32[]{:S(2)}) collective-permute-start(bf16[128,640]{1,0:T(8,128)(2,1)S(1)} %get-tuple-element.45), channel_id=1, source_target_pairs={{0,32},{32,64},{64,96},{96,0},{1,33},{33,65},{65,97},{97,1},{2,34}... | collective-permute-start | bytes 491528 | tf_op jit(solution)/shard_map/ppermute | solution.py:409
  34.7 8.6 %collective-permute-start.8 = (bf16[128,640]{1,0:T(8,128)(2,1)S(1)}, bf16[128,640]{1,0:T(8,128)(2,1)S(1)}, u32[]{:S(2)}, u32[]{:S(2)}) collective-permute-start(bf16[128,640]{1,0:T(8,128)(2,1)S(1)} %get-tuple-element.46), channel_id=1, source_target_pairs={{0,64},{32,96},{64,0},{96,32},{1,65},{33,97},{65,1},{97,33},{2,66}... | collective-permute-start | bytes 491528 | tf_op jit(solution)/shard_map/ppermute | solution.py:409
  37.1 9.4 %collective-permute-start.9 = (bf16[128,640]{1,0:T(8,128)(2,1)S(1)}, bf16[128,640]{1,0:T(8,128)(2,1)S(1)}, u32[]{:S(2)}, u32[]{:S(2)}) collective-permute-start(bf16[128,640]{1,0:T(8,128)(2,1)S(1)} %get-tuple-element.47), channel_id=1, source_target_pairs={{0,96},{32,0},{64,32},{96,64},{1,97},{33,1},{65,33},{97,65},{2,98}... | collective-permute-start | bytes 491528 | tf_op jit(solution)/shard_map/ppermute | solution.py:409
  47.5 5.9 %collective-permute-start.10 = (bf16[32,512]{1,0:T(8,128)(2,1)S(1)}, bf16[32,512]{1,0:T(8,128)(2,1)S(1)}, u32[]{:S(2)}, u32[]{:S(2)}) collective-permute-start(bf16[32,512]{1,0:T(8,128)(2,1)S(1)} %get-tuple-element.49), channel_id=1, source_target_pairs={{0,1},{1,0},{2,3},{3,2},{4,5},{5,4},{6,7},{7,6},{8,9},{9,8},{10,11... | collective-permute-start | bytes 98312 | tf_op jit(solution)/shard_map/ppermute | solution.py:356
  48.3 5.1 %collective-permute-start.11 = (bf16[32,512]{1,0:T(8,128)(2,1)S(1)}, bf16[32,512]{1,0:T(8,128)(2,1)S(1)}, u32[]{:S(2)}, u32[]{:S(2)}) collective-permute-start(bf16[32,512]{1,0:T(8,128)(2,1)S(1)} %get-tuple-element.50), channel_id=1, source_target_pairs={{0,2},{1,3},{2,0},{3,1},{4,6},{5,7},{6,4},{7,5},{8,10},{9,11},{10,... | collective-permute-start | bytes 98312 | tf_op jit(solution)/shard_map/ppermute | solution.py:356
  48.5 6.3 %collective-permute-start.12 = (bf16[32,512]{1,0:T(8,128)(2,1)S(1)}, bf16[32,512]{1,0:T(8,128)(2,1)S(1)}, u32[]{:S(2)}, u32[]{:S(2)}) collective-permute-start(bf16[32,512]{1,0:T(8,128)(2,1)S(1)} %get-tuple-element.51), channel_id=1, source_target_pairs={{0,3},{1,2},{2,1},{3,0},{4,7},{5,6},{6,5},{7,4},{8,11},{9,10},{10,... | collective-permute-start | bytes 98312 | tf_op jit(solution)/shard_map/ppermute | solution.py:356
  54.9 10.8 %collective-permute-start.18 = (bf16[448,512]{1,0:T(8,128)(2,1)S(1)}, bf16[448,512]{1,0:T(8,128)(2,1)S(1)}, u32[]{:S(2)}, u32[]{:S(2)}) collective-permute-start(bf16[448,512]{1,0:T(8,128)(2,1)S(1)} %slice_bitcast_fusion.1), channel_id=1, source_target_pairs={{0,128},{1,129},{128,0},{129,1},{2,130},{3,131},{130,2},{131,3},{4... | collective-permute-start | bytes 1376264 | tf_op jit(solution)/shard_map/ppermute | solution.py:356
  55.8 11.7 %collective-permute-start.19 = (bf16[448,512]{1,0:T(8,128)(2,1)S(1)}, bf16[448,512]{1,0:T(8,128)(2,1)S(1)}, u32[]{:S(2)}, u32[]{:S(2)}) collective-permute-start(bf16[448,512]{1,0:T(8,128)(2,1)S(1)} %slice_bitcast_fusion), channel_id=1, source_target_pairs={{0,129},{1,128},{128,1},{129,0},{2,131},{3,130},{130,3},{131,2},{4... | collective-permute-start | bytes 1376264 | tf_op jit(solution)/shard_map/ppermute | solution.py:356
  58.6 5.6 %collective-permute-start.17 = (bf16[32,2048]{1,0:T(8,128)(2,1)S(1)}, bf16[32,2048]{1,0:T(8,128)(2,1)S(1)}, u32[]{:S(2)}, u32[]{:S(2)}) collective-permute-start(bf16[32,2048]{1,0:T(8,128)(2,1)S(1)} %get-tuple-element.53.refs_0_), channel_id=1, source_target_pairs={{96,0},{0,32},{32,64},{64,96},{97,1},{1,33},{33,65},{65,97},{98,2}... | collective-permute-start | bytes 393224 | tf_op jit(solution)/shard_map/ppermute | solution.py:352
  59.5 8.1 %collective-permute-start.15 = (bf16[32,2048]{1,0:T(8,128)(2,1)S(1)}, bf16[32,2048]{1,0:T(8,128)(2,1)S(1)}, u32[]{:S(2)}, u32[]{:S(2)}) collective-permute-start(bf16[32,2048]{1,0:T(8,128)(2,1)S(1)} %get-tuple-element.53.refs_0_), channel_id=1, source_target_pairs={{32,0},{64,32},{96,64},{0,96},{33,1},{65,33},{97,65},{1,97},{34,2}... | collective-permute-start | bytes 393224 | tf_op jit(solution)/shard_map/ppermute | solution.py:352
  60.6 7.0 %collective-permute-start.16 = (bf16[32,2048]{1,0:T(8,128)(2,1)S(1)}, bf16[32,2048]{1,0:T(8,128)(2,1)S(1)}, u32[]{:S(2)}, u32[]{:S(2)}) collective-permute-start(bf16[32,2048]{1,0:T(8,128)(2,1)S(1)} %get-tuple-element.53.refs_0_), channel_id=1, source_target_pairs={{64,0},{96,32},{0,64},{32,96},{65,1},{97,33},{1,65},{33,97},{66,2}... | collective-permute-start | bytes 393224 | tf_op jit(solution)/shard_map/ppermute | solution.py:352
  67.6 2.0 %collective-permute-start.20 = (bf16[4,32,2048]{2,1,0:T(8,128)(2,1)S(1)}, bf16[4,32,2048]{2,1,0:T(8,128)(2,1)S(1)}, u32[]{:S(2)}, u32[]{:S(2)}) collective-permute-start(bf16[4,32,2048]{2,1,0:T(8,128)(2,1)S(1)} %stack.25.own), channel_id=1, source_target_pairs={{0,16},{16,0},{1,17},{17,1},{2,18},{18,2},{3,19},{19,3},{4,20},{20... | collective-permute-start | bytes 1572872 | tf_op jit(solution)/shard_map/ppermute | solution.py:356
  71.6 11.4 %collective-permute-start.21 = (bf16[64,896]{1,0:T(8,128)(2,1)S(1)}, bf16[64,896]{1,0:T(8,128)(2,1)S(1)}, u32[]{:S(2)}, u32[]{:S(2)}) collective-permute-start(bf16[64,896]{1,0:T(8,128)(2,1)S(1)} %get-tuple-element.60), channel_id=1, source_target_pairs={{0,4},{4,8},{8,12},{12,0},{1,5},{5,9},{9,13},{13,1},{2,6},{6,10},{... | collective-permute-start | bytes 344072 | tf_op jit(solution)/shard_map/ppermute | solution.py:434
  74.9 13.6 %collective-permute-start.22 = (bf16[64,896]{1,0:T(8,128)(2,1)S(1)}, bf16[64,896]{1,0:T(8,128)(2,1)S(1)}, u32[]{:S(2)}, u32[]{:S(2)}) collective-permute-start(bf16[64,896]{1,0:T(8,128)(2,1)S(1)} %get-tuple-element.61), channel_id=1, source_target_pairs={{0,8},{4,12},{8,0},{12,4},{1,9},{5,13},{9,1},{13,5},{2,10},{6,14},... | collective-permute-start | bytes 344072 | tf_op jit(solution)/shard_map/ppermute | solution.py:434
  80.3 11.1 %collective-permute-start.23 = (bf16[64,896]{1,0:T(8,128)(2,1)S(1)}, bf16[64,896]{1,0:T(8,128)(2,1)S(1)}, u32[]{:S(2)}, u32[]{:S(2)}) collective-permute-start(bf16[64,896]{1,0:T(8,128)(2,1)S(1)} %get-tuple-element.62), channel_id=1, source_target_pairs={{0,12},{4,0},{8,4},{12,8},{1,13},{5,1},{9,5},{13,9},{2,14},{6,2},{... | collective-permute-start | bytes 344072 | tf_op jit(solution)/shard_map/ppermute | solution.py:434
  91.5 1.3 %collective-permute-start.24 = (bf16[32,896]{1,0:T(8,128)(2,1)S(1)}, bf16[32,896]{1,0:T(8,128)(2,1)S(1)}, u32[]{:S(2)}, u32[]{:S(2)}) collective-permute-start(bf16[32,896]{1,0:T(8,128)(2,1)S(1)} %get-tuple-element.64), channel_id=1, source_target_pairs={{0,16},{16,0},{1,17},{17,1},{2,18},{18,2},{3,19},{19,3},{4,20},{20... | collective-permute-start | bytes 172040 | tf_op jit(solution)/shard_map/ppermute | solution.py:356
  92.9 3.9 %collective-permute-start.25 = (bf16[16,896]{1,0:T(8,128)(2,1)S(1)}, bf16[16,896]{1,0:T(8,128)(2,1)S(1)}, u32[]{:S(2)}, u32[]{:S(2)}) collective-permute-start(bf16[16,896]{1,0:T(8,128)(2,1)S(1)} %get-tuple-element.66), channel_id=1, source_target_pairs={{0,32},{32,64},{64,96},{96,0},{1,33},{33,65},{65,97},{97,1},{2,34}... | collective-permute-start | bytes 86024 | tf_op jit(solution)/shard_map/ppermute | solution.py:444
  94.3 5.6 %collective-permute-start.26 = (bf16[16,896]{1,0:T(8,128)(2,1)S(1)}, bf16[16,896]{1,0:T(8,128)(2,1)S(1)}, u32[]{:S(2)}, u32[]{:S(2)}) collective-permute-start(bf16[16,896]{1,0:T(8,128)(2,1)S(1)} %get-tuple-element.67), channel_id=1, source_target_pairs={{0,64},{32,96},{64,0},{96,32},{1,65},{33,97},{65,1},{97,33},{2,66}... | collective-permute-start | bytes 86024 | tf_op jit(solution)/shard_map/ppermute | solution.py:444
  94.3 5.6 %collective-permute-start.27 = (bf16[16,896]{1,0:T(8,128)(2,1)S(1)}, bf16[16,896]{1,0:T(8,128)(2,1)S(1)}, u32[]{:S(2)}, u32[]{:S(2)}) collective-permute-start(bf16[16,896]{1,0:T(8,128)(2,1)S(1)} %get-tuple-element.68), channel_id=1, source_target_pairs={{0,96},{32,0},{64,32},{96,64},{1,97},{33,1},{65,33},{97,65},{2,98}... | collective-permute-start | bytes 86024 | tf_op jit(solution)/shard_map/ppermute | solution.py:444

commit v14 on v12

--- a/solution.py
+++ b/solution.py
@@ -280,7 +280,7 @@
         sides.append(value)
     total[...] = jnp.concatenate(sides, axis=0).T
     for d in range(4):
-        first = pl.multiple_of(((zb + d) % 4) * 8, 8)
+        first = pl.multiple_of((zb ^ d) * 8, 8)
         parts = [total[pl.ds(first + s * 32, 8), :] for s in range(8)]
         outs[d][...] = jnp.concatenate(parts, axis=0).astype(jnp.bfloat16)
 
@@ -423,9 +423,7 @@
         [ids, *heads, *[flip(h, "k", 2, 1) for h in heads], *mine, *far],
         scratch=[pltpu.VMEM((256, 896), jnp.float32)],
     )
-    sums = [partial[0]] + [
-        lax.ppermute(partial[d], "zb", [(i, (i + d) % 4) for i in range(4)]) for d in (1, 2, 3)
-    ]
+    sums = [partial[0]] + [flip(partial[d], "zb", 4, d) for d in (1, 2, 3)]
     keep, give = simple(share_kernel, "share", [jax.ShapeDtypeStruct((32, 896), jnp.float32)] * 2, sums)
     pieces = simple(
         merge_kernel,

time: 104 us -> 102 us (0.981)
  starting transfers between devices: 44.2 us -> 37.1 us
  waiting for transfers between devices: 33.8 us -> 38.1 us
  Pallas kernels: 22.9 us -> 24 us
    ppermute x3 -> x0, starting transfers between devices: 11.5 us -> none  [local(): lax.ppermute(partial[d], 'zb', [(i, (i + d) % 4) for i in range(4)])]
    ppermute x16 -> x19, waiting for transfers between devices: 9 us -> 18.5 us  [flip(): return lax.ppermute(value, axis, [(i, i ^ bits) for i in range(size)])]
    ppermute x3 -> x0, waiting for transfers between devices: 8.54 us -> none  [local(): lax.ppermute(partial[d], 'zb', [(i, (i + d) % 4) for i in range(4)])]
    ppermute x16 -> x19, starting transfers between devices: 18.5 us -> 25.1 us  [flip(): return lax.ppermute(value, axis, [(i, i ^ bits) for i in range(size)])]
    ppermute x3, waiting for transfers between devices: 3.7 us -> 5.43 us  [local(): lax.ppermute(part, 'x', [(i, (i + s) % 4) for i in range(4)])]
    ppermute x6, waiting for transfers between devices: 7.73 us -> 8.95 us  [turn(): lax.ppermute(value, axis, [((i + shift) % size, i) for i in range(size)])]
    pallas_call x2, Pallas kernels: 12.2 us -> 13.4 us  [attention(): pl.pallas_call(functools.partial(attention_kernel, slots, own), out_shape...]
    ppermute x6, starting transfers between devices: 8.41 us -> 7.28 us  [turn(): lax.ppermute(value, axis, [((i + shift) % size, i) for i in range(size)])]
  transfers between devices with their start and end apart: 31 -> 31, of which waited for: 18 -> 21; matrix products, arithmetic and copies ran while one was open for 0% -> 0% of each run, Pallas kernels for 17% -> 18%
where the time goes in v14:
time: 102 us; the launch traced here: 101 us
  waiting for transfers between devices  38.1 us (37%)
  starting transfers between devices  37.1 us (36%)
  Pallas kernels  24 us (24%)
  local copies, waits for them, and re-layouts  1.52 us (1%)
    ppermute x19, starting transfers between devices, flip(): return lax.ppermute(value, axis, [(i, i ^ bits) for i in range(size)])  25.1 us
    ppermute x19, waiting for transfers between devices, flip(): return lax.ppermute(value, axis, [(i, i ^ bits) for i in range(size)])  18.5 us
    pallas_call x2, Pallas kernels, attention(): pl.pallas_call(functools.partial(attention_kernel, slots, own), out_shape...  13.4 us
    ppermute x6, waiting for transfers between devices, turn(): lax.ppermute(value, axis, [((i + shift) % size, i) for i in range(size)])  8.95 us
    ppermute x6, starting transfers between devices, turn(): lax.ppermute(value, axis, [((i + shift) % size, i) for i in range(size)])  7.28 us
    pallas_call x8, Pallas kernels, simple(): pl.pallas_call(kernel, out_shape=out_shape, in_specs=[pl.BlockSpec(memory...  5.71 us
    ppermute x3, waiting for transfers between devices, local(): lax.ppermute(part, 'x', [(i, (i + s) % 4) for i in range(4)])  5.43 us
    ppermute x3, waiting for transfers between devices, local(): lax.ppermute(pieces[s], 'x', [(i, (i + s) % 4) for i in range(4)])  5.25 us
  transfers between devices with their start and end apart: 31, of which 21 were waited for; matrix products, arithmetic and copies ran while one was open for 0% of the time, Pallas kernels for 18%

profile of v14, /device:TPU:6, one launch (start us, length us, event | category | flops | bytes accessed | tf_op | source)
XLA Modules:
  0.0 101.0 jit_solution(16663093977786625877)
XLA Ops:
  0.0 2.3 %pack.1 = (bf16[128,768]{1,0:T(8,128)(2,1)}, bf16[576,512]{1,0:T(8,128)(2,1)}) custom-call(bf16[128,512]{1,0:T(8,128)(2,1)} %q_nope.1, bf16[128,256]{1,0:T(8,128)(2,1)} %q_rope.1, bf16[4,128,512]{2,1,0:T(8,128)(2,1)} %pool_latent.1, bf16[4,64,128]{2,1,0:T(8,128)(2,1)} %pool_rope.1), custom_call_target="tpu_custom_call" | custom-call | tf_op jit(solution)/shard_map/pack/pallas_call | solution.py:244
  2.3 1.7 %collective-permute-start = (bf16[576,512]{1,0:T(8,128)(2,1)}, bf16[576,512]{1,0:T(8,128)(2,1)S(1)}, u32[]{:S(2)}, u32[]{:S(2)}) collective-permute-start(bf16[576,512]{1,0:T(8,128)(2,1)} %get-tuple-element.38.refs_0_), channel_id=1, source_target_pairs={{0,128},{128,0},{1,129},{129,1},{2,130},{130,2},{3,131},{131,3},{4... | collective-permute-start | bytes 1769480 | tf_op jit(solution)/shard_map/ppermute | solution.py:350
  4.0 1.9 %collective-permute-start.1 = (bf16[448,512]{1,0:T(8,128)(2,1)}, bf16[448,512]{1,0:T(8,128)(2,1)S(1)}, u32[]{:S(2)}, u32[]{:S(2)}) collective-permute-start(bf16[448,512]{1,0:T(8,128)(2,1)} %bitcast.11), channel_id=1, source_target_pairs={{0,2},{2,0},{1,3},{3,1},{4,6},{6,4},{5,7},{7,5},{8,10},{10,8},{9,1... | collective-permute-start | bytes 1376264 | tf_op jit(solution)/shard_map/ppermute | solution.py:350
  5.9 0.8 collective-permute-start.2
  6.7 1.1 %collective-permute-start.3 = (bf16[128,768]{1,0:T(8,128)(2,1)}, bf16[128,768]{1,0:T(8,128)(2,1)S(1)}, u32[]{:S(2)}, u32[]{:S(2)}) collective-permute-start(bf16[128,768]{1,0:T(8,128)(2,1)} %get-tuple-element.40.refs_0_), channel_id=1, source_target_pairs={{64,0},{96,32},{0,64},{32,96},{65,1},{97,33},{1,65},{33,97},{66,2}... | collective-permute-start | bytes 589832 | tf_op jit(solution)/shard_map/ppermute | solution.py:346
  7.9 2.1 %collective-permute-start.4 = (bf16[128,768]{1,0:T(8,128)(2,1)}, bf16[128,768]{1,0:T(8,128)(2,1)S(1)}, u32[]{:S(2)}, u32[]{:S(2)}) collective-permute-start(bf16[128,768]{1,0:T(8,128)(2,1)} %get-tuple-element.40.refs_0_), channel_id=1, source_target_pairs={{96,0},{0,32},{32,64},{64,96},{97,1},{1,33},{33,65},{65,97},{98,2}... | collective-permute-start | bytes 589832 | tf_op jit(solution)/shard_map/ppermute | solution.py:346
  10.0 0.1 stack.23.ids
  10.0 0.7 copy-done.7
  10.7 0.7 copy-done.8
  11.4 2.6 %plan.1 = (s32[64]{0:T(128)S(1)}, s32[8]{0:T(128)S(1)}) custom-call(s32[5]{0:T(128)S(1)} %stack.23.ids, s32[16,32]{1,0:T(8,128)S(1)} %copy-done.7, s32[16]{0:T(128)S(1)} %copy-done.8), custom_call_target="tpu_custom_call" | custom-call | tf_op jit(solution)/shard_map/plan/pallas_call | solution.py:65
  14.0 3.6 %collective-permute-done.2.refs_3_.refs_1_ = bf16[128,768]{1,0:T(8,128)(2,1)S(1)} collective-permute-done((bf16[128,768]{1,0:T(8,128)(2,1)}, bf16[128,768]{1,0:T(8,128)(2,1)S(1)}, u32[]{:S(2)}, u32[]{:S(2)}) %collective-permute-start.2) | collective-permute-done | bytes 196640 | tf_op jit(solution)/shard_map/ppermute | solution.py:346
  17.6 0.0 collective-permute-done.3.refs_4_.refs_2_
  17.6 0.6 collective-permute-done.4.refs_5_.refs_3_
  18.3 0.1 pair.1.refs_8_
  18.4 1.1 %collective-permute-start.13 = (bf16[2,448,512]{2,1,0:T(8,128)(2,1)S(1)}, bf16[2,448,512]{2,1,0:T(8,128)(2,1)S(1)}, u32[]{:S(2)}, u32[]{:S(2)}) collective-permute-start(bf16[2,448,512]{2,1,0:T(8,128)(2,1)S(1)} %pair.1.refs_8_), channel_id=1, source_target_pairs={{0,128},{1,129},{128,0},{129,1},{2,130},{3,131},{130,2},{131,3},{4... | collective-permute-start | bytes 2752520 | tf_op jit(solution)/shard_map/ppermute | solution.py:350
  19.4 2.5 %collective-permute-start.14 = (bf16[2,448,512]{2,1,0:T(8,128)(2,1)S(1)}, bf16[2,448,512]{2,1,0:T(8,128)(2,1)S(1)}, u32[]{:S(2)}, u32[]{:S(2)}) collective-permute-start(bf16[2,448,512]{2,1,0:T(8,128)(2,1)S(1)} %pair.1.refs_8_), channel_id=1, source_target_pairs={{0,129},{1,128},{128,1},{129,0},{2,131},{3,130},{130,3},{131,2},{4... | collective-permute-start | bytes 2752520 | tf_op jit(solution)/shard_map/ppermute | solution.py:350
  21.9 0.5 collective-permute-start.6
  22.4 1.3 %prepare.1 = (bf16[4,512,512]{2,1,0:T(8,128)(2,1)S(1)}, bf16[4,512,64]{2,1,0:T(8,128)(2,1)S(1)}) custom-call(s32[8]{0:T(128)S(1)} %get-tuple-element.41.counts, bf16[128,768]{1,0:T(8,128)(2,1)S(1)} %copy-done.4, bf16[128,768]{1,0:T(8,128)(2,1)S(1)} %collective-permute-done.2.refs_3_.refs_1_, bf16[128,768]{1,0:T(8,128)(2,1)S(1)} %collective-permute-done.3.refs_4_.refs_2_, ...), custom_call_target="tpu_custom_call" | custom-call | tf_op jit(solution)/shard_map/prepare/pallas_call | solution.py:334
  23.7 0.2 collective-permute-done.5.refs_2_
  23.9 0.8 collective-permute-done.6.refs_3_
  24.8 10.6 %attend.3 = (bf16[128,640]{1,0:T(8,128)(2,1)S(1)}, bf16[128,640]{1,0:T(8,128)(2,1)S(1)}, bf16[128,640]{1,0:T(8,128)(2,1)S(1)}) custom-call(s32[64]{0:T(128)S(1)} %get-tuple-element.37.lists, s32[8]{0:T(128)S(1)} %get-tuple-element.41.counts, bf16[4,512,512]{2,1,0:T(8,128)(2,1)S(1)} %get-tuple-element.42.q_lat, ...), custom_call_target="tpu_custom_call" | custom-call | tf_op jit(solution)/shard_map/attend/pallas_call | solution.py:185
  35.4 0.1 collective-permute-start.7
  35.5 0.1 collective-permute-start.8
  35.6 1.9 %collective-permute-start.9 = (bf16[128,640]{1,0:T(8,128)(2,1)S(1)}, bf16[128,640]{1,0:T(8,128)(2,1)S(1)}, u32[]{:S(2)}, u32[]{:S(2)}) collective-permute-start(bf16[128,640]{1,0:T(8,128)(2,1)S(1)} %get-tuple-element.47), channel_id=1, source_target_pairs={{0,96},{32,0},{64,32},{96,64},{1,97},{33,1},{65,33},{97,65},{2,98}... | collective-permute-start | bytes 491528 | tf_op jit(solution)/shard_map/ppermute | solution.py:403
  37.5 2.8 %attend.2.refs_0_ = bf16[128,640]{1,0:T(8,128)(2,1)S(1)} custom-call(s32[64]{0:T(128)S(1)} %get-tuple-element.37.lists, s32[8]{0:T(128)S(1)} %get-tuple-element.41.counts, bf16[4,512,512]{2,1,0:T(8,128)(2,1)S(1)} %get-tuple-element.42.q_lat, bf16[4,512,64]{2,1,0:T(8,128)(2,1)S(1)} %get-tuple-element.43.q_rot, bf16[576,512]{1,0:T(8,128)(2,1)S(1)} %copy-done, ...), custom_call_target="tpu_custom_call" | custom-call | tf_op jit(solution)/shard_map/attend/pallas_call | solution.py:185
  40.3 2.0 %collective-permute-done.7.refs_1_ = bf16[128,640]{1,0:T(8,128)(2,1)S(1)} collective-permute-done((bf16[128,640]{1,0:T(8,128)(2,1)S(1)}, bf16[128,640]{1,0:T(8,128)(2,1)S(1)}, u32[]{:S(2)}, u32[]{:S(2)}) %collective-permute-start.7) | collective-permute-done | bytes 163872 | tf_op jit(solution)/shard_map/ppermute | solution.py:403
  42.3 1.8 %collective-permute-done.8.refs_2_ = bf16[128,640]{1,0:T(8,128)(2,1)S(1)} collective-permute-done((bf16[128,640]{1,0:T(8,128)(2,1)S(1)}, bf16[128,640]{1,0:T(8,128)(2,1)S(1)}, u32[]{:S(2)}, u32[]{:S(2)}) %collective-permute-start.8) | collective-permute-done | bytes 163872 | tf_op jit(solution)/shard_map/ppermute | solution.py:403
  44.1 1.6 %collective-permute-done.9.refs_3_ = bf16[128,640]{1,0:T(8,128)(2,1)S(1)} collective-permute-done((bf16[128,640]{1,0:T(8,128)(2,1)S(1)}, bf16[128,640]{1,0:T(8,128)(2,1)S(1)}, u32[]{:S(2)}, u32[]{:S(2)}) %collective-permute-start.9) | collective-permute-done | bytes 163872 | tf_op jit(solution)/shard_map/ppermute | solution.py:403
  45.7 1.1 %combine.1 = (bf16[32,512]{1,0:T(8,128)(2,1)S(1)}, bf16[32,512]{1,0:T(8,128)(2,1)S(1)}, bf16[32,512]{1,0:T(8,128)(2,1)S(1)}, bf16[32,512]{1,0:T(8,128)(2,1)S(1)}) custom-call(s32[5]{0:T(128)S(1)} %stack.23.ids, bf16[128,640]{1,0:T(8,128)(2,1)S(1)} %attend.2.refs_0_, bf16[128,640]{1,0:T(8,128)(2,1)S(1)} %collective-permute-done.7.refs_1_, ...), custom_call_target="tpu_custom_call" | custom-call | tf_op jit(solution)/shard_map/combine/pallas_call | solution.py:334
  46.8 0.7 collective-permute-start.10
  47.5 1.7 %collective-permute-start.11 = (bf16[32,512]{1,0:T(8,128)(2,1)S(1)}, bf16[32,512]{1,0:T(8,128)(2,1)S(1)}, u32[]{:S(2)}, u32[]{:S(2)}) collective-permute-start(bf16[32,512]{1,0:T(8,128)(2,1)S(1)} %get-tuple-element.50), channel_id=1, source_target_pairs={{0,2},{1,3},{2,0},{3,1},{4,6},{5,7},{6,4},{7,5},{8,10},{9,11},{10,... | collective-permute-start | bytes 98312 | tf_op jit(solution)/shard_map/ppermute | solution.py:350
  49.2 2.7 %collective-permute-start.12 = (bf16[32,512]{1,0:T(8,128)(2,1)S(1)}, bf16[32,512]{1,0:T(8,128)(2,1)S(1)}, u32[]{:S(2)}, u32[]{:S(2)}) collective-permute-start(bf16[32,512]{1,0:T(8,128)(2,1)S(1)} %get-tuple-element.51), channel_id=1, source_target_pairs={{0,3},{1,2},{2,1},{3,0},{4,7},{5,6},{6,5},{7,4},{8,11},{9,10},{10,... | collective-permute-start | bytes 98312 | tf_op jit(solution)/shard_map/ppermute | solution.py:350
  51.9 0.4 collective-permute-done.10.refs_1_
  52.3 0.0 collective-permute-done.11.refs_2_
  52.3 3.2 %collective-permute-done.12.refs_3_ = bf16[32,512]{1,0:T(8,128)(2,1)S(1)} collective-permute-done((bf16[32,512]{1,0:T(8,128)(2,1)S(1)}, bf16[32,512]{1,0:T(8,128)(2,1)S(1)}, u32[]{:S(2)}, u32[]{:S(2)}) %collective-permute-start.12) | collective-permute-done | bytes 32800 | tf_op jit(solution)/shard_map/ppermute | solution.py:350
  55.5 0.0 collective-permute-done.13.refs_1_
  55.6 1.1 %collective-permute-start.16 = (bf16[448,512]{1,0:T(8,128)(2,1)S(1)}, bf16[448,512]{1,0:T(8,128)(2,1)S(1)}, u32[]{:S(2)}, u32[]{:S(2)}) collective-permute-start(bf16[448,512]{1,0:T(8,128)(2,1)S(1)} %slice_bitcast_fusion.1), channel_id=1, source_target_pairs={{0,128},{1,129},{128,0},{129,1},{2,130},{3,131},{130,2},{131,3},{4... | collective-permute-start | bytes 1376264 | tf_op jit(solution)/shard_map/ppermute | solution.py:350
  56.7 2.5 %collective-permute-start.17 = (bf16[448,512]{1,0:T(8,128)(2,1)S(1)}, bf16[448,512]{1,0:T(8,128)(2,1)S(1)}, u32[]{:S(2)}, u32[]{:S(2)}) collective-permute-start(bf16[448,512]{1,0:T(8,128)(2,1)S(1)} %slice_bitcast_fusion), channel_id=1, source_target_pairs={{0,129},{1,128},{128,1},{129,0},{2,131},{3,130},{130,3},{131,2},{4... | collective-permute-start | bytes 1376264 | tf_op jit(solution)/shard_map/ppermute | solution.py:350
  59.2 0.0 collective-permute-start.15
  59.2 2.5 %collective-permute-start.18 = (bf16[32,2048]{1,0:T(8,128)(2,1)S(1)}, bf16[32,2048]{1,0:T(8,128)(2,1)S(1)}, u32[]{:S(2)}, u32[]{:S(2)}) collective-permute-start(bf16[32,2048]{1,0:T(8,128)(2,1)S(1)} %get-tuple-element.53.refs_0_), channel_id=1, source_target_pairs={{64,0},{96,32},{0,64},{32,96},{65,1},{97,33},{1,65},{33,97},{66,2}... | collective-permute-start | bytes 393224 | tf_op jit(solution)/shard_map/ppermute | solution.py:346
  61.7 0.7 collective-permute-start.19
  62.4 4.3 %collective-permute-done.15.refs_0_ = bf16[32,2048]{1,0:T(8,128)(2,1)S(1)} collective-permute-done((bf16[32,2048]{1,0:T(8,128)(2,1)S(1)}, bf16[32,2048]{1,0:T(8,128)(2,1)S(1)}, u32[]{:S(2)}, u32[]{:S(2)}) %collective-permute-start.15) | collective-permute-done | bytes 131104 | tf_op jit(solution)/shard_map/ppermute | solution.py:346
  66.7 0.0 collective-permute-start.20
  66.7 0.5 collective-permute-start.22
  67.3 0.4 collective-permute-done.19.refs_3_
  67.6 0.9 collective-permute-done.17.refs_2_
  68.5 0.5 collective-permute-done.23.refs_7_
  69.0 0.9 collective-permute-done.21.refs_5_
  69.9 1.9 %project.1 = (bf16[64,896]{1,0:T(8,128)(2,1)S(1)}, bf16[64,896]{1,0:T(8,128)(2,1)S(1)}, bf16[64,896]{1,0:T(8,128)(2,1)S(1)}, bf16[64,896]{1,0:T(8,128)(2,1)S(1)}) custom-call(s32[5]{0:T(128)S(1)} %stack.23.ids, bf16[32,2048]{1,0:T(8,128)(2,1)S(1)} %get-tuple-element.53.refs_0_, bf16[32,2048]{1,0:T(8,128)(2,1)S(1)} %get-tuple-element.56.refs_1_, ...), custom_call_target="tpu_custom_call" | custom-call | tf_op jit(solution)/shard_map/project/pallas_call | solution.py:334
  71.8 3.4 %collective-permute-start.24 = (bf16[64,896]{1,0:T(8,128)(2,1)S(1)}, bf16[64,896]{1,0:T(8,128)(2,1)S(1)}, u32[]{:S(2)}, u32[]{:S(2)}) collective-permute-start(bf16[64,896]{1,0:T(8,128)(2,1)S(1)} %get-tuple-element.60), channel_id=1, source_target_pairs={{0,4},{4,0},{8,12},{12,8},{1,5},{5,1},{9,13},{13,9},{2,6},{6,2},{1... | collective-permute-start | bytes 344072 | tf_op jit(solution)/shard_map/ppermute | solution.py:350
  75.1 4.9 %collective-permute-start.25 = (bf16[64,896]{1,0:T(8,128)(2,1)S(1)}, bf16[64,896]{1,0:T(8,128)(2,1)S(1)}, u32[]{:S(2)}, u32[]{:S(2)}) collective-permute-start(bf16[64,896]{1,0:T(8,128)(2,1)S(1)} %get-tuple-element.61), channel_id=1, source_target_pairs={{0,8},{4,12},{8,0},{12,4},{1,9},{5,13},{9,1},{13,5},{2,10},{6,14},... | collective-permute-start | bytes 344072 | tf_op jit(solution)/shard_map/ppermute | solution.py:350
  80.0 1.0 %collective-permute-done.24.refs_1_ = bf16[64,896]{1,0:T(8,128)(2,1)S(1)} collective-permute-done((bf16[64,896]{1,0:T(8,128)(2,1)S(1)}, bf16[64,896]{1,0:T(8,128)(2,1)S(1)}, u32[]{:S(2)}, u32[]{:S(2)}) %collective-permute-start.24) | collective-permute-done | bytes 114720 | tf_op jit(solution)/shard_map/ppermute | solution.py:350
  81.1 7.2 %collective-permute-done.25.refs_2_ = bf16[64,896]{1,0:T(8,128)(2,1)S(1)} collective-permute-done((bf16[64,896]{1,0:T(8,128)(2,1)S(1)}, bf16[64,896]{1,0:T(8,128)(2,1)S(1)}, u32[]{:S(2)}, u32[]{:S(2)}) %collective-permute-start.25) | collective-permute-done | bytes 114720 | tf_op jit(solution)/shard_map/ppermute | solution.py:350
  88.2 2.1 %collective-permute-done.26.refs_3_ = bf16[64,896]{1,0:T(8,128)(2,1)S(1)} collective-permute-done((bf16[64,896]{1,0:T(8,128)(2,1)S(1)}, bf16[64,896]{1,0:T(8,128)(2,1)S(1)}, u32[]{:S(2)}, u32[]{:S(2)}) %collective-permute-start.26) | collective-permute-done | bytes 114720 | tf_op jit(solution)/shard_map/ppermute | solution.py:350
  90.3 0.1 share.1
  90.4 0.1 collective-permute-start.27
  90.5 1.3 %collective-permute-done.27.got = f32[32,896]{1,0:T(8,128)S(1)} collective-permute-done((f32[32,896]{1,0:T(8,128)S(1)}, f32[32,896]{1,0:T(8,128)S(1)}, u32[]{:S(2)}, u32[]{:S(2)}) %collective-permute-start.27) | collective-permute-done | bytes 114720 | tf_op jit(solution)/shard_map/ppermute | solution.py:350
  91.8 1.6 %collective-permute-start.28 = (f32[8,1792]{1,0:T(8,128)S(1)}, f32[8,1792]{1,0:T(8,128)S(1)}, u32[]{:S(2)}, u32[]{:S(2)}) collective-permute-start(f32[8,1792]{1,0:T(8,128)S(1)} %get-tuple-element.66), channel_id=1, source_target_pairs={{0,32},{32,64},{64,96},{96,0},{1,33},{33,65},{65,97},{97,1},{2,34}... | collective-permute-start | bytes 172040 | tf_op jit(solution)/shard_map/ppermute | solution.py:435
  93.4 0.3 collective-permute-start.29
  93.7 0.7 collective-permute-start.30
  94.4 2.0 %collective-permute-done.28.refs_1_ = f32[8,1792]{1,0:T(8,128)S(1)} collective-permute-done((f32[8,1792]{1,0:T(8,128)S(1)}, f32[8,1792]{1,0:T(8,128)S(1)}, u32[]{:S(2)}, u32[]{:S(2)}) %collective-permute-start.28) | collective-permute-done | bytes 57376 | tf_op jit(solution)/shard_map/ppermute | solution.py:435
  96.5 3.0 %collective-permute-done.29.refs_2_ = f32[8,1792]{1,0:T(8,128)S(1)} collective-permute-done((f32[8,1792]{1,0:T(8,128)S(1)}, f32[8,1792]{1,0:T(8,128)S(1)}, u32[]{:S(2)}, u32[]{:S(2)}) %collective-permute-start.29) | collective-permute-done | bytes 57376 | tf_op jit(solution)/shard_map/ppermute | solution.py:435
  99.4 0.2 collective-permute-done.30.refs_3_
  99.7 1.3 %place.1 = bf16[8,7168]{1,0:T(8,128)(2,1)} custom-call(s32[5]{0:T(128)S(1)} %stack.23.ids, f32[8,1792]{1,0:T(8,128)S(1)} %get-tuple-element.65.refs_0_, f32[8,1792]{1,0:T(8,128)S(1)} %collective-permute-done.28.refs_1_, f32[8,1792]{1,0:T(8,128)S(1)} %collective-permute-done.29.refs_2_, f32[8,1792]{1,0:T(8,128)S(1)} %collective-permute-done.30.refs_3_), custom_call_target="tpu_custom_call" | custom-call | tf_op jit(solution)/shard_map/place/pallas_call | solution.py:334
  (34 shorter events, 0.2 us)
Async XLA Ops:
  0.0 18.3 %copy-start.3 = (bf16[512,448]{0,1:T(8,128)(2,1)S(1)}, bf16[512,448]{0,1:T(8,128)(2,1)}, u32[]{:S(2)}) copy-start(bf16[512,448]{0,1:T(8,128)(2,1)} %param.21) | copy-start | bytes 1376260
  0.0 22.4 %copy-start.2 = (bf16[4,128,512]{2,1,0:T(8,128)(2,1)S(1)}, bf16[4,128,512]{2,1,0:T(8,128)(2,1)}, u32[]{:S(2)}) copy-start(bf16[4,128,512]{2,1,0:T(8,128)(2,1)} %refs_4_.3) | copy-start | bytes 1572868
  2.3 19.6 %copy-start = (bf16[576,512]{1,0:T(8,128)(2,1)S(1)}, bf16[576,512]{1,0:T(8,128)(2,1)}, u32[]{:S(2)}) copy-start(bf16[576,512]{1,0:T(8,128)(2,1)} %get-tuple-element.38.refs_0_) | copy-start | bytes 1769476
  2.3 20.1 %copy-start.4 = (bf16[128,768]{1,0:T(8,128)(2,1)S(1)}, bf16[128,768]{1,0:T(8,128)(2,1)}, u32[]{:S(2)}) copy-start(bf16[128,768]{1,0:T(8,128)(2,1)} %get-tuple-element.40.refs_0_) | copy-start | bytes 589828
  2.3 15.9 %collective-permute-start = (bf16[576,512]{1,0:T(8,128)(2,1)}, bf16[576,512]{1,0:T(8,128)(2,1)S(1)}, u32[]{:S(2)}, u32[]{:S(2)}) collective-permute-start(bf16[576,512]{1,0:T(8,128)(2,1)} %get-tuple-element.38.refs_0_), channel_id=1, source_target_pairs={{0,128},{128,0},{1,129},{129,1},{2,130},{130,2},{3,131},{131,3},{4... | collective-permute-start | bytes 1769480 | tf_op jit(solution)/shard_map/ppermute | solution.py:350
  4.0 14.3 %collective-permute-start.1 = (bf16[448,512]{1,0:T(8,128)(2,1)}, bf16[448,512]{1,0:T(8,128)(2,1)S(1)}, u32[]{:S(2)}, u32[]{:S(2)}) collective-permute-start(bf16[448,512]{1,0:T(8,128)(2,1)} %bitcast.11), channel_id=1, source_target_pairs={{0,2},{2,0},{1,3},{3,1},{4,6},{6,4},{5,7},{7,5},{8,10},{10,8},{9,1... | collective-permute-start | bytes 1376264 | tf_op jit(solution)/shard_map/ppermute | solution.py:350
  5.9 11.7 %collective-permute-start.2 = (bf16[128,768]{1,0:T(8,128)(2,1)}, bf16[128,768]{1,0:T(8,128)(2,1)S(1)}, u32[]{:S(2)}, u32[]{:S(2)}) collective-permute-start(bf16[128,768]{1,0:T(8,128)(2,1)} %get-tuple-element.40.refs_0_), channel_id=1, source_target_pairs={{32,0},{64,32},{96,64},{0,96},{33,1},{65,33},{97,65},{1,97},{34,2}... | collective-permute-start | bytes 589832 | tf_op jit(solution)/shard_map/ppermute | solution.py:346
  6.7 10.9 %collective-permute-start.3 = (bf16[128,768]{1,0:T(8,128)(2,1)}, bf16[128,768]{1,0:T(8,128)(2,1)S(1)}, u32[]{:S(2)}, u32[]{:S(2)}) collective-permute-start(bf16[128,768]{1,0:T(8,128)(2,1)} %get-tuple-element.40.refs_0_), channel_id=1, source_target_pairs={{64,0},{96,32},{0,64},{32,96},{65,1},{97,33},{1,65},{33,97},{66,2}... | collective-permute-start | bytes 589832 | tf_op jit(solution)/shard_map/ppermute | solution.py:346
  7.9 10.4 %collective-permute-start.4 = (bf16[128,768]{1,0:T(8,128)(2,1)}, bf16[128,768]{1,0:T(8,128)(2,1)S(1)}, u32[]{:S(2)}, u32[]{:S(2)}) collective-permute-start(bf16[128,768]{1,0:T(8,128)(2,1)} %get-tuple-element.40.refs_0_), channel_id=1, source_target_pairs={{96,0},{0,32},{32,64},{64,96},{97,1},{1,33},{33,65},{65,97},{98,2}... | collective-permute-start | bytes 589832 | tf_op jit(solution)/shard_map/ppermute | solution.py:346
  10.0 0.7 copy-start.7
  10.7 0.7 copy-start.8
  18.3 6.5 %copy-start.1 = (bf16[4,512,128]{2,1,0:T(8,128)(2,1)S(1)}, bf16[4,512,128]{2,1,0:T(8,128)(2,1)}, u32[]{:S(2)}) copy-start(bf16[4,512,128]{2,1,0:T(8,128)(2,1)} %refs_4_.5) | copy-start | bytes 1572868
  18.4 37.2 %collective-permute-start.13 = (bf16[2,448,512]{2,1,0:T(8,128)(2,1)S(1)}, bf16[2,448,512]{2,1,0:T(8,128)(2,1)S(1)}, u32[]{:S(2)}, u32[]{:S(2)}) collective-permute-start(bf16[2,448,512]{2,1,0:T(8,128)(2,1)S(1)} %pair.1.refs_8_), channel_id=1, source_target_pairs={{0,128},{1,129},{128,0},{129,1},{2,130},{3,131},{130,2},{131,3},{4... | collective-permute-start | bytes 2752520 | tf_op jit(solution)/shard_map/ppermute | solution.py:350
  19.4 36.1 %collective-permute-start.14 = (bf16[2,448,512]{2,1,0:T(8,128)(2,1)S(1)}, bf16[2,448,512]{2,1,0:T(8,128)(2,1)S(1)}, u32[]{:S(2)}, u32[]{:S(2)}) collective-permute-start(bf16[2,448,512]{2,1,0:T(8,128)(2,1)S(1)} %pair.1.refs_8_), channel_id=1, source_target_pairs={{0,129},{1,128},{128,1},{129,0},{2,131},{3,130},{130,3},{131,2},{4... | collective-permute-start | bytes 2752520 | tf_op jit(solution)/shard_map/ppermute | solution.py:350
  21.9 2.0 %collective-permute-start.5 = (bf16[576,512]{1,0:T(8,128)(2,1)S(1)}, bf16[576,512]{1,0:T(8,128)(2,1)S(1)}, u32[]{:S(2)}, u32[]{:S(2)}) collective-permute-start(bf16[576,512]{1,0:T(8,128)(2,1)S(1)} %copy-done), channel_id=1, source_target_pairs={{0,16},{16,0},{1,17},{17,1},{2,18},{18,2},{3,19},{19,3},{4,20},{20... | collective-permute-start | bytes 1769480 | tf_op jit(solution)/shard_map/ppermute | solution.py:350
  21.9 2.8 %collective-permute-start.6 = (bf16[576,512]{1,0:T(8,128)(2,1)S(1)}, bf16[576,512]{1,0:T(8,128)(2,1)S(1)}, u32[]{:S(2)}, u32[]{:S(2)}) collective-permute-start(bf16[576,512]{1,0:T(8,128)(2,1)S(1)} %get-tuple-element.44.refs_1_), channel_id=1, source_target_pairs={{0,16},{16,0},{1,17},{17,1},{2,18},{18,2},{3,19},{19,3},{4,20},{20... | collective-permute-start | bytes 1769480 | tf_op jit(solution)/shard_map/ppermute | solution.py:350
  24.8 12.7 %copy-start.5 = (bf16[128,512]{1,0:T(8,128)(2,1)S(1)}, bf16[128,512]{1,0:T(8,128)(2,1)}, u32[]{:S(2)}) copy-start(bf16[128,512]{1,0:T(8,128)(2,1)} %refs_5_.1) | copy-start | bytes 393220
  24.8 12.7 %copy-start.6 = (bf16[1,64,128]{2,1,0:T(8,128)(2,1)S(1)}, bf16[1,64,128]{2,1,0:T(8,128)(2,1)}, u32[]{:S(2)}) copy-start(bf16[1,64,128]{2,1,0:T(8,128)(2,1)} %param.14) | copy-start | bytes 49156
  35.4 6.9 %collective-permute-start.7 = (bf16[128,640]{1,0:T(8,128)(2,1)S(1)}, bf16[128,640]{1,0:T(8,128)(2,1)S(1)}, u32[]{:S(2)}, u32[]{:S(2)}) collective-permute-start(bf16[128,640]{1,0:T(8,128)(2,1)S(1)} %get-tuple-element.45), channel_id=1, source_target_pairs={{0,32},{32,64},{64,96},{96,0},{1,33},{33,65},{65,97},{97,1},{2,34}... | collective-permute-start | bytes 491528 | tf_op jit(solution)/shard_map/ppermute | solution.py:403
  35.5 8.7 %collective-permute-start.8 = (bf16[128,640]{1,0:T(8,128)(2,1)S(1)}, bf16[128,640]{1,0:T(8,128)(2,1)S(1)}, u32[]{:S(2)}, u32[]{:S(2)}) collective-permute-start(bf16[128,640]{1,0:T(8,128)(2,1)S(1)} %get-tuple-element.46), channel_id=1, source_target_pairs={{0,64},{32,96},{64,0},{96,32},{1,65},{33,97},{65,1},{97,33},{2,66}... | collective-permute-start | bytes 491528 | tf_op jit(solution)/shard_map/ppermute | solution.py:403
  35.6 10.1 %collective-permute-start.9 = (bf16[128,640]{1,0:T(8,128)(2,1)S(1)}, bf16[128,640]{1,0:T(8,128)(2,1)S(1)}, u32[]{:S(2)}, u32[]{:S(2)}) collective-permute-start(bf16[128,640]{1,0:T(8,128)(2,1)S(1)} %get-tuple-element.47), channel_id=1, source_target_pairs={{0,96},{32,0},{64,32},{96,64},{1,97},{33,1},{65,33},{97,65},{2,98}... | collective-permute-start | bytes 491528 | tf_op jit(solution)/shard_map/ppermute | solution.py:403
  46.8 5.5 %collective-permute-start.10 = (bf16[32,512]{1,0:T(8,128)(2,1)S(1)}, bf16[32,512]{1,0:T(8,128)(2,1)S(1)}, u32[]{:S(2)}, u32[]{:S(2)}) collective-permute-start(bf16[32,512]{1,0:T(8,128)(2,1)S(1)} %get-tuple-element.49), channel_id=1, source_target_pairs={{0,1},{1,0},{2,3},{3,2},{4,5},{5,4},{6,7},{7,6},{8,9},{9,8},{10,11... | collective-permute-start | bytes 98312 | tf_op jit(solution)/shard_map/ppermute | solution.py:350
  47.5 4.8 %collective-permute-start.11 = (bf16[32,512]{1,0:T(8,128)(2,1)S(1)}, bf16[32,512]{1,0:T(8,128)(2,1)S(1)}, u32[]{:S(2)}, u32[]{:S(2)}) collective-permute-start(bf16[32,512]{1,0:T(8,128)(2,1)S(1)} %get-tuple-element.50), channel_id=1, source_target_pairs={{0,2},{1,3},{2,0},{3,1},{4,6},{5,7},{6,4},{7,5},{8,10},{9,11},{10,... | collective-permute-start | bytes 98312 | tf_op jit(solution)/shard_map/ppermute | solution.py:350
  49.2 6.3 %collective-permute-start.12 = (bf16[32,512]{1,0:T(8,128)(2,1)S(1)}, bf16[32,512]{1,0:T(8,128)(2,1)S(1)}, u32[]{:S(2)}, u32[]{:S(2)}) collective-permute-start(bf16[32,512]{1,0:T(8,128)(2,1)S(1)} %get-tuple-element.51), channel_id=1, source_target_pairs={{0,3},{1,2},{2,1},{3,0},{4,7},{5,6},{6,5},{7,4},{8,11},{9,10},{10,... | collective-permute-start | bytes 98312 | tf_op jit(solution)/shard_map/ppermute | solution.py:350
  55.6 12.1 %collective-permute-start.16 = (bf16[448,512]{1,0:T(8,128)(2,1)S(1)}, bf16[448,512]{1,0:T(8,128)(2,1)S(1)}, u32[]{:S(2)}, u32[]{:S(2)}) collective-permute-start(bf16[448,512]{1,0:T(8,128)(2,1)S(1)} %slice_bitcast_fusion.1), channel_id=1, source_target_pairs={{0,128},{1,129},{128,0},{129,1},{2,130},{3,131},{130,2},{131,3},{4... | collective-permute-start | bytes 1376264 | tf_op jit(solution)/shard_map/ppermute | solution.py:350
  56.7 11.8 %collective-permute-start.17 = (bf16[448,512]{1,0:T(8,128)(2,1)S(1)}, bf16[448,512]{1,0:T(8,128)(2,1)S(1)}, u32[]{:S(2)}, u32[]{:S(2)}) collective-permute-start(bf16[448,512]{1,0:T(8,128)(2,1)S(1)} %slice_bitcast_fusion), channel_id=1, source_target_pairs={{0,129},{1,128},{128,1},{129,0},{2,131},{3,130},{130,3},{131,2},{4... | collective-permute-start | bytes 1376264 | tf_op jit(solution)/shard_map/ppermute | solution.py:350
  59.2 7.6 %collective-permute-start.15 = (bf16[32,2048]{1,0:T(8,128)(2,1)S(1)}, bf16[32,2048]{1,0:T(8,128)(2,1)S(1)}, u32[]{:S(2)}, u32[]{:S(2)}) collective-permute-start(bf16[32,2048]{1,0:T(8,128)(2,1)S(1)} %get-tuple-element.53.refs_0_), channel_id=1, source_target_pairs={{32,0},{64,32},{96,64},{0,96},{33,1},{65,33},{97,65},{1,97},{34,2}... | collective-permute-start | bytes 393224 | tf_op jit(solution)/shard_map/ppermute | solution.py:346
  59.2 7.6 %collective-permute-start.18 = (bf16[32,2048]{1,0:T(8,128)(2,1)S(1)}, bf16[32,2048]{1,0:T(8,128)(2,1)S(1)}, u32[]{:S(2)}, u32[]{:S(2)}) collective-permute-start(bf16[32,2048]{1,0:T(8,128)(2,1)S(1)} %get-tuple-element.53.refs_0_), channel_id=1, source_target_pairs={{64,0},{96,32},{0,64},{32,96},{65,1},{97,33},{1,65},{33,97},{66,2}... | collective-permute-start | bytes 393224 | tf_op jit(solution)/shard_map/ppermute | solution.py:346
  61.7 5.9 %collective-permute-start.19 = (bf16[32,2048]{1,0:T(8,128)(2,1)S(1)}, bf16[32,2048]{1,0:T(8,128)(2,1)S(1)}, u32[]{:S(2)}, u32[]{:S(2)}) collective-permute-start(bf16[32,2048]{1,0:T(8,128)(2,1)S(1)} %get-tuple-element.53.refs_0_), channel_id=1, source_target_pairs={{96,0},{0,32},{32,64},{64,96},{97,1},{1,33},{33,65},{65,97},{98,2}... | collective-permute-start | bytes 393224 | tf_op jit(solution)/shard_map/ppermute | solution.py:346
  66.7 1.8 %collective-permute-start.20 = (bf16[32,2048]{1,0:T(8,128)(2,1)S(1)}, bf16[32,2048]{1,0:T(8,128)(2,1)S(1)}, u32[]{:S(2)}, u32[]{:S(2)}) collective-permute-start(bf16[32,2048]{1,0:T(8,128)(2,1)S(1)} %get-tuple-element.53.refs_0_), channel_id=1, source_target_pairs={{0,16},{16,0},{1,17},{17,1},{2,18},{18,2},{3,19},{19,3},{4,20},{20... | collective-permute-start | bytes 393224 | tf_op jit(solution)/shard_map/ppermute | solution.py:350
  66.7 1.8 %collective-permute-start.22 = (bf16[32,2048]{1,0:T(8,128)(2,1)S(1)}, bf16[32,2048]{1,0:T(8,128)(2,1)S(1)}, u32[]{:S(2)}, u32[]{:S(2)}) collective-permute-start(bf16[32,2048]{1,0:T(8,128)(2,1)S(1)} %collective-permute-done.18.refs_2_), channel_id=1, source_target_pairs={{0,16},{16,0},{1,17},{17,1},{2,18},{18,2},{3,19},{19,3},{4,20},{20... | collective-permute-start | bytes 393224 | tf_op jit(solution)/shard_map/ppermute | solution.py:350
  67.6 1.3 %collective-permute-start.23 = (bf16[32,2048]{1,0:T(8,128)(2,1)S(1)}, bf16[32,2048]{1,0:T(8,128)(2,1)S(1)}, u32[]{:S(2)}, u32[]{:S(2)}) collective-permute-start(bf16[32,2048]{1,0:T(8,128)(2,1)S(1)} %collective-permute-done.19.refs_3_), channel_id=1, source_target_pairs={{0,16},{16,0},{1,17},{17,1},{2,18},{18,2},{3,19},{19,3},{4,20},{20... | collective-permute-start | bytes 393224 | tf_op jit(solution)/shard_map/ppermute | solution.py:350
  68.5 1.3 %collective-permute-start.21 = (bf16[32,2048]{1,0:T(8,128)(2,1)S(1)}, bf16[32,2048]{1,0:T(8,128)(2,1)S(1)}, u32[]{:S(2)}, u32[]{:S(2)}) collective-permute-start(bf16[32,2048]{1,0:T(8,128)(2,1)S(1)} %get-tuple-element.56.refs_1_), channel_id=1, source_target_pairs={{0,16},{16,0},{1,17},{17,1},{2,18},{18,2},{3,19},{19,3},{4,20},{20... | collective-permute-start | bytes 393224 | tf_op jit(solution)/shard_map/ppermute | solution.py:350
  71.8 9.3 %collective-permute-start.24 = (bf16[64,896]{1,0:T(8,128)(2,1)S(1)}, bf16[64,896]{1,0:T(8,128)(2,1)S(1)}, u32[]{:S(2)}, u32[]{:S(2)}) collective-permute-start(bf16[64,896]{1,0:T(8,128)(2,1)S(1)} %get-tuple-element.60), channel_id=1, source_target_pairs={{0,4},{4,0},{8,12},{12,8},{1,5},{5,1},{9,13},{13,9},{2,6},{6,2},{1... | collective-permute-start | bytes 344072 | tf_op jit(solution)/shard_map/ppermute | solution.py:350
  75.1 13.1 %collective-permute-start.25 = (bf16[64,896]{1,0:T(8,128)(2,1)S(1)}, bf16[64,896]{1,0:T(8,128)(2,1)S(1)}, u32[]{:S(2)}, u32[]{:S(2)}) collective-permute-start(bf16[64,896]{1,0:T(8,128)(2,1)S(1)} %get-tuple-element.61), channel_id=1, source_target_pairs={{0,8},{4,12},{8,0},{12,4},{1,9},{5,13},{9,1},{13,5},{2,10},{6,14},... | collective-permute-start | bytes 344072 | tf_op jit(solution)/shard_map/ppermute | solution.py:350
  80.0 10.3 %collective-permute-start.26 = (bf16[64,896]{1,0:T(8,128)(2,1)S(1)}, bf16[64,896]{1,0:T(8,128)(2,1)S(1)}, u32[]{:S(2)}, u32[]{:S(2)}) collective-permute-start(bf16[64,896]{1,0:T(8,128)(2,1)S(1)} %get-tuple-element.62), channel_id=1, source_target_pairs={{0,12},{4,8},{8,4},{12,0},{1,13},{5,9},{9,5},{13,1},{2,14},{6,10},... | collective-permute-start | bytes 344072 | tf_op jit(solution)/shard_map/ppermute | solution.py:350
  90.4 1.4 %collective-permute-start.27 = (f32[32,896]{1,0:T(8,128)S(1)}, f32[32,896]{1,0:T(8,128)S(1)}, u32[]{:S(2)}, u32[]{:S(2)}) collective-permute-start(f32[32,896]{1,0:T(8,128)S(1)} %get-tuple-element.64), channel_id=1, source_target_pairs={{0,16},{16,0},{1,17},{17,1},{2,18},{18,2},{3,19},{19,3},{4,20},{20... | collective-permute-start | bytes 344072 | tf_op jit(solution)/shard_map/ppermute | solution.py:350
  91.8 4.7 %collective-permute-start.28 = (f32[8,1792]{1,0:T(8,128)S(1)}, f32[8,1792]{1,0:T(8,128)S(1)}, u32[]{:S(2)}, u32[]{:S(2)}) collective-permute-start(f32[8,1792]{1,0:T(8,128)S(1)} %get-tuple-element.66), channel_id=1, source_target_pairs={{0,32},{32,64},{64,96},{96,0},{1,33},{33,65},{65,97},{97,1},{2,34}... | collective-permute-start | bytes 172040 | tf_op jit(solution)/shard_map/ppermute | solution.py:435
  93.4 6.1 %collective-permute-start.29 = (f32[8,1792]{1,0:T(8,128)S(1)}, f32[8,1792]{1,0:T(8,128)S(1)}, u32[]{:S(2)}, u32[]{:S(2)}) collective-permute-start(f32[8,1792]{1,0:T(8,128)S(1)} %get-tuple-element.67), channel_id=1, source_target_pairs={{0,64},{32,96},{64,0},{96,32},{1,65},{33,97},{65,1},{97,33},{2,66}... | collective-permute-start | bytes 172040 | tf_op jit(solution)/shard_map/ppermute | solution.py:435
  93.7 6.0 %collective-permute-start.30 = (f32[8,1792]{1,0:T(8,128)S(1)}, f32[8,1792]{1,0:T(8,128)S(1)}, u32[]{:S(2)}, u32[]{:S(2)}) collective-permute-start(f32[8,1792]{1,0:T(8,128)S(1)} %get-tuple-element.68), channel_id=1, source_target_pairs={{0,96},{32,0},{64,32},{96,64},{1,97},{33,1},{65,33},{97,65},{2,98}... | collective-permute-start | bytes 172040 | tf_op jit(solution)/shard_map/ppermute | solution.py:435
